TPU v7x, 32 devices: a whole 2x2x4 slice. The times are simulated.
32 devices in a mesh: inst: 8 (over z, y), feat: 4 (over x, core).
Axes of the slice: x: 2, y: 2, z: 4, core: 2. Of those that a mesh axis runs over, the one named last changes fastest.
Arguments:
- values: bfloat16 [128, 32, 128, 128], P('inst', 'feat'), may hold values from -0.5 to 0.5
- columns: int32 [128, 32], P('inst', 'feat'), may hold values from 0 to 2047
- live_slots: int32 [128, 4], P('inst', 'feat'), may hold values from 1 to 8, as said below
- labels: int32 [16384], P('inst'), may hold values 0 or 1
- weights: float32 [8192, 128], P('feat'), may hold values from -0.75 to 0.75
Outputs:
- step_vector: float32 [8192, 128], P(('feat', 'inst'))
- gradient: float32 [8192, 128], P(('feat', 'inst'))
Inputs may be any that keep to these rules, and one draw needn't show every extreme that they name: Slot j of tile t in feature group g is used when j < live_slots[t, g]; in every draw some tile has 8 used slots in every group. `columns`: block of a slot counted within its feature group's 2048 blocks; slots of one tile may name the same block.
All inputs are finite; a program needn't handle non-finite values. No bound on the sum of `labels` on one device may be relied on, other than what follows from the above.
Results may differ from a plain program's by a relative error of at most 0.0033.
Values sent between devices are 32-bit elements; how exact they have to be, the bound alone decides.
No kernel may reach another device: no remote copies, remote signals or barrier semaphores. Data moves between devices by JAX's collectives and lax.ppermute only.
A program may use at most 64 MiB of HBM per device.

v0:
```python
import jax
import jax.numpy as jnp
from jax import lax
from jax.sharding import PartitionSpec as P

ITERS = 2


def per_device(values, columns, live_slots, labels, weights):
    tile_count, slot_count, tile_rows, width = values.shape
    block_count = weights.shape[0]
    share = block_count // lax.axis_size("inst")
    offset = lax.axis_index("inst") * share
    slot_mask = (lax.broadcasted_iota(jnp.int32, (tile_count, slot_count), 1) < live_slots).astype(
        jnp.float32
    )

    def forward(vector):
        picked = (vector[columns] * slot_mask[:, :, None]).astype(jnp.bfloat16)
        partial_value = jnp.einsum(
            "tjrf,tjf->tr", values, picked, preferred_element_type=jnp.float32
        ).reshape(-1)
        return lax.psum(partial_value, "feat")

    def local_back(rows_term):
        rows_half = rows_term.astype(jnp.bfloat16).reshape(tile_count, tile_rows)
        contrib = jnp.einsum("tjrf,tr->tjf", values, rows_half, preferred_element_type=jnp.float32)
        contrib = contrib * slot_mask[:, :, None]
        return jax.ops.segment_sum(
            contrib.reshape(-1, width), columns.reshape(-1), num_segments=block_count
        )

    def collect(term):
        return lax.psum(term, "inst")

    def inner(value):
        return lax.psum(value, "feat")

    margin = forward(weights)
    prob = jax.nn.sigmoid(margin)
    curvature = prob * (1.0 - prob)
    gradient = weights + collect(local_back(prob - labels.astype(jnp.float32)))
    residual = -gradient
    direction = residual
    step_vector = jnp.zeros_like(gradient)
    norm_now = inner(jnp.sum(residual * residual))
    for turn_index in range(ITERS):
        along = forward(direction)
        image = direction + collect(local_back(curvature * along))
        alpha = norm_now / inner(jnp.sum(direction * image))
        step_vector = step_vector + alpha * direction
        if turn_index + 1 < ITERS:
            residual = residual - alpha * image
            norm_next = inner(jnp.sum(residual * residual))
            direction = residual + norm_next / norm_now * direction
            norm_now = norm_next
    step_vector = lax.dynamic_slice_in_dim(step_vector, offset, share, 0)
    gradient = lax.dynamic_slice_in_dim(gradient, offset, share, 0)
    return (step_vector, gradient)


def solution(mesh):
    in_specs = (
        P("inst", "feat", None, None),
        P("inst", "feat"),
        P("inst", "feat"),
        P("inst"),
        P("feat", None),
    )
    out_specs = (P(("feat", "inst"), None), P(("feat", "inst"), None))
    return jax.shard_map(
        per_device, mesh=mesh, in_specs=in_specs, out_specs=out_specs, check_vma=False
    )
```

profile of v0, /device:TPU:0, one launch (start us, length us, event | category | flops | bytes accessed | tf_op | source)
XLA Modules:
  0.0 332.9 jit_solution(13411470783333228266)
XLA Ops:
  7.2 0.7 compare_select_fusion
  7.9 0.8 copy.9
  8.7 0.1 reshape.63
  8.8 0.7 fusion.35
  9.7 1.9 gather_fusion
  11.6 3.4 %fusion.18 = f32[16,1,128,1]{2,1,3,0:T(1,128)S(1)} fusion(bf16[16,8,128,128]{3,2,1,0:T(8,128)(2,1)} %param.5, bf16[16,8,128,1]{2,1,0,3:T(8,128)(2,1)S(1)} %fusion.23), kind=kOutput, calls=%fused_computation.35 | convolution fusion | flops 4194304 | bytes 4235264 | tf_op jit(solution)/shard_map/tjrf,tjf->tr/dot_general | solution.py:20
  15.0 8.6 %psum.70 = f32[2048]{0:T(1024)S(1)} all-reduce(f32[2048]{0:T(1024)S(1)} %bitcast.76), channel_id=1, replica_groups=mesh['inst'=8,'feat'=4] {'feat'}, use_global_device_ids=true, to_apply=%region_0.0 | all-reduce | flops 2048 | bytes 16384 | tf_op jit(solution)/shard_map/psum | solution.py:23
  23.6 2.8 fusion.33
  26.5 2.1 scatter_custom_fusion
  28.7 78.4 %all-reduce.5.cloned.1.call-done = f32[2048,128]{1,0:T(8,128)} async-done(((f32[2048,128]{1,0:T(8,128)}), f32[2048,128]{1,0:T(8,128)}) %all-reduce.5.cloned.1.call-update) | async-done | bytes 1048592 | tf_op jit(solution)/shard_map/psum | solution.py:34
  107.1 1.4 fusion.39
  108.5 0.6 gather_fusion.1
  109.2 3.4 %fusion.16 = f32[16,1,128,1]{2,1,3,0:T(1,128)S(1)} fusion(bf16[16,8,128,128]{3,2,1,0:T(8,128)(2,1)} %param.5, bf16[16,8,128,1]{2,1,0,3:T(8,128)(2,1)S(1)} %fusion.24), kind=kOutput, calls=%fused_computation.33 | convolution fusion | flops 4194304 | bytes 4235264 | tf_op jit(solution)/shard_map/tjrf,tjf->tr/dot_general | solution.py:20
  112.6 6.0 %psum.73 = f32[2048]{0:T(1024)S(1)} all-reduce(f32[2048]{0:T(1024)S(1)} %bitcast.77), channel_id=1, replica_groups=mesh['inst'=8,'feat'=4] {'feat'}, use_global_device_ids=true, to_apply=%region_5.0 | all-reduce | flops 2048 | bytes 16384 | tf_op jit(solution)/shard_map/psum | solution.py:23
  118.6 2.8 fusion.31
  121.4 2.1 scatter_custom_fusion.1
  123.6 77.8 %all-reduce.7.cloned.1.call-done = f32[2048,128]{1,0:T(8,128)} async-done(((f32[2048,128]{1,0:T(8,128)}), f32[2048,128]{1,0:T(8,128)}) %all-reduce.7.cloned.1.call-update) | async-done | bytes 1048592 | tf_op jit(solution)/shard_map/psum | solution.py:34
  201.4 2.2 multiply_reduce_fusion.1
  203.5 6.5 %all-reduce = (f32[]{:T(128)}, f32[]{:T(128)}) all-reduce(f32[]{:T(128)} %get-tuple-element.3, f32[]{:T(128)} %get-tuple-element.2), channel_id=1, replica_groups=mesh['inst'=8,'feat'=4] {'feat'}, use_global_device_ids=true, to_apply=%region_4.0 | all-reduce | flops 2 | bytes 16 | tf_op jit(solution)/shard_map/psum | solution.py:37
  211.4 2.1 multiply_reduce_fusion
  213.5 6.9 %psum.76 = f32[]{:T(128)} all-reduce(f32[]{:T(128)} %multiply_reduce_fusion), channel_id=1, replica_groups=mesh['inst'=8,'feat'=4] {'feat'}, use_global_device_ids=true, to_apply=%region_11.0 | all-reduce | flops 1 | bytes 8 | tf_op jit(solution)/shard_map/psum | solution.py:37
  221.7 0.2 multiply_add_fusion
  221.9 0.6 gather_fusion.2
  222.6 3.4 %fusion.14 = f32[16,1,128,1]{2,1,3,0:T(1,128)S(1)} fusion(bf16[16,8,128,128]{3,2,1,0:T(8,128)(2,1)} %param.5, bf16[16,8,128,1]{2,1,0,3:T(8,128)(2,1)S(1)} %fusion.25), kind=kOutput, calls=%fused_computation.31 | convolution fusion | flops 4194304 | bytes 4235264 | tf_op jit(solution)/shard_map/tjrf,tjf->tr/dot_general | solution.py:20
  226.0 6.0 %psum.77 = f32[2048]{0:T(1024)S(1)} all-reduce(f32[2048]{0:T(1024)S(1)} %bitcast.78), channel_id=1, replica_groups=mesh['inst'=8,'feat'=4] {'feat'}, use_global_device_ids=true, to_apply=%region_12.0 | all-reduce | flops 2048 | bytes 16384 | tf_op jit(solution)/shard_map/psum | solution.py:23
  232.0 2.8 fusion.29
  234.9 2.1 scatter_custom_fusion.2
  237.0 77.3 %all-reduce.9.cloned.1.call-done = f32[2048,128]{1,0:T(8,128)} async-done(((f32[2048,128]{1,0:T(8,128)}), f32[2048,128]{1,0:T(8,128)}) %all-reduce.9.cloned.1.call-update) | async-done | bytes 1048592 | tf_op jit(solution)/shard_map/psum | solution.py:34
  314.3 2.1 fusion
  316.4 0.7 constant_dynamic-slice_fusion
  317.1 6.5 %psum.79 = f32[]{:T(128)} all-reduce(f32[]{:T(128)} %fusion), channel_id=1, replica_groups=mesh['inst'=8,'feat'=4] {'feat'}, use_global_device_ids=true, to_apply=%region_16.0 | all-reduce | flops 1 | bytes 8 | tf_op jit(solution)/shard_map/psum | solution.py:37
  324.8 1.6 fusion.7
  (23 shorter events, 0.6 us)
Async XLA Ops:
  7.2 16.4 %copy-start.3 = (s32[2048]{0:T(1024)S(1)}, s32[2048]{0:T(1024)}, u32[]{:S(2)}) copy-start(s32[2048]{0:T(1024)} %param.8) | copy-start | bytes 24580
  7.2 99.9 %all-reduce.5.cloned.1.call-start = ((), (), s32[]{:S(2)}) async-start(), calls=%async_computation | async-start | bytes 2097152 | tf_op jit(solution)/shard_map/psum | solution.py:34
  15.0 92.1 %copy-start.2 = (f32[2048,128]{1,0:T(8,128)S(1)}, f32[2048,128]{1,0:T(8,128)}, u32[]{:S(2)}) copy-start(f32[2048,128]{1,0:T(8,128)} %param.9) | copy-start | bytes 3145732
  28.6 172.7 %all-reduce.7.cloned.1.call-start = ((), (), s32[]{:S(2)}) async-start(), calls=%async_computation.1 | async-start | bytes 2097152 | tf_op jit(solution)/shard_map/psum | solution.py:34
  108.5 13.0 %copy-start.1 = (f32[2048,128]{1,0:T(8,128)}, f32[2048,128]{1,0:T(8,128)S(1)}, u32[]{:S(2)}) copy-start(f32[2048,128]{1,0:T(8,128)S(1)} %get-tuple-element.6) | copy-start | bytes 3145732
  123.6 190.8 %all-reduce.9.cloned.1.call-start = ((), (), s32[]{:S(2)}) async-start(), calls=%async_computation.2 | async-start | bytes 2097152 | tf_op jit(solution)/shard_map/psum | solution.py:34
  201.4 20.3 %copy-start = (f32[2048,128]{1,0:T(8,128)S(1)}, f32[2048,128]{1,0:T(8,128)}, u32[]{:S(2)}) copy-start(f32[2048,128]{1,0:T(8,128)} %all-reduce.7.cloned.1.call-done) | copy-start | bytes 3145732
Sparse Core Ops, SparseCore 0:
  28.8 78.2 all-reduce.4
  123.7 77.6 all-reduce.6
  237.1 77.1 all-reduce.8
where the time goes:
time: 334 us; the launch traced here: 333 us
  waiting for transfers between devices  234 us (70%)
  blocking collectives  40.5 us (12%)
  matrix products  18.6 us (6%)
  between operations  17.7 us (5%)
  other arithmetic  17.6 us (5%)
  local copies, waits for them, and re-layouts  4.84 us (1%)
    psum x3, waiting for transfers between devices, collect(): return lax.psum(term, 'inst')  233 us
    psum x3, blocking collectives, forward(): return lax.psum(partial_value, 'feat')  20.6 us
    psum x3, blocking collectives, inner(): return lax.psum(value, 'feat')  19.9 us
    dot_general x3, matrix products, forward(): jnp.einsum('tjrf,tjf->tr', values, picked, preferred_element_type=jnp.flo...  10.1 us
    dot_general x3, matrix products, local_back(): jnp.einsum('tjrf,tr->tjf', values, rows_half, preferred_element_type=jnp....  8.52 us
  transfers between devices with their start and end apart: 3, of which 3 were waited for; matrix products, arithmetic and copies ran while one was open for 0% of the time, Pallas kernels for 0%

commit v1 on v0

v1 whole, which is shorter than its diff:
```python
import jax
import jax.numpy as jnp
from jax import lax
from jax.sharding import PartitionSpec as P


def split_halves(array):
    high = array.astype(jnp.bfloat16)
    low = (array - high.astype(jnp.float32)).astype(jnp.bfloat16)
    return high, low


def pick_sum(onehot, array):
    high, low = split_halves(array)
    both = jnp.dot(
        onehot, jnp.concatenate([high, low], axis=1), preferred_element_type=jnp.float32
    )
    width = array.shape[1]
    return both[:, :width] + both[:, width:]


def swap(array, axis, distance):
    size = lax.axis_size(axis)
    return lax.ppermute(array, axis, [(i, i ^ distance) for i in range(size)])


def feat_parts(array):
    size = lax.axis_size("feat")
    return [array] + [
        lax.ppermute(array, "feat", [(i, (i + k) % size) for i in range(size)])
        for k in range(1, size)
    ]


def feat_sum(array):
    parts = feat_parts(array)
    total = parts[0]
    for part in parts[1:]:
        total = total + part
    return total


def inst_parts(array):
    size = lax.axis_size("inst")
    if size != 8:
        gathered = lax.all_gather(array, "inst", axis=0)
        return [gathered[i] for i in range(size)]
    parts = [array] + [swap(array, "inst", k) for k in (2, 4, 6)]
    return parts + [swap(part, "inst", 1) for part in parts]


def inst_sum(array):
    size = lax.axis_size("inst")
    distance = 1
    while distance < size:
        array = array + swap(array, "inst", distance)
        distance *= 2
    return array


def per_device(values, columns, live_slots, labels, weights):
    tiles, slots, rows, width = values.shape
    block_count = weights.shape[0]
    share = block_count // lax.axis_size("inst")
    offset = lax.axis_index("inst") * share
    live = lax.broadcasted_iota(jnp.int32, (tiles, slots), 1) < live_slots
    mask = live.astype(jnp.float32).reshape(-1, 1)
    own_ids = jnp.where(live, columns, -2).reshape(-1)
    sent_ids = jnp.where(live, columns, -1).reshape(1, -1).astype(jnp.float32)
    slot_count = tiles * slots

    def forward(picked):
        return jnp.einsum(
            "tjrf,tjf->tr",
            values,
            picked.astype(jnp.bfloat16).reshape(tiles, slots, width),
            preferred_element_type=jnp.float32,
        )

    def back(rows_term):
        out = jnp.einsum(
            "tjrf,tr->tjf",
            values,
            rows_term.astype(jnp.bfloat16),
            preferred_element_type=jnp.float32,
        )
        return out.reshape(slot_count, width) * mask

    def scalar_row(*scalars):
        lane = lax.broadcasted_iota(jnp.int32, (8, width), 1)
        row = jnp.zeros((8, width), jnp.float32)
        for place, scalar in enumerate(scalars):
            row = jnp.where(lane == place, scalar, row)
        return row

    weights_slot = weights[columns.reshape(-1)] * mask
    weights_share = lax.dynamic_slice_in_dim(weights, offset, share, 0)

    margin = feat_sum(forward(weights_slot))
    prob = jax.nn.sigmoid(margin)
    curvature = prob * (1.0 - prob)
    first = back(prob - labels.astype(jnp.float32).reshape(tiles, rows))

    ids_block = jnp.broadcast_to(sent_ids.reshape(-1, width), (8, width))
    parts = inst_parts(jnp.concatenate([first, ids_block], axis=0))
    all_ids = jnp.concatenate([p[slot_count] for p in parts]).astype(jnp.int32)
    wanted = jnp.concatenate([own_ids, offset + jnp.arange(share, dtype=jnp.int32)])
    onehot = (wanted[:, None] == all_ids[None, :]).astype(jnp.bfloat16)
    summed = pick_sum(onehot, jnp.concatenate([p[:slot_count] for p in parts], axis=0))
    start_slot = -(weights_slot + summed[:slot_count])
    gradient = weights_share + summed[slot_count:]
    start_share = -gradient

    along_part = forward(start_slot)
    total = feat_sum(
        jnp.concatenate([along_part, scalar_row(jnp.sum(gradient * gradient))], axis=0)
    )
    along = total[:tiles]
    norm_part = total[tiles, 0]
    curved = curvature * along
    second = back(curved)
    extra = scalar_row(norm_part, jnp.sum(curved * along))
    parts = inst_parts(jnp.concatenate([second, extra], axis=0))
    summed = pick_sum(onehot, jnp.concatenate([p[:slot_count] for p in parts], axis=0))
    scalars = sum(p[slot_count] for p in parts)
    norm_now = scalars[0]
    curve_now = scalars[1]
    alpha = norm_now / (norm_now + curve_now)
    next_slot = start_slot - alpha * (start_slot + summed[:slot_count])
    next_share = start_share - alpha * (start_share + summed[slot_count:])
    total = feat_sum(
        jnp.concatenate(
            [
                forward(next_slot),
                scalar_row(jnp.sum(next_share * next_share), jnp.sum(next_share * start_share)),
            ],
            axis=0,
        )
    )
    turn = total[:tiles]
    scalars = inst_sum(
        scalar_row(
            total[tiles, 0],
            total[tiles, 1],
            jnp.sum(curvature * turn * turn),
            jnp.sum(curvature * turn * along),
        )
    )
    norm_next, cross, turn_turn, turn_along = (scalars[0, i] for i in range(4))
    ratio = norm_next / norm_now
    bottom = (
        norm_next
        + 2.0 * ratio * cross
        + ratio * ratio * norm_now
        + turn_turn
        + 2.0 * ratio * turn_along
        + ratio * ratio * curve_now
    )
    alpha_next = norm_next / bottom
    step = alpha * start_share + alpha_next * (next_share + ratio * start_share)
    return (step, gradient)


def solution(mesh):
    in_specs = (
        P("inst", "feat", None, None),
        P("inst", "feat"),
        P("inst", "feat"),
        P("inst"),
        P("feat", None),
    )
    out_specs = (P(("feat", "inst"), None), P(("feat", "inst"), None))
    return jax.shard_map(
        per_device, mesh=mesh, in_specs=in_specs, out_specs=out_specs, check_vma=False
    )
```

time: 334 us -> 98.2 us (0.29)
  waiting for transfers between devices: 234 us -> 28.6 us
  blocking collectives: 40.5 us -> 0 us
  starting transfers between devices: 0.12 us -> 26.2 us
  between operations: 17.7 us -> 9.2 us
  matrix products: 18.6 us -> 12.4 us
    psum x3 -> x0, waiting for transfers between devices: 233 us -> none  [collect(): return lax.psum(term, 'inst')]
    psum x6 -> x0, blocking collectives: 40.5 us -> none  [the longest x3 20.6 us: forward(): return lax.psum(partial_value, 'feat')]
    ppermute x0 -> x26, waiting for transfers between devices: none -> 28.6 us  [the longest x17 20.9 us: swap(): return lax.ppermute(array, axis, [(i, i ^ distance) for i in range(size)])]
    ppermute x0 -> x26, starting transfers between devices: none -> 26.2 us  [the longest x17 19.9 us: swap(): return lax.ppermute(array, axis, [(i, i ^ distance) for i in range(size)])]
    scatter-add x3 -> x0, other arithmetic: 6.33 us -> none  [local_back(): jax.ops.segment_sum(contrib.reshape(-1, width), columns.reshape(-1), num_...]
    dot_general x6 -> x7, matrix products: 18.6 us -> 12.4 us  [the longest x3 7.92 us: forward(): jnp.einsum('tjrf,tjf->tr', values, picked.astype(jnp.bfloat16).reshape(ti...]
    select_n x1 -> x9, other arithmetic: 0.69 us -> 5.9 us  [the longest x7 5.89 us: scalar_row(): row = jnp.where(lane == place, scalar, row)]
  transfers between devices with their start and end apart: 3 -> 26, of which waited for: 3 -> 15; matrix products, arithmetic and copies ran while one was open for 0% -> 1% of each run, Pallas kernels for 0% -> 0%
where the time goes in v1:
time: 98.2 us; the launch traced here: 97.6 us
  waiting for transfers between devices  28.6 us (29%)
  starting transfers between devices  26.2 us (27%)
  other arithmetic  15.5 us (16%)
  matrix products  12.4 us (13%)
  between operations  9.2 us (9%)
  local copies, waits for them, and re-layouts  5.75 us (6%)
    ppermute x17, waiting for transfers between devices, swap(): return lax.ppermute(array, axis, [(i, i ^ distance) for i in range(size)])  20.9 us
    ppermute x17, starting transfers between devices, swap(): return lax.ppermute(array, axis, [(i, i ^ distance) for i in range(size)])  19.9 us
    dot_general x3, matrix products, forward(): jnp.einsum('tjrf,tjf->tr', values, picked.astype(jnp.bfloat16).reshape(ti...  7.92 us
    ppermute x9, waiting for transfers between devices, feat_parts(): lax.ppermute(array, 'feat', [(i, (i + k) % size) for i in range(size)])  7.74 us
    ppermute x9, starting transfers between devices, feat_parts(): lax.ppermute(array, 'feat', [(i, (i + k) % size) for i in range(size)])  6.23 us
    select_n x7, other arithmetic, scalar_row(): row = jnp.where(lane == place, scalar, row)  5.89 us
    add x3, other arithmetic, inst_sum(): array = array + swap(array, 'inst', distance)  3.87 us
    dot_general x2, matrix products, back(): jnp.einsum('tjrf,tr->tjf', values, rows_term.astype(jnp.bfloat16), prefer...  3.64 us
  transfers between devices with their start and end apart: 26, of which 15 were waited for; matrix products, arithmetic and copies ran while one was open for 1% of the time, Pallas kernels for 0%

profile of v1, /device:TPU:0, one launch (start us, length us, event | category | flops | bytes accessed | tf_op | source)
XLA Modules:
  0.0 97.6 jit_solution(18169919218494601672)
XLA Ops:
  2.3 1.9 %gather_fusion = f32[128,128]{1,0:T(8,128)S(1)} fusion(f32[2048,128]{1,0:T(8,128)} %param.9, s32[1024]{0:T(1024)S(1)} %pad_clamp_fusion), kind=kCustom, calls=%fused_computation | custom fusion | bytes 131584 | tf_op jit(solution)/shard_map/gather | solution.py:96
  4.3 3.4 %fusion.25 = f32[16,1,128,1]{2,1,3,0:T(1,128)S(1)} fusion(bf16[16,8,128,128]{3,2,1,0:T(8,128)(2,1)} %param.5, bf16[16,8,128,1]{2,1,0,3:T(8,128)(2,1)S(1)} %fusion.27), kind=kOutput, calls=%fused_computation.55 | convolution fusion | flops 4194304 | bytes 4235264 | tf_op jit(solution)/shard_map/tjrf,tjf->tr/dot_general | solution.py:73
  7.6 2.4 %collective-permute-start.2 = (f32[16,128]{1,0:T(8,128)S(1)}, f32[16,128]{1,0:T(8,128)S(1)}, u32[]{:S(2)}, u32[]{:S(2)}) collective-permute-start(f32[16,128]{1,0:T(8,128)S(1)} %bitcast.94), channel_id=1, source_target_pairs={{0,3},{1,0},{2,1},{3,2},{4,7},{5,4},{6,5},{7,6},{8,11},{9,8},{10,9... | collective-permute-start | bytes 24584 | tf_op jit(solution)/shard_map/ppermute | solution.py:30
  11.4 2.4 %collective-permute-done.1 = f32[16,128]{1,0:T(8,128)S(1)} collective-permute-done((f32[16,128]{1,0:T(8,128)S(1)}, f32[16,128]{1,0:T(8,128)S(1)}, u32[]{:S(2)}, u32[]{:S(2)}) %collective-permute-start.1) | collective-permute-done | bytes 8224 | tf_op jit(solution)/shard_map/ppermute | solution.py:30
  13.8 3.0 %fusion.32 = f32[16,1,8,128]{3,1,2,0:T(1,128)S(1)} fusion(bf16[16,8,128,128]{3,2,1,0:T(8,128)(2,1)} %param.5, bf16[16,128,1,1]{1,0,2,3:T(8,128)(2,1)S(1)} %get-tuple-element.16), kind=kOutput, calls=%fused_computation.81 | convolution fusion | flops 4194304 | bytes 4263936 | tf_op jit(solution)/shard_map/tjrf,tr->tjf/dot_general | solution.py:81
  16.9 3.7 %collective-permute-start.5 = (f32[136,128]{1,0:T(8,128)S(1)}, f32[136,128]{1,0:T(8,128)S(1)}, u32[]{:S(2)}, u32[]{:S(2)}) collective-permute-start(f32[136,128]{1,0:T(8,128)S(1)} %pad_maximum_fusion), channel_id=1, source_target_pairs={{0,24},{4,28},{8,16},{12,20},{16,8},{20,12},{24,0},{28,4},{1,25},{... | collective-permute-start | bytes 208904 | tf_op jit(solution)/shard_map/ppermute | solution.py:24
  21.4 1.5 %collective-permute-start.6 = (f32[136,128]{1,0:T(8,128)S(1)}, f32[136,128]{1,0:T(8,128)S(1)}, u32[]{:S(2)}, u32[]{:S(2)}) collective-permute-start(f32[136,128]{1,0:T(8,128)S(1)} %pad_maximum_fusion), channel_id=1, source_target_pairs={{0,4},{4,0},{8,12},{12,8},{16,20},{20,16},{24,28},{28,24},{1,5},{5... | collective-permute-start | bytes 208904 | tf_op jit(solution)/shard_map/ppermute | solution.py:24
  23.6 1.5 %collective-permute-start.9 = (f32[136,128]{1,0:T(8,128)S(1)}, f32[136,128]{1,0:T(8,128)S(1)}, u32[]{:S(2)}, u32[]{:S(2)}) collective-permute-start(f32[136,128]{1,0:T(8,128)S(1)} %collective-permute-done.5), channel_id=1, source_target_pairs={{0,4},{4,0},{8,12},{12,8},{16,20},{20,16},{24,28},{28,24},{1,5},{5... | collective-permute-start | bytes 208904 | tf_op jit(solution)/shard_map/ppermute | solution.py:24
  25.1 0.9 collective-permute-done.4
  26.0 1.5 %collective-permute-start.8 = (f32[136,128]{1,0:T(8,128)S(1)}, f32[136,128]{1,0:T(8,128)S(1)}, u32[]{:S(2)}, u32[]{:S(2)}) collective-permute-start(f32[136,128]{1,0:T(8,128)S(1)} %collective-permute-done.4), channel_id=1, source_target_pairs={{0,4},{4,0},{8,12},{12,8},{16,20},{20,16},{24,28},{28,24},{1,5},{5... | collective-permute-start | bytes 208904 | tf_op jit(solution)/shard_map/ppermute | solution.py:24
  28.2 3.7 %collective-permute-done.7 = f32[136,128]{1,0:T(8,128)S(1)} collective-permute-done((f32[136,128]{1,0:T(8,128)S(1)}, f32[136,128]{1,0:T(8,128)S(1)}, u32[]{:S(2)}, u32[]{:S(2)}) %collective-permute-start.7) | collective-permute-done | bytes 69664 | tf_op jit(solution)/shard_map/ppermute | solution.py:24
  32.6 1.2 %fusion.23 = f32[16,1,128,1]{2,1,3,0:T(1,128)S(1)} fusion(bf16[16,8,128,128]{3,2,1,0:T(8,128)(2,1)S(1)} %copy-done, bf16[16,8,128,1]{2,1,0,3:T(8,128)(2,1)S(1)} %convert_bitcast_fusion), kind=kOutput, calls=%fused_computation.53 | convolution fusion | flops 4194304 | bytes 4235264 | tf_op jit(solution)/shard_map/tjrf,tjf->tr/dot_general | solution.py:73
  33.8 1.6 %multiply_reduce_fusion.2 = (f32[]{:T(128)}, f32[256,128]{1,0:T(8,128)S(1)}) fusion(f32[384,128]{1,0:T(8,128)S(1)} %slice_add_fusion.1, f32[2048,128]{1,0:T(8,128)} %param.9, s32[]{:T(128)S(6)} %select_n.55), kind=kLoop, calls=%fused_computation.26 | loop fusion | flops 98303 | bytes 393224 | tf_op jit(solution)/shard_map/reduce_sum | solution.py:116
  36.0 1.2 %collective-permute-start.11 = (f32[24,128]{1,0:T(8,128)S(1)}, f32[24,128]{1,0:T(8,128)S(1)}, u32[]{:S(2)}, u32[]{:S(2)}) collective-permute-start(f32[24,128]{1,0:T(8,128)S(1)} %pad_maximum_fusion.2), channel_id=1, source_target_pairs={{0,2},{1,3},{2,0},{3,1},{4,6},{5,7},{6,4},{7,5},{8,10},{9,11},{10,... | collective-permute-start | bytes 36872 | tf_op jit(solution)/shard_map/ppermute | solution.py:30
  37.7 2.1 %collective-permute-done.11 = f32[24,128]{1,0:T(8,128)S(1)} collective-permute-done((f32[24,128]{1,0:T(8,128)S(1)}, f32[24,128]{1,0:T(8,128)S(1)}, u32[]{:S(2)}, u32[]{:S(2)}) %collective-permute-start.11) | collective-permute-done | bytes 12320 | tf_op jit(solution)/shard_map/ppermute | solution.py:30
  43.5 2.3 %collective-permute-start.15 = (f32[136,128]{1,0:T(8,128)S(1)}, f32[136,128]{1,0:T(8,128)S(1)}, u32[]{:S(2)}, u32[]{:S(2)}) collective-permute-start(f32[136,128]{1,0:T(8,128)S(1)} %pad_maximum_fusion.1), channel_id=1, source_target_pairs={{0,24},{4,28},{8,16},{12,20},{16,8},{20,12},{24,0},{28,4},{1,25},{... | collective-permute-start | bytes 208904 | tf_op jit(solution)/shard_map/ppermute | solution.py:24
  45.9 2.1 %collective-permute-start.13 = (f32[136,128]{1,0:T(8,128)S(1)}, f32[136,128]{1,0:T(8,128)S(1)}, u32[]{:S(2)}, u32[]{:S(2)}) collective-permute-start(f32[136,128]{1,0:T(8,128)S(1)} %pad_maximum_fusion.1), channel_id=1, source_target_pairs={{0,8},{4,12},{8,0},{12,4},{16,24},{20,28},{24,16},{28,20},{1,9},{5... | collective-permute-start | bytes 208904 | tf_op jit(solution)/shard_map/ppermute | solution.py:24
  48.7 1.2 %collective-permute-done.15 = f32[136,128]{1,0:T(8,128)S(1)} collective-permute-done((f32[136,128]{1,0:T(8,128)S(1)}, f32[136,128]{1,0:T(8,128)S(1)}, u32[]{:S(2)}, u32[]{:S(2)}) %collective-permute-start.15) | collective-permute-done | bytes 69664 | tf_op jit(solution)/shard_map/ppermute | solution.py:24
  50.7 1.4 %collective-permute-done.14 = f32[136,128]{1,0:T(8,128)S(1)} collective-permute-done((f32[136,128]{1,0:T(8,128)S(1)}, f32[136,128]{1,0:T(8,128)S(1)}, u32[]{:S(2)}, u32[]{:S(2)}) %collective-permute-start.14) | collective-permute-done | bytes 69664 | tf_op jit(solution)/shard_map/ppermute | solution.py:24
  52.8 1.3 %collective-permute-start.17 = (f32[136,128]{1,0:T(8,128)S(1)}, f32[136,128]{1,0:T(8,128)S(1)}, u32[]{:S(2)}, u32[]{:S(2)}) collective-permute-start(f32[136,128]{1,0:T(8,128)S(1)} %collective-permute-done.13), channel_id=1, source_target_pairs={{0,4},{4,0},{8,12},{12,8},{16,20},{20,16},{24,28},{28,24},{1,5},{5... | collective-permute-start | bytes 208904 | tf_op jit(solution)/shard_map/ppermute | solution.py:24
  54.1 3.5 %collective-permute-done.17 = f32[136,128]{1,0:T(8,128)S(1)} collective-permute-done((f32[136,128]{1,0:T(8,128)S(1)}, f32[136,128]{1,0:T(8,128)S(1)}, u32[]{:S(2)}, u32[]{:S(2)}) %collective-permute-start.17) | collective-permute-done | bytes 69664 | tf_op jit(solution)/shard_map/ppermute | solution.py:24
  60.9 3.4 %fusion.21 = f32[16,1,128,1]{2,1,3,0:T(1,128)S(1)} fusion(bf16[16,8,128,128]{3,2,1,0:T(8,128)(2,1)} %param.5, bf16[16,8,128,1]{2,1,0,3:T(8,128)(2,1)S(1)} %fusion.28), kind=kOutput, calls=%fused_computation.51 | convolution fusion | flops 4194304 | bytes 4235264 | tf_op jit(solution)/shard_map/tjrf,tjf->tr/dot_general | solution.py:73
  66.4 0.9 collective-permute-start.21
  67.8 2.4 %collective-permute-done.21 = f32[24,128]{1,0:T(8,128)S(1)} collective-permute-done((f32[24,128]{1,0:T(8,128)S(1)}, f32[24,128]{1,0:T(8,128)S(1)}, u32[]{:S(2)}, u32[]{:S(2)}) %collective-permute-start.21) | collective-permute-done | bytes 12320 | tf_op jit(solution)/shard_map/ppermute | solution.py:30
  72.4 1.9 %select_select_fusion = f32[8,128]{1,0:T(8,128)S(1)} fusion(f32[128]{0:T(128)S(1)} %fusion.39, f32[]{:T(128)} %bitcast.34, f32[]{:T(128)} %get-tuple-element.5, f32[]{:T(128)} %get-tuple-element.4, pred[128]{0:T(512)(128)(4,1)S(1)} %get-tuple-element.30, pred[128]{0:T(512)(128)(4,1)S(1)} %get-tuple-element.31, pred[128]{0:T(512)(128)(4,1)S(1)} %iota_compare_fusion.4), kind=kLoop, calls=%fused_computation.92 | loop fusion | flops 3072 | bytes 5004 | tf_op jit(solution)/shard_map/jit(_where)/select_n | solution.py:93
  74.4 1.1 %collective-permute-start.23 = (f32[8,128]{1,0:T(8,128)S(1)}, f32[8,128]{1,0:T(8,128)S(1)}, u32[]{:S(2)}, u32[]{:S(2)}) collective-permute-start(f32[8,128]{1,0:T(8,128)S(1)} %select_select_fusion), channel_id=1, source_target_pairs={{0,4},{4,0},{8,12},{12,8},{16,20},{20,16},{24,28},{28,24},{1,5},{5... | collective-permute-start | bytes 12296 | tf_op jit(solution)/shard_map/ppermute | solution.py:24
  75.5 2.6 %collective-permute-done.23 = f32[8,128]{1,0:T(8,128)S(1)} collective-permute-done((f32[8,128]{1,0:T(8,128)S(1)}, f32[8,128]{1,0:T(8,128)S(1)}, u32[]{:S(2)}, u32[]{:S(2)}) %collective-permute-start.23) | collective-permute-done | bytes 4128 | tf_op jit(solution)/shard_map/ppermute | solution.py:24
  78.0 1.9 %fusion.45 = f32[8,128]{1,0:T(8,128)S(1)} fusion(f32[8,128]{1,0:T(8,128)S(1)} %collective-permute-done.23, f32[128]{0:T(128)S(1)} %fusion.39, f32[]{:T(128)} %bitcast.34, pred[128]{0:T(512)(128)(4,1)S(1)} %iota_compare_fusion.4, f32[]{:T(128)} %get-tuple-element.5, pred[128]{0:T(512)(128)(4,1)S(1)} %get-tuple-element.30, f32[]{:T(128)} %get-tuple-element.4, ...), kind=kLoop, calls=%fused_computation.127 | loop fusion | flops 4096 | bytes 9100 | tf_op jit(solution)/shard_map/add | solution.py:56
  80.1 3.6 %collective-permute-done.24 = f32[8,128]{1,0:T(8,128)S(1)} collective-permute-done((f32[8,128]{1,0:T(8,128)S(1)}, f32[8,128]{1,0:T(8,128)S(1)}, u32[]{:S(2)}, u32[]{:S(2)}) %collective-permute-start.24) | collective-permute-done | bytes 4128 | tf_op jit(solution)/shard_map/ppermute | solution.py:24
  83.7 1.9 %fusion.54 = f32[8,128]{1,0:T(8,128)S(1)} fusion(f32[8,128]{1,0:T(8,128)S(1)} %collective-permute-done.24, f32[8,128]{1,0:T(8,128)S(1)} %collective-permute-done.23, f32[128]{0:T(128)S(1)} %fusion.39, f32[]{:T(128)} %bitcast.34, pred[128]{0:T(512)(128)(4,1)S(1)} %iota_compare_fusion.4, f32[]{:T(128)} %get-tuple-element.5, ...), kind=kLoop, calls=%fused_computation.131 | loop fusion | flops 5120 | bytes 13196 | tf_op jit(solution)/shard_map/add | solution.py:56
  85.6 1.3 %collective-permute-start.25 = (f32[8,128]{1,0:T(8,128)S(1)}, f32[8,128]{1,0:T(8,128)S(1)}, u32[]{:S(2)}, u32[]{:S(2)}) collective-permute-start(f32[8,128]{1,0:T(8,128)S(1)} %fusion.54), channel_id=1, source_target_pairs={{0,16},{4,20},{8,24},{12,28},{16,0},{20,4},{24,8},{28,12},{1,17},{... | collective-permute-start | bytes 12296 | tf_op jit(solution)/shard_map/ppermute | solution.py:24
  86.9 3.3 %collective-permute-done.25 = f32[8,128]{1,0:T(8,128)S(1)} collective-permute-done((f32[8,128]{1,0:T(8,128)S(1)}, f32[8,128]{1,0:T(8,128)S(1)}, u32[]{:S(2)}, u32[]{:S(2)}) %collective-permute-start.25) | collective-permute-done | bytes 4128 | tf_op jit(solution)/shard_map/ppermute | solution.py:24
  (116 shorter events, 20.5 us)
Async XLA Ops:
  0.6 10.2 %copy-start.4 = (s32[16,1]{0,1:T(1,128)S(1)}, s32[16,1]{0,1:T(1,128)}, u32[]{:S(2)}) copy-start(s32[16,1]{0,1:T(1,128)} %param.7) | copy-start | bytes 196
  0.6 10.2 %copy-start.2 = (s32[16,8]{0,1:T(8,128)S(1)}, s32[16,8]{0,1:T(8,128)}, u32[]{:S(2)}) copy-start(s32[16,8]{0,1:T(8,128)} %param.6) | copy-start | bytes 1540
  0.7 13.1 %copy-start.3 = (s32[2048]{0:T(1024)S(1)}, s32[2048]{0:T(1024)}, u32[]{:S(2)}) copy-start(s32[2048]{0:T(1024)} %param.8) | copy-start | bytes 24580
  7.6 3.8 %collective-permute-start.2 = (f32[16,128]{1,0:T(8,128)S(1)}, f32[16,128]{1,0:T(8,128)S(1)}, u32[]{:S(2)}, u32[]{:S(2)}) collective-permute-start(f32[16,128]{1,0:T(8,128)S(1)} %bitcast.94), channel_id=1, source_target_pairs={{0,3},{1,0},{2,1},{3,2},{4,7},{5,4},{6,5},{7,6},{8,11},{9,8},{10,9... | collective-permute-start | bytes 24584 | tf_op jit(solution)/shard_map/ppermute | solution.py:30
  10.0 3.7 %collective-permute-start.1 = (f32[16,128]{1,0:T(8,128)S(1)}, f32[16,128]{1,0:T(8,128)S(1)}, u32[]{:S(2)}, u32[]{:S(2)}) collective-permute-start(f32[16,128]{1,0:T(8,128)S(1)} %bitcast.95), channel_id=1, source_target_pairs={{0,2},{1,3},{2,0},{3,1},{4,6},{5,7},{6,4},{7,5},{8,10},{9,11},{10,... | collective-permute-start | bytes 24584 | tf_op jit(solution)/shard_map/ppermute | solution.py:30
  10.6 3.2 %collective-permute-start = (f32[16,128]{1,0:T(8,128)S(1)}, f32[16,128]{1,0:T(8,128)S(1)}, u32[]{:S(2)}, u32[]{:S(2)}) collective-permute-start(f32[16,128]{1,0:T(8,128)S(1)} %bitcast.96), channel_id=1, source_target_pairs={{0,1},{1,2},{2,3},{3,0},{4,5},{5,6},{6,7},{7,4},{8,9},{9,10},{10,1... | collective-permute-start | bytes 24584 | tf_op jit(solution)/shard_map/ppermute | solution.py:30
  13.8 18.8 %copy-start = (bf16[16,8,128,128]{3,2,1,0:T(8,128)(2,1)S(1)}, bf16[16,8,128,128]{3,2,1,0:T(8,128)(2,1)}, u32[]{:S(2)}) copy-start(bf16[16,8,128,128]{3,2,1,0:T(8,128)(2,1)} %param.5) | copy-start | bytes 12582916
  16.9 6.7 %collective-permute-start.5 = (f32[136,128]{1,0:T(8,128)S(1)}, f32[136,128]{1,0:T(8,128)S(1)}, u32[]{:S(2)}, u32[]{:S(2)}) collective-permute-start(f32[136,128]{1,0:T(8,128)S(1)} %pad_maximum_fusion), channel_id=1, source_target_pairs={{0,24},{4,28},{8,16},{12,20},{16,8},{20,12},{24,0},{28,4},{1,25},{... | collective-permute-start | bytes 208904 | tf_op jit(solution)/shard_map/ppermute | solution.py:24
  20.6 5.5 %collective-permute-start.4 = (f32[136,128]{1,0:T(8,128)S(1)}, f32[136,128]{1,0:T(8,128)S(1)}, u32[]{:S(2)}, u32[]{:S(2)}) collective-permute-start(f32[136,128]{1,0:T(8,128)S(1)} %pad_maximum_fusion), channel_id=1, source_target_pairs={{0,16},{4,20},{8,24},{12,28},{16,0},{20,4},{24,8},{28,12},{1,17},{... | collective-permute-start | bytes 208904 | tf_op jit(solution)/shard_map/ppermute | solution.py:24
  20.6 7.0 %collective-permute-start.3 = (f32[136,128]{1,0:T(8,128)S(1)}, f32[136,128]{1,0:T(8,128)S(1)}, u32[]{:S(2)}, u32[]{:S(2)}) collective-permute-start(f32[136,128]{1,0:T(8,128)S(1)} %pad_maximum_fusion), channel_id=1, source_target_pairs={{0,8},{4,12},{8,0},{12,4},{16,24},{20,28},{24,16},{28,20},{1,9},{5... | collective-permute-start | bytes 208904 | tf_op jit(solution)/shard_map/ppermute | solution.py:24
  21.4 6.8 %collective-permute-start.6 = (f32[136,128]{1,0:T(8,128)S(1)}, f32[136,128]{1,0:T(8,128)S(1)}, u32[]{:S(2)}, u32[]{:S(2)}) collective-permute-start(f32[136,128]{1,0:T(8,128)S(1)} %pad_maximum_fusion), channel_id=1, source_target_pairs={{0,4},{4,0},{8,12},{12,8},{16,20},{20,16},{24,28},{28,24},{1,5},{5... | collective-permute-start | bytes 208904 | tf_op jit(solution)/shard_map/ppermute | solution.py:24
  23.6 8.3 %collective-permute-start.9 = (f32[136,128]{1,0:T(8,128)S(1)}, f32[136,128]{1,0:T(8,128)S(1)}, u32[]{:S(2)}, u32[]{:S(2)}) collective-permute-start(f32[136,128]{1,0:T(8,128)S(1)} %collective-permute-done.5), channel_id=1, source_target_pairs={{0,4},{4,0},{8,12},{12,8},{16,20},{20,16},{24,28},{28,24},{1,5},{5... | collective-permute-start | bytes 208904 | tf_op jit(solution)/shard_map/ppermute | solution.py:24
  26.0 5.8 %collective-permute-start.8 = (f32[136,128]{1,0:T(8,128)S(1)}, f32[136,128]{1,0:T(8,128)S(1)}, u32[]{:S(2)}, u32[]{:S(2)}) collective-permute-start(f32[136,128]{1,0:T(8,128)S(1)} %collective-permute-done.4), channel_id=1, source_target_pairs={{0,4},{4,0},{8,12},{12,8},{16,20},{20,16},{24,28},{28,24},{1,5},{5... | collective-permute-start | bytes 208904 | tf_op jit(solution)/shard_map/ppermute | solution.py:24
  27.6 4.3 %collective-permute-start.7 = (f32[136,128]{1,0:T(8,128)S(1)}, f32[136,128]{1,0:T(8,128)S(1)}, u32[]{:S(2)}, u32[]{:S(2)}) collective-permute-start(f32[136,128]{1,0:T(8,128)S(1)} %collective-permute-done.3), channel_id=1, source_target_pairs={{0,4},{4,0},{8,12},{12,8},{16,20},{20,16},{24,28},{28,24},{1,5},{5... | collective-permute-start | bytes 208904 | tf_op jit(solution)/shard_map/ppermute | solution.py:24
  35.4 61.5 %copy-start.1 = (f32[256,128]{1,0:T(8,128)}, f32[256,128]{1,0:T(8,128)S(1)}, u32[]{:S(2)}) copy-start(f32[256,128]{1,0:T(8,128)S(1)} %get-tuple-element.11) | copy-start | bytes 393220
  36.0 3.8 %collective-permute-start.11 = (f32[24,128]{1,0:T(8,128)S(1)}, f32[24,128]{1,0:T(8,128)S(1)}, u32[]{:S(2)}, u32[]{:S(2)}) collective-permute-start(f32[24,128]{1,0:T(8,128)S(1)} %pad_maximum_fusion.2), channel_id=1, source_target_pairs={{0,2},{1,3},{2,0},{3,1},{4,6},{5,7},{6,4},{7,5},{8,10},{9,11},{10,... | collective-permute-start | bytes 36872 | tf_op jit(solution)/shard_map/ppermute | solution.py:30
  37.2 2.6 %collective-permute-start.12 = (f32[24,128]{1,0:T(8,128)S(1)}, f32[24,128]{1,0:T(8,128)S(1)}, u32[]{:S(2)}, u32[]{:S(2)}) collective-permute-start(f32[24,128]{1,0:T(8,128)S(1)} %pad_maximum_fusion.2), channel_id=1, source_target_pairs={{0,3},{1,0},{2,1},{3,2},{4,7},{5,4},{6,5},{7,6},{8,11},{9,8},{10,9... | collective-permute-start | bytes 36872 | tf_op jit(solution)/shard_map/ppermute | solution.py:30
  37.2 3.1 %collective-permute-start.10 = (f32[24,128]{1,0:T(8,128)S(1)}, f32[24,128]{1,0:T(8,128)S(1)}, u32[]{:S(2)}, u32[]{:S(2)}) collective-permute-start(f32[24,128]{1,0:T(8,128)S(1)} %pad_maximum_fusion.2), channel_id=1, source_target_pairs={{0,1},{1,2},{2,3},{3,0},{4,5},{5,6},{6,7},{7,4},{8,9},{9,10},{10,1... | collective-permute-start | bytes 36872 | tf_op jit(solution)/shard_map/ppermute | solution.py:30
  43.5 6.4 %collective-permute-start.15 = (f32[136,128]{1,0:T(8,128)S(1)}, f32[136,128]{1,0:T(8,128)S(1)}, u32[]{:S(2)}, u32[]{:S(2)}) collective-permute-start(f32[136,128]{1,0:T(8,128)S(1)} %pad_maximum_fusion.1), channel_id=1, source_target_pairs={{0,24},{4,28},{8,16},{12,20},{16,8},{20,12},{24,0},{28,4},{1,25},{... | collective-permute-start | bytes 208904 | tf_op jit(solution)/shard_map/ppermute | solution.py:24
  45.9 6.2 %collective-permute-start.14 = (f32[136,128]{1,0:T(8,128)S(1)}, f32[136,128]{1,0:T(8,128)S(1)}, u32[]{:S(2)}, u32[]{:S(2)}) collective-permute-start(f32[136,128]{1,0:T(8,128)S(1)} %pad_maximum_fusion.1), channel_id=1, source_target_pairs={{0,16},{4,20},{8,24},{12,28},{16,0},{20,4},{24,8},{28,12},{1,17},{... | collective-permute-start | bytes 208904 | tf_op jit(solution)/shard_map/ppermute | solution.py:24
  45.9 6.9 %collective-permute-start.13 = (f32[136,128]{1,0:T(8,128)S(1)}, f32[136,128]{1,0:T(8,128)S(1)}, u32[]{:S(2)}, u32[]{:S(2)}) collective-permute-start(f32[136,128]{1,0:T(8,128)S(1)} %pad_maximum_fusion.1), channel_id=1, source_target_pairs={{0,8},{4,12},{8,0},{12,4},{16,24},{20,28},{24,16},{28,20},{1,9},{5... | collective-permute-start | bytes 208904 | tf_op jit(solution)/shard_map/ppermute | solution.py:24
  48.0 6.1 %collective-permute-start.16 = (f32[136,128]{1,0:T(8,128)S(1)}, f32[136,128]{1,0:T(8,128)S(1)}, u32[]{:S(2)}, u32[]{:S(2)}) collective-permute-start(f32[136,128]{1,0:T(8,128)S(1)} %pad_maximum_fusion.1), channel_id=1, source_target_pairs={{0,4},{4,0},{8,12},{12,8},{16,20},{20,16},{24,28},{28,24},{1,5},{5... | collective-permute-start | bytes 208904 | tf_op jit(solution)/shard_map/ppermute | solution.py:24
  49.9 7.8 %collective-permute-start.19 = (f32[136,128]{1,0:T(8,128)S(1)}, f32[136,128]{1,0:T(8,128)S(1)}, u32[]{:S(2)}, u32[]{:S(2)}) collective-permute-start(f32[136,128]{1,0:T(8,128)S(1)} %collective-permute-done.15), channel_id=1, source_target_pairs={{0,4},{4,0},{8,12},{12,8},{16,20},{20,16},{24,28},{28,24},{1,5},{5... | collective-permute-start | bytes 208904 | tf_op jit(solution)/shard_map/ppermute | solution.py:24
  52.1 5.6 %collective-permute-start.18 = (f32[136,128]{1,0:T(8,128)S(1)}, f32[136,128]{1,0:T(8,128)S(1)}, u32[]{:S(2)}, u32[]{:S(2)}) collective-permute-start(f32[136,128]{1,0:T(8,128)S(1)} %collective-permute-done.14), channel_id=1, source_target_pairs={{0,4},{4,0},{8,12},{12,8},{16,20},{20,16},{24,28},{28,24},{1,5},{5... | collective-permute-start | bytes 208904 | tf_op jit(solution)/shard_map/ppermute | solution.py:24
  52.8 4.8 %collective-permute-start.17 = (f32[136,128]{1,0:T(8,128)S(1)}, f32[136,128]{1,0:T(8,128)S(1)}, u32[]{:S(2)}, u32[]{:S(2)}) collective-permute-start(f32[136,128]{1,0:T(8,128)S(1)} %collective-permute-done.13), channel_id=1, source_target_pairs={{0,4},{4,0},{8,12},{12,8},{16,20},{20,16},{24,28},{28,24},{1,5},{5... | collective-permute-start | bytes 208904 | tf_op jit(solution)/shard_map/ppermute | solution.py:24
  66.4 3.8 %collective-permute-start.21 = (f32[24,128]{1,0:T(8,128)S(1)}, f32[24,128]{1,0:T(8,128)S(1)}, u32[]{:S(2)}, u32[]{:S(2)}) collective-permute-start(f32[24,128]{1,0:T(8,128)S(1)} %pad_maximum_fusion.3), channel_id=1, source_target_pairs={{0,2},{1,3},{2,0},{3,1},{4,6},{5,7},{6,4},{7,5},{8,10},{9,11},{10,... | collective-permute-start | bytes 36872 | tf_op jit(solution)/shard_map/ppermute | solution.py:30
  67.3 2.9 %collective-permute-start.22 = (f32[24,128]{1,0:T(8,128)S(1)}, f32[24,128]{1,0:T(8,128)S(1)}, u32[]{:S(2)}, u32[]{:S(2)}) collective-permute-start(f32[24,128]{1,0:T(8,128)S(1)} %pad_maximum_fusion.3), channel_id=1, source_target_pairs={{0,3},{1,0},{2,1},{3,2},{4,7},{5,4},{6,5},{7,6},{8,11},{9,8},{10,9... | collective-permute-start | bytes 36872 | tf_op jit(solution)/shard_map/ppermute | solution.py:30
  67.3 3.2 %collective-permute-start.20 = (f32[24,128]{1,0:T(8,128)S(1)}, f32[24,128]{1,0:T(8,128)S(1)}, u32[]{:S(2)}, u32[]{:S(2)}) collective-permute-start(f32[24,128]{1,0:T(8,128)S(1)} %pad_maximum_fusion.3), channel_id=1, source_target_pairs={{0,1},{1,2},{2,3},{3,0},{4,5},{5,6},{6,7},{7,4},{8,9},{9,10},{10,1... | collective-permute-start | bytes 36872 | tf_op jit(solution)/shard_map/ppermute | solution.py:30
  74.4 3.7 %collective-permute-start.23 = (f32[8,128]{1,0:T(8,128)S(1)}, f32[8,128]{1,0:T(8,128)S(1)}, u32[]{:S(2)}, u32[]{:S(2)}) collective-permute-start(f32[8,128]{1,0:T(8,128)S(1)} %select_select_fusion), channel_id=1, source_target_pairs={{0,4},{4,0},{8,12},{12,8},{16,20},{20,16},{24,28},{28,24},{1,5},{5... | collective-permute-start | bytes 12296 | tf_op jit(solution)/shard_map/ppermute | solution.py:24
  80.0 3.7 %collective-permute-start.24 = (f32[8,128]{1,0:T(8,128)S(1)}, f32[8,128]{1,0:T(8,128)S(1)}, u32[]{:S(2)}, u32[]{:S(2)}) collective-permute-start(f32[8,128]{1,0:T(8,128)S(1)} %fusion.45), channel_id=1, source_target_pairs={{0,8},{4,12},{8,0},{12,4},{16,24},{20,28},{24,16},{28,20},{1,9},{5... | collective-permute-start | bytes 12296 | tf_op jit(solution)/shard_map/ppermute | solution.py:24
  85.6 4.6 %collective-permute-start.25 = (f32[8,128]{1,0:T(8,128)S(1)}, f32[8,128]{1,0:T(8,128)S(1)}, u32[]{:S(2)}, u32[]{:S(2)}) collective-permute-start(f32[8,128]{1,0:T(8,128)S(1)} %fusion.54), channel_id=1, source_target_pairs={{0,16},{4,20},{8,24},{12,28},{16,0},{20,4},{24,8},{28,12},{1,17},{... | collective-permute-start | bytes 12296 | tf_op jit(solution)/shard_map/ppermute | solution.py:24

commit v2 on v0

v2 whole, which is shorter than its diff:
```python
import functools

import jax
import jax.numpy as jnp
from jax import lax
from jax.experimental import pallas as pl
from jax.experimental.pallas import tpu as pltpu
from jax.sharding import PartitionSpec as P

F32 = jnp.float32
BF16 = jnp.bfloat16
SUB = 8
LIMIT = 24 * 1024 * 1024


def row_iota(shape):
    return lax.broadcasted_iota(jnp.int32, shape, 0)


def lane_iota(shape):
    return lax.broadcasted_iota(jnp.int32, shape, 1)


def total(array):
    return jnp.sum(jnp.sum(array, axis=0, keepdims=True), axis=1, keepdims=True)


def scalar_rows(width, *scalars):
    lane = lane_iota((SUB, width))
    block = jnp.zeros((SUB, width), F32)
    for place, scalar in enumerate(scalars):
        block = jnp.where(lane == place, scalar, block)
    return block


def read_scalar(block, place):
    lane = lane_iota(block.shape)
    return jnp.sum(jnp.where(lane == place, block, 0.0), axis=1, keepdims=True)


def forward_tile(tile, picked):
    slots, rows, width = tile.shape
    product = lax.dot_general(
        picked.astype(BF16),
        tile.reshape(slots * rows, width),
        (((1,), (1,)), ((), ())),
        preferred_element_type=F32,
    )
    mine = row_iota((slots, rows))
    kept = jnp.where(mine == 0, product[:, :rows], 0.0)
    for s in range(1, slots):
        kept = kept + jnp.where(mine == s, product[:, s * rows : (s + 1) * rows], 0.0)
    return jnp.sum(kept, axis=0, keepdims=True)


def back_tile(tile, rows_term):
    slots, rows, width = tile.shape
    mine = row_iota((slots, rows))
    spread = jnp.concatenate(
        [jnp.where(mine == s, rows_term, 0.0) for s in range(slots)], axis=1
    ).astype(BF16)
    return jnp.dot(spread, tile.reshape(slots * rows, width), preferred_element_type=F32)


def forward_all(values, picked, out):
    tiles, slots = values.shape[:2]
    for t in range(tiles):
        out[t : t + 1, :] = forward_tile(values[t], picked[t * slots : (t + 1) * slots, :])


def back_all(values, rows_term, ids, out):
    tiles, slots = values.shape[:2]
    for t in range(tiles):
        block = slice(t * slots, (t + 1) * slots)
        out[block, :] = jnp.where(
            ids[block, :] >= 0.0, back_tile(values[t], rows_term[t : t + 1, :]), 0.0
        )


def first_kernel(share, columns, live, weights, values_in, values, ids, picked, own, along,
                 weights_here, weights_sem, values_sem):
    tiles, slots, rows, width = values.shape
    whole = pltpu.make_async_copy(weights, weights_here, weights_sem)
    whole.start()
    loads = [
        pltpu.make_async_copy(values_in.at[t], values.at[t], values_sem.at[t])
        for t in range(tiles)
    ]
    for load in loads:
        load.start()
    whole.wait()
    for t in range(tiles):
        count = live[0, t]
        for j in range(slots):
            slot = t * slots + j
            column = columns[j, t]
            used = j < count
            row = weights_here[pl.ds(column, 1), :]
            picked[slot : slot + 1, :] = jnp.where(used, row, 0.0)
            ids[slot : slot + 1, :] = jnp.full(
                (1, width), jnp.where(used, column, -2), jnp.int32
            ).astype(F32)
    offset = pl.multiple_of(lax.axis_index("inst") * share, SUB)
    own[...] = weights_here[pl.ds(offset, share), :]
    for t in range(tiles):
        loads[t].wait()
        along[t : t + 1, :] = forward_tile(values[t], picked[t * slots : (t + 1) * slots, :])


def gradient_kernel(count, labels, values, ids, *refs):
    parts, (payload, curvature) = refs[:count], refs[count:]
    slots = ids.shape[0]
    margin = parts[0][...]
    for part in parts[1:]:
        margin = margin + part[...]
    prob = 1.0 / (1.0 + jnp.exp(-margin))
    curvature[...] = prob * (1.0 - prob)
    back_all(values, prob - labels[...].astype(F32), ids, payload)
    square = ids[...]
    diagonal = row_iota(square.shape) == lane_iota(square.shape)
    sent = jnp.sum(jnp.where(diagonal, square, 0.0), axis=0, keepdims=True)
    sent = jnp.where(sent < 0.0, -1.0, sent)
    payload[slots:, :] = jnp.broadcast_to(sent, (SUB, sent.shape[1]))


def stack_halves(parts, slots, halves):
    width = parts[0].shape[1]
    for k, part in enumerate(parts):
        block = part[:slots, :]
        high = block.astype(BF16)
        halves[k * slots : (k + 1) * slots, :width] = high
        halves[k * slots : (k + 1) * slots, width:] = (block - high.astype(F32)).astype(BF16)


def pick_sums(onehot, halves):
    both = jnp.dot(onehot[...], halves[...], preferred_element_type=F32)
    width = both.shape[1] // 2
    return both[:, :width] + both[:, width:]


def start_kernel(count, values, ids, picked, own, *refs):
    parts = refs[:count]
    gradient, start_slot, onehot, payload, halves = refs[count:]
    tiles = values.shape[0]
    slots, width = ids.shape
    share = own.shape[0]
    offset = lax.axis_index("inst") * share
    blocks = (row_iota((share, width)) + offset).astype(F32)
    for k, part in enumerate(parts):
        sent = part[slots : slots + 1, :]
        place = slice(k * slots, (k + 1) * slots)
        onehot[:slots, place] = jnp.where(ids[...] == sent, 1.0, 0.0).astype(BF16)
        onehot[slots:, place] = jnp.where(blocks == sent, 1.0, 0.0).astype(BF16)
    stack_halves(parts, slots, halves)
    summed = pick_sums(onehot, halves)
    start_slot[...] = -(picked[...] + summed[:slots, :])
    forward_all(values, start_slot, payload)
    slope = own[...] + summed[slots:, :]
    gradient[...] = slope
    payload[tiles:, :] = scalar_rows(width, total(slope * slope))


def curve_kernel(count, values, ids, curvature, *refs):
    parts, (along, payload) = refs[:count], refs[count:]
    tiles = values.shape[0]
    slots, width = ids.shape
    summed = parts[0][...]
    for part in parts[1:]:
        summed = summed + part[...]
    here = summed[:tiles, :]
    along[...] = here
    curved = curvature[...] * here
    back_all(values, curved, ids, payload)
    rounded = curved.astype(BF16).astype(F32)
    norm_part = summed[tiles : tiles + 1, 0:1]
    payload[slots:, :] = scalar_rows(width, norm_part, total(rounded * here))


def turn_kernel(count, values, onehot, start_slot, gradient, *refs):
    parts = refs[:count]
    next_share, known, payload, halves, next_slot = refs[count:]
    tiles = values.shape[0]
    slots, width = start_slot.shape
    scalars = parts[0][slots:, :]
    for part in parts[1:]:
        scalars = scalars + part[slots:, :]
    norm_now = read_scalar(scalars[0:1, :], 0)
    curve_now = read_scalar(scalars[0:1, :], 1)
    alpha = norm_now / (norm_now + curve_now)
    stack_halves(parts, slots, halves)
    summed = pick_sums(onehot, halves)
    start = start_slot[...]
    next_slot[...] = start - alpha * (start + summed[:slots, :])
    forward_all(values, next_slot, payload)
    start_own = -gradient[...]
    turned = start_own - alpha * (start_own + summed[slots:, :])
    next_share[...] = turned
    payload[tiles:, :] = scalar_rows(width, total(turned * turned), total(turned * start_own))
    known[...] = scalar_rows(width, norm_now, curve_now, alpha)


def inner_kernel(count, curvature, along, *refs):
    parts, (scalars,) = refs[:count], refs[count:]
    tiles, width = along.shape
    summed = parts[0][...]
    for part in parts[1:]:
        summed = summed + part[...]
    turn = summed[:tiles, :]
    bent = curvature[...] * turn
    scalars[...] = scalar_rows(
        width,
        summed[tiles : tiles + 1, 0:1],
        summed[tiles : tiles + 1, 1:2],
        total(bent * turn),
        total(bent * along[...]),
    )


def last_kernel(scalars, known, gradient, next_share, step):
    row = scalars[0:1, :]
    norm_next, cross, turn_turn, turn_along = (read_scalar(row, i) for i in range(4))
    row = known[0:1, :]
    norm_now, curve_now, alpha = (read_scalar(row, i) for i in range(3))
    ratio = norm_next / norm_now
    bottom = (
        norm_next
        + turn_turn
        + 2.0 * ratio * (cross + turn_along)
        + ratio * ratio * (norm_now + curve_now)
    )
    alpha_next = norm_next / bottom
    start = -gradient[...]
    step[...] = alpha * start + alpha_next * (next_share[...] + ratio * start)


def near(shape, dtype=F32):
    return pltpu.VMEM(shape, dtype)


def call(kernel, out_shape, args, in_specs=None, scratch_shapes=(), keep=None):
    vmem = pl.BlockSpec(memory_space=pltpu.VMEM)
    if in_specs is None:
        in_specs = [vmem] * len(args)
        args = [pltpu.with_memory_space_constraint(a, pltpu.VMEM) for a in args]
    return pl.pallas_call(
        kernel,
        out_shape=out_shape,
        in_specs=in_specs,
        out_specs=jax.tree.map(lambda _: vmem, out_shape),
        scratch_shapes=list(scratch_shapes),
        compiler_params=pltpu.CompilerParams(vmem_limit_bytes=LIMIT),
    )(*args)


def swap(array, axis, distance):
    size = lax.axis_size(axis)
    return lax.ppermute(array, axis, [(i, i ^ distance) for i in range(size)])


def feat_parts(array):
    size = lax.axis_size("feat")
    return [array] + [
        lax.ppermute(array, "feat", [(i, (i + k) % size) for i in range(size)])
        for k in range(1, size)
    ]


def inst_parts(array):
    size = lax.axis_size("inst")
    if size != 8:
        gathered = lax.all_gather(array, "inst", axis=0)
        return [gathered[i] for i in range(size)]
    parts = [array] + [swap(array, "inst", k) for k in (2, 4, 6)]
    return parts + [swap(part, "inst", 1) for part in parts]


def inst_sum(array):
    size = lax.axis_size("inst")
    distance = 1
    while distance < size:
        array = array + swap(array, "inst", distance)
        distance *= 2
    return array


def per_device(values, columns, live_slots, labels, weights):
    tiles, slots_of, rows, width = values.shape
    slots = tiles * slots_of
    share = weights.shape[0] // lax.axis_size("inst")
    feats, insts = lax.axis_size("feat"), lax.axis_size("inst")
    smem = pl.BlockSpec(memory_space=pltpu.SMEM)
    hbm = pl.BlockSpec(memory_space=pl.ANY)

    values_here, ids, picked, own, part = call(
        functools.partial(first_kernel, share),
        (
            near(values.shape, BF16),
            near((slots, width)),
            near((slots, width)),
            near((share, width)),
            near((tiles, rows)),
        ),
        (columns.T, live_slots.T, weights, values),
        in_specs=[smem, smem, hbm, hbm],
        scratch_shapes=[
            pltpu.VMEM(weights.shape, F32),
            pltpu.SemaphoreType.DMA,
            pltpu.SemaphoreType.DMA((tiles,)),
        ],
    )
    payload, curvature = call(
        functools.partial(gradient_kernel, feats),
        (near((slots + SUB, width)), near((tiles, rows))),
        (labels.reshape(tiles, rows), values_here, ids, *feat_parts(part)),
    )
    halves = pltpu.VMEM((insts * slots, 2 * width), BF16)
    gradient, start_slot, onehot, payload = call(
        functools.partial(start_kernel, insts),
        (
            near((share, width)),
            near((slots, width)),
            near((slots + share, insts * slots), BF16),
            near((tiles + SUB, rows)),
        ),
        (values_here, ids, picked, own, *inst_parts(payload)),
        scratch_shapes=[halves],
    )
    along, payload = call(
        functools.partial(curve_kernel, feats),
        (near((tiles, rows)), near((slots + SUB, width))),
        (values_here, ids, curvature, *feat_parts(payload)),
    )
    next_share, known, payload = call(
        functools.partial(turn_kernel, insts),
        (near((share, width)), near((SUB, width)), near((tiles + SUB, rows))),
        (values_here, onehot, start_slot, gradient, *inst_parts(payload)),
        scratch_shapes=[halves, pltpu.VMEM((slots, width), F32)],
    )
    scalars = call(
        functools.partial(inner_kernel, feats),
        near((SUB, width)),
        (curvature, along, *feat_parts(payload)),
    )
    step = call(
        last_kernel,
        near((share, width)),
        (inst_sum(scalars), known, gradient, next_share),
    )
    return (step, gradient)


def solution(mesh):
    in_specs = (
        P("inst", "feat", None, None),
        P("inst", "feat"),
        P("inst", "feat"),
        P("inst"),
        P("feat", None),
    )
    out_specs = (P(("feat", "inst"), None), P(("feat", "inst"), None))
    return jax.shard_map(
        per_device, mesh=mesh, in_specs=in_specs, out_specs=out_specs, check_vma=False
    )
```

time: 334 us -> 71 us (0.21)
  waiting for transfers between devices: 234 us -> 27.5 us
  blocking collectives: 40.5 us -> 0 us
  starting transfers between devices: 0.12 us -> 26.6 us
  matrix products: 18.6 us -> 0 us
  other arithmetic: 17.6 us -> 0.01 us
  between operations: 17.7 us -> 0.71 us
  Pallas kernels: 0 us -> 9.77 us
    psum x3 -> x0, waiting for transfers between devices: 233 us -> none  [collect(): return lax.psum(term, 'inst')]
    psum x6 -> x0, blocking collectives: 40.5 us -> none  [the longest x3 20.6 us: forward(): return lax.psum(partial_value, 'feat')]
    ppermute x0 -> x26, waiting for transfers between devices: none -> 27.5 us  [the longest x17 18.7 us: swap(): return lax.ppermute(array, axis, [(i, i ^ distance) for i in range(size)])]
    ppermute x0 -> x26, starting transfers between devices: none -> 26.6 us  [the longest x17 20.7 us: swap(): return lax.ppermute(array, axis, [(i, i ^ distance) for i in range(size)])]
    dot_general x6 -> x0, matrix products: 18.6 us -> none  [the longest x3 10.1 us: forward(): jnp.einsum('tjrf,tjf->tr', values, picked, preferred_element_type=jnp.flo...]
    pallas_call x0 -> x7, Pallas kernels: none -> 9.77 us  [call(): pl.pallas_call(kernel, out_shape=out_shape, in_specs=in_specs, out_specs=...]
    reduce_sum x3 -> x0, other arithmetic: 6.4 us -> none  [the longest x2 4.29 us: per_device(): alpha = norm_now / inner(jnp.sum(direction * image))]
    scatter-add x3 -> x0, other arithmetic: 6.33 us -> none  [local_back(): jax.ops.segment_sum(contrib.reshape(-1, width), columns.reshape(-1), num_...]
  transfers between devices with their start and end apart: 3 -> 26, of which waited for: 3 -> 22; matrix products, arithmetic and copies ran while one was open for 0% -> 1% of each run, Pallas kernels for 0% -> 0%
where the time goes in v2:
time: 71 us; the launch traced here: 70.7 us
  waiting for transfers between devices  27.5 us (39%)
  starting transfers between devices  26.6 us (37%)
  Pallas kernels  9.77 us (14%)
  local copies, waits for them, and re-layouts  6.06 us (9%)
  between operations  0.71 us (1%)
    ppermute x17, starting transfers between devices, swap(): return lax.ppermute(array, axis, [(i, i ^ distance) for i in range(size)])  20.7 us
    ppermute x17, waiting for transfers between devices, swap(): return lax.ppermute(array, axis, [(i, i ^ distance) for i in range(size)])  18.7 us
    pallas_call x7, Pallas kernels, call(): pl.pallas_call(kernel, out_shape=out_shape, in_specs=in_specs, out_specs=...  9.77 us
    ppermute x9, waiting for transfers between devices, feat_parts(): lax.ppermute(array, 'feat', [(i, (i + k) % size) for i in range(size)])  8.84 us
    unnamed x12, local copies, waits for them, and re-layouts  6.06 us
    ppermute x9, starting transfers between devices, feat_parts(): lax.ppermute(array, 'feat', [(i, (i + k) % size) for i in range(size)])  5.89 us
  transfers between devices with their start and end apart: 26, of which 22 were waited for; matrix products, arithmetic and copies ran while one was open for 1% of the time, Pallas kernels for 0%

profile of v2, /device:TPU:0, one launch (start us, length us, event | category | flops | bytes accessed | tf_op | source)
XLA Modules:
  0.0 70.7 jit_solution(2833220430131729453)
XLA Ops:
  0.6 2.2 %copy-done = bf16[16,8,128,128]{3,2,1,0:T(8,128)(2,1)S(1)} copy-done((bf16[16,8,128,128]{3,2,1,0:T(8,128)(2,1)S(1)}, bf16[16,8,128,128]{3,2,1,0:T(8,128)(2,1)}, u32[]{:S(2)}) %copy-start) | copy-done | bytes 4194328
  2.8 1.2 %copy-done.1 = f32[2048,128]{1,0:T(8,128)S(1)} copy-done((f32[2048,128]{1,0:T(8,128)S(1)}, f32[2048,128]{1,0:T(8,128)}, u32[]{:S(2)}) %copy-start.1) | copy-done | bytes 1048600
  5.4 4.5 %shard_map.68 = (bf16[16,8,128,128]{3,2,1,0:T(8,128)(2,1)S(1)}, f32[128,128]{1,0:T(8,128)S(1)}, f32[128,128]{1,0:T(8,128)S(1)}, f32[256,128]{1,0:T(8,128)S(1)}, f32[16,128]{1,0:T(8,128)S(1)}) custom-call(s32[8,16]{1,0:T(8,128)S(1)} %bitcast.4, s32[1,16]{1,0:T(1,128)S(1)} %bitcast.5, f32[2048,128]{1,0:T(8,128)S(1)} %copy-done.1, ...), custom_call_target="tpu_custom_call" | custom-call | tf_op jit(solution)/shard_map/pallas_call | solution.py:245
  9.9 2.4 %collective-permute-start.2 = (f32[16,128]{1,0:T(8,128)S(1)}, f32[16,128]{1,0:T(8,128)S(1)}, u32[]{:S(2)}, u32[]{:S(2)}) collective-permute-start(f32[16,128]{1,0:T(8,128)S(1)} %get-tuple-element.20.refs_0_), channel_id=1, source_target_pairs={{0,3},{1,0},{2,1},{3,2},{4,7},{5,4},{6,5},{7,6},{8,11},{9,8},{10,9... | collective-permute-start | bytes 24584 | tf_op jit(solution)/shard_map/ppermute | solution.py:263
  13.7 2.3 %collective-permute-done.1.refs_2_ = f32[16,128]{1,0:T(8,128)S(1)} collective-permute-done((f32[16,128]{1,0:T(8,128)S(1)}, f32[16,128]{1,0:T(8,128)S(1)}, u32[]{:S(2)}, u32[]{:S(2)}) %collective-permute-start.1) | collective-permute-done | bytes 8224 | tf_op jit(solution)/shard_map/ppermute | solution.py:263
  16.7 3.7 %collective-permute-start.5 = (f32[136,128]{1,0:T(8,128)S(1)}, f32[136,128]{1,0:T(8,128)S(1)}, u32[]{:S(2)}, u32[]{:S(2)}) collective-permute-start(f32[136,128]{1,0:T(8,128)S(1)} %get-tuple-element.24.refs_0_), channel_id=1, source_target_pairs={{0,24},{4,28},{8,16},{12,20},{16,8},{20,12},{24,0},{28,4},{1,25},{... | collective-permute-start | bytes 208904 | tf_op jit(solution)/shard_map/ppermute | solution.py:257
  21.1 1.5 %collective-permute-start.6 = (f32[136,128]{1,0:T(8,128)S(1)}, f32[136,128]{1,0:T(8,128)S(1)}, u32[]{:S(2)}, u32[]{:S(2)}) collective-permute-start(f32[136,128]{1,0:T(8,128)S(1)} %get-tuple-element.24.refs_0_), channel_id=1, source_target_pairs={{0,4},{4,0},{8,12},{12,8},{16,20},{20,16},{24,28},{28,24},{1,5},{5... | collective-permute-start | bytes 208904 | tf_op jit(solution)/shard_map/ppermute | solution.py:257
  23.4 1.5 %collective-permute-start.9 = (f32[136,128]{1,0:T(8,128)S(1)}, f32[136,128]{1,0:T(8,128)S(1)}, u32[]{:S(2)}, u32[]{:S(2)}) collective-permute-start(f32[136,128]{1,0:T(8,128)S(1)} %collective-permute-done.5.refs_3_), channel_id=1, source_target_pairs={{0,4},{4,0},{8,12},{12,8},{16,20},{20,16},{24,28},{28,24},{1,5},{5... | collective-permute-start | bytes 208904 | tf_op jit(solution)/shard_map/ppermute | solution.py:257
  24.9 0.9 %collective-permute-done.4.refs_2_ = f32[136,128]{1,0:T(8,128)S(1)} collective-permute-done((f32[136,128]{1,0:T(8,128)S(1)}, f32[136,128]{1,0:T(8,128)S(1)}, u32[]{:S(2)}, u32[]{:S(2)}) %collective-permute-start.4) | collective-permute-done | bytes 69664 | tf_op jit(solution)/shard_map/ppermute | solution.py:257
  25.8 1.5 %collective-permute-start.8 = (f32[136,128]{1,0:T(8,128)S(1)}, f32[136,128]{1,0:T(8,128)S(1)}, u32[]{:S(2)}, u32[]{:S(2)}) collective-permute-start(f32[136,128]{1,0:T(8,128)S(1)} %collective-permute-done.4.refs_2_), channel_id=1, source_target_pairs={{0,4},{4,0},{8,12},{12,8},{16,20},{20,16},{24,28},{28,24},{1,5},{5... | collective-permute-start | bytes 208904 | tf_op jit(solution)/shard_map/ppermute | solution.py:257
  28.0 2.1 %collective-permute-done.8.refs_6_ = f32[136,128]{1,0:T(8,128)S(1)} collective-permute-done((f32[136,128]{1,0:T(8,128)S(1)}, f32[136,128]{1,0:T(8,128)S(1)}, u32[]{:S(2)}, u32[]{:S(2)}) %collective-permute-start.8) | collective-permute-done | bytes 69664 | tf_op jit(solution)/shard_map/ppermute | solution.py:257
  30.1 1.5 %collective-permute-done.7.refs_5_ = f32[136,128]{1,0:T(8,128)S(1)} collective-permute-done((f32[136,128]{1,0:T(8,128)S(1)}, f32[136,128]{1,0:T(8,128)S(1)}, u32[]{:S(2)}, u32[]{:S(2)}) %collective-permute-start.7) | collective-permute-done | bytes 69664 | tf_op jit(solution)/shard_map/ppermute | solution.py:257
  31.7 1.9 %shard_map.70 = (f32[256,128]{1,0:T(8,128)S(1)}, f32[128,128]{1,0:T(8,128)S(1)}, bf16[384,1024]{1,0:T(8,128)(2,1)S(1)}, f32[24,128]{1,0:T(8,128)S(1)}) custom-call(bf16[16,8,128,128]{3,2,1,0:T(8,128)(2,1)S(1)} %get-tuple-element.18.values, f32[128,128]{1,0:T(8,128)S(1)} %get-tuple-element.19.ids, f32[128,128]{1,0:T(8,128)S(1)} %get-tuple-element.22.picked, ...), custom_call_target="tpu_custom_call" | custom-call | tf_op jit(solution)/shard_map/pallas_call | solution.py:245
  33.6 1.2 %collective-permute-start.11 = (f32[24,128]{1,0:T(8,128)S(1)}, f32[24,128]{1,0:T(8,128)S(1)}, u32[]{:S(2)}, u32[]{:S(2)}) collective-permute-start(f32[24,128]{1,0:T(8,128)S(1)} %get-tuple-element.25.refs_0_), channel_id=1, source_target_pairs={{0,2},{1,3},{2,0},{3,1},{4,6},{5,7},{6,4},{7,5},{8,10},{9,11},{10,... | collective-permute-start | bytes 36872 | tf_op jit(solution)/shard_map/ppermute | solution.py:263
  35.0 2.4 %collective-permute-done.11.refs_2_ = f32[24,128]{1,0:T(8,128)S(1)} collective-permute-done((f32[24,128]{1,0:T(8,128)S(1)}, f32[24,128]{1,0:T(8,128)S(1)}, u32[]{:S(2)}, u32[]{:S(2)}) %collective-permute-start.11) | collective-permute-done | bytes 12320 | tf_op jit(solution)/shard_map/ppermute | solution.py:263
  38.5 2.2 %collective-permute-start.15 = (f32[136,128]{1,0:T(8,128)S(1)}, f32[136,128]{1,0:T(8,128)S(1)}, u32[]{:S(2)}, u32[]{:S(2)}) collective-permute-start(f32[136,128]{1,0:T(8,128)S(1)} %get-tuple-element.30.refs_0_), channel_id=1, source_target_pairs={{0,24},{4,28},{8,16},{12,20},{16,8},{20,12},{24,0},{28,4},{1,25},{... | collective-permute-start | bytes 208904 | tf_op jit(solution)/shard_map/ppermute | solution.py:257
  40.7 2.2 %collective-permute-start.13 = (f32[136,128]{1,0:T(8,128)S(1)}, f32[136,128]{1,0:T(8,128)S(1)}, u32[]{:S(2)}, u32[]{:S(2)}) collective-permute-start(f32[136,128]{1,0:T(8,128)S(1)} %get-tuple-element.30.refs_0_), channel_id=1, source_target_pairs={{0,8},{4,12},{8,0},{12,4},{16,24},{20,28},{24,16},{28,20},{1,9},{5... | collective-permute-start | bytes 208904 | tf_op jit(solution)/shard_map/ppermute | solution.py:257
  43.7 1.4 %collective-permute-done.15.refs_3_ = f32[136,128]{1,0:T(8,128)S(1)} collective-permute-done((f32[136,128]{1,0:T(8,128)S(1)}, f32[136,128]{1,0:T(8,128)S(1)}, u32[]{:S(2)}, u32[]{:S(2)}) %collective-permute-start.15) | collective-permute-done | bytes 69664 | tf_op jit(solution)/shard_map/ppermute | solution.py:257
  45.1 0.8 %collective-permute-start.19 = (f32[136,128]{1,0:T(8,128)S(1)}, f32[136,128]{1,0:T(8,128)S(1)}, u32[]{:S(2)}, u32[]{:S(2)}) collective-permute-start(f32[136,128]{1,0:T(8,128)S(1)} %collective-permute-done.15.refs_3_), channel_id=1, source_target_pairs={{0,4},{4,0},{8,12},{12,8},{16,20},{20,16},{24,28},{28,24},{1,5},{5... | collective-permute-start | bytes 208904 | tf_op jit(solution)/shard_map/ppermute | solution.py:257
  46.6 1.0 %collective-permute-start.18 = (f32[136,128]{1,0:T(8,128)S(1)}, f32[136,128]{1,0:T(8,128)S(1)}, u32[]{:S(2)}, u32[]{:S(2)}) collective-permute-start(f32[136,128]{1,0:T(8,128)S(1)} %collective-permute-done.14.refs_2_), channel_id=1, source_target_pairs={{0,4},{4,0},{8,12},{12,8},{16,20},{20,16},{24,28},{28,24},{1,5},{5... | collective-permute-start | bytes 208904 | tf_op jit(solution)/shard_map/ppermute | solution.py:257
  47.6 1.1 %collective-permute-start.17 = (f32[136,128]{1,0:T(8,128)S(1)}, f32[136,128]{1,0:T(8,128)S(1)}, u32[]{:S(2)}, u32[]{:S(2)}) collective-permute-start(f32[136,128]{1,0:T(8,128)S(1)} %collective-permute-done.13.refs_1_), channel_id=1, source_target_pairs={{0,4},{4,0},{8,12},{12,8},{16,20},{20,16},{24,28},{28,24},{1,5},{5... | collective-permute-start | bytes 208904 | tf_op jit(solution)/shard_map/ppermute | solution.py:257
  48.7 1.4 %collective-permute-done.19.refs_7_ = f32[136,128]{1,0:T(8,128)S(1)} collective-permute-done((f32[136,128]{1,0:T(8,128)S(1)}, f32[136,128]{1,0:T(8,128)S(1)}, u32[]{:S(2)}, u32[]{:S(2)}) %collective-permute-start.19) | collective-permute-done | bytes 69664 | tf_op jit(solution)/shard_map/ppermute | solution.py:257
  50.1 0.9 %collective-permute-done.18.refs_6_ = f32[136,128]{1,0:T(8,128)S(1)} collective-permute-done((f32[136,128]{1,0:T(8,128)S(1)}, f32[136,128]{1,0:T(8,128)S(1)}, u32[]{:S(2)}, u32[]{:S(2)}) %collective-permute-start.18) | collective-permute-done | bytes 69664 | tf_op jit(solution)/shard_map/ppermute | solution.py:257
  51.0 1.0 %collective-permute-done.17.refs_5_ = f32[136,128]{1,0:T(8,128)S(1)} collective-permute-done((f32[136,128]{1,0:T(8,128)S(1)}, f32[136,128]{1,0:T(8,128)S(1)}, u32[]{:S(2)}, u32[]{:S(2)}) %collective-permute-start.17) | collective-permute-done | bytes 69664 | tf_op jit(solution)/shard_map/ppermute | solution.py:257
  51.9 1.9 %shard_map.72 = (f32[256,128]{1,0:T(8,128)S(1)}, f32[8,128]{1,0:T(8,128)S(1)}, f32[24,128]{1,0:T(8,128)S(1)}) custom-call(bf16[16,8,128,128]{3,2,1,0:T(8,128)(2,1)S(1)} %get-tuple-element.18.values, bf16[384,1024]{1,0:T(8,128)(2,1)S(1)} %get-tuple-element.27.onehot, f32[128,128]{1,0:T(8,128)S(1)} %get-tuple-element.28.start_slot, ...), custom_call_target="tpu_custom_call" | custom-call | tf_op jit(solution)/shard_map/pallas_call | solution.py:245
  53.8 1.1 %collective-permute-start.21 = (f32[24,128]{1,0:T(8,128)S(1)}, f32[24,128]{1,0:T(8,128)S(1)}, u32[]{:S(2)}, u32[]{:S(2)}) collective-permute-start(f32[24,128]{1,0:T(8,128)S(1)} %get-tuple-element.31.refs_0_), channel_id=1, source_target_pairs={{0,2},{1,3},{2,0},{3,1},{4,6},{5,7},{6,4},{7,5},{8,10},{9,11},{10,... | collective-permute-start | bytes 36872 | tf_op jit(solution)/shard_map/ppermute | solution.py:263
  55.2 2.4 %collective-permute-done.21.refs_2_ = f32[24,128]{1,0:T(8,128)S(1)} collective-permute-done((f32[24,128]{1,0:T(8,128)S(1)}, f32[24,128]{1,0:T(8,128)S(1)}, u32[]{:S(2)}, u32[]{:S(2)}) %collective-permute-start.21) | collective-permute-done | bytes 12320 | tf_op jit(solution)/shard_map/ppermute | solution.py:263
  58.1 1.3 %collective-permute-start.23 = (f32[8,128]{1,0:T(8,128)S(1)}, f32[8,128]{1,0:T(8,128)S(1)}, u32[]{:S(2)}, u32[]{:S(2)}) collective-permute-start(f32[8,128]{1,0:T(8,128)S(1)} %shard_map.73), channel_id=1, source_target_pairs={{0,4},{4,0},{8,12},{12,8},{16,20},{20,16},{24,28},{28,24},{1,5},{5... | collective-permute-start | bytes 12296 | tf_op jit(solution)/shard_map/ppermute | solution.py:257
  59.5 2.3 %collective-permute-done.23 = f32[8,128]{1,0:T(8,128)S(1)} collective-permute-done((f32[8,128]{1,0:T(8,128)S(1)}, f32[8,128]{1,0:T(8,128)S(1)}, u32[]{:S(2)}, u32[]{:S(2)}) %collective-permute-start.23) | collective-permute-done | bytes 4128 | tf_op jit(solution)/shard_map/ppermute | solution.py:257
  61.8 3.6 %collective-permute-done.24 = f32[8,128]{1,0:T(8,128)S(1)} collective-permute-done((f32[8,128]{1,0:T(8,128)S(1)}, f32[8,128]{1,0:T(8,128)S(1)}, u32[]{:S(2)}, u32[]{:S(2)}) %collective-permute-start.24) | collective-permute-done | bytes 4128 | tf_op jit(solution)/shard_map/ppermute | solution.py:257
  65.4 1.9 %collective-permute-start.25 = (f32[8,128]{1,0:T(8,128)S(1)}, f32[8,128]{1,0:T(8,128)S(1)}, u32[]{:S(2)}, u32[]{:S(2)}) collective-permute-start(f32[8,128]{1,0:T(8,128)S(1)} %add.10), channel_id=1, source_target_pairs={{0,16},{4,20},{8,24},{12,28},{16,0},{20,4},{24,8},{28,12},{1,17},{... | collective-permute-start | bytes 12296 | tf_op jit(solution)/shard_map/ppermute | solution.py:257
  67.9 2.0 %collective-permute-done.25 = f32[8,128]{1,0:T(8,128)S(1)} collective-permute-done((f32[8,128]{1,0:T(8,128)S(1)}, f32[8,128]{1,0:T(8,128)S(1)}, u32[]{:S(2)}, u32[]{:S(2)}) %collective-permute-start.25) | collective-permute-done | bytes 4128 | tf_op jit(solution)/shard_map/ppermute | solution.py:257
  (42 shorter events, 10.9 us)
Async XLA Ops:
  0.6 2.2 %copy-start = (bf16[16,8,128,128]{3,2,1,0:T(8,128)(2,1)S(1)}, bf16[16,8,128,128]{3,2,1,0:T(8,128)(2,1)}, u32[]{:S(2)}) copy-start(bf16[16,8,128,128]{3,2,1,0:T(8,128)(2,1)} %values_in.1) | copy-start | bytes 12582916
  2.8 1.2 %copy-start.1 = (f32[2048,128]{1,0:T(8,128)S(1)}, f32[2048,128]{1,0:T(8,128)}, u32[]{:S(2)}) copy-start(f32[2048,128]{1,0:T(8,128)} %weights.1) | copy-start | bytes 3145732
  4.0 0.7 copy-start.3
  4.7 0.7 copy-start.4
  5.4 10.6 %copy-start.2 = (s32[2048]{0:T(1024)S(1)}, s32[2048]{0:T(1024)}, u32[]{:S(2)}) copy-start(s32[2048]{0:T(1024)} %param.8) | copy-start | bytes 24580
  9.9 3.8 %collective-permute-start.2 = (f32[16,128]{1,0:T(8,128)S(1)}, f32[16,128]{1,0:T(8,128)S(1)}, u32[]{:S(2)}, u32[]{:S(2)}) collective-permute-start(f32[16,128]{1,0:T(8,128)S(1)} %get-tuple-element.20.refs_0_), channel_id=1, source_target_pairs={{0,3},{1,0},{2,1},{3,2},{4,7},{5,4},{6,5},{7,6},{8,11},{9,8},{10,9... | collective-permute-start | bytes 24584 | tf_op jit(solution)/shard_map/ppermute | solution.py:263
  12.3 3.7 %collective-permute-start.1 = (f32[16,128]{1,0:T(8,128)S(1)}, f32[16,128]{1,0:T(8,128)S(1)}, u32[]{:S(2)}, u32[]{:S(2)}) collective-permute-start(f32[16,128]{1,0:T(8,128)S(1)} %get-tuple-element.20.refs_0_), channel_id=1, source_target_pairs={{0,2},{1,3},{2,0},{3,1},{4,6},{5,7},{6,4},{7,5},{8,10},{9,11},{10,... | collective-permute-start | bytes 24584 | tf_op jit(solution)/shard_map/ppermute | solution.py:263
  12.9 3.1 %collective-permute-start = (f32[16,128]{1,0:T(8,128)S(1)}, f32[16,128]{1,0:T(8,128)S(1)}, u32[]{:S(2)}, u32[]{:S(2)}) collective-permute-start(f32[16,128]{1,0:T(8,128)S(1)} %get-tuple-element.20.refs_0_), channel_id=1, source_target_pairs={{0,1},{1,2},{2,3},{3,0},{4,5},{5,6},{6,7},{7,4},{8,9},{9,10},{10,1... | collective-permute-start | bytes 24584 | tf_op jit(solution)/shard_map/ppermute | solution.py:263
  16.7 6.7 %collective-permute-start.5 = (f32[136,128]{1,0:T(8,128)S(1)}, f32[136,128]{1,0:T(8,128)S(1)}, u32[]{:S(2)}, u32[]{:S(2)}) collective-permute-start(f32[136,128]{1,0:T(8,128)S(1)} %get-tuple-element.24.refs_0_), channel_id=1, source_target_pairs={{0,24},{4,28},{8,16},{12,20},{16,8},{20,12},{24,0},{28,4},{1,25},{... | collective-permute-start | bytes 208904 | tf_op jit(solution)/shard_map/ppermute | solution.py:257
  20.4 5.5 %collective-permute-start.4 = (f32[136,128]{1,0:T(8,128)S(1)}, f32[136,128]{1,0:T(8,128)S(1)}, u32[]{:S(2)}, u32[]{:S(2)}) collective-permute-start(f32[136,128]{1,0:T(8,128)S(1)} %get-tuple-element.24.refs_0_), channel_id=1, source_target_pairs={{0,16},{4,20},{8,24},{12,28},{16,0},{20,4},{24,8},{28,12},{1,17},{... | collective-permute-start | bytes 208904 | tf_op jit(solution)/shard_map/ppermute | solution.py:257
  20.4 7.0 %collective-permute-start.3 = (f32[136,128]{1,0:T(8,128)S(1)}, f32[136,128]{1,0:T(8,128)S(1)}, u32[]{:S(2)}, u32[]{:S(2)}) collective-permute-start(f32[136,128]{1,0:T(8,128)S(1)} %get-tuple-element.24.refs_0_), channel_id=1, source_target_pairs={{0,8},{4,12},{8,0},{12,4},{16,24},{20,28},{24,16},{28,20},{1,9},{5... | collective-permute-start | bytes 208904 | tf_op jit(solution)/shard_map/ppermute | solution.py:257
  21.1 6.7 %collective-permute-start.6 = (f32[136,128]{1,0:T(8,128)S(1)}, f32[136,128]{1,0:T(8,128)S(1)}, u32[]{:S(2)}, u32[]{:S(2)}) collective-permute-start(f32[136,128]{1,0:T(8,128)S(1)} %get-tuple-element.24.refs_0_), channel_id=1, source_target_pairs={{0,4},{4,0},{8,12},{12,8},{16,20},{20,16},{24,28},{28,24},{1,5},{5... | collective-permute-start | bytes 208904 | tf_op jit(solution)/shard_map/ppermute | solution.py:257
  23.4 4.7 %collective-permute-start.9 = (f32[136,128]{1,0:T(8,128)S(1)}, f32[136,128]{1,0:T(8,128)S(1)}, u32[]{:S(2)}, u32[]{:S(2)}) collective-permute-start(f32[136,128]{1,0:T(8,128)S(1)} %collective-permute-done.5.refs_3_), channel_id=1, source_target_pairs={{0,4},{4,0},{8,12},{12,8},{16,20},{20,16},{24,28},{28,24},{1,5},{5... | collective-permute-start | bytes 208904 | tf_op jit(solution)/shard_map/ppermute | solution.py:257
  25.8 4.3 %collective-permute-start.8 = (f32[136,128]{1,0:T(8,128)S(1)}, f32[136,128]{1,0:T(8,128)S(1)}, u32[]{:S(2)}, u32[]{:S(2)}) collective-permute-start(f32[136,128]{1,0:T(8,128)S(1)} %collective-permute-done.4.refs_2_), channel_id=1, source_target_pairs={{0,4},{4,0},{8,12},{12,8},{16,20},{20,16},{24,28},{28,24},{1,5},{5... | collective-permute-start | bytes 208904 | tf_op jit(solution)/shard_map/ppermute | solution.py:257
  27.3 4.3 %collective-permute-start.7 = (f32[136,128]{1,0:T(8,128)S(1)}, f32[136,128]{1,0:T(8,128)S(1)}, u32[]{:S(2)}, u32[]{:S(2)}) collective-permute-start(f32[136,128]{1,0:T(8,128)S(1)} %collective-permute-done.3.refs_1_), channel_id=1, source_target_pairs={{0,4},{4,0},{8,12},{12,8},{16,20},{20,16},{24,28},{28,24},{1,5},{5... | collective-permute-start | bytes 208904 | tf_op jit(solution)/shard_map/ppermute | solution.py:257
  33.5 1.5 %collective-permute-start.12 = (f32[24,128]{1,0:T(8,128)S(1)}, f32[24,128]{1,0:T(8,128)S(1)}, u32[]{:S(2)}, u32[]{:S(2)}) collective-permute-start(f32[24,128]{1,0:T(8,128)S(1)} %get-tuple-element.25.refs_0_), channel_id=1, source_target_pairs={{0,3},{1,0},{2,1},{3,2},{4,7},{5,4},{6,5},{7,6},{8,11},{9,8},{10,9... | collective-permute-start | bytes 36872 | tf_op jit(solution)/shard_map/ppermute | solution.py:263
  33.6 3.8 %collective-permute-start.11 = (f32[24,128]{1,0:T(8,128)S(1)}, f32[24,128]{1,0:T(8,128)S(1)}, u32[]{:S(2)}, u32[]{:S(2)}) collective-permute-start(f32[24,128]{1,0:T(8,128)S(1)} %get-tuple-element.25.refs_0_), channel_id=1, source_target_pairs={{0,2},{1,3},{2,0},{3,1},{4,6},{5,7},{6,4},{7,5},{8,10},{9,11},{10,... | collective-permute-start | bytes 36872 | tf_op jit(solution)/shard_map/ppermute | solution.py:263
  34.8 3.1 %collective-permute-start.10 = (f32[24,128]{1,0:T(8,128)S(1)}, f32[24,128]{1,0:T(8,128)S(1)}, u32[]{:S(2)}, u32[]{:S(2)}) collective-permute-start(f32[24,128]{1,0:T(8,128)S(1)} %get-tuple-element.25.refs_0_), channel_id=1, source_target_pairs={{0,1},{1,2},{2,3},{3,0},{4,5},{5,6},{6,7},{7,4},{8,9},{9,10},{10,1... | collective-permute-start | bytes 36872 | tf_op jit(solution)/shard_map/ppermute | solution.py:263
  38.5 6.6 %collective-permute-start.15 = (f32[136,128]{1,0:T(8,128)S(1)}, f32[136,128]{1,0:T(8,128)S(1)}, u32[]{:S(2)}, u32[]{:S(2)}) collective-permute-start(f32[136,128]{1,0:T(8,128)S(1)} %get-tuple-element.30.refs_0_), channel_id=1, source_target_pairs={{0,24},{4,28},{8,16},{12,20},{16,8},{20,12},{24,0},{28,4},{1,25},{... | collective-permute-start | bytes 208904 | tf_op jit(solution)/shard_map/ppermute | solution.py:257
  40.7 5.9 %collective-permute-start.14 = (f32[136,128]{1,0:T(8,128)S(1)}, f32[136,128]{1,0:T(8,128)S(1)}, u32[]{:S(2)}, u32[]{:S(2)}) collective-permute-start(f32[136,128]{1,0:T(8,128)S(1)} %get-tuple-element.30.refs_0_), channel_id=1, source_target_pairs={{0,16},{4,20},{8,24},{12,28},{16,0},{20,4},{24,8},{28,12},{1,17},{... | collective-permute-start | bytes 208904 | tf_op jit(solution)/shard_map/ppermute | solution.py:257
  40.7 6.9 %collective-permute-start.13 = (f32[136,128]{1,0:T(8,128)S(1)}, f32[136,128]{1,0:T(8,128)S(1)}, u32[]{:S(2)}, u32[]{:S(2)}) collective-permute-start(f32[136,128]{1,0:T(8,128)S(1)} %get-tuple-element.30.refs_0_), channel_id=1, source_target_pairs={{0,8},{4,12},{8,0},{12,4},{16,24},{20,28},{24,16},{28,20},{1,9},{5... | collective-permute-start | bytes 208904 | tf_op jit(solution)/shard_map/ppermute | solution.py:257
  43.0 5.7 %collective-permute-start.16 = (f32[136,128]{1,0:T(8,128)S(1)}, f32[136,128]{1,0:T(8,128)S(1)}, u32[]{:S(2)}, u32[]{:S(2)}) collective-permute-start(f32[136,128]{1,0:T(8,128)S(1)} %get-tuple-element.30.refs_0_), channel_id=1, source_target_pairs={{0,4},{4,0},{8,12},{12,8},{16,20},{20,16},{24,28},{28,24},{1,5},{5... | collective-permute-start | bytes 208904 | tf_op jit(solution)/shard_map/ppermute | solution.py:257
  45.1 5.0 %collective-permute-start.19 = (f32[136,128]{1,0:T(8,128)S(1)}, f32[136,128]{1,0:T(8,128)S(1)}, u32[]{:S(2)}, u32[]{:S(2)}) collective-permute-start(f32[136,128]{1,0:T(8,128)S(1)} %collective-permute-done.15.refs_3_), channel_id=1, source_target_pairs={{0,4},{4,0},{8,12},{12,8},{16,20},{20,16},{24,28},{28,24},{1,5},{5... | collective-permute-start | bytes 208904 | tf_op jit(solution)/shard_map/ppermute | solution.py:257
  46.6 4.3 %collective-permute-start.18 = (f32[136,128]{1,0:T(8,128)S(1)}, f32[136,128]{1,0:T(8,128)S(1)}, u32[]{:S(2)}, u32[]{:S(2)}) collective-permute-start(f32[136,128]{1,0:T(8,128)S(1)} %collective-permute-done.14.refs_2_), channel_id=1, source_target_pairs={{0,4},{4,0},{8,12},{12,8},{16,20},{20,16},{24,28},{28,24},{1,5},{5... | collective-permute-start | bytes 208904 | tf_op jit(solution)/shard_map/ppermute | solution.py:257
  47.6 4.3 %collective-permute-start.17 = (f32[136,128]{1,0:T(8,128)S(1)}, f32[136,128]{1,0:T(8,128)S(1)}, u32[]{:S(2)}, u32[]{:S(2)}) collective-permute-start(f32[136,128]{1,0:T(8,128)S(1)} %collective-permute-done.13.refs_1_), channel_id=1, source_target_pairs={{0,4},{4,0},{8,12},{12,8},{16,20},{20,16},{24,28},{28,24},{1,5},{5... | collective-permute-start | bytes 208904 | tf_op jit(solution)/shard_map/ppermute | solution.py:257
  53.8 1.5 %collective-permute-start.22 = (f32[24,128]{1,0:T(8,128)S(1)}, f32[24,128]{1,0:T(8,128)S(1)}, u32[]{:S(2)}, u32[]{:S(2)}) collective-permute-start(f32[24,128]{1,0:T(8,128)S(1)} %get-tuple-element.31.refs_0_), channel_id=1, source_target_pairs={{0,3},{1,0},{2,1},{3,2},{4,7},{5,4},{6,5},{7,6},{8,11},{9,8},{10,9... | collective-permute-start | bytes 36872 | tf_op jit(solution)/shard_map/ppermute | solution.py:263
  53.8 3.8 %collective-permute-start.21 = (f32[24,128]{1,0:T(8,128)S(1)}, f32[24,128]{1,0:T(8,128)S(1)}, u32[]{:S(2)}, u32[]{:S(2)}) collective-permute-start(f32[24,128]{1,0:T(8,128)S(1)} %get-tuple-element.31.refs_0_), channel_id=1, source_target_pairs={{0,2},{1,3},{2,0},{3,1},{4,6},{5,7},{6,4},{7,5},{8,10},{9,11},{10,... | collective-permute-start | bytes 36872 | tf_op jit(solution)/shard_map/ppermute | solution.py:263
  54.9 3.1 %collective-permute-start.20 = (f32[24,128]{1,0:T(8,128)S(1)}, f32[24,128]{1,0:T(8,128)S(1)}, u32[]{:S(2)}, u32[]{:S(2)}) collective-permute-start(f32[24,128]{1,0:T(8,128)S(1)} %get-tuple-element.31.refs_0_), channel_id=1, source_target_pairs={{0,1},{1,2},{2,3},{3,0},{4,5},{5,6},{6,7},{7,4},{8,9},{9,10},{10,1... | collective-permute-start | bytes 36872 | tf_op jit(solution)/shard_map/ppermute | solution.py:263
  58.1 3.7 %collective-permute-start.23 = (f32[8,128]{1,0:T(8,128)S(1)}, f32[8,128]{1,0:T(8,128)S(1)}, u32[]{:S(2)}, u32[]{:S(2)}) collective-permute-start(f32[8,128]{1,0:T(8,128)S(1)} %shard_map.73), channel_id=1, source_target_pairs={{0,4},{4,0},{8,12},{12,8},{16,20},{20,16},{24,28},{28,24},{1,5},{5... | collective-permute-start | bytes 12296 | tf_op jit(solution)/shard_map/ppermute | solution.py:257
  61.8 3.6 %collective-permute-start.24 = (f32[8,128]{1,0:T(8,128)S(1)}, f32[8,128]{1,0:T(8,128)S(1)}, u32[]{:S(2)}, u32[]{:S(2)}) collective-permute-start(f32[8,128]{1,0:T(8,128)S(1)} %add.9), channel_id=1, source_target_pairs={{0,8},{4,12},{8,0},{12,4},{16,24},{20,28},{24,16},{28,20},{1,9},{5... | collective-permute-start | bytes 12296 | tf_op jit(solution)/shard_map/ppermute | solution.py:257
  65.4 4.5 %collective-permute-start.25 = (f32[8,128]{1,0:T(8,128)S(1)}, f32[8,128]{1,0:T(8,128)S(1)}, u32[]{:S(2)}, u32[]{:S(2)}) collective-permute-start(f32[8,128]{1,0:T(8,128)S(1)} %add.10), channel_id=1, source_target_pairs={{0,16},{4,20},{8,24},{12,28},{16,0},{20,4},{24,8},{28,12},{1,17},{... | collective-permute-start | bytes 12296 | tf_op jit(solution)/shard_map/ppermute | solution.py:257

commit v3 on v2

--- a/solution.py
+++ b/solution.py
@@ -77,18 +77,24 @@
         )
 
 
-def first_kernel(share, columns, live, weights, values_in, values, ids, picked, own, along,
-                 weights_here, weights_sem, values_sem):
+def first_kernel(share, columns_in, live_in, weights, values_in, values, ids, picked, own, along,
+                 columns, live, weights_here, small_sem, values_sem):
     tiles, slots, rows, width = values.shape
-    whole = pltpu.make_async_copy(weights, weights_here, weights_sem)
-    whole.start()
+    smalls = [
+        pltpu.make_async_copy(columns_in, columns, small_sem.at[0]),
+        pltpu.make_async_copy(live_in, live, small_sem.at[1]),
+        pltpu.make_async_copy(weights, weights_here, small_sem.at[2]),
+    ]
+    for small in smalls:
+        small.start()
     loads = [
         pltpu.make_async_copy(values_in.at[t], values.at[t], values_sem.at[t])
         for t in range(tiles)
     ]
     for load in loads:
         load.start()
-    whole.wait()
+    for small in smalls:
+        small.wait()
     for t in range(tiles):
         count = live[0, t]
         for j in range(slots):
@@ -200,24 +206,29 @@
 
 
 def inner_kernel(count, curvature, along, *refs):
-    parts, (scalars,) = refs[:count], refs[count:]
+    parts, (scalars, first_only) = refs[:count], refs[count:]
     tiles, width = along.shape
     summed = parts[0][...]
     for part in parts[1:]:
         summed = summed + part[...]
     turn = summed[:tiles, :]
     bent = curvature[...] * turn
-    scalars[...] = scalar_rows(
+    block = scalar_rows(
         width,
         summed[tiles : tiles + 1, 0:1],
         summed[tiles : tiles + 1, 1:2],
         total(bent * turn),
         total(bent * along[...]),
     )
-
-
-def last_kernel(scalars, known, gradient, next_share, step):
-    row = scalars[0:1, :]
+    scalars[...] = block
+    first_only[...] = jnp.where(lax.axis_index("feat") == 0, block, 0.0)
+
+
+def last_kernel(known, gradient, next_share, *refs):
+    parts, step = refs[:-1], refs[-1]
+    row = parts[0][0:1, :]
+    for part in parts[1:]:
+        row = row + part[0:1, :]
     norm_next, cross, turn_turn, turn_along = (read_scalar(row, i) for i in range(4))
     row = known[0:1, :]
     norm_now, curve_now, alpha = (read_scalar(row, i) for i in range(3))
@@ -237,7 +248,7 @@
     return pltpu.VMEM(shape, dtype)
 
 
-def call(kernel, out_shape, args, in_specs=None, scratch_shapes=(), keep=None):
+def call(kernel, out_shape, args, in_specs=None, scratch_shapes=()):
     vmem = pl.BlockSpec(memory_space=pltpu.VMEM)
     if in_specs is None:
         in_specs = [vmem] * len(args)
@@ -274,13 +285,24 @@
     return parts + [swap(part, "inst", 1) for part in parts]
 
 
-def inst_sum(array):
-    size = lax.axis_size("inst")
+def inst_sum(array, first_only):
+    size, feats = lax.axis_size("inst"), lax.axis_size("feat")
+    if size == 2 * feats:
+        fetched = first_only
+        for low in (0, 1):
+            pairs = [
+                (i * feats + f, (i ^ (2 * f + low)) * feats + f)
+                for i in range(size)
+                for f in range(feats)
+                if 2 * f + low
+            ]
+            fetched = fetched + lax.ppermute(array, ("inst", "feat"), pairs)
+        return feat_parts(fetched)
     distance = 1
     while distance < size:
         array = array + swap(array, "inst", distance)
         distance *= 2
-    return array
+    return [array]
 
 
 def per_device(values, columns, live_slots, labels, weights):
@@ -288,8 +310,6 @@
     slots = tiles * slots_of
     share = weights.shape[0] // lax.axis_size("inst")
     feats, insts = lax.axis_size("feat"), lax.axis_size("inst")
-    smem = pl.BlockSpec(memory_space=pltpu.SMEM)
-    hbm = pl.BlockSpec(memory_space=pl.ANY)
 
     values_here, ids, picked, own, part = call(
         functools.partial(first_kernel, share),
@@ -300,11 +320,16 @@
             near((share, width)),
             near((tiles, rows)),
         ),
-        (columns.T, live_slots.T, weights, values),
-        in_specs=[smem, smem, hbm, hbm],
+        [
+            pltpu.with_memory_space_constraint(a, pltpu.HBM)
+            for a in (columns.T, live_slots.T, weights, values)
+        ],
+        in_specs=[pl.BlockSpec(memory_space=pltpu.HBM)] * 4,
         scratch_shapes=[
+            pltpu.SMEM((slots_of, tiles), jnp.int32),
+            pltpu.SMEM((1, tiles), jnp.int32),
             pltpu.VMEM(weights.shape, F32),
-            pltpu.SemaphoreType.DMA,
+            pltpu.SemaphoreType.DMA((3,)),
             pltpu.SemaphoreType.DMA((tiles,)),
         ],
     )
@@ -336,15 +361,15 @@
         (values_here, onehot, start_slot, gradient, *inst_parts(payload)),
         scratch_shapes=[halves, pltpu.VMEM((slots, width), F32)],
     )
-    scalars = call(
+    scalars, first_only = call(
         functools.partial(inner_kernel, feats),
-        near((SUB, width)),
+        (near((SUB, width)), near((SUB, width))),
         (curvature, along, *feat_parts(payload)),
     )
     step = call(
         last_kernel,
         near((share, width)),
-        (inst_sum(scalars), known, gradient, next_share),
+        (known, gradient, next_share, *inst_sum(scalars, first_only)),
     )
     return (step, gradient)
 

time: 71 us -> 68.8 us (0.969)
  starting transfers between devices: 26.6 us -> 31.9 us
  local copies, waits for them, and re-layouts: 6.06 us -> 1.32 us
  waiting for transfers between devices: 27.5 us -> 23.4 us
  Pallas kernels: 9.77 us -> 11.2 us
    ppermute x17 -> x14, waiting for transfers between devices: 18.7 us -> 10.8 us  [swap(): return lax.ppermute(array, axis, [(i, i ^ distance) for i in range(size)])]
    ppermute x9 -> x12, starting transfers between devices: 5.89 us -> 12.4 us  [feat_parts(): lax.ppermute(array, 'feat', [(i, (i + k) % size) for i in range(size)])]
    unnamed x12 -> x4, local copies, waits for them, and re-layouts: 6.06 us -> 1.32 us
    ppermute x17 -> x14, starting transfers between devices: 20.7 us -> 17.5 us  [swap(): return lax.ppermute(array, axis, [(i, i ^ distance) for i in range(size)])]
    ppermute x9 -> x12, waiting for transfers between devices: 8.84 us -> 11 us  [feat_parts(): lax.ppermute(array, 'feat', [(i, (i + k) % size) for i in range(size)])]
    ppermute x0 -> x2, starting transfers between devices: none -> 2 us  [inst_sum(): fetched = fetched + lax.ppermute(array, ('inst', 'feat'), pairs)]
    ppermute x0 -> x2, waiting for transfers between devices: none -> 1.67 us  [inst_sum(): fetched = fetched + lax.ppermute(array, ('inst', 'feat'), pairs)]
    pallas_call x7, Pallas kernels: 9.77 us -> 11.2 us  [call(): pl.pallas_call(kernel, out_shape=out_shape, in_specs=in_specs, out_specs=...]
  transfers between devices with their start and end apart: 26 -> 28, of which waited for: 22 -> 22; matrix products, arithmetic and copies ran while one was open for 1% -> 1% of each run, Pallas kernels for 0% -> 0%
where the time goes in v3:
time: 68.8 us; the launch traced here: 68.6 us
  starting transfers between devices  31.9 us (46%)
  waiting for transfers between devices  23.4 us (34%)
  Pallas kernels  11.2 us (16%)
  local copies, waits for them, and re-layouts  1.32 us (2%)
  between operations  0.71 us (1%)
    ppermute x14, starting transfers between devices, swap(): return lax.ppermute(array, axis, [(i, i ^ distance) for i in range(size)])  17.5 us
    ppermute x12, starting transfers between devices, feat_parts(): lax.ppermute(array, 'feat', [(i, (i + k) % size) for i in range(size)])  12.4 us
    pallas_call x7, Pallas kernels, call(): pl.pallas_call(kernel, out_shape=out_shape, in_specs=in_specs, out_specs=...  11.2 us
    ppermute x12, waiting for transfers between devices, feat_parts(): lax.ppermute(array, 'feat', [(i, (i + k) % size) for i in range(size)])  11 us
    ppermute x14, waiting for transfers between devices, swap(): return lax.ppermute(array, axis, [(i, i ^ distance) for i in range(size)])  10.8 us
    ppermute x2, starting transfers between devices, inst_sum(): fetched = fetched + lax.ppermute(array, ('inst', 'feat'), pairs)  2 us
    ppermute x2, waiting for transfers between devices, inst_sum(): fetched = fetched + lax.ppermute(array, ('inst', 'feat'), pairs)  1.67 us
  transfers between devices with their start and end apart: 28, of which 22 were waited for; matrix products, arithmetic and copies ran while one was open for 1% of the time, Pallas kernels for 0%

profile of v3, /device:TPU:0, one launch (start us, length us, event | category | flops | bytes accessed | tf_op | source)
XLA Modules:
  0.0 68.6 jit_solution(17043752322759839291)
XLA Ops:
  0.6 5.9 %shard_map.68 = (bf16[16,8,128,128]{3,2,1,0:T(8,128)(2,1)S(1)}, f32[128,128]{1,0:T(8,128)S(1)}, f32[128,128]{1,0:T(8,128)S(1)}, f32[256,128]{1,0:T(8,128)S(1)}, f32[16,128]{1,0:T(8,128)S(1)}) custom-call(s32[8,16]{1,0:T(8,128)} %bitcast.4, s32[1,16]{1,0:T(1,128)} %bitcast.5, f32[2048,128]{1,0:T(8,128)} %weights.1, bf16[16,8,128,128]{3,2,1,0:T(8,128)(2,1)} %values_in.1), custom_call_target="tpu_custom_call" | custom-call | tf_op jit(solution)/shard_map/pallas_call | solution.py:256
  6.6 2.4 %collective-permute-start.2 = (f32[16,128]{1,0:T(8,128)S(1)}, f32[16,128]{1,0:T(8,128)S(1)}, u32[]{:S(2)}, u32[]{:S(2)}) collective-permute-start(f32[16,128]{1,0:T(8,128)S(1)} %get-tuple-element.24.refs_0_), channel_id=1, source_target_pairs={{0,3},{1,0},{2,1},{3,2},{4,7},{5,4},{6,5},{7,6},{8,11},{9,8},{10,9... | collective-permute-start | bytes 24584 | tf_op jit(solution)/shard_map/ppermute | solution.py:274
  10.4 2.3 %collective-permute-done.1.refs_2_ = f32[16,128]{1,0:T(8,128)S(1)} collective-permute-done((f32[16,128]{1,0:T(8,128)S(1)}, f32[16,128]{1,0:T(8,128)S(1)}, u32[]{:S(2)}, u32[]{:S(2)}) %collective-permute-start.1) | collective-permute-done | bytes 8224 | tf_op jit(solution)/shard_map/ppermute | solution.py:274
  13.4 3.7 %collective-permute-start.5 = (f32[136,128]{1,0:T(8,128)S(1)}, f32[136,128]{1,0:T(8,128)S(1)}, u32[]{:S(2)}, u32[]{:S(2)}) collective-permute-start(f32[136,128]{1,0:T(8,128)S(1)} %get-tuple-element.25.refs_0_), channel_id=1, source_target_pairs={{0,24},{4,28},{8,16},{12,20},{16,8},{20,12},{24,0},{28,4},{1,25},{... | collective-permute-start | bytes 208904 | tf_op jit(solution)/shard_map/ppermute | solution.py:268
  17.1 0.8 %collective-permute-start.3 = (f32[136,128]{1,0:T(8,128)S(1)}, f32[136,128]{1,0:T(8,128)S(1)}, u32[]{:S(2)}, u32[]{:S(2)}) collective-permute-start(f32[136,128]{1,0:T(8,128)S(1)} %get-tuple-element.25.refs_0_), channel_id=1, source_target_pairs={{0,8},{4,12},{8,0},{12,4},{16,24},{20,28},{24,16},{28,20},{1,9},{5... | collective-permute-start | bytes 208904 | tf_op jit(solution)/shard_map/ppermute | solution.py:268
  17.9 1.5 %collective-permute-start.6 = (f32[136,128]{1,0:T(8,128)S(1)}, f32[136,128]{1,0:T(8,128)S(1)}, u32[]{:S(2)}, u32[]{:S(2)}) collective-permute-start(f32[136,128]{1,0:T(8,128)S(1)} %get-tuple-element.25.refs_0_), channel_id=1, source_target_pairs={{0,4},{4,0},{8,12},{12,8},{16,20},{20,16},{24,28},{28,24},{1,5},{5... | collective-permute-start | bytes 208904 | tf_op jit(solution)/shard_map/ppermute | solution.py:268
  20.1 1.5 %collective-permute-start.9 = (f32[136,128]{1,0:T(8,128)S(1)}, f32[136,128]{1,0:T(8,128)S(1)}, u32[]{:S(2)}, u32[]{:S(2)}) collective-permute-start(f32[136,128]{1,0:T(8,128)S(1)} %collective-permute-done.5.refs_3_), channel_id=1, source_target_pairs={{0,4},{4,0},{8,12},{12,8},{16,20},{20,16},{24,28},{28,24},{1,5},{5... | collective-permute-start | bytes 208904 | tf_op jit(solution)/shard_map/ppermute | solution.py:268
  21.6 0.9 %collective-permute-done.4.refs_2_ = f32[136,128]{1,0:T(8,128)S(1)} collective-permute-done((f32[136,128]{1,0:T(8,128)S(1)}, f32[136,128]{1,0:T(8,128)S(1)}, u32[]{:S(2)}, u32[]{:S(2)}) %collective-permute-start.4) | collective-permute-done | bytes 69664 | tf_op jit(solution)/shard_map/ppermute | solution.py:268
  22.5 1.5 %collective-permute-start.8 = (f32[136,128]{1,0:T(8,128)S(1)}, f32[136,128]{1,0:T(8,128)S(1)}, u32[]{:S(2)}, u32[]{:S(2)}) collective-permute-start(f32[136,128]{1,0:T(8,128)S(1)} %collective-permute-done.4.refs_2_), channel_id=1, source_target_pairs={{0,4},{4,0},{8,12},{12,8},{16,20},{20,16},{24,28},{28,24},{1,5},{5... | collective-permute-start | bytes 208904 | tf_op jit(solution)/shard_map/ppermute | solution.py:268
  24.8 2.1 %collective-permute-done.8.refs_6_ = f32[136,128]{1,0:T(8,128)S(1)} collective-permute-done((f32[136,128]{1,0:T(8,128)S(1)}, f32[136,128]{1,0:T(8,128)S(1)}, u32[]{:S(2)}, u32[]{:S(2)}) %collective-permute-start.8) | collective-permute-done | bytes 69664 | tf_op jit(solution)/shard_map/ppermute | solution.py:268
  26.8 1.5 %collective-permute-done.7.refs_5_ = f32[136,128]{1,0:T(8,128)S(1)} collective-permute-done((f32[136,128]{1,0:T(8,128)S(1)}, f32[136,128]{1,0:T(8,128)S(1)}, u32[]{:S(2)}, u32[]{:S(2)}) %collective-permute-start.7) | collective-permute-done | bytes 69664 | tf_op jit(solution)/shard_map/ppermute | solution.py:268
  28.4 1.9 %shard_map.70 = (f32[256,128]{1,0:T(8,128)S(1)}, f32[128,128]{1,0:T(8,128)S(1)}, bf16[384,1024]{1,0:T(8,128)(2,1)S(1)}, f32[24,128]{1,0:T(8,128)S(1)}) custom-call(bf16[16,8,128,128]{3,2,1,0:T(8,128)(2,1)S(1)} %get-tuple-element.20.values, f32[128,128]{1,0:T(8,128)S(1)} %get-tuple-element.21.ids, f32[128,128]{1,0:T(8,128)S(1)} %get-tuple-element.22.picked, ...), custom_call_target="tpu_custom_call" | custom-call | tf_op jit(solution)/shard_map/pallas_call | solution.py:256
  30.3 1.2 %collective-permute-start.11 = (f32[24,128]{1,0:T(8,128)S(1)}, f32[24,128]{1,0:T(8,128)S(1)}, u32[]{:S(2)}, u32[]{:S(2)}) collective-permute-start(f32[24,128]{1,0:T(8,128)S(1)} %get-tuple-element.30.refs_0_), channel_id=1, source_target_pairs={{0,2},{1,3},{2,0},{3,1},{4,6},{5,7},{6,4},{7,5},{8,10},{9,11},{10,... | collective-permute-start | bytes 36872 | tf_op jit(solution)/shard_map/ppermute | solution.py:274
  31.7 2.4 %collective-permute-done.11.refs_2_ = f32[24,128]{1,0:T(8,128)S(1)} collective-permute-done((f32[24,128]{1,0:T(8,128)S(1)}, f32[24,128]{1,0:T(8,128)S(1)}, u32[]{:S(2)}, u32[]{:S(2)}) %collective-permute-start.11) | collective-permute-done | bytes 12320 | tf_op jit(solution)/shard_map/ppermute | solution.py:274
  35.2 2.2 %collective-permute-start.15 = (f32[136,128]{1,0:T(8,128)S(1)}, f32[136,128]{1,0:T(8,128)S(1)}, u32[]{:S(2)}, u32[]{:S(2)}) collective-permute-start(f32[136,128]{1,0:T(8,128)S(1)} %get-tuple-element.31.refs_0_), channel_id=1, source_target_pairs={{0,24},{4,28},{8,16},{12,20},{16,8},{20,12},{24,0},{28,4},{1,25},{... | collective-permute-start | bytes 208904 | tf_op jit(solution)/shard_map/ppermute | solution.py:268
  37.4 2.2 %collective-permute-start.13 = (f32[136,128]{1,0:T(8,128)S(1)}, f32[136,128]{1,0:T(8,128)S(1)}, u32[]{:S(2)}, u32[]{:S(2)}) collective-permute-start(f32[136,128]{1,0:T(8,128)S(1)} %get-tuple-element.31.refs_0_), channel_id=1, source_target_pairs={{0,8},{4,12},{8,0},{12,4},{16,24},{20,28},{24,16},{28,20},{1,9},{5... | collective-permute-start | bytes 208904 | tf_op jit(solution)/shard_map/ppermute | solution.py:268
  40.4 1.4 %collective-permute-done.15.refs_3_ = f32[136,128]{1,0:T(8,128)S(1)} collective-permute-done((f32[136,128]{1,0:T(8,128)S(1)}, f32[136,128]{1,0:T(8,128)S(1)}, u32[]{:S(2)}, u32[]{:S(2)}) %collective-permute-start.15) | collective-permute-done | bytes 69664 | tf_op jit(solution)/shard_map/ppermute | solution.py:268
  41.8 0.8 %collective-permute-start.19 = (f32[136,128]{1,0:T(8,128)S(1)}, f32[136,128]{1,0:T(8,128)S(1)}, u32[]{:S(2)}, u32[]{:S(2)}) collective-permute-start(f32[136,128]{1,0:T(8,128)S(1)} %collective-permute-done.15.refs_3_), channel_id=1, source_target_pairs={{0,4},{4,0},{8,12},{12,8},{16,20},{20,16},{24,28},{28,24},{1,5},{5... | collective-permute-start | bytes 208904 | tf_op jit(solution)/shard_map/ppermute | solution.py:268
  43.4 1.0 %collective-permute-start.18 = (f32[136,128]{1,0:T(8,128)S(1)}, f32[136,128]{1,0:T(8,128)S(1)}, u32[]{:S(2)}, u32[]{:S(2)}) collective-permute-start(f32[136,128]{1,0:T(8,128)S(1)} %collective-permute-done.14.refs_2_), channel_id=1, source_target_pairs={{0,4},{4,0},{8,12},{12,8},{16,20},{20,16},{24,28},{28,24},{1,5},{5... | collective-permute-start | bytes 208904 | tf_op jit(solution)/shard_map/ppermute | solution.py:268
  44.3 1.1 %collective-permute-start.17 = (f32[136,128]{1,0:T(8,128)S(1)}, f32[136,128]{1,0:T(8,128)S(1)}, u32[]{:S(2)}, u32[]{:S(2)}) collective-permute-start(f32[136,128]{1,0:T(8,128)S(1)} %collective-permute-done.13.refs_1_), channel_id=1, source_target_pairs={{0,4},{4,0},{8,12},{12,8},{16,20},{20,16},{24,28},{28,24},{1,5},{5... | collective-permute-start | bytes 208904 | tf_op jit(solution)/shard_map/ppermute | solution.py:268
  45.4 1.4 %collective-permute-done.19.refs_7_ = f32[136,128]{1,0:T(8,128)S(1)} collective-permute-done((f32[136,128]{1,0:T(8,128)S(1)}, f32[136,128]{1,0:T(8,128)S(1)}, u32[]{:S(2)}, u32[]{:S(2)}) %collective-permute-start.19) | collective-permute-done | bytes 69664 | tf_op jit(solution)/shard_map/ppermute | solution.py:268
  46.8 0.9 %collective-permute-done.18.refs_6_ = f32[136,128]{1,0:T(8,128)S(1)} collective-permute-done((f32[136,128]{1,0:T(8,128)S(1)}, f32[136,128]{1,0:T(8,128)S(1)}, u32[]{:S(2)}, u32[]{:S(2)}) %collective-permute-start.18) | collective-permute-done | bytes 69664 | tf_op jit(solution)/shard_map/ppermute | solution.py:268
  47.7 1.0 %collective-permute-done.17.refs_5_ = f32[136,128]{1,0:T(8,128)S(1)} collective-permute-done((f32[136,128]{1,0:T(8,128)S(1)}, f32[136,128]{1,0:T(8,128)S(1)}, u32[]{:S(2)}, u32[]{:S(2)}) %collective-permute-start.17) | collective-permute-done | bytes 69664 | tf_op jit(solution)/shard_map/ppermute | solution.py:268
  48.6 1.9 %shard_map.72 = (f32[256,128]{1,0:T(8,128)S(1)}, f32[8,128]{1,0:T(8,128)S(1)}, f32[24,128]{1,0:T(8,128)S(1)}) custom-call(bf16[16,8,128,128]{3,2,1,0:T(8,128)(2,1)S(1)} %get-tuple-element.20.values, bf16[384,1024]{1,0:T(8,128)(2,1)S(1)} %get-tuple-element.26.onehot, f32[128,128]{1,0:T(8,128)S(1)} %get-tuple-element.27.start_slot, ...), custom_call_target="tpu_custom_call" | custom-call | tf_op jit(solution)/shard_map/pallas_call | solution.py:256
  50.5 1.1 %collective-permute-start.21 = (f32[24,128]{1,0:T(8,128)S(1)}, f32[24,128]{1,0:T(8,128)S(1)}, u32[]{:S(2)}, u32[]{:S(2)}) collective-permute-start(f32[24,128]{1,0:T(8,128)S(1)} %get-tuple-element.35.refs_0_), channel_id=1, source_target_pairs={{0,2},{1,3},{2,0},{3,1},{4,6},{5,7},{6,4},{7,5},{8,10},{9,11},{10,... | collective-permute-start | bytes 36872 | tf_op jit(solution)/shard_map/ppermute | solution.py:274
  51.9 2.4 %collective-permute-done.21.refs_2_ = f32[24,128]{1,0:T(8,128)S(1)} collective-permute-done((f32[24,128]{1,0:T(8,128)S(1)}, f32[24,128]{1,0:T(8,128)S(1)}, u32[]{:S(2)}, u32[]{:S(2)}) %collective-permute-start.21) | collective-permute-done | bytes 12320 | tf_op jit(solution)/shard_map/ppermute | solution.py:274
  54.8 1.3 %collective-permute-start.24 = (f32[8,128]{1,0:T(8,128)S(1)}, f32[8,128]{1,0:T(8,128)S(1)}, u32[]{:S(2)}, u32[]{:S(2)}) collective-permute-start(f32[8,128]{1,0:T(8,128)S(1)} %get-tuple-element.37), channel_id=1, source_target_pairs={{0,4},{1,13},{2,22},{3,31},{4,0},{5,9},{6,18},{7,27},{8,12},{9,5},... | collective-permute-start | bytes 12296 | tf_op jit(solution)/shard_map/ppermute | solution.py:299
  56.9 1.7 %collective-permute-done.24 = f32[8,128]{1,0:T(8,128)S(1)} collective-permute-done((f32[8,128]{1,0:T(8,128)S(1)}, f32[8,128]{1,0:T(8,128)S(1)}, u32[]{:S(2)}, u32[]{:S(2)}) %collective-permute-start.24) | collective-permute-done | bytes 4128 | tf_op jit(solution)/shard_map/ppermute | solution.py:299
  58.5 4.8 %collective-permute-start.27 = (f32[8,128]{1,0:T(8,128)S(1)}, f32[8,128]{1,0:T(8,128)S(1)}, u32[]{:S(2)}, u32[]{:S(2)}) collective-permute-start(f32[8,128]{1,0:T(8,128)S(1)} %add_add_fusion.refs_0_), channel_id=1, source_target_pairs={{0,3},{1,0},{2,1},{3,2},{4,7},{5,4},{6,5},{7,6},{8,11},{9,8},{10,9... | collective-permute-start | bytes 12296 | tf_op jit(solution)/shard_map/ppermute | solution.py:274
  63.3 1.5 %collective-permute-start.26 = (f32[8,128]{1,0:T(8,128)S(1)}, f32[8,128]{1,0:T(8,128)S(1)}, u32[]{:S(2)}, u32[]{:S(2)}) collective-permute-start(f32[8,128]{1,0:T(8,128)S(1)} %add_add_fusion.refs_0_), channel_id=1, source_target_pairs={{0,2},{1,3},{2,0},{3,1},{4,6},{5,7},{6,4},{7,5},{8,10},{9,11},{10,... | collective-permute-start | bytes 12296 | tf_op jit(solution)/shard_map/ppermute | solution.py:274
  65.7 1.2 %collective-permute-done.26.refs_2_ = f32[8,128]{1,0:T(8,128)S(1)} collective-permute-done((f32[8,128]{1,0:T(8,128)S(1)}, f32[8,128]{1,0:T(8,128)S(1)}, u32[]{:S(2)}, u32[]{:S(2)}) %collective-permute-start.26) | collective-permute-done | bytes 4128 | tf_op jit(solution)/shard_map/ppermute | solution.py:274
  66.9 0.9 %collective-permute-done.25.refs_1_ = f32[8,128]{1,0:T(8,128)S(1)} collective-permute-done((f32[8,128]{1,0:T(8,128)S(1)}, f32[8,128]{1,0:T(8,128)S(1)}, u32[]{:S(2)}, u32[]{:S(2)}) %collective-permute-start.25) | collective-permute-done | bytes 4128 | tf_op jit(solution)/shard_map/ppermute | solution.py:274
  (36 shorter events, 9.6 us)
Async XLA Ops:
  0.6 12.1 %copy-start = (s32[2048]{0:T(1024)S(1)}, s32[2048]{0:T(1024)}, u32[]{:S(2)}) copy-start(s32[2048]{0:T(1024)} %param.8) | copy-start | bytes 24580
  6.6 3.8 %collective-permute-start.2 = (f32[16,128]{1,0:T(8,128)S(1)}, f32[16,128]{1,0:T(8,128)S(1)}, u32[]{:S(2)}, u32[]{:S(2)}) collective-permute-start(f32[16,128]{1,0:T(8,128)S(1)} %get-tuple-element.24.refs_0_), channel_id=1, source_target_pairs={{0,3},{1,0},{2,1},{3,2},{4,7},{5,4},{6,5},{7,6},{8,11},{9,8},{10,9... | collective-permute-start | bytes 24584 | tf_op jit(solution)/shard_map/ppermute | solution.py:274
  9.0 3.7 %collective-permute-start.1 = (f32[16,128]{1,0:T(8,128)S(1)}, f32[16,128]{1,0:T(8,128)S(1)}, u32[]{:S(2)}, u32[]{:S(2)}) collective-permute-start(f32[16,128]{1,0:T(8,128)S(1)} %get-tuple-element.24.refs_0_), channel_id=1, source_target_pairs={{0,2},{1,3},{2,0},{3,1},{4,6},{5,7},{6,4},{7,5},{8,10},{9,11},{10,... | collective-permute-start | bytes 24584 | tf_op jit(solution)/shard_map/ppermute | solution.py:274
  9.6 3.1 %collective-permute-start = (f32[16,128]{1,0:T(8,128)S(1)}, f32[16,128]{1,0:T(8,128)S(1)}, u32[]{:S(2)}, u32[]{:S(2)}) collective-permute-start(f32[16,128]{1,0:T(8,128)S(1)} %get-tuple-element.24.refs_0_), channel_id=1, source_target_pairs={{0,1},{1,2},{2,3},{3,0},{4,5},{5,6},{6,7},{7,4},{8,9},{9,10},{10,1... | collective-permute-start | bytes 24584 | tf_op jit(solution)/shard_map/ppermute | solution.py:274
  13.4 6.7 %collective-permute-start.5 = (f32[136,128]{1,0:T(8,128)S(1)}, f32[136,128]{1,0:T(8,128)S(1)}, u32[]{:S(2)}, u32[]{:S(2)}) collective-permute-start(f32[136,128]{1,0:T(8,128)S(1)} %get-tuple-element.25.refs_0_), channel_id=1, source_target_pairs={{0,24},{4,28},{8,16},{12,20},{16,8},{20,12},{24,0},{28,4},{1,25},{... | collective-permute-start | bytes 208904 | tf_op jit(solution)/shard_map/ppermute | solution.py:268
  17.1 5.5 %collective-permute-start.4 = (f32[136,128]{1,0:T(8,128)S(1)}, f32[136,128]{1,0:T(8,128)S(1)}, u32[]{:S(2)}, u32[]{:S(2)}) collective-permute-start(f32[136,128]{1,0:T(8,128)S(1)} %get-tuple-element.25.refs_0_), channel_id=1, source_target_pairs={{0,16},{4,20},{8,24},{12,28},{16,0},{20,4},{24,8},{28,12},{1,17},{... | collective-permute-start | bytes 208904 | tf_op jit(solution)/shard_map/ppermute | solution.py:268
  17.1 7.0 %collective-permute-start.3 = (f32[136,128]{1,0:T(8,128)S(1)}, f32[136,128]{1,0:T(8,128)S(1)}, u32[]{:S(2)}, u32[]{:S(2)}) collective-permute-start(f32[136,128]{1,0:T(8,128)S(1)} %get-tuple-element.25.refs_0_), channel_id=1, source_target_pairs={{0,8},{4,12},{8,0},{12,4},{16,24},{20,28},{24,16},{28,20},{1,9},{5... | collective-permute-start | bytes 208904 | tf_op jit(solution)/shard_map/ppermute | solution.py:268
  17.9 6.7 %collective-permute-start.6 = (f32[136,128]{1,0:T(8,128)S(1)}, f32[136,128]{1,0:T(8,128)S(1)}, u32[]{:S(2)}, u32[]{:S(2)}) collective-permute-start(f32[136,128]{1,0:T(8,128)S(1)} %get-tuple-element.25.refs_0_), channel_id=1, source_target_pairs={{0,4},{4,0},{8,12},{12,8},{16,20},{20,16},{24,28},{28,24},{1,5},{5... | collective-permute-start | bytes 208904 | tf_op jit(solution)/shard_map/ppermute | solution.py:268
  20.1 4.7 %collective-permute-start.9 = (f32[136,128]{1,0:T(8,128)S(1)}, f32[136,128]{1,0:T(8,128)S(1)}, u32[]{:S(2)}, u32[]{:S(2)}) collective-permute-start(f32[136,128]{1,0:T(8,128)S(1)} %collective-permute-done.5.refs_3_), channel_id=1, source_target_pairs={{0,4},{4,0},{8,12},{12,8},{16,20},{20,16},{24,28},{28,24},{1,5},{5... | collective-permute-start | bytes 208904 | tf_op jit(solution)/shard_map/ppermute | solution.py:268
  22.5 4.3 %collective-permute-start.8 = (f32[136,128]{1,0:T(8,128)S(1)}, f32[136,128]{1,0:T(8,128)S(1)}, u32[]{:S(2)}, u32[]{:S(2)}) collective-permute-start(f32[136,128]{1,0:T(8,128)S(1)} %collective-permute-done.4.refs_2_), channel_id=1, source_target_pairs={{0,4},{4,0},{8,12},{12,8},{16,20},{20,16},{24,28},{28,24},{1,5},{5... | collective-permute-start | bytes 208904 | tf_op jit(solution)/shard_map/ppermute | solution.py:268
  24.1 4.3 %collective-permute-start.7 = (f32[136,128]{1,0:T(8,128)S(1)}, f32[136,128]{1,0:T(8,128)S(1)}, u32[]{:S(2)}, u32[]{:S(2)}) collective-permute-start(f32[136,128]{1,0:T(8,128)S(1)} %collective-permute-done.3.refs_1_), channel_id=1, source_target_pairs={{0,4},{4,0},{8,12},{12,8},{16,20},{20,16},{24,28},{28,24},{1,5},{5... | collective-permute-start | bytes 208904 | tf_op jit(solution)/shard_map/ppermute | solution.py:268
  30.2 1.5 %collective-permute-start.12 = (f32[24,128]{1,0:T(8,128)S(1)}, f32[24,128]{1,0:T(8,128)S(1)}, u32[]{:S(2)}, u32[]{:S(2)}) collective-permute-start(f32[24,128]{1,0:T(8,128)S(1)} %get-tuple-element.30.refs_0_), channel_id=1, source_target_pairs={{0,3},{1,0},{2,1},{3,2},{4,7},{5,4},{6,5},{7,6},{8,11},{9,8},{10,9... | collective-permute-start | bytes 36872 | tf_op jit(solution)/shard_map/ppermute | solution.py:274
  30.3 3.8 %collective-permute-start.11 = (f32[24,128]{1,0:T(8,128)S(1)}, f32[24,128]{1,0:T(8,128)S(1)}, u32[]{:S(2)}, u32[]{:S(2)}) collective-permute-start(f32[24,128]{1,0:T(8,128)S(1)} %get-tuple-element.30.refs_0_), channel_id=1, source_target_pairs={{0,2},{1,3},{2,0},{3,1},{4,6},{5,7},{6,4},{7,5},{8,10},{9,11},{10,... | collective-permute-start | bytes 36872 | tf_op jit(solution)/shard_map/ppermute | solution.py:274
  31.5 3.1 %collective-permute-start.10 = (f32[24,128]{1,0:T(8,128)S(1)}, f32[24,128]{1,0:T(8,128)S(1)}, u32[]{:S(2)}, u32[]{:S(2)}) collective-permute-start(f32[24,128]{1,0:T(8,128)S(1)} %get-tuple-element.30.refs_0_), channel_id=1, source_target_pairs={{0,1},{1,2},{2,3},{3,0},{4,5},{5,6},{6,7},{7,4},{8,9},{9,10},{10,1... | collective-permute-start | bytes 36872 | tf_op jit(solution)/shard_map/ppermute | solution.py:274
  35.2 6.6 %collective-permute-start.15 = (f32[136,128]{1,0:T(8,128)S(1)}, f32[136,128]{1,0:T(8,128)S(1)}, u32[]{:S(2)}, u32[]{:S(2)}) collective-permute-start(f32[136,128]{1,0:T(8,128)S(1)} %get-tuple-element.31.refs_0_), channel_id=1, source_target_pairs={{0,24},{4,28},{8,16},{12,20},{16,8},{20,12},{24,0},{28,4},{1,25},{... | collective-permute-start | bytes 208904 | tf_op jit(solution)/shard_map/ppermute | solution.py:268
  37.4 5.9 %collective-permute-start.14 = (f32[136,128]{1,0:T(8,128)S(1)}, f32[136,128]{1,0:T(8,128)S(1)}, u32[]{:S(2)}, u32[]{:S(2)}) collective-permute-start(f32[136,128]{1,0:T(8,128)S(1)} %get-tuple-element.31.refs_0_), channel_id=1, source_target_pairs={{0,16},{4,20},{8,24},{12,28},{16,0},{20,4},{24,8},{28,12},{1,17},{... | collective-permute-start | bytes 208904 | tf_op jit(solution)/shard_map/ppermute | solution.py:268
  37.4 6.9 %collective-permute-start.13 = (f32[136,128]{1,0:T(8,128)S(1)}, f32[136,128]{1,0:T(8,128)S(1)}, u32[]{:S(2)}, u32[]{:S(2)}) collective-permute-start(f32[136,128]{1,0:T(8,128)S(1)} %get-tuple-element.31.refs_0_), channel_id=1, source_target_pairs={{0,8},{4,12},{8,0},{12,4},{16,24},{20,28},{24,16},{28,20},{1,9},{5... | collective-permute-start | bytes 208904 | tf_op jit(solution)/shard_map/ppermute | solution.py:268
  39.7 5.7 %collective-permute-start.16 = (f32[136,128]{1,0:T(8,128)S(1)}, f32[136,128]{1,0:T(8,128)S(1)}, u32[]{:S(2)}, u32[]{:S(2)}) collective-permute-start(f32[136,128]{1,0:T(8,128)S(1)} %get-tuple-element.31.refs_0_), channel_id=1, source_target_pairs={{0,4},{4,0},{8,12},{12,8},{16,20},{20,16},{24,28},{28,24},{1,5},{5... | collective-permute-start | bytes 208904 | tf_op jit(solution)/shard_map/ppermute | solution.py:268
  41.8 5.0 %collective-permute-start.19 = (f32[136,128]{1,0:T(8,128)S(1)}, f32[136,128]{1,0:T(8,128)S(1)}, u32[]{:S(2)}, u32[]{:S(2)}) collective-permute-start(f32[136,128]{1,0:T(8,128)S(1)} %collective-permute-done.15.refs_3_), channel_id=1, source_target_pairs={{0,4},{4,0},{8,12},{12,8},{16,20},{20,16},{24,28},{28,24},{1,5},{5... | collective-permute-start | bytes 208904 | tf_op jit(solution)/shard_map/ppermute | solution.py:268
  43.4 4.3 %collective-permute-start.18 = (f32[136,128]{1,0:T(8,128)S(1)}, f32[136,128]{1,0:T(8,128)S(1)}, u32[]{:S(2)}, u32[]{:S(2)}) collective-permute-start(f32[136,128]{1,0:T(8,128)S(1)} %collective-permute-done.14.refs_2_), channel_id=1, source_target_pairs={{0,4},{4,0},{8,12},{12,8},{16,20},{20,16},{24,28},{28,24},{1,5},{5... | collective-permute-start | bytes 208904 | tf_op jit(solution)/shard_map/ppermute | solution.py:268
  44.3 4.3 %collective-permute-start.17 = (f32[136,128]{1,0:T(8,128)S(1)}, f32[136,128]{1,0:T(8,128)S(1)}, u32[]{:S(2)}, u32[]{:S(2)}) collective-permute-start(f32[136,128]{1,0:T(8,128)S(1)} %collective-permute-done.13.refs_1_), channel_id=1, source_target_pairs={{0,4},{4,0},{8,12},{12,8},{16,20},{20,16},{24,28},{28,24},{1,5},{5... | collective-permute-start | bytes 208904 | tf_op jit(solution)/shard_map/ppermute | solution.py:268
  50.5 1.5 %collective-permute-start.22 = (f32[24,128]{1,0:T(8,128)S(1)}, f32[24,128]{1,0:T(8,128)S(1)}, u32[]{:S(2)}, u32[]{:S(2)}) collective-permute-start(f32[24,128]{1,0:T(8,128)S(1)} %get-tuple-element.35.refs_0_), channel_id=1, source_target_pairs={{0,3},{1,0},{2,1},{3,2},{4,7},{5,4},{6,5},{7,6},{8,11},{9,8},{10,9... | collective-permute-start | bytes 36872 | tf_op jit(solution)/shard_map/ppermute | solution.py:274
  50.5 3.8 %collective-permute-start.21 = (f32[24,128]{1,0:T(8,128)S(1)}, f32[24,128]{1,0:T(8,128)S(1)}, u32[]{:S(2)}, u32[]{:S(2)}) collective-permute-start(f32[24,128]{1,0:T(8,128)S(1)} %get-tuple-element.35.refs_0_), channel_id=1, source_target_pairs={{0,2},{1,3},{2,0},{3,1},{4,6},{5,7},{6,4},{7,5},{8,10},{9,11},{10,... | collective-permute-start | bytes 36872 | tf_op jit(solution)/shard_map/ppermute | solution.py:274
  51.6 3.1 %collective-permute-start.20 = (f32[24,128]{1,0:T(8,128)S(1)}, f32[24,128]{1,0:T(8,128)S(1)}, u32[]{:S(2)}, u32[]{:S(2)}) collective-permute-start(f32[24,128]{1,0:T(8,128)S(1)} %get-tuple-element.35.refs_0_), channel_id=1, source_target_pairs={{0,1},{1,2},{2,3},{3,0},{4,5},{5,6},{6,7},{7,4},{8,9},{9,10},{10,1... | collective-permute-start | bytes 36872 | tf_op jit(solution)/shard_map/ppermute | solution.py:274
  54.8 3.7 %collective-permute-start.24 = (f32[8,128]{1,0:T(8,128)S(1)}, f32[8,128]{1,0:T(8,128)S(1)}, u32[]{:S(2)}, u32[]{:S(2)}) collective-permute-start(f32[8,128]{1,0:T(8,128)S(1)} %get-tuple-element.37), channel_id=1, source_target_pairs={{0,4},{1,13},{2,22},{3,31},{4,0},{5,9},{6,18},{7,27},{8,12},{9,5},... | collective-permute-start | bytes 12296 | tf_op jit(solution)/shard_map/ppermute | solution.py:299
  56.2 2.3 %collective-permute-start.23 = (f32[8,128]{1,0:T(8,128)S(1)}, f32[8,128]{1,0:T(8,128)S(1)}, u32[]{:S(2)}, u32[]{:S(2)}) collective-permute-start(f32[8,128]{1,0:T(8,128)S(1)} %get-tuple-element.37), channel_id=1, source_target_pairs={{1,9},{2,18},{3,27},{5,13},{6,22},{7,31},{9,1},{10,26},{11,19},{13... | collective-permute-start | bytes 12296 | tf_op jit(solution)/shard_map/ppermute | solution.py:299
  58.5 7.2 %collective-permute-start.27 = (f32[8,128]{1,0:T(8,128)S(1)}, f32[8,128]{1,0:T(8,128)S(1)}, u32[]{:S(2)}, u32[]{:S(2)}) collective-permute-start(f32[8,128]{1,0:T(8,128)S(1)} %add_add_fusion.refs_0_), channel_id=1, source_target_pairs={{0,3},{1,0},{2,1},{3,2},{4,7},{5,4},{6,5},{7,6},{8,11},{9,8},{10,9... | collective-permute-start | bytes 12296 | tf_op jit(solution)/shard_map/ppermute | solution.py:274
  63.3 3.6 %collective-permute-start.26 = (f32[8,128]{1,0:T(8,128)S(1)}, f32[8,128]{1,0:T(8,128)S(1)}, u32[]{:S(2)}, u32[]{:S(2)}) collective-permute-start(f32[8,128]{1,0:T(8,128)S(1)} %add_add_fusion.refs_0_), channel_id=1, source_target_pairs={{0,2},{1,3},{2,0},{3,1},{4,6},{5,7},{6,4},{7,5},{8,10},{9,11},{10,... | collective-permute-start | bytes 12296 | tf_op jit(solution)/shard_map/ppermute | solution.py:274
  64.8 3.0 %collective-permute-start.25 = (f32[8,128]{1,0:T(8,128)S(1)}, f32[8,128]{1,0:T(8,128)S(1)}, u32[]{:S(2)}, u32[]{:S(2)}) collective-permute-start(f32[8,128]{1,0:T(8,128)S(1)} %add_add_fusion.refs_0_), channel_id=1, source_target_pairs={{0,1},{1,2},{2,3},{3,0},{4,5},{5,6},{6,7},{7,4},{8,9},{9,10},{10,1... | collective-permute-start | bytes 12296 | tf_op jit(solution)/shard_map/ppermute | solution.py:274

commit v4 on v3

--- a/solution.py
+++ b/solution.py
@@ -87,12 +87,8 @@
     ]
     for small in smalls:
         small.start()
-    loads = [
-        pltpu.make_async_copy(values_in.at[t], values.at[t], values_sem.at[t])
-        for t in range(tiles)
-    ]
-    for load in loads:
-        load.start()
+    load = pltpu.make_async_copy(values_in, values, values_sem)
+    load.start()
     for small in smalls:
         small.wait()
     for t in range(tiles):
@@ -108,9 +104,8 @@
             ).astype(F32)
     offset = pl.multiple_of(lax.axis_index("inst") * share, SUB)
     own[...] = weights_here[pl.ds(offset, share), :]
-    for t in range(tiles):
-        loads[t].wait()
-        along[t : t + 1, :] = forward_tile(values[t], picked[t * slots : (t + 1) * slots, :])
+    load.wait()
+    forward_all(values, picked, along)
 
 
 def gradient_kernel(count, labels, values, ids, *refs):
@@ -206,22 +201,20 @@
 
 
 def inner_kernel(count, curvature, along, *refs):
-    parts, (scalars, first_only) = refs[:count], refs[count:]
+    parts, (scalars,) = refs[:count], refs[count:]
     tiles, width = along.shape
     summed = parts[0][...]
     for part in parts[1:]:
         summed = summed + part[...]
     turn = summed[:tiles, :]
     bent = curvature[...] * turn
-    block = scalar_rows(
+    scalars[...] = scalar_rows(
         width,
         summed[tiles : tiles + 1, 0:1],
         summed[tiles : tiles + 1, 1:2],
         total(bent * turn),
         total(bent * along[...]),
     )
-    scalars[...] = block
-    first_only[...] = jnp.where(lax.axis_index("feat") == 0, block, 0.0)
 
 
 def last_kernel(known, gradient, next_share, *refs):
@@ -268,12 +261,24 @@
     return lax.ppermute(array, axis, [(i, i ^ distance) for i in range(size)])
 
 
+def swap_both(array, distance):
+    size, feats = lax.axis_size("inst"), lax.axis_size("feat")
+    pairs = [
+        (i * feats + f, (i ^ distance) * feats + (f ^ 1))
+        for i in range(size)
+        for f in range(feats)
+    ]
+    return lax.ppermute(array, ("inst", "feat"), pairs)
+
+
 def feat_parts(array):
-    size = lax.axis_size("feat")
-    return [array] + [
-        lax.ppermute(array, "feat", [(i, (i + k) % size) for i in range(size)])
-        for k in range(1, size)
-    ]
+    distance = 1
+    parts = [array]
+    while distance < lax.axis_size("feat"):
+        array = sum(parts[1:], parts[0])
+        parts = [array, swap(array, "feat", distance | 1)]
+        distance *= 2
+    return parts
 
 
 def inst_parts(array):
@@ -281,35 +286,29 @@
     if size != 8:
         gathered = lax.all_gather(array, "inst", axis=0)
         return [gathered[i] for i in range(size)]
-    parts = [array] + [swap(array, "inst", k) for k in (2, 4, 6)]
-    return parts + [swap(part, "inst", 1) for part in parts]
-
-
-def inst_sum(array, first_only):
-    size, feats = lax.axis_size("inst"), lax.axis_size("feat")
-    if size == 2 * feats:
-        fetched = first_only
-        for low in (0, 1):
-            pairs = [
-                (i * feats + f, (i ^ (2 * f + low)) * feats + f)
-                for i in range(size)
-                for f in range(feats)
-                if 2 * f + low
-            ]
-            fetched = fetched + lax.ppermute(array, ("inst", "feat"), pairs)
-        return feat_parts(fetched)
-    distance = 1
-    while distance < size:
-        array = array + swap(array, "inst", distance)
-        distance *= 2
-    return [array]
+    parts = {0: array}
+    for distance in (6, 4, 2, 1, 3):
+        parts[distance] = swap(array, "inst", distance)
+    for distance in (4, 6):
+        parts[distance ^ 1] = swap(parts[distance], "inst", 1)
+    return list(parts.values())
+
+
+def inst_sum_parts(array):
+    size = lax.axis_size("inst")
+    stages = [(2, 4, 6), (1,)] if size == 8 else [(1 << b,) for b in range(size.bit_length() - 1)]
+    parts = [array]
+    for stage in stages:
+        array = sum(parts[1:], parts[0])
+        parts = [array] + [swap_both(array, distance) for distance in stage]
+    return parts
 
 
 def per_device(values, columns, live_slots, labels, weights):
     tiles, slots_of, rows, width = values.shape
     slots = tiles * slots_of
     share = weights.shape[0] // lax.axis_size("inst")
-    feats, insts = lax.axis_size("feat"), lax.axis_size("inst")
+    insts, pair = lax.axis_size("inst"), 2
 
     values_here, ids, picked, own, part = call(
         functools.partial(first_kernel, share),
@@ -330,11 +329,11 @@
             pltpu.SMEM((1, tiles), jnp.int32),
             pltpu.VMEM(weights.shape, F32),
             pltpu.SemaphoreType.DMA((3,)),
-            pltpu.SemaphoreType.DMA((tiles,)),
+            pltpu.SemaphoreType.DMA,
         ],
     )
     payload, curvature = call(
-        functools.partial(gradient_kernel, feats),
+        functools.partial(gradient_kernel, pair),
         (near((slots + SUB, width)), near((tiles, rows))),
         (labels.reshape(tiles, rows), values_here, ids, *feat_parts(part)),
     )
@@ -351,7 +350,7 @@
         scratch_shapes=[halves],
     )
     along, payload = call(
-        functools.partial(curve_kernel, feats),
+        functools.partial(curve_kernel, pair),
         (near((tiles, rows)), near((slots + SUB, width))),
         (values_here, ids, curvature, *feat_parts(payload)),
     )
@@ -361,15 +360,15 @@
         (values_here, onehot, start_slot, gradient, *inst_parts(payload)),
         scratch_shapes=[halves, pltpu.VMEM((slots, width), F32)],
     )
-    scalars, first_only = call(
-        functools.partial(inner_kernel, feats),
-        (near((SUB, width)), near((SUB, width))),
+    scalars = call(
+        functools.partial(inner_kernel, pair),
+        near((SUB, width)),
         (curvature, along, *feat_parts(payload)),
     )
     step = call(
         last_kernel,
         near((share, width)),
-        (known, gradient, next_share, *inst_sum(scalars, first_only)),
+        (known, gradient, next_share, *inst_sum_parts(scalars)),
     )
     return (step, gradient)
 

time: 68.8 us -> 63.6 us (0.924)
  waiting for transfers between devices: 23.4 us -> 19.4 us
  Pallas kernels: 11.2 us -> 9.05 us
  starting transfers between devices: 31.9 us -> 32.9 us
    ppermute x14 -> x20, starting transfers between devices: 17.5 us -> 27.8 us  [swap(): return lax.ppermute(array, axis, [(i, i ^ distance) for i in range(size)])]
    ppermute x14 -> x4, starting transfers between devices: 14.4 us -> 5.12 us  [swap_both(): return lax.ppermute(array, ('inst', 'feat'), pairs)]
    ppermute x14 -> x4, waiting for transfers between devices: 12.7 us -> 4.95 us  [swap_both(): return lax.ppermute(array, ('inst', 'feat'), pairs)]
    ppermute x14 -> x20, waiting for transfers between devices: 10.8 us -> 14.5 us  [swap(): return lax.ppermute(array, axis, [(i, i ^ distance) for i in range(size)])]
    pallas_call x7, Pallas kernels: 11.2 us -> 9.05 us  [call(): pl.pallas_call(kernel, out_shape=out_shape, in_specs=in_specs, out_specs=...]
  transfers between devices with their start and end apart: 28 -> 24, of which waited for: 22 -> 18; matrix products, arithmetic and copies ran while one was open for 1% -> 1% of each run, Pallas kernels for 0% -> 0%
where the time goes in v4:
time: 63.6 us; the launch traced here: 63.4 us
  starting transfers between devices  32.9 us (52%)
  waiting for transfers between devices  19.4 us (31%)
  Pallas kernels  9.05 us (14%)
  local copies, waits for them, and re-layouts  1.32 us (2%)
  between operations  0.71 us (1%)
    ppermute x20, starting transfers between devices, swap(): return lax.ppermute(array, axis, [(i, i ^ distance) for i in range(size)])  27.8 us
    ppermute x20, waiting for transfers between devices, swap(): return lax.ppermute(array, axis, [(i, i ^ distance) for i in range(size)])  14.5 us
    pallas_call x7, Pallas kernels, call(): pl.pallas_call(kernel, out_shape=out_shape, in_specs=in_specs, out_specs=...  9.05 us
    ppermute x4, starting transfers between devices, swap_both(): return lax.ppermute(array, ('inst', 'feat'), pairs)  5.12 us
    ppermute x4, waiting for transfers between devices, swap_both(): return lax.ppermute(array, ('inst', 'feat'), pairs)  4.95 us
    unnamed x4, local copies, waits for them, and re-layouts  1.32 us
  transfers between devices with their start and end apart: 24, of which 18 were waited for; matrix products, arithmetic and copies ran while one was open for 1% of the time, Pallas kernels for 0%

profile of v4, /device:TPU:0, one launch (start us, length us, event | category | flops | bytes accessed | tf_op | source)
XLA Modules:
  0.0 63.4 jit_solution(5203394200256151311)
XLA Ops:
  0.6 3.8 %shard_map.68 = (bf16[16,8,128,128]{3,2,1,0:T(8,128)(2,1)S(1)}, f32[128,128]{1,0:T(8,128)S(1)}, f32[128,128]{1,0:T(8,128)S(1)}, f32[256,128]{1,0:T(8,128)S(1)}, f32[16,128]{1,0:T(8,128)S(1)}) custom-call(s32[8,16]{1,0:T(8,128)} %bitcast.4, s32[1,16]{1,0:T(1,128)} %bitcast.5, f32[2048,128]{1,0:T(8,128)} %weights.1, bf16[16,8,128,128]{3,2,1,0:T(8,128)(2,1)} %values_in.1), custom_call_target="tpu_custom_call" | custom-call | tf_op jit(solution)/shard_map/pallas_call | solution.py:249
  4.9 0.8 %collective-permute-done = f32[16,128]{1,0:T(8,128)S(1)} collective-permute-done((f32[16,128]{1,0:T(8,128)S(1)}, f32[16,128]{1,0:T(8,128)S(1)}, u32[]{:S(2)}, u32[]{:S(2)}) %collective-permute-start) | collective-permute-done | bytes 8224 | tf_op jit(solution)/shard_map/ppermute | solution.py:261
  5.8 2.6 %collective-permute-start.1 = (f32[16,128]{1,0:T(8,128)S(1)}, f32[16,128]{1,0:T(8,128)S(1)}, u32[]{:S(2)}, u32[]{:S(2)}) collective-permute-start(f32[16,128]{1,0:T(8,128)S(1)} %add.18.refs_0_), channel_id=1, source_target_pairs={{0,3},{1,2},{2,1},{3,0},{4,7},{5,6},{6,5},{7,4},{8,11},{9,10},{10,... | collective-permute-start | bytes 24584 | tf_op jit(solution)/shard_map/ppermute | solution.py:261
  8.4 1.4 %collective-permute-done.1.refs_1_ = f32[16,128]{1,0:T(8,128)S(1)} collective-permute-done((f32[16,128]{1,0:T(8,128)S(1)}, f32[16,128]{1,0:T(8,128)S(1)}, u32[]{:S(2)}, u32[]{:S(2)}) %collective-permute-start.1) | collective-permute-done | bytes 8224 | tf_op jit(solution)/shard_map/ppermute | solution.py:261
  10.4 3.1 %collective-permute-start.3 = (f32[136,128]{1,0:T(8,128)S(1)}, f32[136,128]{1,0:T(8,128)S(1)}, u32[]{:S(2)}, u32[]{:S(2)}) collective-permute-start(f32[136,128]{1,0:T(8,128)S(1)} %get-tuple-element.23.refs_0_), channel_id=1, source_target_pairs={{0,16},{4,20},{8,24},{12,28},{16,0},{20,4},{24,8},{28,12},{1,17},{... | collective-permute-start | bytes 208904 | tf_op jit(solution)/shard_map/ppermute | solution.py:261
  13.5 1.3 %collective-permute-start.2 = (f32[136,128]{1,0:T(8,128)S(1)}, f32[136,128]{1,0:T(8,128)S(1)}, u32[]{:S(2)}, u32[]{:S(2)}) collective-permute-start(f32[136,128]{1,0:T(8,128)S(1)} %get-tuple-element.23.refs_0_), channel_id=1, source_target_pairs={{0,24},{4,28},{8,16},{12,20},{16,8},{20,12},{24,0},{28,4},{1,25},{... | collective-permute-start | bytes 208904 | tf_op jit(solution)/shard_map/ppermute | solution.py:261
  14.8 1.2 %collective-permute-start.6 = (f32[136,128]{1,0:T(8,128)S(1)}, f32[136,128]{1,0:T(8,128)S(1)}, u32[]{:S(2)}, u32[]{:S(2)}) collective-permute-start(f32[136,128]{1,0:T(8,128)S(1)} %get-tuple-element.23.refs_0_), channel_id=1, source_target_pairs={{0,12},{4,8},{8,4},{12,0},{16,28},{20,24},{24,20},{28,16},{1,13},{... | collective-permute-start | bytes 208904 | tf_op jit(solution)/shard_map/ppermute | solution.py:261
  16.5 1.8 %collective-permute-start.4 = (f32[136,128]{1,0:T(8,128)S(1)}, f32[136,128]{1,0:T(8,128)S(1)}, u32[]{:S(2)}, u32[]{:S(2)}) collective-permute-start(f32[136,128]{1,0:T(8,128)S(1)} %get-tuple-element.23.refs_0_), channel_id=1, source_target_pairs={{0,8},{4,12},{8,0},{12,4},{16,24},{20,28},{24,16},{28,20},{1,9},{5... | collective-permute-start | bytes 208904 | tf_op jit(solution)/shard_map/ppermute | solution.py:261
  18.3 2.0 %collective-permute-start.7 = (f32[136,128]{1,0:T(8,128)S(1)}, f32[136,128]{1,0:T(8,128)S(1)}, u32[]{:S(2)}, u32[]{:S(2)}) collective-permute-start(f32[136,128]{1,0:T(8,128)S(1)} %collective-permute-done.3.refs_2_), channel_id=1, source_target_pairs={{0,4},{4,0},{8,12},{12,8},{16,20},{20,16},{24,28},{28,24},{1,5},{5... | collective-permute-start | bytes 208904 | tf_op jit(solution)/shard_map/ppermute | solution.py:261
  20.3 1.3 %collective-permute-start.8 = (f32[136,128]{1,0:T(8,128)S(1)}, f32[136,128]{1,0:T(8,128)S(1)}, u32[]{:S(2)}, u32[]{:S(2)}) collective-permute-start(f32[136,128]{1,0:T(8,128)S(1)} %collective-permute-done.2.refs_1_), channel_id=1, source_target_pairs={{0,4},{4,0},{8,12},{12,8},{16,20},{20,16},{24,28},{28,24},{1,5},{5... | collective-permute-start | bytes 208904 | tf_op jit(solution)/shard_map/ppermute | solution.py:261
  22.3 1.2 %collective-permute-done.7.refs_6_ = f32[136,128]{1,0:T(8,128)S(1)} collective-permute-done((f32[136,128]{1,0:T(8,128)S(1)}, f32[136,128]{1,0:T(8,128)S(1)}, u32[]{:S(2)}, u32[]{:S(2)}) %collective-permute-start.7) | collective-permute-done | bytes 69664 | tf_op jit(solution)/shard_map/ppermute | solution.py:261
  23.5 1.1 %collective-permute-done.8.refs_7_ = f32[136,128]{1,0:T(8,128)S(1)} collective-permute-done((f32[136,128]{1,0:T(8,128)S(1)}, f32[136,128]{1,0:T(8,128)S(1)}, u32[]{:S(2)}, u32[]{:S(2)}) %collective-permute-start.8) | collective-permute-done | bytes 69664 | tf_op jit(solution)/shard_map/ppermute | solution.py:261
  24.6 1.9 %shard_map.70 = (f32[256,128]{1,0:T(8,128)S(1)}, f32[128,128]{1,0:T(8,128)S(1)}, bf16[384,1024]{1,0:T(8,128)(2,1)S(1)}, f32[24,128]{1,0:T(8,128)S(1)}) custom-call(bf16[16,8,128,128]{3,2,1,0:T(8,128)(2,1)S(1)} %get-tuple-element.18.values, f32[128,128]{1,0:T(8,128)S(1)} %get-tuple-element.19.ids, f32[128,128]{1,0:T(8,128)S(1)} %get-tuple-element.20.picked, ...), custom_call_target="tpu_custom_call" | custom-call | tf_op jit(solution)/shard_map/pallas_call | solution.py:249
  26.6 1.2 %collective-permute-done.9 = f32[24,128]{1,0:T(8,128)S(1)} collective-permute-done((f32[24,128]{1,0:T(8,128)S(1)}, f32[24,128]{1,0:T(8,128)S(1)}, u32[]{:S(2)}, u32[]{:S(2)}) %collective-permute-start.9) | collective-permute-done | bytes 12320 | tf_op jit(solution)/shard_map/ppermute | solution.py:261
  27.7 1.3 %collective-permute-start.10 = (f32[24,128]{1,0:T(8,128)S(1)}, f32[24,128]{1,0:T(8,128)S(1)}, u32[]{:S(2)}, u32[]{:S(2)}) collective-permute-start(f32[24,128]{1,0:T(8,128)S(1)} %add.19.refs_0_), channel_id=1, source_target_pairs={{0,3},{1,2},{2,1},{3,0},{4,7},{5,6},{6,5},{7,4},{8,11},{9,10},{10,... | collective-permute-start | bytes 36872 | tf_op jit(solution)/shard_map/ppermute | solution.py:261
  29.0 1.9 %collective-permute-done.10.refs_1_ = f32[24,128]{1,0:T(8,128)S(1)} collective-permute-done((f32[24,128]{1,0:T(8,128)S(1)}, f32[24,128]{1,0:T(8,128)S(1)}, u32[]{:S(2)}, u32[]{:S(2)}) %collective-permute-start.10) | collective-permute-done | bytes 12320 | tf_op jit(solution)/shard_map/ppermute | solution.py:261
  31.5 2.9 %collective-permute-start.12 = (f32[136,128]{1,0:T(8,128)S(1)}, f32[136,128]{1,0:T(8,128)S(1)}, u32[]{:S(2)}, u32[]{:S(2)}) collective-permute-start(f32[136,128]{1,0:T(8,128)S(1)} %get-tuple-element.29.refs_0_), channel_id=1, source_target_pairs={{0,16},{4,20},{8,24},{12,28},{16,0},{20,4},{24,8},{28,12},{1,17},{... | collective-permute-start | bytes 208904 | tf_op jit(solution)/shard_map/ppermute | solution.py:261
  34.4 1.1 %collective-permute-start.11 = (f32[136,128]{1,0:T(8,128)S(1)}, f32[136,128]{1,0:T(8,128)S(1)}, u32[]{:S(2)}, u32[]{:S(2)}) collective-permute-start(f32[136,128]{1,0:T(8,128)S(1)} %get-tuple-element.29.refs_0_), channel_id=1, source_target_pairs={{0,24},{4,28},{8,16},{12,20},{16,8},{20,12},{24,0},{28,4},{1,25},{... | collective-permute-start | bytes 208904 | tf_op jit(solution)/shard_map/ppermute | solution.py:261
  35.5 1.2 %collective-permute-start.15 = (f32[136,128]{1,0:T(8,128)S(1)}, f32[136,128]{1,0:T(8,128)S(1)}, u32[]{:S(2)}, u32[]{:S(2)}) collective-permute-start(f32[136,128]{1,0:T(8,128)S(1)} %get-tuple-element.29.refs_0_), channel_id=1, source_target_pairs={{0,12},{4,8},{8,4},{12,0},{16,28},{20,24},{24,20},{28,16},{1,13},{... | collective-permute-start | bytes 208904 | tf_op jit(solution)/shard_map/ppermute | solution.py:261
  37.4 1.5 %collective-permute-start.13 = (f32[136,128]{1,0:T(8,128)S(1)}, f32[136,128]{1,0:T(8,128)S(1)}, u32[]{:S(2)}, u32[]{:S(2)}) collective-permute-start(f32[136,128]{1,0:T(8,128)S(1)} %get-tuple-element.29.refs_0_), channel_id=1, source_target_pairs={{0,8},{4,12},{8,0},{12,4},{16,24},{20,28},{24,16},{28,20},{1,9},{5... | collective-permute-start | bytes 208904 | tf_op jit(solution)/shard_map/ppermute | solution.py:261
  39.0 2.1 %collective-permute-start.16 = (f32[136,128]{1,0:T(8,128)S(1)}, f32[136,128]{1,0:T(8,128)S(1)}, u32[]{:S(2)}, u32[]{:S(2)}) collective-permute-start(f32[136,128]{1,0:T(8,128)S(1)} %collective-permute-done.12.refs_2_), channel_id=1, source_target_pairs={{0,4},{4,0},{8,12},{12,8},{16,20},{20,16},{24,28},{28,24},{1,5},{5... | collective-permute-start | bytes 208904 | tf_op jit(solution)/shard_map/ppermute | solution.py:261
  41.2 1.2 %collective-permute-start.17 = (f32[136,128]{1,0:T(8,128)S(1)}, f32[136,128]{1,0:T(8,128)S(1)}, u32[]{:S(2)}, u32[]{:S(2)}) collective-permute-start(f32[136,128]{1,0:T(8,128)S(1)} %collective-permute-done.11.refs_1_), channel_id=1, source_target_pairs={{0,4},{4,0},{8,12},{12,8},{16,20},{20,16},{24,28},{28,24},{1,5},{5... | collective-permute-start | bytes 208904 | tf_op jit(solution)/shard_map/ppermute | solution.py:261
  43.2 1.1 %collective-permute-done.16.refs_6_ = f32[136,128]{1,0:T(8,128)S(1)} collective-permute-done((f32[136,128]{1,0:T(8,128)S(1)}, f32[136,128]{1,0:T(8,128)S(1)}, u32[]{:S(2)}, u32[]{:S(2)}) %collective-permute-start.16) | collective-permute-done | bytes 69664 | tf_op jit(solution)/shard_map/ppermute | solution.py:261
  44.3 1.3 %collective-permute-done.17.refs_7_ = f32[136,128]{1,0:T(8,128)S(1)} collective-permute-done((f32[136,128]{1,0:T(8,128)S(1)}, f32[136,128]{1,0:T(8,128)S(1)}, u32[]{:S(2)}, u32[]{:S(2)}) %collective-permute-start.17) | collective-permute-done | bytes 69664 | tf_op jit(solution)/shard_map/ppermute | solution.py:261
  45.5 1.9 %shard_map.72 = (f32[256,128]{1,0:T(8,128)S(1)}, f32[8,128]{1,0:T(8,128)S(1)}, f32[24,128]{1,0:T(8,128)S(1)}) custom-call(bf16[16,8,128,128]{3,2,1,0:T(8,128)(2,1)S(1)} %get-tuple-element.18.values, bf16[384,1024]{1,0:T(8,128)(2,1)S(1)} %get-tuple-element.24.onehot, f32[128,128]{1,0:T(8,128)S(1)} %get-tuple-element.25.start_slot, ...), custom_call_target="tpu_custom_call" | custom-call | tf_op jit(solution)/shard_map/pallas_call | solution.py:249
  47.5 1.2 %collective-permute-done.18 = f32[24,128]{1,0:T(8,128)S(1)} collective-permute-done((f32[24,128]{1,0:T(8,128)S(1)}, f32[24,128]{1,0:T(8,128)S(1)}, u32[]{:S(2)}, u32[]{:S(2)}) %collective-permute-start.18) | collective-permute-done | bytes 12320 | tf_op jit(solution)/shard_map/ppermute | solution.py:261
  48.7 1.3 %collective-permute-start.19 = (f32[24,128]{1,0:T(8,128)S(1)}, f32[24,128]{1,0:T(8,128)S(1)}, u32[]{:S(2)}, u32[]{:S(2)}) collective-permute-start(f32[24,128]{1,0:T(8,128)S(1)} %add.20.refs_0_), channel_id=1, source_target_pairs={{0,3},{1,2},{2,1},{3,0},{4,7},{5,6},{6,5},{7,4},{8,11},{9,10},{10,... | collective-permute-start | bytes 36872 | tf_op jit(solution)/shard_map/ppermute | solution.py:261
  49.9 1.9 %collective-permute-done.19.refs_1_ = f32[24,128]{1,0:T(8,128)S(1)} collective-permute-done((f32[24,128]{1,0:T(8,128)S(1)}, f32[24,128]{1,0:T(8,128)S(1)}, u32[]{:S(2)}, u32[]{:S(2)}) %collective-permute-start.19) | collective-permute-done | bytes 12320 | tf_op jit(solution)/shard_map/ppermute | solution.py:261
  51.9 3.7 %collective-permute-start.22 = (f32[8,128]{1,0:T(8,128)S(1)}, f32[8,128]{1,0:T(8,128)S(1)}, u32[]{:S(2)}, u32[]{:S(2)}) collective-permute-start(f32[8,128]{1,0:T(8,128)S(1)} %shard_map.73), channel_id=1, source_target_pairs={{0,25},{1,24},{2,27},{3,26},{4,29},{5,28},{6,31},{7,30},{8,17},{9,... | collective-permute-start | bytes 12296 | tf_op jit(solution)/shard_map/ppermute | solution.py:271
  56.9 2.6 %collective-permute-done.21 = f32[8,128]{1,0:T(8,128)S(1)} collective-permute-done((f32[8,128]{1,0:T(8,128)S(1)}, f32[8,128]{1,0:T(8,128)S(1)}, u32[]{:S(2)}, u32[]{:S(2)}) %collective-permute-start.21) | collective-permute-done | bytes 4128 | tf_op jit(solution)/shard_map/ppermute | solution.py:271
  59.5 0.8 %collective-permute-start.23 = (f32[8,128]{1,0:T(8,128)S(1)}, f32[8,128]{1,0:T(8,128)S(1)}, u32[]{:S(2)}, u32[]{:S(2)}) collective-permute-start(f32[8,128]{1,0:T(8,128)S(1)} %add_add_fusion.refs_0_), channel_id=1, source_target_pairs={{0,5},{1,4},{2,7},{3,6},{4,1},{5,0},{6,3},{7,2},{8,13},{9,12},{10,... | collective-permute-start | bytes 12296 | tf_op jit(solution)/shard_map/ppermute | solution.py:271
  61.0 1.6 %collective-permute-done.23.refs_1_ = f32[8,128]{1,0:T(8,128)S(1)} collective-permute-done((f32[8,128]{1,0:T(8,128)S(1)}, f32[8,128]{1,0:T(8,128)S(1)}, u32[]{:S(2)}, u32[]{:S(2)}) %collective-permute-start.23) | collective-permute-done | bytes 4128 | tf_op jit(solution)/shard_map/ppermute | solution.py:271
  (31 shorter events, 7.7 us)
Async XLA Ops:
  0.6 9.1 %copy-start = (s32[2048]{0:T(1024)S(1)}, s32[2048]{0:T(1024)}, u32[]{:S(2)}) copy-start(s32[2048]{0:T(1024)} %param.8) | copy-start | bytes 24580
  4.4 1.3 %collective-permute-start = (f32[16,128]{1,0:T(8,128)S(1)}, f32[16,128]{1,0:T(8,128)S(1)}, u32[]{:S(2)}, u32[]{:S(2)}) collective-permute-start(f32[16,128]{1,0:T(8,128)S(1)} %get-tuple-element.22), channel_id=1, source_target_pairs={{0,1},{1,0},{2,3},{3,2},{4,5},{5,4},{6,7},{7,6},{8,9},{9,8},{10,11... | collective-permute-start | bytes 24584 | tf_op jit(solution)/shard_map/ppermute | solution.py:261
  5.8 4.0 %collective-permute-start.1 = (f32[16,128]{1,0:T(8,128)S(1)}, f32[16,128]{1,0:T(8,128)S(1)}, u32[]{:S(2)}, u32[]{:S(2)}) collective-permute-start(f32[16,128]{1,0:T(8,128)S(1)} %add.18.refs_0_), channel_id=1, source_target_pairs={{0,3},{1,2},{2,1},{3,0},{4,7},{5,6},{6,5},{7,4},{8,11},{9,10},{10,... | collective-permute-start | bytes 24584 | tf_op jit(solution)/shard_map/ppermute | solution.py:261
  10.4 7.9 %collective-permute-start.3 = (f32[136,128]{1,0:T(8,128)S(1)}, f32[136,128]{1,0:T(8,128)S(1)}, u32[]{:S(2)}, u32[]{:S(2)}) collective-permute-start(f32[136,128]{1,0:T(8,128)S(1)} %get-tuple-element.23.refs_0_), channel_id=1, source_target_pairs={{0,16},{4,20},{8,24},{12,28},{16,0},{20,4},{24,8},{28,12},{1,17},{... | collective-permute-start | bytes 208904 | tf_op jit(solution)/shard_map/ppermute | solution.py:261
  13.5 6.8 %collective-permute-start.2 = (f32[136,128]{1,0:T(8,128)S(1)}, f32[136,128]{1,0:T(8,128)S(1)}, u32[]{:S(2)}, u32[]{:S(2)}) collective-permute-start(f32[136,128]{1,0:T(8,128)S(1)} %get-tuple-element.23.refs_0_), channel_id=1, source_target_pairs={{0,24},{4,28},{8,16},{12,20},{16,8},{20,12},{24,0},{28,4},{1,25},{... | collective-permute-start | bytes 208904 | tf_op jit(solution)/shard_map/ppermute | solution.py:261
  14.8 7.1 %collective-permute-start.6 = (f32[136,128]{1,0:T(8,128)S(1)}, f32[136,128]{1,0:T(8,128)S(1)}, u32[]{:S(2)}, u32[]{:S(2)}) collective-permute-start(f32[136,128]{1,0:T(8,128)S(1)} %get-tuple-element.23.refs_0_), channel_id=1, source_target_pairs={{0,12},{4,8},{8,4},{12,0},{16,28},{20,24},{24,20},{28,16},{1,13},{... | collective-permute-start | bytes 208904 | tf_op jit(solution)/shard_map/ppermute | solution.py:261
  16.0 6.0 %collective-permute-start.5 = (f32[136,128]{1,0:T(8,128)S(1)}, f32[136,128]{1,0:T(8,128)S(1)}, u32[]{:S(2)}, u32[]{:S(2)}) collective-permute-start(f32[136,128]{1,0:T(8,128)S(1)} %get-tuple-element.23.refs_0_), channel_id=1, source_target_pairs={{0,4},{4,0},{8,12},{12,8},{16,20},{20,16},{24,28},{28,24},{1,5},{5... | collective-permute-start | bytes 208904 | tf_op jit(solution)/shard_map/ppermute | solution.py:261
  16.5 5.8 %collective-permute-start.4 = (f32[136,128]{1,0:T(8,128)S(1)}, f32[136,128]{1,0:T(8,128)S(1)}, u32[]{:S(2)}, u32[]{:S(2)}) collective-permute-start(f32[136,128]{1,0:T(8,128)S(1)} %get-tuple-element.23.refs_0_), channel_id=1, source_target_pairs={{0,8},{4,12},{8,0},{12,4},{16,24},{20,28},{24,16},{28,20},{1,9},{5... | collective-permute-start | bytes 208904 | tf_op jit(solution)/shard_map/ppermute | solution.py:261
  18.3 5.2 %collective-permute-start.7 = (f32[136,128]{1,0:T(8,128)S(1)}, f32[136,128]{1,0:T(8,128)S(1)}, u32[]{:S(2)}, u32[]{:S(2)}) collective-permute-start(f32[136,128]{1,0:T(8,128)S(1)} %collective-permute-done.3.refs_2_), channel_id=1, source_target_pairs={{0,4},{4,0},{8,12},{12,8},{16,20},{20,16},{24,28},{28,24},{1,5},{5... | collective-permute-start | bytes 208904 | tf_op jit(solution)/shard_map/ppermute | solution.py:261
  20.3 4.3 %collective-permute-start.8 = (f32[136,128]{1,0:T(8,128)S(1)}, f32[136,128]{1,0:T(8,128)S(1)}, u32[]{:S(2)}, u32[]{:S(2)}) collective-permute-start(f32[136,128]{1,0:T(8,128)S(1)} %collective-permute-done.2.refs_1_), channel_id=1, source_target_pairs={{0,4},{4,0},{8,12},{12,8},{16,20},{20,16},{24,28},{28,24},{1,5},{5... | collective-permute-start | bytes 208904 | tf_op jit(solution)/shard_map/ppermute | solution.py:261
  26.5 1.2 %collective-permute-start.9 = (f32[24,128]{1,0:T(8,128)S(1)}, f32[24,128]{1,0:T(8,128)S(1)}, u32[]{:S(2)}, u32[]{:S(2)}) collective-permute-start(f32[24,128]{1,0:T(8,128)S(1)} %get-tuple-element.28), channel_id=1, source_target_pairs={{0,1},{1,0},{2,3},{3,2},{4,5},{5,4},{6,7},{7,6},{8,9},{9,8},{10,11... | collective-permute-start | bytes 36872 | tf_op jit(solution)/shard_map/ppermute | solution.py:261
  27.7 3.1 %collective-permute-start.10 = (f32[24,128]{1,0:T(8,128)S(1)}, f32[24,128]{1,0:T(8,128)S(1)}, u32[]{:S(2)}, u32[]{:S(2)}) collective-permute-start(f32[24,128]{1,0:T(8,128)S(1)} %add.19.refs_0_), channel_id=1, source_target_pairs={{0,3},{1,2},{2,1},{3,0},{4,7},{5,6},{6,5},{7,4},{8,11},{9,10},{10,... | collective-permute-start | bytes 36872 | tf_op jit(solution)/shard_map/ppermute | solution.py:261
  31.5 7.5 %collective-permute-start.12 = (f32[136,128]{1,0:T(8,128)S(1)}, f32[136,128]{1,0:T(8,128)S(1)}, u32[]{:S(2)}, u32[]{:S(2)}) collective-permute-start(f32[136,128]{1,0:T(8,128)S(1)} %get-tuple-element.29.refs_0_), channel_id=1, source_target_pairs={{0,16},{4,20},{8,24},{12,28},{16,0},{20,4},{24,8},{28,12},{1,17},{... | collective-permute-start | bytes 208904 | tf_op jit(solution)/shard_map/ppermute | solution.py:261
  34.4 6.8 %collective-permute-start.11 = (f32[136,128]{1,0:T(8,128)S(1)}, f32[136,128]{1,0:T(8,128)S(1)}, u32[]{:S(2)}, u32[]{:S(2)}) collective-permute-start(f32[136,128]{1,0:T(8,128)S(1)} %get-tuple-element.29.refs_0_), channel_id=1, source_target_pairs={{0,24},{4,28},{8,16},{12,20},{16,8},{20,12},{24,0},{28,4},{1,25},{... | collective-permute-start | bytes 208904 | tf_op jit(solution)/shard_map/ppermute | solution.py:261
  35.5 7.3 %collective-permute-start.15 = (f32[136,128]{1,0:T(8,128)S(1)}, f32[136,128]{1,0:T(8,128)S(1)}, u32[]{:S(2)}, u32[]{:S(2)}) collective-permute-start(f32[136,128]{1,0:T(8,128)S(1)} %get-tuple-element.29.refs_0_), channel_id=1, source_target_pairs={{0,12},{4,8},{8,4},{12,0},{16,28},{20,24},{24,20},{28,16},{1,13},{... | collective-permute-start | bytes 208904 | tf_op jit(solution)/shard_map/ppermute | solution.py:261
  36.6 6.1 %collective-permute-start.14 = (f32[136,128]{1,0:T(8,128)S(1)}, f32[136,128]{1,0:T(8,128)S(1)}, u32[]{:S(2)}, u32[]{:S(2)}) collective-permute-start(f32[136,128]{1,0:T(8,128)S(1)} %get-tuple-element.29.refs_0_), channel_id=1, source_target_pairs={{0,4},{4,0},{8,12},{12,8},{16,20},{20,16},{24,28},{28,24},{1,5},{5... | collective-permute-start | bytes 208904 | tf_op jit(solution)/shard_map/ppermute | solution.py:261
  37.4 5.7 %collective-permute-start.13 = (f32[136,128]{1,0:T(8,128)S(1)}, f32[136,128]{1,0:T(8,128)S(1)}, u32[]{:S(2)}, u32[]{:S(2)}) collective-permute-start(f32[136,128]{1,0:T(8,128)S(1)} %get-tuple-element.29.refs_0_), channel_id=1, source_target_pairs={{0,8},{4,12},{8,0},{12,4},{16,24},{20,28},{24,16},{28,20},{1,9},{5... | collective-permute-start | bytes 208904 | tf_op jit(solution)/shard_map/ppermute | solution.py:261
  39.0 5.3 %collective-permute-start.16 = (f32[136,128]{1,0:T(8,128)S(1)}, f32[136,128]{1,0:T(8,128)S(1)}, u32[]{:S(2)}, u32[]{:S(2)}) collective-permute-start(f32[136,128]{1,0:T(8,128)S(1)} %collective-permute-done.12.refs_2_), channel_id=1, source_target_pairs={{0,4},{4,0},{8,12},{12,8},{16,20},{20,16},{24,28},{28,24},{1,5},{5... | collective-permute-start | bytes 208904 | tf_op jit(solution)/shard_map/ppermute | solution.py:261
  41.2 4.3 %collective-permute-start.17 = (f32[136,128]{1,0:T(8,128)S(1)}, f32[136,128]{1,0:T(8,128)S(1)}, u32[]{:S(2)}, u32[]{:S(2)}) collective-permute-start(f32[136,128]{1,0:T(8,128)S(1)} %collective-permute-done.11.refs_1_), channel_id=1, source_target_pairs={{0,4},{4,0},{8,12},{12,8},{16,20},{20,16},{24,28},{28,24},{1,5},{5... | collective-permute-start | bytes 208904 | tf_op jit(solution)/shard_map/ppermute | solution.py:261
  47.4 1.2 %collective-permute-start.18 = (f32[24,128]{1,0:T(8,128)S(1)}, f32[24,128]{1,0:T(8,128)S(1)}, u32[]{:S(2)}, u32[]{:S(2)}) collective-permute-start(f32[24,128]{1,0:T(8,128)S(1)} %get-tuple-element.33), channel_id=1, source_target_pairs={{0,1},{1,0},{2,3},{3,2},{4,5},{5,4},{6,7},{7,6},{8,9},{9,8},{10,11... | collective-permute-start | bytes 36872 | tf_op jit(solution)/shard_map/ppermute | solution.py:261
  48.7 3.1 %collective-permute-start.19 = (f32[24,128]{1,0:T(8,128)S(1)}, f32[24,128]{1,0:T(8,128)S(1)}, u32[]{:S(2)}, u32[]{:S(2)}) collective-permute-start(f32[24,128]{1,0:T(8,128)S(1)} %add.20.refs_0_), channel_id=1, source_target_pairs={{0,3},{1,2},{2,1},{3,0},{4,7},{5,6},{6,5},{7,4},{8,11},{9,10},{10,... | collective-permute-start | bytes 36872 | tf_op jit(solution)/shard_map/ppermute | solution.py:261
  51.9 5.0 %collective-permute-start.22 = (f32[8,128]{1,0:T(8,128)S(1)}, f32[8,128]{1,0:T(8,128)S(1)}, u32[]{:S(2)}, u32[]{:S(2)}) collective-permute-start(f32[8,128]{1,0:T(8,128)S(1)} %shard_map.73), channel_id=1, source_target_pairs={{0,25},{1,24},{2,27},{3,26},{4,29},{5,28},{6,31},{7,30},{8,17},{9,... | collective-permute-start | bytes 12296 | tf_op jit(solution)/shard_map/ppermute | solution.py:271
  55.6 3.9 %collective-permute-start.21 = (f32[8,128]{1,0:T(8,128)S(1)}, f32[8,128]{1,0:T(8,128)S(1)}, u32[]{:S(2)}, u32[]{:S(2)}) collective-permute-start(f32[8,128]{1,0:T(8,128)S(1)} %shard_map.73), channel_id=1, source_target_pairs={{0,17},{1,16},{2,19},{3,18},{4,21},{5,20},{6,23},{7,22},{8,25},{9,... | collective-permute-start | bytes 12296 | tf_op jit(solution)/shard_map/ppermute | solution.py:271
  55.6 3.9 %collective-permute-start.20 = (f32[8,128]{1,0:T(8,128)S(1)}, f32[8,128]{1,0:T(8,128)S(1)}, u32[]{:S(2)}, u32[]{:S(2)}) collective-permute-start(f32[8,128]{1,0:T(8,128)S(1)} %shard_map.73), channel_id=1, source_target_pairs={{0,9},{1,8},{2,11},{3,10},{4,13},{5,12},{6,15},{7,14},{8,1},{9,0},... | collective-permute-start | bytes 12296 | tf_op jit(solution)/shard_map/ppermute | solution.py:271
  59.5 3.1 %collective-permute-start.23 = (f32[8,128]{1,0:T(8,128)S(1)}, f32[8,128]{1,0:T(8,128)S(1)}, u32[]{:S(2)}, u32[]{:S(2)}) collective-permute-start(f32[8,128]{1,0:T(8,128)S(1)} %add_add_fusion.refs_0_), channel_id=1, source_target_pairs={{0,5},{1,4},{2,7},{3,6},{4,1},{5,0},{6,3},{7,2},{8,13},{9,12},{10,... | collective-permute-start | bytes 12296 | tf_op jit(solution)/shard_map/ppermute | solution.py:271

commit v5 on v4

--- a/solution.py
+++ b/solution.py
@@ -36,6 +36,14 @@
 def read_scalar(block, place):
     lane = lane_iota(block.shape)
     return jnp.sum(jnp.where(lane == place, block, 0.0), axis=1, keepdims=True)
+
+
+def forward_tile_vector(tile, picked):
+    picked = picked.astype(BF16).astype(F32)
+    kept = tile[0].astype(F32) * picked[0:1, :]
+    for s in range(1, tile.shape[0]):
+        kept = kept + tile[s].astype(F32) * picked[s : s + 1, :]
+    return jnp.sum(kept.T, axis=0, keepdims=True)
 
 
 def forward_tile(tile, picked):
@@ -65,7 +73,8 @@
 def forward_all(values, picked, out):
     tiles, slots = values.shape[:2]
     for t in range(tiles):
-        out[t : t + 1, :] = forward_tile(values[t], picked[t * slots : (t + 1) * slots, :])
+        one = forward_tile if t % 4 == 0 else forward_tile_vector
+        out[t : t + 1, :] = one(values[t], picked[t * slots : (t + 1) * slots, :])
 
 
 def back_all(values, rows_term, ids, out):
@@ -287,7 +296,7 @@
         gathered = lax.all_gather(array, "inst", axis=0)
         return [gathered[i] for i in range(size)]
     parts = {0: array}
-    for distance in (6, 4, 2, 1, 3):
+    for distance in (2, 4, 6, 1, 3):
         parts[distance] = swap(array, "inst", distance)
     for distance in (4, 6):
         parts[distance ^ 1] = swap(parts[distance], "inst", 1)

time: 63.6 us -> 60.6 us (0.953)
  starting transfers between devices: 32.9 us -> 30.5 us
  Pallas kernels: 9.05 us -> 7.75 us
  waiting for transfers between devices: 19.4 us -> 20.2 us
    ppermute x20, waiting for transfers between devices: 14.5 us -> 17.4 us  [swap(): return lax.ppermute(array, axis, [(i, i ^ distance) for i in range(size)])]
    ppermute x20, starting transfers between devices: 27.8 us -> 25.1 us  [swap(): return lax.ppermute(array, axis, [(i, i ^ distance) for i in range(size)])]
    ppermute x4, waiting for transfers between devices: 4.95 us -> 2.78 us  [swap_both(): return lax.ppermute(array, ('inst', 'feat'), pairs)]
    pallas_call x7, Pallas kernels: 9.05 us -> 7.75 us  [call(): pl.pallas_call(kernel, out_shape=out_shape, in_specs=in_specs, out_specs=...]
where the time goes in v5:
time: 60.6 us; the launch traced here: 60.5 us
  starting transfers between devices  30.5 us (50%)
  waiting for transfers between devices  20.2 us (33%)
  Pallas kernels  7.75 us (13%)
  local copies, waits for them, and re-layouts  1.32 us (2%)
  between operations  0.71 us (1%)
    ppermute x20, starting transfers between devices, swap(): return lax.ppermute(array, axis, [(i, i ^ distance) for i in range(size)])  25.1 us
    ppermute x20, waiting for transfers between devices, swap(): return lax.ppermute(array, axis, [(i, i ^ distance) for i in range(size)])  17.4 us
    pallas_call x7, Pallas kernels, call(): pl.pallas_call(kernel, out_shape=out_shape, in_specs=in_specs, out_specs=...  7.75 us
    ppermute x4, starting transfers between devices, swap_both(): return lax.ppermute(array, ('inst', 'feat'), pairs)  5.46 us
    ppermute x4, waiting for transfers between devices, swap_both(): return lax.ppermute(array, ('inst', 'feat'), pairs)  2.78 us
    unnamed x4, local copies, waits for them, and re-layouts  1.32 us
  transfers between devices with their start and end apart: 24, of which 18 were waited for; matrix products, arithmetic and copies ran while one was open for 1% of the time, Pallas kernels for 0%

profile of v5, /device:TPU:0, one launch (start us, length us, event | category | flops | bytes accessed | tf_op | source)
XLA Modules:
  0.0 60.5 jit_solution(13006291478295031257)
XLA Ops:
  0.6 3.3 %shard_map.68 = (bf16[16,8,128,128]{3,2,1,0:T(8,128)(2,1)S(1)}, f32[128,128]{1,0:T(8,128)S(1)}, f32[128,128]{1,0:T(8,128)S(1)}, f32[256,128]{1,0:T(8,128)S(1)}, f32[16,128]{1,0:T(8,128)S(1)}) custom-call(s32[8,16]{1,0:T(8,128)} %bitcast.4, s32[1,16]{1,0:T(1,128)} %bitcast.5, f32[2048,128]{1,0:T(8,128)} %weights.1, bf16[16,8,128,128]{3,2,1,0:T(8,128)(2,1)} %values_in.1), custom_call_target="tpu_custom_call" | custom-call | tf_op jit(solution)/shard_map/pallas_call | solution.py:258
  4.5 0.8 %collective-permute-done = f32[16,128]{1,0:T(8,128)S(1)} collective-permute-done((f32[16,128]{1,0:T(8,128)S(1)}, f32[16,128]{1,0:T(8,128)S(1)}, u32[]{:S(2)}, u32[]{:S(2)}) %collective-permute-start) | collective-permute-done | bytes 8224 | tf_op jit(solution)/shard_map/ppermute | solution.py:270
  5.3 2.6 %collective-permute-start.1 = (f32[16,128]{1,0:T(8,128)S(1)}, f32[16,128]{1,0:T(8,128)S(1)}, u32[]{:S(2)}, u32[]{:S(2)}) collective-permute-start(f32[16,128]{1,0:T(8,128)S(1)} %add.18.refs_0_), channel_id=1, source_target_pairs={{0,3},{1,2},{2,1},{3,0},{4,7},{5,6},{6,5},{7,4},{8,11},{9,10},{10,... | collective-permute-start | bytes 24584 | tf_op jit(solution)/shard_map/ppermute | solution.py:270
  7.9 1.4 %collective-permute-done.1.refs_1_ = f32[16,128]{1,0:T(8,128)S(1)} collective-permute-done((f32[16,128]{1,0:T(8,128)S(1)}, f32[16,128]{1,0:T(8,128)S(1)}, u32[]{:S(2)}, u32[]{:S(2)}) %collective-permute-start.1) | collective-permute-done | bytes 8224 | tf_op jit(solution)/shard_map/ppermute | solution.py:270
  9.9 4.1 %collective-permute-start.4 = (f32[136,128]{1,0:T(8,128)S(1)}, f32[136,128]{1,0:T(8,128)S(1)}, u32[]{:S(2)}, u32[]{:S(2)}) collective-permute-start(f32[136,128]{1,0:T(8,128)S(1)} %get-tuple-element.23.refs_0_), channel_id=1, source_target_pairs={{0,24},{4,28},{8,16},{12,20},{16,8},{20,12},{24,0},{28,4},{1,25},{... | collective-permute-start | bytes 208904 | tf_op jit(solution)/shard_map/ppermute | solution.py:270
  14.1 1.7 %collective-permute-start.6 = (f32[136,128]{1,0:T(8,128)S(1)}, f32[136,128]{1,0:T(8,128)S(1)}, u32[]{:S(2)}, u32[]{:S(2)}) collective-permute-start(f32[136,128]{1,0:T(8,128)S(1)} %get-tuple-element.23.refs_0_), channel_id=1, source_target_pairs={{0,12},{4,8},{8,4},{12,0},{16,28},{20,24},{24,20},{28,16},{1,13},{... | collective-permute-start | bytes 208904 | tf_op jit(solution)/shard_map/ppermute | solution.py:270
  16.2 1.4 %collective-permute-start.2 = (f32[136,128]{1,0:T(8,128)S(1)}, f32[136,128]{1,0:T(8,128)S(1)}, u32[]{:S(2)}, u32[]{:S(2)}) collective-permute-start(f32[136,128]{1,0:T(8,128)S(1)} %get-tuple-element.23.refs_0_), channel_id=1, source_target_pairs={{0,8},{4,12},{8,0},{12,4},{16,24},{20,28},{24,16},{28,20},{1,9},{5... | collective-permute-start | bytes 208904 | tf_op jit(solution)/shard_map/ppermute | solution.py:270
  17.5 1.5 %collective-permute-start.8 = (f32[136,128]{1,0:T(8,128)S(1)}, f32[136,128]{1,0:T(8,128)S(1)}, u32[]{:S(2)}, u32[]{:S(2)}) collective-permute-start(f32[136,128]{1,0:T(8,128)S(1)} %collective-permute-done.4.refs_3_), channel_id=1, source_target_pairs={{0,4},{4,0},{8,12},{12,8},{16,20},{20,16},{24,28},{28,24},{1,5},{5... | collective-permute-start | bytes 208904 | tf_op jit(solution)/shard_map/ppermute | solution.py:270
  19.1 1.3 %collective-permute-done.3.refs_2_ = f32[136,128]{1,0:T(8,128)S(1)} collective-permute-done((f32[136,128]{1,0:T(8,128)S(1)}, f32[136,128]{1,0:T(8,128)S(1)}, u32[]{:S(2)}, u32[]{:S(2)}) %collective-permute-start.3) | collective-permute-done | bytes 69664 | tf_op jit(solution)/shard_map/ppermute | solution.py:270
  20.3 1.5 %collective-permute-start.7 = (f32[136,128]{1,0:T(8,128)S(1)}, f32[136,128]{1,0:T(8,128)S(1)}, u32[]{:S(2)}, u32[]{:S(2)}) collective-permute-start(f32[136,128]{1,0:T(8,128)S(1)} %collective-permute-done.3.refs_2_), channel_id=1, source_target_pairs={{0,4},{4,0},{8,12},{12,8},{16,20},{20,16},{24,28},{28,24},{1,5},{5... | collective-permute-start | bytes 208904 | tf_op jit(solution)/shard_map/ppermute | solution.py:270
  22.1 2.6 %collective-permute-done.7.refs_6_ = f32[136,128]{1,0:T(8,128)S(1)} collective-permute-done((f32[136,128]{1,0:T(8,128)S(1)}, f32[136,128]{1,0:T(8,128)S(1)}, u32[]{:S(2)}, u32[]{:S(2)}) %collective-permute-start.7) | collective-permute-done | bytes 69664 | tf_op jit(solution)/shard_map/ppermute | solution.py:270
  24.7 1.4 %shard_map.70 = (f32[256,128]{1,0:T(8,128)S(1)}, f32[128,128]{1,0:T(8,128)S(1)}, bf16[384,1024]{1,0:T(8,128)(2,1)S(1)}, f32[24,128]{1,0:T(8,128)S(1)}) custom-call(bf16[16,8,128,128]{3,2,1,0:T(8,128)(2,1)S(1)} %get-tuple-element.18.values, f32[128,128]{1,0:T(8,128)S(1)} %get-tuple-element.19.ids, f32[128,128]{1,0:T(8,128)S(1)} %get-tuple-element.20.picked, ...), custom_call_target="tpu_custom_call" | custom-call | tf_op jit(solution)/shard_map/pallas_call | solution.py:258
  26.2 1.2 %collective-permute-done.9 = f32[24,128]{1,0:T(8,128)S(1)} collective-permute-done((f32[24,128]{1,0:T(8,128)S(1)}, f32[24,128]{1,0:T(8,128)S(1)}, u32[]{:S(2)}, u32[]{:S(2)}) %collective-permute-start.9) | collective-permute-done | bytes 12320 | tf_op jit(solution)/shard_map/ppermute | solution.py:270
  27.3 1.3 %collective-permute-start.10 = (f32[24,128]{1,0:T(8,128)S(1)}, f32[24,128]{1,0:T(8,128)S(1)}, u32[]{:S(2)}, u32[]{:S(2)}) collective-permute-start(f32[24,128]{1,0:T(8,128)S(1)} %add.19.refs_0_), channel_id=1, source_target_pairs={{0,3},{1,2},{2,1},{3,0},{4,7},{5,6},{6,5},{7,4},{8,11},{9,10},{10,... | collective-permute-start | bytes 36872 | tf_op jit(solution)/shard_map/ppermute | solution.py:270
  28.6 1.9 %collective-permute-done.10.refs_1_ = f32[24,128]{1,0:T(8,128)S(1)} collective-permute-done((f32[24,128]{1,0:T(8,128)S(1)}, f32[24,128]{1,0:T(8,128)S(1)}, u32[]{:S(2)}, u32[]{:S(2)}) %collective-permute-start.10) | collective-permute-done | bytes 12320 | tf_op jit(solution)/shard_map/ppermute | solution.py:270
  31.1 2.4 %collective-permute-start.13 = (f32[136,128]{1,0:T(8,128)S(1)}, f32[136,128]{1,0:T(8,128)S(1)}, u32[]{:S(2)}, u32[]{:S(2)}) collective-permute-start(f32[136,128]{1,0:T(8,128)S(1)} %get-tuple-element.29.refs_0_), channel_id=1, source_target_pairs={{0,24},{4,28},{8,16},{12,20},{16,8},{20,12},{24,0},{28,4},{1,25},{... | collective-permute-start | bytes 208904 | tf_op jit(solution)/shard_map/ppermute | solution.py:270
  33.7 2.8 %collective-permute-start.15 = (f32[136,128]{1,0:T(8,128)S(1)}, f32[136,128]{1,0:T(8,128)S(1)}, u32[]{:S(2)}, u32[]{:S(2)}) collective-permute-start(f32[136,128]{1,0:T(8,128)S(1)} %get-tuple-element.29.refs_0_), channel_id=1, source_target_pairs={{0,12},{4,8},{8,4},{12,0},{16,28},{20,24},{24,20},{28,16},{1,13},{... | collective-permute-start | bytes 208904 | tf_op jit(solution)/shard_map/ppermute | solution.py:270
  37.2 1.0 %collective-permute-done.13.refs_3_ = f32[136,128]{1,0:T(8,128)S(1)} collective-permute-done((f32[136,128]{1,0:T(8,128)S(1)}, f32[136,128]{1,0:T(8,128)S(1)}, u32[]{:S(2)}, u32[]{:S(2)}) %collective-permute-start.13) | collective-permute-done | bytes 69664 | tf_op jit(solution)/shard_map/ppermute | solution.py:270
  38.1 1.4 %collective-permute-start.17 = (f32[136,128]{1,0:T(8,128)S(1)}, f32[136,128]{1,0:T(8,128)S(1)}, u32[]{:S(2)}, u32[]{:S(2)}) collective-permute-start(f32[136,128]{1,0:T(8,128)S(1)} %collective-permute-done.13.refs_3_), channel_id=1, source_target_pairs={{0,4},{4,0},{8,12},{12,8},{16,20},{20,16},{24,28},{28,24},{1,5},{5... | collective-permute-start | bytes 208904 | tf_op jit(solution)/shard_map/ppermute | solution.py:270
  39.6 1.0 %collective-permute-done.12.refs_2_ = f32[136,128]{1,0:T(8,128)S(1)} collective-permute-done((f32[136,128]{1,0:T(8,128)S(1)}, f32[136,128]{1,0:T(8,128)S(1)}, u32[]{:S(2)}, u32[]{:S(2)}) %collective-permute-start.12) | collective-permute-done | bytes 69664 | tf_op jit(solution)/shard_map/ppermute | solution.py:270
  40.5 1.2 %collective-permute-start.16 = (f32[136,128]{1,0:T(8,128)S(1)}, f32[136,128]{1,0:T(8,128)S(1)}, u32[]{:S(2)}, u32[]{:S(2)}) collective-permute-start(f32[136,128]{1,0:T(8,128)S(1)} %collective-permute-done.12.refs_2_), channel_id=1, source_target_pairs={{0,4},{4,0},{8,12},{12,8},{16,20},{20,16},{24,28},{28,24},{1,5},{5... | collective-permute-start | bytes 208904 | tf_op jit(solution)/shard_map/ppermute | solution.py:270
  42.5 2.4 %collective-permute-done.16.refs_6_ = f32[136,128]{1,0:T(8,128)S(1)} collective-permute-done((f32[136,128]{1,0:T(8,128)S(1)}, f32[136,128]{1,0:T(8,128)S(1)}, u32[]{:S(2)}, u32[]{:S(2)}) %collective-permute-start.16) | collective-permute-done | bytes 69664 | tf_op jit(solution)/shard_map/ppermute | solution.py:270
  44.9 1.5 %shard_map.72 = (f32[256,128]{1,0:T(8,128)S(1)}, f32[8,128]{1,0:T(8,128)S(1)}, f32[24,128]{1,0:T(8,128)S(1)}) custom-call(bf16[16,8,128,128]{3,2,1,0:T(8,128)(2,1)S(1)} %get-tuple-element.18.values, bf16[384,1024]{1,0:T(8,128)(2,1)S(1)} %get-tuple-element.24.onehot, f32[128,128]{1,0:T(8,128)S(1)} %get-tuple-element.25.start_slot, ...), custom_call_target="tpu_custom_call" | custom-call | tf_op jit(solution)/shard_map/pallas_call | solution.py:258
  46.4 1.2 %collective-permute-done.18 = f32[24,128]{1,0:T(8,128)S(1)} collective-permute-done((f32[24,128]{1,0:T(8,128)S(1)}, f32[24,128]{1,0:T(8,128)S(1)}, u32[]{:S(2)}, u32[]{:S(2)}) %collective-permute-start.18) | collective-permute-done | bytes 12320 | tf_op jit(solution)/shard_map/ppermute | solution.py:270
  47.5 1.3 %collective-permute-start.19 = (f32[24,128]{1,0:T(8,128)S(1)}, f32[24,128]{1,0:T(8,128)S(1)}, u32[]{:S(2)}, u32[]{:S(2)}) collective-permute-start(f32[24,128]{1,0:T(8,128)S(1)} %add.20.refs_0_), channel_id=1, source_target_pairs={{0,3},{1,2},{2,1},{3,0},{4,7},{5,6},{6,5},{7,4},{8,11},{9,10},{10,... | collective-permute-start | bytes 36872 | tf_op jit(solution)/shard_map/ppermute | solution.py:270
  48.8 1.9 %collective-permute-done.19.refs_1_ = f32[24,128]{1,0:T(8,128)S(1)} collective-permute-done((f32[24,128]{1,0:T(8,128)S(1)}, f32[24,128]{1,0:T(8,128)S(1)}, u32[]{:S(2)}, u32[]{:S(2)}) %collective-permute-start.19) | collective-permute-done | bytes 12320 | tf_op jit(solution)/shard_map/ppermute | solution.py:270
  50.8 1.9 %collective-permute-start.22 = (f32[8,128]{1,0:T(8,128)S(1)}, f32[8,128]{1,0:T(8,128)S(1)}, u32[]{:S(2)}, u32[]{:S(2)}) collective-permute-start(f32[8,128]{1,0:T(8,128)S(1)} %shard_map.73), channel_id=1, source_target_pairs={{0,25},{1,24},{2,27},{3,26},{4,29},{5,28},{6,31},{7,30},{8,17},{9,... | collective-permute-start | bytes 12296 | tf_op jit(solution)/shard_map/ppermute | solution.py:280
  52.6 2.1 %collective-permute-start.20 = (f32[8,128]{1,0:T(8,128)S(1)}, f32[8,128]{1,0:T(8,128)S(1)}, u32[]{:S(2)}, u32[]{:S(2)}) collective-permute-start(f32[8,128]{1,0:T(8,128)S(1)} %shard_map.73), channel_id=1, source_target_pairs={{0,9},{1,8},{2,11},{3,10},{4,13},{5,12},{6,15},{7,14},{8,1},{9,0},... | collective-permute-start | bytes 12296 | tf_op jit(solution)/shard_map/ppermute | solution.py:280
  54.7 1.0 %collective-permute-done.22 = f32[8,128]{1,0:T(8,128)S(1)} collective-permute-done((f32[8,128]{1,0:T(8,128)S(1)}, f32[8,128]{1,0:T(8,128)S(1)}, u32[]{:S(2)}, u32[]{:S(2)}) %collective-permute-start.22) | collective-permute-done | bytes 4128 | tf_op jit(solution)/shard_map/ppermute | solution.py:280
  55.7 0.9 %collective-permute-done.21 = f32[8,128]{1,0:T(8,128)S(1)} collective-permute-done((f32[8,128]{1,0:T(8,128)S(1)}, f32[8,128]{1,0:T(8,128)S(1)}, u32[]{:S(2)}, u32[]{:S(2)}) %collective-permute-start.21) | collective-permute-done | bytes 4128 | tf_op jit(solution)/shard_map/ppermute | solution.py:280
  56.6 1.5 %collective-permute-start.23 = (f32[8,128]{1,0:T(8,128)S(1)}, f32[8,128]{1,0:T(8,128)S(1)}, u32[]{:S(2)}, u32[]{:S(2)}) collective-permute-start(f32[8,128]{1,0:T(8,128)S(1)} %add_add_fusion.refs_0_), channel_id=1, source_target_pairs={{0,5},{1,4},{2,7},{3,6},{4,1},{5,0},{6,3},{7,2},{8,13},{9,12},{10,... | collective-permute-start | bytes 12296 | tf_op jit(solution)/shard_map/ppermute | solution.py:280
  58.8 0.9 %collective-permute-done.23.refs_1_ = f32[8,128]{1,0:T(8,128)S(1)} collective-permute-done((f32[8,128]{1,0:T(8,128)S(1)}, f32[8,128]{1,0:T(8,128)S(1)}, u32[]{:S(2)}, u32[]{:S(2)}) %collective-permute-start.23) | collective-permute-done | bytes 4128 | tf_op jit(solution)/shard_map/ppermute | solution.py:280
  (31 shorter events, 5.7 us)
Async XLA Ops:
  0.6 8.7 %copy-start = (s32[2048]{0:T(1024)S(1)}, s32[2048]{0:T(1024)}, u32[]{:S(2)}) copy-start(s32[2048]{0:T(1024)} %param.8) | copy-start | bytes 24580
  4.0 1.3 %collective-permute-start = (f32[16,128]{1,0:T(8,128)S(1)}, f32[16,128]{1,0:T(8,128)S(1)}, u32[]{:S(2)}, u32[]{:S(2)}) collective-permute-start(f32[16,128]{1,0:T(8,128)S(1)} %get-tuple-element.22), channel_id=1, source_target_pairs={{0,1},{1,0},{2,3},{3,2},{4,5},{5,4},{6,7},{7,6},{8,9},{9,8},{10,11... | collective-permute-start | bytes 24584 | tf_op jit(solution)/shard_map/ppermute | solution.py:270
  5.3 4.0 %collective-permute-start.1 = (f32[16,128]{1,0:T(8,128)S(1)}, f32[16,128]{1,0:T(8,128)S(1)}, u32[]{:S(2)}, u32[]{:S(2)}) collective-permute-start(f32[16,128]{1,0:T(8,128)S(1)} %add.18.refs_0_), channel_id=1, source_target_pairs={{0,3},{1,2},{2,1},{3,0},{4,7},{5,6},{6,5},{7,4},{8,11},{9,10},{10,... | collective-permute-start | bytes 24584 | tf_op jit(solution)/shard_map/ppermute | solution.py:270
  9.9 7.6 %collective-permute-start.4 = (f32[136,128]{1,0:T(8,128)S(1)}, f32[136,128]{1,0:T(8,128)S(1)}, u32[]{:S(2)}, u32[]{:S(2)}) collective-permute-start(f32[136,128]{1,0:T(8,128)S(1)} %get-tuple-element.23.refs_0_), channel_id=1, source_target_pairs={{0,24},{4,28},{8,16},{12,20},{16,8},{20,12},{24,0},{28,4},{1,25},{... | collective-permute-start | bytes 208904 | tf_op jit(solution)/shard_map/ppermute | solution.py:270
  14.0 6.3 %collective-permute-start.3 = (f32[136,128]{1,0:T(8,128)S(1)}, f32[136,128]{1,0:T(8,128)S(1)}, u32[]{:S(2)}, u32[]{:S(2)}) collective-permute-start(f32[136,128]{1,0:T(8,128)S(1)} %get-tuple-element.23.refs_0_), channel_id=1, source_target_pairs={{0,16},{4,20},{8,24},{12,28},{16,0},{20,4},{24,8},{28,12},{1,17},{... | collective-permute-start | bytes 208904 | tf_op jit(solution)/shard_map/ppermute | solution.py:270
  14.1 7.8 %collective-permute-start.6 = (f32[136,128]{1,0:T(8,128)S(1)}, f32[136,128]{1,0:T(8,128)S(1)}, u32[]{:S(2)}, u32[]{:S(2)}) collective-permute-start(f32[136,128]{1,0:T(8,128)S(1)} %get-tuple-element.23.refs_0_), channel_id=1, source_target_pairs={{0,12},{4,8},{8,4},{12,0},{16,28},{20,24},{24,20},{28,16},{1,13},{... | collective-permute-start | bytes 208904 | tf_op jit(solution)/shard_map/ppermute | solution.py:270
  15.8 6.1 %collective-permute-start.5 = (f32[136,128]{1,0:T(8,128)S(1)}, f32[136,128]{1,0:T(8,128)S(1)}, u32[]{:S(2)}, u32[]{:S(2)}) collective-permute-start(f32[136,128]{1,0:T(8,128)S(1)} %get-tuple-element.23.refs_0_), channel_id=1, source_target_pairs={{0,4},{4,0},{8,12},{12,8},{16,20},{20,16},{24,28},{28,24},{1,5},{5... | collective-permute-start | bytes 208904 | tf_op jit(solution)/shard_map/ppermute | solution.py:270
  16.2 5.8 %collective-permute-start.2 = (f32[136,128]{1,0:T(8,128)S(1)}, f32[136,128]{1,0:T(8,128)S(1)}, u32[]{:S(2)}, u32[]{:S(2)}) collective-permute-start(f32[136,128]{1,0:T(8,128)S(1)} %get-tuple-element.23.refs_0_), channel_id=1, source_target_pairs={{0,8},{4,12},{8,0},{12,4},{16,24},{20,28},{24,16},{28,20},{1,9},{5... | collective-permute-start | bytes 208904 | tf_op jit(solution)/shard_map/ppermute | solution.py:270
  17.5 4.5 %collective-permute-start.8 = (f32[136,128]{1,0:T(8,128)S(1)}, f32[136,128]{1,0:T(8,128)S(1)}, u32[]{:S(2)}, u32[]{:S(2)}) collective-permute-start(f32[136,128]{1,0:T(8,128)S(1)} %collective-permute-done.4.refs_3_), channel_id=1, source_target_pairs={{0,4},{4,0},{8,12},{12,8},{16,20},{20,16},{24,28},{28,24},{1,5},{5... | collective-permute-start | bytes 208904 | tf_op jit(solution)/shard_map/ppermute | solution.py:270
  20.3 4.3 %collective-permute-start.7 = (f32[136,128]{1,0:T(8,128)S(1)}, f32[136,128]{1,0:T(8,128)S(1)}, u32[]{:S(2)}, u32[]{:S(2)}) collective-permute-start(f32[136,128]{1,0:T(8,128)S(1)} %collective-permute-done.3.refs_2_), channel_id=1, source_target_pairs={{0,4},{4,0},{8,12},{12,8},{16,20},{20,16},{24,28},{28,24},{1,5},{5... | collective-permute-start | bytes 208904 | tf_op jit(solution)/shard_map/ppermute | solution.py:270
  26.1 1.2 %collective-permute-start.9 = (f32[24,128]{1,0:T(8,128)S(1)}, f32[24,128]{1,0:T(8,128)S(1)}, u32[]{:S(2)}, u32[]{:S(2)}) collective-permute-start(f32[24,128]{1,0:T(8,128)S(1)} %get-tuple-element.28), channel_id=1, source_target_pairs={{0,1},{1,0},{2,3},{3,2},{4,5},{5,4},{6,7},{7,6},{8,9},{9,8},{10,11... | collective-permute-start | bytes 36872 | tf_op jit(solution)/shard_map/ppermute | solution.py:270
  27.3 3.1 %collective-permute-start.10 = (f32[24,128]{1,0:T(8,128)S(1)}, f32[24,128]{1,0:T(8,128)S(1)}, u32[]{:S(2)}, u32[]{:S(2)}) collective-permute-start(f32[24,128]{1,0:T(8,128)S(1)} %add.19.refs_0_), channel_id=1, source_target_pairs={{0,3},{1,2},{2,1},{3,0},{4,7},{5,6},{6,5},{7,4},{8,11},{9,10},{10,... | collective-permute-start | bytes 36872 | tf_op jit(solution)/shard_map/ppermute | solution.py:270
  31.1 7.0 %collective-permute-start.13 = (f32[136,128]{1,0:T(8,128)S(1)}, f32[136,128]{1,0:T(8,128)S(1)}, u32[]{:S(2)}, u32[]{:S(2)}) collective-permute-start(f32[136,128]{1,0:T(8,128)S(1)} %get-tuple-element.29.refs_0_), channel_id=1, source_target_pairs={{0,24},{4,28},{8,16},{12,20},{16,8},{20,12},{24,0},{28,4},{1,25},{... | collective-permute-start | bytes 208904 | tf_op jit(solution)/shard_map/ppermute | solution.py:270
  33.5 7.0 %collective-permute-start.12 = (f32[136,128]{1,0:T(8,128)S(1)}, f32[136,128]{1,0:T(8,128)S(1)}, u32[]{:S(2)}, u32[]{:S(2)}) collective-permute-start(f32[136,128]{1,0:T(8,128)S(1)} %get-tuple-element.29.refs_0_), channel_id=1, source_target_pairs={{0,16},{4,20},{8,24},{12,28},{16,0},{20,4},{24,8},{28,12},{1,17},{... | collective-permute-start | bytes 208904 | tf_op jit(solution)/shard_map/ppermute | solution.py:270
  33.7 8.0 %collective-permute-start.15 = (f32[136,128]{1,0:T(8,128)S(1)}, f32[136,128]{1,0:T(8,128)S(1)}, u32[]{:S(2)}, u32[]{:S(2)}) collective-permute-start(f32[136,128]{1,0:T(8,128)S(1)} %get-tuple-element.29.refs_0_), channel_id=1, source_target_pairs={{0,12},{4,8},{8,4},{12,0},{16,28},{20,24},{24,20},{28,16},{1,13},{... | collective-permute-start | bytes 208904 | tf_op jit(solution)/shard_map/ppermute | solution.py:270
  36.5 5.2 %collective-permute-start.14 = (f32[136,128]{1,0:T(8,128)S(1)}, f32[136,128]{1,0:T(8,128)S(1)}, u32[]{:S(2)}, u32[]{:S(2)}) collective-permute-start(f32[136,128]{1,0:T(8,128)S(1)} %get-tuple-element.29.refs_0_), channel_id=1, source_target_pairs={{0,4},{4,0},{8,12},{12,8},{16,20},{20,16},{24,28},{28,24},{1,5},{5... | collective-permute-start | bytes 208904 | tf_op jit(solution)/shard_map/ppermute | solution.py:270
  37.0 5.0 %collective-permute-start.11 = (f32[136,128]{1,0:T(8,128)S(1)}, f32[136,128]{1,0:T(8,128)S(1)}, u32[]{:S(2)}, u32[]{:S(2)}) collective-permute-start(f32[136,128]{1,0:T(8,128)S(1)} %get-tuple-element.29.refs_0_), channel_id=1, source_target_pairs={{0,8},{4,12},{8,0},{12,4},{16,24},{20,28},{24,16},{28,20},{1,9},{5... | collective-permute-start | bytes 208904 | tf_op jit(solution)/shard_map/ppermute | solution.py:270
  38.1 4.3 %collective-permute-start.17 = (f32[136,128]{1,0:T(8,128)S(1)}, f32[136,128]{1,0:T(8,128)S(1)}, u32[]{:S(2)}, u32[]{:S(2)}) collective-permute-start(f32[136,128]{1,0:T(8,128)S(1)} %collective-permute-done.13.refs_3_), channel_id=1, source_target_pairs={{0,4},{4,0},{8,12},{12,8},{16,20},{20,16},{24,28},{28,24},{1,5},{5... | collective-permute-start | bytes 208904 | tf_op jit(solution)/shard_map/ppermute | solution.py:270
  40.5 4.3 %collective-permute-start.16 = (f32[136,128]{1,0:T(8,128)S(1)}, f32[136,128]{1,0:T(8,128)S(1)}, u32[]{:S(2)}, u32[]{:S(2)}) collective-permute-start(f32[136,128]{1,0:T(8,128)S(1)} %collective-permute-done.12.refs_2_), channel_id=1, source_target_pairs={{0,4},{4,0},{8,12},{12,8},{16,20},{20,16},{24,28},{28,24},{1,5},{5... | collective-permute-start | bytes 208904 | tf_op jit(solution)/shard_map/ppermute | solution.py:270
  46.3 1.2 %collective-permute-start.18 = (f32[24,128]{1,0:T(8,128)S(1)}, f32[24,128]{1,0:T(8,128)S(1)}, u32[]{:S(2)}, u32[]{:S(2)}) collective-permute-start(f32[24,128]{1,0:T(8,128)S(1)} %get-tuple-element.33), channel_id=1, source_target_pairs={{0,1},{1,0},{2,3},{3,2},{4,5},{5,4},{6,7},{7,6},{8,9},{9,8},{10,11... | collective-permute-start | bytes 36872 | tf_op jit(solution)/shard_map/ppermute | solution.py:270
  47.5 3.1 %collective-permute-start.19 = (f32[24,128]{1,0:T(8,128)S(1)}, f32[24,128]{1,0:T(8,128)S(1)}, u32[]{:S(2)}, u32[]{:S(2)}) collective-permute-start(f32[24,128]{1,0:T(8,128)S(1)} %add.20.refs_0_), channel_id=1, source_target_pairs={{0,3},{1,2},{2,1},{3,0},{4,7},{5,6},{6,5},{7,4},{8,11},{9,10},{10,... | collective-permute-start | bytes 36872 | tf_op jit(solution)/shard_map/ppermute | solution.py:270
  50.8 4.9 %collective-permute-start.22 = (f32[8,128]{1,0:T(8,128)S(1)}, f32[8,128]{1,0:T(8,128)S(1)}, u32[]{:S(2)}, u32[]{:S(2)}) collective-permute-start(f32[8,128]{1,0:T(8,128)S(1)} %shard_map.73), channel_id=1, source_target_pairs={{0,25},{1,24},{2,27},{3,26},{4,29},{5,28},{6,31},{7,30},{8,17},{9,... | collective-permute-start | bytes 12296 | tf_op jit(solution)/shard_map/ppermute | solution.py:280
  52.6 3.9 %collective-permute-start.21 = (f32[8,128]{1,0:T(8,128)S(1)}, f32[8,128]{1,0:T(8,128)S(1)}, u32[]{:S(2)}, u32[]{:S(2)}) collective-permute-start(f32[8,128]{1,0:T(8,128)S(1)} %shard_map.73), channel_id=1, source_target_pairs={{0,17},{1,16},{2,19},{3,18},{4,21},{5,20},{6,23},{7,22},{8,25},{9,... | collective-permute-start | bytes 12296 | tf_op jit(solution)/shard_map/ppermute | solution.py:280
  52.6 3.9 %collective-permute-start.20 = (f32[8,128]{1,0:T(8,128)S(1)}, f32[8,128]{1,0:T(8,128)S(1)}, u32[]{:S(2)}, u32[]{:S(2)}) collective-permute-start(f32[8,128]{1,0:T(8,128)S(1)} %shard_map.73), channel_id=1, source_target_pairs={{0,9},{1,8},{2,11},{3,10},{4,13},{5,12},{6,15},{7,14},{8,1},{9,0},... | collective-permute-start | bytes 12296 | tf_op jit(solution)/shard_map/ppermute | solution.py:280
  56.6 3.1 %collective-permute-start.23 = (f32[8,128]{1,0:T(8,128)S(1)}, f32[8,128]{1,0:T(8,128)S(1)}, u32[]{:S(2)}, u32[]{:S(2)}) collective-permute-start(f32[8,128]{1,0:T(8,128)S(1)} %add_add_fusion.refs_0_), channel_id=1, source_target_pairs={{0,5},{1,4},{2,7},{3,6},{4,1},{5,0},{6,3},{7,2},{8,13},{9,12},{10,... | collective-permute-start | bytes 12296 | tf_op jit(solution)/shard_map/ppermute | solution.py:280

commit v6 on v5

--- a/solution.py
+++ b/solution.py
@@ -143,7 +143,7 @@
 
 
 def pick_sums(onehot, halves):
-    both = jnp.dot(onehot[...], halves[...], preferred_element_type=F32)
+    both = jnp.dot(onehot, halves[...], preferred_element_type=F32)
     width = both.shape[1] // 2
     return both[:, :width] + both[:, width:]
 
@@ -162,11 +162,10 @@
         onehot[:slots, place] = jnp.where(ids[...] == sent, 1.0, 0.0).astype(BF16)
         onehot[slots:, place] = jnp.where(blocks == sent, 1.0, 0.0).astype(BF16)
     stack_halves(parts, slots, halves)
-    summed = pick_sums(onehot, halves)
-    start_slot[...] = -(picked[...] + summed[:slots, :])
+    start_slot[...] = -(picked[...] + pick_sums(onehot[:slots, :], halves))
+    slope = own[...] + pick_sums(onehot[slots:, :], halves)
+    gradient[...] = slope
     forward_all(values, start_slot, payload)
-    slope = own[...] + summed[slots:, :]
-    gradient[...] = slope
     payload[tiles:, :] = scalar_rows(width, total(slope * slope))
 
 
@@ -198,13 +197,12 @@
     curve_now = read_scalar(scalars[0:1, :], 1)
     alpha = norm_now / (norm_now + curve_now)
     stack_halves(parts, slots, halves)
-    summed = pick_sums(onehot, halves)
     start = start_slot[...]
-    next_slot[...] = start - alpha * (start + summed[:slots, :])
+    next_slot[...] = start - alpha * (start + pick_sums(onehot[:slots, :], halves))
+    start_own = -gradient[...]
+    turned = start_own - alpha * (start_own + pick_sums(onehot[slots:, :], halves))
+    next_share[...] = turned
     forward_all(values, next_slot, payload)
-    start_own = -gradient[...]
-    turned = start_own - alpha * (start_own + summed[slots:, :])
-    next_share[...] = turned
     payload[tiles:, :] = scalar_rows(width, total(turned * turned), total(turned * start_own))
     known[...] = scalar_rows(width, norm_now, curve_now, alpha)
 
@@ -296,7 +294,7 @@
         gathered = lax.all_gather(array, "inst", axis=0)
         return [gathered[i] for i in range(size)]
     parts = {0: array}
-    for distance in (2, 4, 6, 1, 3):
+    for distance in (2, 6, 3, 1, 4):
         parts[distance] = swap(array, "inst", distance)
     for distance in (4, 6):
         parts[distance ^ 1] = swap(parts[distance], "inst", 1)

time: 60.6 us -> 61.7 us (1.018)
  starting transfers between devices: 30.5 us -> 33 us
  waiting for transfers between devices: 20.2 us -> 19.3 us
    ppermute x20, waiting for transfers between devices: 17.4 us -> 14.3 us  [swap(): return lax.ppermute(array, axis, [(i, i ^ distance) for i in range(size)])]
    ppermute x20, starting transfers between devices: 25.1 us -> 27.8 us  [swap(): return lax.ppermute(array, axis, [(i, i ^ distance) for i in range(size)])]
    ppermute x4, waiting for transfers between devices: 2.78 us -> 4.95 us  [swap_both(): return lax.ppermute(array, ('inst', 'feat'), pairs)]
  transfers between devices with their start and end apart: 24 -> 24, of which waited for: 18 -> 16; matrix products, arithmetic and copies ran while one was open for 1% -> 1% of each run, Pallas kernels for 0% -> 0%
where the time goes in v6:
time: 61.7 us; the launch traced here: 61.5 us
  starting transfers between devices  33 us (53%)
  waiting for transfers between devices  19.3 us (31%)
  Pallas kernels  7.23 us (12%)
  local copies, waits for them, and re-layouts  1.32 us (2%)
  between operations  0.71 us (1%)
    ppermute x20, starting transfers between devices, swap(): return lax.ppermute(array, axis, [(i, i ^ distance) for i in range(size)])  27.8 us
    ppermute x20, waiting for transfers between devices, swap(): return lax.ppermute(array, axis, [(i, i ^ distance) for i in range(size)])  14.3 us
    pallas_call x7, Pallas kernels, call(): pl.pallas_call(kernel, out_shape=out_shape, in_specs=in_specs, out_specs=...  7.23 us
    ppermute x4, starting transfers between devices, swap_both(): return lax.ppermute(array, ('inst', 'feat'), pairs)  5.15 us
    ppermute x4, waiting for transfers between devices, swap_both(): return lax.ppermute(array, ('inst', 'feat'), pairs)  4.95 us
    unnamed x4, local copies, waits for them, and re-layouts  1.32 us
  transfers between devices with their start and end apart: 24, of which 16 were waited for; matrix products, arithmetic and copies ran while one was open for 1% of the time, Pallas kernels for 0%

profile of v6, /device:TPU:0, one launch (start us, length us, event | category | flops | bytes accessed | tf_op | source)
XLA Modules:
  0.0 61.5 jit_solution(2822157475358819498)
XLA Ops:
  0.6 3.3 %shard_map.68 = (bf16[16,8,128,128]{3,2,1,0:T(8,128)(2,1)S(1)}, f32[128,128]{1,0:T(8,128)S(1)}, f32[128,128]{1,0:T(8,128)S(1)}, f32[256,128]{1,0:T(8,128)S(1)}, f32[16,128]{1,0:T(8,128)S(1)}) custom-call(s32[8,16]{1,0:T(8,128)} %bitcast.4, s32[1,16]{1,0:T(1,128)} %bitcast.5, f32[2048,128]{1,0:T(8,128)} %weights.1, bf16[16,8,128,128]{3,2,1,0:T(8,128)(2,1)} %values_in.1), custom_call_target="tpu_custom_call" | custom-call | tf_op jit(solution)/shard_map/pallas_call | solution.py:256
  5.3 2.6 %collective-permute-start.1 = (f32[16,128]{1,0:T(8,128)S(1)}, f32[16,128]{1,0:T(8,128)S(1)}, u32[]{:S(2)}, u32[]{:S(2)}) collective-permute-start(f32[16,128]{1,0:T(8,128)S(1)} %add.18.refs_0_), channel_id=1, source_target_pairs={{0,3},{1,2},{2,1},{3,0},{4,7},{5,6},{6,5},{7,4},{8,11},{9,10},{10,... | collective-permute-start | bytes 24584 | tf_op jit(solution)/shard_map/ppermute | solution.py:268
  7.9 1.4 %collective-permute-done.1.refs_1_ = f32[16,128]{1,0:T(8,128)S(1)} collective-permute-done((f32[16,128]{1,0:T(8,128)S(1)}, f32[16,128]{1,0:T(8,128)S(1)}, u32[]{:S(2)}, u32[]{:S(2)}) %collective-permute-start.1) | collective-permute-done | bytes 8224 | tf_op jit(solution)/shard_map/ppermute | solution.py:268
  9.9 3.1 %collective-permute-start.6 = (f32[136,128]{1,0:T(8,128)S(1)}, f32[136,128]{1,0:T(8,128)S(1)}, u32[]{:S(2)}, u32[]{:S(2)}) collective-permute-start(f32[136,128]{1,0:T(8,128)S(1)} %get-tuple-element.23.refs_0_), channel_id=1, source_target_pairs={{0,16},{4,20},{8,24},{12,28},{16,0},{20,4},{24,8},{28,12},{1,17},{... | collective-permute-start | bytes 208904 | tf_op jit(solution)/shard_map/ppermute | solution.py:268
  13.0 1.3 %collective-permute-start.3 = (f32[136,128]{1,0:T(8,128)S(1)}, f32[136,128]{1,0:T(8,128)S(1)}, u32[]{:S(2)}, u32[]{:S(2)}) collective-permute-start(f32[136,128]{1,0:T(8,128)S(1)} %get-tuple-element.23.refs_0_), channel_id=1, source_target_pairs={{0,24},{4,28},{8,16},{12,20},{16,8},{20,12},{24,0},{28,4},{1,25},{... | collective-permute-start | bytes 208904 | tf_op jit(solution)/shard_map/ppermute | solution.py:268
  14.4 1.5 %collective-permute-start.5 = (f32[136,128]{1,0:T(8,128)S(1)}, f32[136,128]{1,0:T(8,128)S(1)}, u32[]{:S(2)}, u32[]{:S(2)}) collective-permute-start(f32[136,128]{1,0:T(8,128)S(1)} %get-tuple-element.23.refs_0_), channel_id=1, source_target_pairs={{0,4},{4,0},{8,12},{12,8},{16,20},{20,16},{24,28},{28,24},{1,5},{5... | collective-permute-start | bytes 208904 | tf_op jit(solution)/shard_map/ppermute | solution.py:268
  16.1 1.8 %collective-permute-start.2 = (f32[136,128]{1,0:T(8,128)S(1)}, f32[136,128]{1,0:T(8,128)S(1)}, u32[]{:S(2)}, u32[]{:S(2)}) collective-permute-start(f32[136,128]{1,0:T(8,128)S(1)} %get-tuple-element.23.refs_0_), channel_id=1, source_target_pairs={{0,8},{4,12},{8,0},{12,4},{16,24},{20,28},{24,16},{28,20},{1,9},{5... | collective-permute-start | bytes 208904 | tf_op jit(solution)/shard_map/ppermute | solution.py:268
  17.9 2.0 %collective-permute-start.7 = (f32[136,128]{1,0:T(8,128)S(1)}, f32[136,128]{1,0:T(8,128)S(1)}, u32[]{:S(2)}, u32[]{:S(2)}) collective-permute-start(f32[136,128]{1,0:T(8,128)S(1)} %collective-permute-done.6.refs_5_), channel_id=1, source_target_pairs={{0,4},{4,0},{8,12},{12,8},{16,20},{20,16},{24,28},{28,24},{1,5},{5... | collective-permute-start | bytes 208904 | tf_op jit(solution)/shard_map/ppermute | solution.py:268
  19.8 1.1 %collective-permute-start.8 = (f32[136,128]{1,0:T(8,128)S(1)}, f32[136,128]{1,0:T(8,128)S(1)}, u32[]{:S(2)}, u32[]{:S(2)}) collective-permute-start(f32[136,128]{1,0:T(8,128)S(1)} %collective-permute-done.3.refs_2_), channel_id=1, source_target_pairs={{0,4},{4,0},{8,12},{12,8},{16,20},{20,16},{24,28},{28,24},{1,5},{5... | collective-permute-start | bytes 208904 | tf_op jit(solution)/shard_map/ppermute | solution.py:268
  21.0 1.0 %collective-permute-done.4.refs_3_ = f32[136,128]{1,0:T(8,128)S(1)} collective-permute-done((f32[136,128]{1,0:T(8,128)S(1)}, f32[136,128]{1,0:T(8,128)S(1)}, u32[]{:S(2)}, u32[]{:S(2)}) %collective-permute-start.4) | collective-permute-done | bytes 69664 | tf_op jit(solution)/shard_map/ppermute | solution.py:268
  22.0 1.0 %collective-permute-done.7.refs_6_ = f32[136,128]{1,0:T(8,128)S(1)} collective-permute-done((f32[136,128]{1,0:T(8,128)S(1)}, f32[136,128]{1,0:T(8,128)S(1)}, u32[]{:S(2)}, u32[]{:S(2)}) %collective-permute-start.7) | collective-permute-done | bytes 69664 | tf_op jit(solution)/shard_map/ppermute | solution.py:268
  22.9 1.2 %collective-permute-done.8.refs_7_ = f32[136,128]{1,0:T(8,128)S(1)} collective-permute-done((f32[136,128]{1,0:T(8,128)S(1)}, f32[136,128]{1,0:T(8,128)S(1)}, u32[]{:S(2)}, u32[]{:S(2)}) %collective-permute-start.8) | collective-permute-done | bytes 69664 | tf_op jit(solution)/shard_map/ppermute | solution.py:268
  24.2 1.2 %shard_map.70 = (f32[256,128]{1,0:T(8,128)S(1)}, f32[128,128]{1,0:T(8,128)S(1)}, bf16[384,1024]{1,0:T(8,128)(2,1)S(1)}, f32[24,128]{1,0:T(8,128)S(1)}) custom-call(bf16[16,8,128,128]{3,2,1,0:T(8,128)(2,1)S(1)} %get-tuple-element.18.values, f32[128,128]{1,0:T(8,128)S(1)} %get-tuple-element.19.ids, f32[128,128]{1,0:T(8,128)S(1)} %get-tuple-element.20.picked, ...), custom_call_target="tpu_custom_call" | custom-call | tf_op jit(solution)/shard_map/pallas_call | solution.py:256
  25.5 1.2 %collective-permute-done.9 = f32[24,128]{1,0:T(8,128)S(1)} collective-permute-done((f32[24,128]{1,0:T(8,128)S(1)}, f32[24,128]{1,0:T(8,128)S(1)}, u32[]{:S(2)}, u32[]{:S(2)}) %collective-permute-start.9) | collective-permute-done | bytes 12320 | tf_op jit(solution)/shard_map/ppermute | solution.py:268
  26.6 1.3 %collective-permute-start.10 = (f32[24,128]{1,0:T(8,128)S(1)}, f32[24,128]{1,0:T(8,128)S(1)}, u32[]{:S(2)}, u32[]{:S(2)}) collective-permute-start(f32[24,128]{1,0:T(8,128)S(1)} %add.19.refs_0_), channel_id=1, source_target_pairs={{0,3},{1,2},{2,1},{3,0},{4,7},{5,6},{6,5},{7,4},{8,11},{9,10},{10,... | collective-permute-start | bytes 36872 | tf_op jit(solution)/shard_map/ppermute | solution.py:268
  27.9 1.9 %collective-permute-done.10.refs_1_ = f32[24,128]{1,0:T(8,128)S(1)} collective-permute-done((f32[24,128]{1,0:T(8,128)S(1)}, f32[24,128]{1,0:T(8,128)S(1)}, u32[]{:S(2)}, u32[]{:S(2)}) %collective-permute-start.10) | collective-permute-done | bytes 12320 | tf_op jit(solution)/shard_map/ppermute | solution.py:268
  30.4 2.9 %collective-permute-start.15 = (f32[136,128]{1,0:T(8,128)S(1)}, f32[136,128]{1,0:T(8,128)S(1)}, u32[]{:S(2)}, u32[]{:S(2)}) collective-permute-start(f32[136,128]{1,0:T(8,128)S(1)} %get-tuple-element.29.refs_0_), channel_id=1, source_target_pairs={{0,16},{4,20},{8,24},{12,28},{16,0},{20,4},{24,8},{28,12},{1,17},{... | collective-permute-start | bytes 208904 | tf_op jit(solution)/shard_map/ppermute | solution.py:268
  33.3 1.1 %collective-permute-start.12 = (f32[136,128]{1,0:T(8,128)S(1)}, f32[136,128]{1,0:T(8,128)S(1)}, u32[]{:S(2)}, u32[]{:S(2)}) collective-permute-start(f32[136,128]{1,0:T(8,128)S(1)} %get-tuple-element.29.refs_0_), channel_id=1, source_target_pairs={{0,24},{4,28},{8,16},{12,20},{16,8},{20,12},{24,0},{28,4},{1,25},{... | collective-permute-start | bytes 208904 | tf_op jit(solution)/shard_map/ppermute | solution.py:268
  34.4 1.2 %collective-permute-start.14 = (f32[136,128]{1,0:T(8,128)S(1)}, f32[136,128]{1,0:T(8,128)S(1)}, u32[]{:S(2)}, u32[]{:S(2)}) collective-permute-start(f32[136,128]{1,0:T(8,128)S(1)} %get-tuple-element.29.refs_0_), channel_id=1, source_target_pairs={{0,4},{4,0},{8,12},{12,8},{16,20},{20,16},{24,28},{28,24},{1,5},{5... | collective-permute-start | bytes 208904 | tf_op jit(solution)/shard_map/ppermute | solution.py:268
  36.3 1.5 %collective-permute-start.11 = (f32[136,128]{1,0:T(8,128)S(1)}, f32[136,128]{1,0:T(8,128)S(1)}, u32[]{:S(2)}, u32[]{:S(2)}) collective-permute-start(f32[136,128]{1,0:T(8,128)S(1)} %get-tuple-element.29.refs_0_), channel_id=1, source_target_pairs={{0,8},{4,12},{8,0},{12,4},{16,24},{20,28},{24,16},{28,20},{1,9},{5... | collective-permute-start | bytes 208904 | tf_op jit(solution)/shard_map/ppermute | solution.py:268
  37.9 2.2 %collective-permute-start.16 = (f32[136,128]{1,0:T(8,128)S(1)}, f32[136,128]{1,0:T(8,128)S(1)}, u32[]{:S(2)}, u32[]{:S(2)}) collective-permute-start(f32[136,128]{1,0:T(8,128)S(1)} %collective-permute-done.15.refs_5_), channel_id=1, source_target_pairs={{0,4},{4,0},{8,12},{12,8},{16,20},{20,16},{24,28},{28,24},{1,5},{5... | collective-permute-start | bytes 208904 | tf_op jit(solution)/shard_map/ppermute | solution.py:268
  40.1 1.4 %collective-permute-start.17 = (f32[136,128]{1,0:T(8,128)S(1)}, f32[136,128]{1,0:T(8,128)S(1)}, u32[]{:S(2)}, u32[]{:S(2)}) collective-permute-start(f32[136,128]{1,0:T(8,128)S(1)} %collective-permute-done.12.refs_2_), channel_id=1, source_target_pairs={{0,4},{4,0},{8,12},{12,8},{16,20},{20,16},{24,28},{28,24},{1,5},{5... | collective-permute-start | bytes 208904 | tf_op jit(solution)/shard_map/ppermute | solution.py:268
  42.2 1.0 %collective-permute-done.16.refs_6_ = f32[136,128]{1,0:T(8,128)S(1)} collective-permute-done((f32[136,128]{1,0:T(8,128)S(1)}, f32[136,128]{1,0:T(8,128)S(1)}, u32[]{:S(2)}, u32[]{:S(2)}) %collective-permute-start.16) | collective-permute-done | bytes 69664 | tf_op jit(solution)/shard_map/ppermute | solution.py:268
  43.1 1.2 %collective-permute-done.17.refs_7_ = f32[136,128]{1,0:T(8,128)S(1)} collective-permute-done((f32[136,128]{1,0:T(8,128)S(1)}, f32[136,128]{1,0:T(8,128)S(1)}, u32[]{:S(2)}, u32[]{:S(2)}) %collective-permute-start.17) | collective-permute-done | bytes 69664 | tf_op jit(solution)/shard_map/ppermute | solution.py:268
  44.4 1.1 %shard_map.72 = (f32[256,128]{1,0:T(8,128)S(1)}, f32[8,128]{1,0:T(8,128)S(1)}, f32[24,128]{1,0:T(8,128)S(1)}) custom-call(bf16[16,8,128,128]{3,2,1,0:T(8,128)(2,1)S(1)} %get-tuple-element.18.values, bf16[384,1024]{1,0:T(8,128)(2,1)S(1)} %get-tuple-element.24.onehot, f32[128,128]{1,0:T(8,128)S(1)} %get-tuple-element.25.start_slot, ...), custom_call_target="tpu_custom_call" | custom-call | tf_op jit(solution)/shard_map/pallas_call | solution.py:256
  45.6 1.2 %collective-permute-done.18 = f32[24,128]{1,0:T(8,128)S(1)} collective-permute-done((f32[24,128]{1,0:T(8,128)S(1)}, f32[24,128]{1,0:T(8,128)S(1)}, u32[]{:S(2)}, u32[]{:S(2)}) %collective-permute-start.18) | collective-permute-done | bytes 12320 | tf_op jit(solution)/shard_map/ppermute | solution.py:268
  46.7 1.3 %collective-permute-start.19 = (f32[24,128]{1,0:T(8,128)S(1)}, f32[24,128]{1,0:T(8,128)S(1)}, u32[]{:S(2)}, u32[]{:S(2)}) collective-permute-start(f32[24,128]{1,0:T(8,128)S(1)} %add.20.refs_0_), channel_id=1, source_target_pairs={{0,3},{1,2},{2,1},{3,0},{4,7},{5,6},{6,5},{7,4},{8,11},{9,10},{10,... | collective-permute-start | bytes 36872 | tf_op jit(solution)/shard_map/ppermute | solution.py:268
  48.0 1.9 %collective-permute-done.19.refs_1_ = f32[24,128]{1,0:T(8,128)S(1)} collective-permute-done((f32[24,128]{1,0:T(8,128)S(1)}, f32[24,128]{1,0:T(8,128)S(1)}, u32[]{:S(2)}, u32[]{:S(2)}) %collective-permute-start.19) | collective-permute-done | bytes 12320 | tf_op jit(solution)/shard_map/ppermute | solution.py:268
  50.0 3.7 %collective-permute-start.22 = (f32[8,128]{1,0:T(8,128)S(1)}, f32[8,128]{1,0:T(8,128)S(1)}, u32[]{:S(2)}, u32[]{:S(2)}) collective-permute-start(f32[8,128]{1,0:T(8,128)S(1)} %shard_map.73), channel_id=1, source_target_pairs={{0,25},{1,24},{2,27},{3,26},{4,29},{5,28},{6,31},{7,30},{8,17},{9,... | collective-permute-start | bytes 12296 | tf_op jit(solution)/shard_map/ppermute | solution.py:278
  55.0 2.6 %collective-permute-done.21 = f32[8,128]{1,0:T(8,128)S(1)} collective-permute-done((f32[8,128]{1,0:T(8,128)S(1)}, f32[8,128]{1,0:T(8,128)S(1)}, u32[]{:S(2)}, u32[]{:S(2)}) %collective-permute-start.21) | collective-permute-done | bytes 4128 | tf_op jit(solution)/shard_map/ppermute | solution.py:278
  57.6 0.8 %collective-permute-start.23 = (f32[8,128]{1,0:T(8,128)S(1)}, f32[8,128]{1,0:T(8,128)S(1)}, u32[]{:S(2)}, u32[]{:S(2)}) collective-permute-start(f32[8,128]{1,0:T(8,128)S(1)} %add_add_fusion.refs_0_), channel_id=1, source_target_pairs={{0,5},{1,4},{2,7},{3,6},{4,1},{5,0},{6,3},{7,2},{8,13},{9,12},{10,... | collective-permute-start | bytes 12296 | tf_op jit(solution)/shard_map/ppermute | solution.py:278
  59.1 1.6 %collective-permute-done.23.refs_1_ = f32[8,128]{1,0:T(8,128)S(1)} collective-permute-done((f32[8,128]{1,0:T(8,128)S(1)}, f32[8,128]{1,0:T(8,128)S(1)}, u32[]{:S(2)}, u32[]{:S(2)}) %collective-permute-start.23) | collective-permute-done | bytes 4128 | tf_op jit(solution)/shard_map/ppermute | solution.py:278
  (31 shorter events, 7.2 us)
Async XLA Ops:
  0.6 8.7 %copy-start = (s32[2048]{0:T(1024)S(1)}, s32[2048]{0:T(1024)}, u32[]{:S(2)}) copy-start(s32[2048]{0:T(1024)} %param.8) | copy-start | bytes 24580
  4.0 1.3 %collective-permute-start = (f32[16,128]{1,0:T(8,128)S(1)}, f32[16,128]{1,0:T(8,128)S(1)}, u32[]{:S(2)}, u32[]{:S(2)}) collective-permute-start(f32[16,128]{1,0:T(8,128)S(1)} %get-tuple-element.22), channel_id=1, source_target_pairs={{0,1},{1,0},{2,3},{3,2},{4,5},{5,4},{6,7},{7,6},{8,9},{9,8},{10,11... | collective-permute-start | bytes 24584 | tf_op jit(solution)/shard_map/ppermute | solution.py:268
  5.3 4.0 %collective-permute-start.1 = (f32[16,128]{1,0:T(8,128)S(1)}, f32[16,128]{1,0:T(8,128)S(1)}, u32[]{:S(2)}, u32[]{:S(2)}) collective-permute-start(f32[16,128]{1,0:T(8,128)S(1)} %add.18.refs_0_), channel_id=1, source_target_pairs={{0,3},{1,2},{2,1},{3,0},{4,7},{5,6},{6,5},{7,4},{8,11},{9,10},{10,... | collective-permute-start | bytes 24584 | tf_op jit(solution)/shard_map/ppermute | solution.py:268
  9.9 7.9 %collective-permute-start.6 = (f32[136,128]{1,0:T(8,128)S(1)}, f32[136,128]{1,0:T(8,128)S(1)}, u32[]{:S(2)}, u32[]{:S(2)}) collective-permute-start(f32[136,128]{1,0:T(8,128)S(1)} %get-tuple-element.23.refs_0_), channel_id=1, source_target_pairs={{0,16},{4,20},{8,24},{12,28},{16,0},{20,4},{24,8},{28,12},{1,17},{... | collective-permute-start | bytes 208904 | tf_op jit(solution)/shard_map/ppermute | solution.py:268
  13.0 6.8 %collective-permute-start.3 = (f32[136,128]{1,0:T(8,128)S(1)}, f32[136,128]{1,0:T(8,128)S(1)}, u32[]{:S(2)}, u32[]{:S(2)}) collective-permute-start(f32[136,128]{1,0:T(8,128)S(1)} %get-tuple-element.23.refs_0_), channel_id=1, source_target_pairs={{0,24},{4,28},{8,16},{12,20},{16,8},{20,12},{24,0},{28,4},{1,25},{... | collective-permute-start | bytes 208904 | tf_op jit(solution)/shard_map/ppermute | solution.py:268
  14.4 6.6 %collective-permute-start.5 = (f32[136,128]{1,0:T(8,128)S(1)}, f32[136,128]{1,0:T(8,128)S(1)}, u32[]{:S(2)}, u32[]{:S(2)}) collective-permute-start(f32[136,128]{1,0:T(8,128)S(1)} %get-tuple-element.23.refs_0_), channel_id=1, source_target_pairs={{0,4},{4,0},{8,12},{12,8},{16,20},{20,16},{24,28},{28,24},{1,5},{5... | collective-permute-start | bytes 208904 | tf_op jit(solution)/shard_map/ppermute | solution.py:268
  15.9 6.0 %collective-permute-start.4 = (f32[136,128]{1,0:T(8,128)S(1)}, f32[136,128]{1,0:T(8,128)S(1)}, u32[]{:S(2)}, u32[]{:S(2)}) collective-permute-start(f32[136,128]{1,0:T(8,128)S(1)} %get-tuple-element.23.refs_0_), channel_id=1, source_target_pairs={{0,12},{4,8},{8,4},{12,0},{16,28},{20,24},{24,20},{28,16},{1,13},{... | collective-permute-start | bytes 208904 | tf_op jit(solution)/shard_map/ppermute | solution.py:268
  16.1 5.9 %collective-permute-start.2 = (f32[136,128]{1,0:T(8,128)S(1)}, f32[136,128]{1,0:T(8,128)S(1)}, u32[]{:S(2)}, u32[]{:S(2)}) collective-permute-start(f32[136,128]{1,0:T(8,128)S(1)} %get-tuple-element.23.refs_0_), channel_id=1, source_target_pairs={{0,8},{4,12},{8,0},{12,4},{16,24},{20,28},{24,16},{28,20},{1,9},{5... | collective-permute-start | bytes 208904 | tf_op jit(solution)/shard_map/ppermute | solution.py:268
  17.9 5.1 %collective-permute-start.7 = (f32[136,128]{1,0:T(8,128)S(1)}, f32[136,128]{1,0:T(8,128)S(1)}, u32[]{:S(2)}, u32[]{:S(2)}) collective-permute-start(f32[136,128]{1,0:T(8,128)S(1)} %collective-permute-done.6.refs_5_), channel_id=1, source_target_pairs={{0,4},{4,0},{8,12},{12,8},{16,20},{20,16},{24,28},{28,24},{1,5},{5... | collective-permute-start | bytes 208904 | tf_op jit(solution)/shard_map/ppermute | solution.py:268
  19.8 4.3 %collective-permute-start.8 = (f32[136,128]{1,0:T(8,128)S(1)}, f32[136,128]{1,0:T(8,128)S(1)}, u32[]{:S(2)}, u32[]{:S(2)}) collective-permute-start(f32[136,128]{1,0:T(8,128)S(1)} %collective-permute-done.3.refs_2_), channel_id=1, source_target_pairs={{0,4},{4,0},{8,12},{12,8},{16,20},{20,16},{24,28},{28,24},{1,5},{5... | collective-permute-start | bytes 208904 | tf_op jit(solution)/shard_map/ppermute | solution.py:268
  25.4 1.2 %collective-permute-start.9 = (f32[24,128]{1,0:T(8,128)S(1)}, f32[24,128]{1,0:T(8,128)S(1)}, u32[]{:S(2)}, u32[]{:S(2)}) collective-permute-start(f32[24,128]{1,0:T(8,128)S(1)} %get-tuple-element.28), channel_id=1, source_target_pairs={{0,1},{1,0},{2,3},{3,2},{4,5},{5,4},{6,7},{7,6},{8,9},{9,8},{10,11... | collective-permute-start | bytes 36872 | tf_op jit(solution)/shard_map/ppermute | solution.py:268
  26.6 3.1 %collective-permute-start.10 = (f32[24,128]{1,0:T(8,128)S(1)}, f32[24,128]{1,0:T(8,128)S(1)}, u32[]{:S(2)}, u32[]{:S(2)}) collective-permute-start(f32[24,128]{1,0:T(8,128)S(1)} %add.19.refs_0_), channel_id=1, source_target_pairs={{0,3},{1,2},{2,1},{3,0},{4,7},{5,6},{6,5},{7,4},{8,11},{9,10},{10,... | collective-permute-start | bytes 36872 | tf_op jit(solution)/shard_map/ppermute | solution.py:268
  30.4 7.5 %collective-permute-start.15 = (f32[136,128]{1,0:T(8,128)S(1)}, f32[136,128]{1,0:T(8,128)S(1)}, u32[]{:S(2)}, u32[]{:S(2)}) collective-permute-start(f32[136,128]{1,0:T(8,128)S(1)} %get-tuple-element.29.refs_0_), channel_id=1, source_target_pairs={{0,16},{4,20},{8,24},{12,28},{16,0},{20,4},{24,8},{28,12},{1,17},{... | collective-permute-start | bytes 208904 | tf_op jit(solution)/shard_map/ppermute | solution.py:268
  33.3 6.8 %collective-permute-start.12 = (f32[136,128]{1,0:T(8,128)S(1)}, f32[136,128]{1,0:T(8,128)S(1)}, u32[]{:S(2)}, u32[]{:S(2)}) collective-permute-start(f32[136,128]{1,0:T(8,128)S(1)} %get-tuple-element.29.refs_0_), channel_id=1, source_target_pairs={{0,24},{4,28},{8,16},{12,20},{16,8},{20,12},{24,0},{28,4},{1,25},{... | collective-permute-start | bytes 208904 | tf_op jit(solution)/shard_map/ppermute | solution.py:268
  34.4 7.1 %collective-permute-start.14 = (f32[136,128]{1,0:T(8,128)S(1)}, f32[136,128]{1,0:T(8,128)S(1)}, u32[]{:S(2)}, u32[]{:S(2)}) collective-permute-start(f32[136,128]{1,0:T(8,128)S(1)} %get-tuple-element.29.refs_0_), channel_id=1, source_target_pairs={{0,4},{4,0},{8,12},{12,8},{16,20},{20,16},{24,28},{28,24},{1,5},{5... | collective-permute-start | bytes 208904 | tf_op jit(solution)/shard_map/ppermute | solution.py:268
  35.6 6.4 %collective-permute-start.13 = (f32[136,128]{1,0:T(8,128)S(1)}, f32[136,128]{1,0:T(8,128)S(1)}, u32[]{:S(2)}, u32[]{:S(2)}) collective-permute-start(f32[136,128]{1,0:T(8,128)S(1)} %get-tuple-element.29.refs_0_), channel_id=1, source_target_pairs={{0,12},{4,8},{8,4},{12,0},{16,28},{20,24},{24,20},{28,16},{1,13},{... | collective-permute-start | bytes 208904 | tf_op jit(solution)/shard_map/ppermute | solution.py:268
  36.3 5.8 %collective-permute-start.11 = (f32[136,128]{1,0:T(8,128)S(1)}, f32[136,128]{1,0:T(8,128)S(1)}, u32[]{:S(2)}, u32[]{:S(2)}) collective-permute-start(f32[136,128]{1,0:T(8,128)S(1)} %get-tuple-element.29.refs_0_), channel_id=1, source_target_pairs={{0,8},{4,12},{8,0},{12,4},{16,24},{20,28},{24,16},{28,20},{1,9},{5... | collective-permute-start | bytes 208904 | tf_op jit(solution)/shard_map/ppermute | solution.py:268
  37.9 5.3 %collective-permute-start.16 = (f32[136,128]{1,0:T(8,128)S(1)}, f32[136,128]{1,0:T(8,128)S(1)}, u32[]{:S(2)}, u32[]{:S(2)}) collective-permute-start(f32[136,128]{1,0:T(8,128)S(1)} %collective-permute-done.15.refs_5_), channel_id=1, source_target_pairs={{0,4},{4,0},{8,12},{12,8},{16,20},{20,16},{24,28},{28,24},{1,5},{5... | collective-permute-start | bytes 208904 | tf_op jit(solution)/shard_map/ppermute | solution.py:268
  40.1 4.3 %collective-permute-start.17 = (f32[136,128]{1,0:T(8,128)S(1)}, f32[136,128]{1,0:T(8,128)S(1)}, u32[]{:S(2)}, u32[]{:S(2)}) collective-permute-start(f32[136,128]{1,0:T(8,128)S(1)} %collective-permute-done.12.refs_2_), channel_id=1, source_target_pairs={{0,4},{4,0},{8,12},{12,8},{16,20},{20,16},{24,28},{28,24},{1,5},{5... | collective-permute-start | bytes 208904 | tf_op jit(solution)/shard_map/ppermute | solution.py:268
  45.5 1.2 %collective-permute-start.18 = (f32[24,128]{1,0:T(8,128)S(1)}, f32[24,128]{1,0:T(8,128)S(1)}, u32[]{:S(2)}, u32[]{:S(2)}) collective-permute-start(f32[24,128]{1,0:T(8,128)S(1)} %get-tuple-element.33), channel_id=1, source_target_pairs={{0,1},{1,0},{2,3},{3,2},{4,5},{5,4},{6,7},{7,6},{8,9},{9,8},{10,11... | collective-permute-start | bytes 36872 | tf_op jit(solution)/shard_map/ppermute | solution.py:268
  46.7 3.1 %collective-permute-start.19 = (f32[24,128]{1,0:T(8,128)S(1)}, f32[24,128]{1,0:T(8,128)S(1)}, u32[]{:S(2)}, u32[]{:S(2)}) collective-permute-start(f32[24,128]{1,0:T(8,128)S(1)} %add.20.refs_0_), channel_id=1, source_target_pairs={{0,3},{1,2},{2,1},{3,0},{4,7},{5,6},{6,5},{7,4},{8,11},{9,10},{10,... | collective-permute-start | bytes 36872 | tf_op jit(solution)/shard_map/ppermute | solution.py:268
  50.0 5.1 %collective-permute-start.22 = (f32[8,128]{1,0:T(8,128)S(1)}, f32[8,128]{1,0:T(8,128)S(1)}, u32[]{:S(2)}, u32[]{:S(2)}) collective-permute-start(f32[8,128]{1,0:T(8,128)S(1)} %shard_map.73), channel_id=1, source_target_pairs={{0,25},{1,24},{2,27},{3,26},{4,29},{5,28},{6,31},{7,30},{8,17},{9,... | collective-permute-start | bytes 12296 | tf_op jit(solution)/shard_map/ppermute | solution.py:278
  53.7 3.9 %collective-permute-start.21 = (f32[8,128]{1,0:T(8,128)S(1)}, f32[8,128]{1,0:T(8,128)S(1)}, u32[]{:S(2)}, u32[]{:S(2)}) collective-permute-start(f32[8,128]{1,0:T(8,128)S(1)} %shard_map.73), channel_id=1, source_target_pairs={{0,17},{1,16},{2,19},{3,18},{4,21},{5,20},{6,23},{7,22},{8,25},{9,... | collective-permute-start | bytes 12296 | tf_op jit(solution)/shard_map/ppermute | solution.py:278
  53.7 3.9 %collective-permute-start.20 = (f32[8,128]{1,0:T(8,128)S(1)}, f32[8,128]{1,0:T(8,128)S(1)}, u32[]{:S(2)}, u32[]{:S(2)}) collective-permute-start(f32[8,128]{1,0:T(8,128)S(1)} %shard_map.73), channel_id=1, source_target_pairs={{0,9},{1,8},{2,11},{3,10},{4,13},{5,12},{6,15},{7,14},{8,1},{9,0},... | collective-permute-start | bytes 12296 | tf_op jit(solution)/shard_map/ppermute | solution.py:278
  57.6 3.1 %collective-permute-start.23 = (f32[8,128]{1,0:T(8,128)S(1)}, f32[8,128]{1,0:T(8,128)S(1)}, u32[]{:S(2)}, u32[]{:S(2)}) collective-permute-start(f32[8,128]{1,0:T(8,128)S(1)} %add_add_fusion.refs_0_), channel_id=1, source_target_pairs={{0,5},{1,4},{2,7},{3,6},{4,1},{5,0},{6,3},{7,2},{8,13},{9,12},{10,... | collective-permute-start | bytes 12296 | tf_op jit(solution)/shard_map/ppermute | solution.py:278

commit v7 on v6

--- a/solution.py
+++ b/solution.py
@@ -294,7 +294,7 @@
         gathered = lax.all_gather(array, "inst", axis=0)
         return [gathered[i] for i in range(size)]
     parts = {0: array}
-    for distance in (2, 6, 3, 1, 4):
+    for distance in (2, 4, 6, 1, 3):
         parts[distance] = swap(array, "inst", distance)
     for distance in (4, 6):
         parts[distance ^ 1] = swap(parts[distance], "inst", 1)
@@ -303,7 +303,7 @@
 
 def inst_sum_parts(array):
     size = lax.axis_size("inst")
-    stages = [(2, 4, 6), (1,)] if size == 8 else [(1 << b,) for b in range(size.bit_length() - 1)]
+    stages = [(1, 2, 3), (4,)] if size == 8 else [(1 << b,) for b in range(size.bit_length() - 1)]
     parts = [array]
     for stage in stages:
         array = sum(parts[1:], parts[0])

time: 61.7 us -> 60.6 us (0.982)
  starting transfers between devices: 33 us -> 29.1 us
  waiting for transfers between devices: 19.3 us -> 22.1 us
    ppermute x20, waiting for transfers between devices: 14.3 us -> 17.4 us  [swap(): return lax.ppermute(array, axis, [(i, i ^ distance) for i in range(size)])]
    ppermute x20, starting transfers between devices: 27.8 us -> 25 us  [swap(): return lax.ppermute(array, axis, [(i, i ^ distance) for i in range(size)])]
    ppermute x4, starting transfers between devices: 5.15 us -> 4.02 us  [swap_both(): return lax.ppermute(array, ('inst', 'feat'), pairs)]
  transfers between devices with their start and end apart: 24 -> 24, of which waited for: 16 -> 18; matrix products, arithmetic and copies ran while one was open for 1% -> 1% of each run, Pallas kernels for 0% -> 0%
where the time goes in v7:
time: 60.6 us; the launch traced here: 60.4 us
  starting transfers between devices  29.1 us (48%)
  waiting for transfers between devices  22.1 us (36%)
  Pallas kernels  7.24 us (12%)
  local copies, waits for them, and re-layouts  1.32 us (2%)
  between operations  0.7 us (1%)
    ppermute x20, starting transfers between devices, swap(): return lax.ppermute(array, axis, [(i, i ^ distance) for i in range(size)])  25 us
    ppermute x20, waiting for transfers between devices, swap(): return lax.ppermute(array, axis, [(i, i ^ distance) for i in range(size)])  17.4 us
    pallas_call x7, Pallas kernels, call(): pl.pallas_call(kernel, out_shape=out_shape, in_specs=in_specs, out_specs=...  7.24 us
    ppermute x4, waiting for transfers between devices, swap_both(): return lax.ppermute(array, ('inst', 'feat'), pairs)  4.7 us
    ppermute x4, starting transfers between devices, swap_both(): return lax.ppermute(array, ('inst', 'feat'), pairs)  4.02 us
    unnamed x4, local copies, waits for them, and re-layouts  1.32 us
  transfers between devices with their start and end apart: 24, of which 18 were waited for; matrix products, arithmetic and copies ran while one was open for 1% of the time, Pallas kernels for 0%

profile of v7, /device:TPU:0, one launch (start us, length us, event | category | flops | bytes accessed | tf_op | source)
XLA Modules:
  0.0 60.4 jit_solution(13525214423240274838)
XLA Ops:
  0.6 3.3 %shard_map.68 = (bf16[16,8,128,128]{3,2,1,0:T(8,128)(2,1)S(1)}, f32[128,128]{1,0:T(8,128)S(1)}, f32[128,128]{1,0:T(8,128)S(1)}, f32[256,128]{1,0:T(8,128)S(1)}, f32[16,128]{1,0:T(8,128)S(1)}) custom-call(s32[8,16]{1,0:T(8,128)} %bitcast.4, s32[1,16]{1,0:T(1,128)} %bitcast.5, f32[2048,128]{1,0:T(8,128)} %weights.1, bf16[16,8,128,128]{3,2,1,0:T(8,128)(2,1)} %values_in.1), custom_call_target="tpu_custom_call" | custom-call | tf_op jit(solution)/shard_map/pallas_call | solution.py:256
  4.5 0.8 %collective-permute-done = f32[16,128]{1,0:T(8,128)S(1)} collective-permute-done((f32[16,128]{1,0:T(8,128)S(1)}, f32[16,128]{1,0:T(8,128)S(1)}, u32[]{:S(2)}, u32[]{:S(2)}) %collective-permute-start) | collective-permute-done | bytes 8224 | tf_op jit(solution)/shard_map/ppermute | solution.py:268
  5.3 2.6 %collective-permute-start.1 = (f32[16,128]{1,0:T(8,128)S(1)}, f32[16,128]{1,0:T(8,128)S(1)}, u32[]{:S(2)}, u32[]{:S(2)}) collective-permute-start(f32[16,128]{1,0:T(8,128)S(1)} %add.18.refs_0_), channel_id=1, source_target_pairs={{0,3},{1,2},{2,1},{3,0},{4,7},{5,6},{6,5},{7,4},{8,11},{9,10},{10,... | collective-permute-start | bytes 24584 | tf_op jit(solution)/shard_map/ppermute | solution.py:268
  7.9 1.4 %collective-permute-done.1.refs_1_ = f32[16,128]{1,0:T(8,128)S(1)} collective-permute-done((f32[16,128]{1,0:T(8,128)S(1)}, f32[16,128]{1,0:T(8,128)S(1)}, u32[]{:S(2)}, u32[]{:S(2)}) %collective-permute-start.1) | collective-permute-done | bytes 8224 | tf_op jit(solution)/shard_map/ppermute | solution.py:268
  9.9 4.1 %collective-permute-start.4 = (f32[136,128]{1,0:T(8,128)S(1)}, f32[136,128]{1,0:T(8,128)S(1)}, u32[]{:S(2)}, u32[]{:S(2)}) collective-permute-start(f32[136,128]{1,0:T(8,128)S(1)} %get-tuple-element.23.refs_0_), channel_id=1, source_target_pairs={{0,24},{4,28},{8,16},{12,20},{16,8},{20,12},{24,0},{28,4},{1,25},{... | collective-permute-start | bytes 208904 | tf_op jit(solution)/shard_map/ppermute | solution.py:268
  14.1 1.7 %collective-permute-start.6 = (f32[136,128]{1,0:T(8,128)S(1)}, f32[136,128]{1,0:T(8,128)S(1)}, u32[]{:S(2)}, u32[]{:S(2)}) collective-permute-start(f32[136,128]{1,0:T(8,128)S(1)} %get-tuple-element.23.refs_0_), channel_id=1, source_target_pairs={{0,12},{4,8},{8,4},{12,0},{16,28},{20,24},{24,20},{28,16},{1,13},{... | collective-permute-start | bytes 208904 | tf_op jit(solution)/shard_map/ppermute | solution.py:268
  16.2 1.4 %collective-permute-start.2 = (f32[136,128]{1,0:T(8,128)S(1)}, f32[136,128]{1,0:T(8,128)S(1)}, u32[]{:S(2)}, u32[]{:S(2)}) collective-permute-start(f32[136,128]{1,0:T(8,128)S(1)} %get-tuple-element.23.refs_0_), channel_id=1, source_target_pairs={{0,8},{4,12},{8,0},{12,4},{16,24},{20,28},{24,16},{28,20},{1,9},{5... | collective-permute-start | bytes 208904 | tf_op jit(solution)/shard_map/ppermute | solution.py:268
  17.5 1.5 %collective-permute-start.8 = (f32[136,128]{1,0:T(8,128)S(1)}, f32[136,128]{1,0:T(8,128)S(1)}, u32[]{:S(2)}, u32[]{:S(2)}) collective-permute-start(f32[136,128]{1,0:T(8,128)S(1)} %collective-permute-done.4.refs_3_), channel_id=1, source_target_pairs={{0,4},{4,0},{8,12},{12,8},{16,20},{20,16},{24,28},{28,24},{1,5},{5... | collective-permute-start | bytes 208904 | tf_op jit(solution)/shard_map/ppermute | solution.py:268
  19.1 1.3 %collective-permute-done.3.refs_2_ = f32[136,128]{1,0:T(8,128)S(1)} collective-permute-done((f32[136,128]{1,0:T(8,128)S(1)}, f32[136,128]{1,0:T(8,128)S(1)}, u32[]{:S(2)}, u32[]{:S(2)}) %collective-permute-start.3) | collective-permute-done | bytes 69664 | tf_op jit(solution)/shard_map/ppermute | solution.py:268
  20.3 1.5 %collective-permute-start.7 = (f32[136,128]{1,0:T(8,128)S(1)}, f32[136,128]{1,0:T(8,128)S(1)}, u32[]{:S(2)}, u32[]{:S(2)}) collective-permute-start(f32[136,128]{1,0:T(8,128)S(1)} %collective-permute-done.3.refs_2_), channel_id=1, source_target_pairs={{0,4},{4,0},{8,12},{12,8},{16,20},{20,16},{24,28},{28,24},{1,5},{5... | collective-permute-start | bytes 208904 | tf_op jit(solution)/shard_map/ppermute | solution.py:268
  22.1 2.6 %collective-permute-done.7.refs_6_ = f32[136,128]{1,0:T(8,128)S(1)} collective-permute-done((f32[136,128]{1,0:T(8,128)S(1)}, f32[136,128]{1,0:T(8,128)S(1)}, u32[]{:S(2)}, u32[]{:S(2)}) %collective-permute-start.7) | collective-permute-done | bytes 69664 | tf_op jit(solution)/shard_map/ppermute | solution.py:268
  24.7 1.2 %shard_map.70 = (f32[256,128]{1,0:T(8,128)S(1)}, f32[128,128]{1,0:T(8,128)S(1)}, bf16[384,1024]{1,0:T(8,128)(2,1)S(1)}, f32[24,128]{1,0:T(8,128)S(1)}) custom-call(bf16[16,8,128,128]{3,2,1,0:T(8,128)(2,1)S(1)} %get-tuple-element.18.values, f32[128,128]{1,0:T(8,128)S(1)} %get-tuple-element.19.ids, f32[128,128]{1,0:T(8,128)S(1)} %get-tuple-element.20.picked, ...), custom_call_target="tpu_custom_call" | custom-call | tf_op jit(solution)/shard_map/pallas_call | solution.py:256
  26.0 1.2 %collective-permute-done.9 = f32[24,128]{1,0:T(8,128)S(1)} collective-permute-done((f32[24,128]{1,0:T(8,128)S(1)}, f32[24,128]{1,0:T(8,128)S(1)}, u32[]{:S(2)}, u32[]{:S(2)}) %collective-permute-start.9) | collective-permute-done | bytes 12320 | tf_op jit(solution)/shard_map/ppermute | solution.py:268
  27.1 1.3 %collective-permute-start.10 = (f32[24,128]{1,0:T(8,128)S(1)}, f32[24,128]{1,0:T(8,128)S(1)}, u32[]{:S(2)}, u32[]{:S(2)}) collective-permute-start(f32[24,128]{1,0:T(8,128)S(1)} %add.19.refs_0_), channel_id=1, source_target_pairs={{0,3},{1,2},{2,1},{3,0},{4,7},{5,6},{6,5},{7,4},{8,11},{9,10},{10,... | collective-permute-start | bytes 36872 | tf_op jit(solution)/shard_map/ppermute | solution.py:268
  28.4 1.9 %collective-permute-done.10.refs_1_ = f32[24,128]{1,0:T(8,128)S(1)} collective-permute-done((f32[24,128]{1,0:T(8,128)S(1)}, f32[24,128]{1,0:T(8,128)S(1)}, u32[]{:S(2)}, u32[]{:S(2)}) %collective-permute-start.10) | collective-permute-done | bytes 12320 | tf_op jit(solution)/shard_map/ppermute | solution.py:268
  30.2 0.7 %shard_map.71 = (f32[16,128]{1,0:T(8,128)S(1)}, f32[136,128]{1,0:T(8,128)S(1)}) custom-call(bf16[16,8,128,128]{3,2,1,0:T(8,128)(2,1)S(1)} %get-tuple-element.18.values, f32[128,128]{1,0:T(8,128)S(1)} %get-tuple-element.19.ids, f32[16,128]{1,0:T(8,128)S(1)} %get-tuple-element.27.curvature, f32[24,128]{1,0:T(8,128)S(1)} %add.19.refs_0_, ...), custom_call_target="tpu_custom_call" | custom-call | tf_op jit(solution)/shard_map/pallas_call | solution.py:256
  30.9 2.4 %collective-permute-start.13 = (f32[136,128]{1,0:T(8,128)S(1)}, f32[136,128]{1,0:T(8,128)S(1)}, u32[]{:S(2)}, u32[]{:S(2)}) collective-permute-start(f32[136,128]{1,0:T(8,128)S(1)} %get-tuple-element.29.refs_0_), channel_id=1, source_target_pairs={{0,24},{4,28},{8,16},{12,20},{16,8},{20,12},{24,0},{28,4},{1,25},{... | collective-permute-start | bytes 208904 | tf_op jit(solution)/shard_map/ppermute | solution.py:268
  33.5 2.8 %collective-permute-start.15 = (f32[136,128]{1,0:T(8,128)S(1)}, f32[136,128]{1,0:T(8,128)S(1)}, u32[]{:S(2)}, u32[]{:S(2)}) collective-permute-start(f32[136,128]{1,0:T(8,128)S(1)} %get-tuple-element.29.refs_0_), channel_id=1, source_target_pairs={{0,12},{4,8},{8,4},{12,0},{16,28},{20,24},{24,20},{28,16},{1,13},{... | collective-permute-start | bytes 208904 | tf_op jit(solution)/shard_map/ppermute | solution.py:268
  37.0 1.0 %collective-permute-done.13.refs_3_ = f32[136,128]{1,0:T(8,128)S(1)} collective-permute-done((f32[136,128]{1,0:T(8,128)S(1)}, f32[136,128]{1,0:T(8,128)S(1)}, u32[]{:S(2)}, u32[]{:S(2)}) %collective-permute-start.13) | collective-permute-done | bytes 69664 | tf_op jit(solution)/shard_map/ppermute | solution.py:268
  37.9 1.4 %collective-permute-start.17 = (f32[136,128]{1,0:T(8,128)S(1)}, f32[136,128]{1,0:T(8,128)S(1)}, u32[]{:S(2)}, u32[]{:S(2)}) collective-permute-start(f32[136,128]{1,0:T(8,128)S(1)} %collective-permute-done.13.refs_3_), channel_id=1, source_target_pairs={{0,4},{4,0},{8,12},{12,8},{16,20},{20,16},{24,28},{28,24},{1,5},{5... | collective-permute-start | bytes 208904 | tf_op jit(solution)/shard_map/ppermute | solution.py:268
  39.4 1.0 %collective-permute-done.12.refs_2_ = f32[136,128]{1,0:T(8,128)S(1)} collective-permute-done((f32[136,128]{1,0:T(8,128)S(1)}, f32[136,128]{1,0:T(8,128)S(1)}, u32[]{:S(2)}, u32[]{:S(2)}) %collective-permute-start.12) | collective-permute-done | bytes 69664 | tf_op jit(solution)/shard_map/ppermute | solution.py:268
  40.3 1.2 %collective-permute-start.16 = (f32[136,128]{1,0:T(8,128)S(1)}, f32[136,128]{1,0:T(8,128)S(1)}, u32[]{:S(2)}, u32[]{:S(2)}) collective-permute-start(f32[136,128]{1,0:T(8,128)S(1)} %collective-permute-done.12.refs_2_), channel_id=1, source_target_pairs={{0,4},{4,0},{8,12},{12,8},{16,20},{20,16},{24,28},{28,24},{1,5},{5... | collective-permute-start | bytes 208904 | tf_op jit(solution)/shard_map/ppermute | solution.py:268
  42.3 2.4 %collective-permute-done.16.refs_6_ = f32[136,128]{1,0:T(8,128)S(1)} collective-permute-done((f32[136,128]{1,0:T(8,128)S(1)}, f32[136,128]{1,0:T(8,128)S(1)}, u32[]{:S(2)}, u32[]{:S(2)}) %collective-permute-start.16) | collective-permute-done | bytes 69664 | tf_op jit(solution)/shard_map/ppermute | solution.py:268
  44.7 1.1 %shard_map.72 = (f32[256,128]{1,0:T(8,128)S(1)}, f32[8,128]{1,0:T(8,128)S(1)}, f32[24,128]{1,0:T(8,128)S(1)}) custom-call(bf16[16,8,128,128]{3,2,1,0:T(8,128)(2,1)S(1)} %get-tuple-element.18.values, bf16[384,1024]{1,0:T(8,128)(2,1)S(1)} %get-tuple-element.24.onehot, f32[128,128]{1,0:T(8,128)S(1)} %get-tuple-element.25.start_slot, ...), custom_call_target="tpu_custom_call" | custom-call | tf_op jit(solution)/shard_map/pallas_call | solution.py:256
  45.9 1.2 %collective-permute-done.18 = f32[24,128]{1,0:T(8,128)S(1)} collective-permute-done((f32[24,128]{1,0:T(8,128)S(1)}, f32[24,128]{1,0:T(8,128)S(1)}, u32[]{:S(2)}, u32[]{:S(2)}) %collective-permute-start.18) | collective-permute-done | bytes 12320 | tf_op jit(solution)/shard_map/ppermute | solution.py:268
  47.0 1.3 %collective-permute-start.19 = (f32[24,128]{1,0:T(8,128)S(1)}, f32[24,128]{1,0:T(8,128)S(1)}, u32[]{:S(2)}, u32[]{:S(2)}) collective-permute-start(f32[24,128]{1,0:T(8,128)S(1)} %add.20.refs_0_), channel_id=1, source_target_pairs={{0,3},{1,2},{2,1},{3,0},{4,7},{5,6},{6,5},{7,4},{8,11},{9,10},{10,... | collective-permute-start | bytes 36872 | tf_op jit(solution)/shard_map/ppermute | solution.py:268
  48.3 1.9 %collective-permute-done.19.refs_1_ = f32[24,128]{1,0:T(8,128)S(1)} collective-permute-done((f32[24,128]{1,0:T(8,128)S(1)}, f32[24,128]{1,0:T(8,128)S(1)}, u32[]{:S(2)}, u32[]{:S(2)}) %collective-permute-start.19) | collective-permute-done | bytes 12320 | tf_op jit(solution)/shard_map/ppermute | solution.py:268
  50.7 2.0 %collective-permute-start.21 = (f32[8,128]{1,0:T(8,128)S(1)}, f32[8,128]{1,0:T(8,128)S(1)}, u32[]{:S(2)}, u32[]{:S(2)}) collective-permute-start(f32[8,128]{1,0:T(8,128)S(1)} %shard_map.73), channel_id=1, source_target_pairs={{0,9},{1,8},{2,11},{3,10},{4,13},{5,12},{6,15},{7,14},{8,1},{9,0},... | collective-permute-start | bytes 12296 | tf_op jit(solution)/shard_map/ppermute | solution.py:278
  53.3 1.0 %collective-permute-done.22 = f32[8,128]{1,0:T(8,128)S(1)} collective-permute-done((f32[8,128]{1,0:T(8,128)S(1)}, f32[8,128]{1,0:T(8,128)S(1)}, u32[]{:S(2)}, u32[]{:S(2)}) %collective-permute-start.22) | collective-permute-done | bytes 4128 | tf_op jit(solution)/shard_map/ppermute | solution.py:278
  54.3 1.4 %collective-permute-done.20 = f32[8,128]{1,0:T(8,128)S(1)} collective-permute-done((f32[8,128]{1,0:T(8,128)S(1)}, f32[8,128]{1,0:T(8,128)S(1)}, u32[]{:S(2)}, u32[]{:S(2)}) %collective-permute-start.20) | collective-permute-done | bytes 4128 | tf_op jit(solution)/shard_map/ppermute | solution.py:278
  55.7 1.0 %collective-permute-start.23 = (f32[8,128]{1,0:T(8,128)S(1)}, f32[8,128]{1,0:T(8,128)S(1)}, u32[]{:S(2)}, u32[]{:S(2)}) collective-permute-start(f32[8,128]{1,0:T(8,128)S(1)} %add_add_fusion.refs_0_), channel_id=1, source_target_pairs={{0,17},{1,16},{2,19},{3,18},{4,21},{5,20},{6,23},{7,22},{8,25},{9,... | collective-permute-start | bytes 12296 | tf_op jit(solution)/shard_map/ppermute | solution.py:278
  57.4 2.3 %collective-permute-done.23.refs_1_ = f32[8,128]{1,0:T(8,128)S(1)} collective-permute-done((f32[8,128]{1,0:T(8,128)S(1)}, f32[8,128]{1,0:T(8,128)S(1)}, u32[]{:S(2)}, u32[]{:S(2)}) %collective-permute-start.23) | collective-permute-done | bytes 4128 | tf_op jit(solution)/shard_map/ppermute | solution.py:278
  (31 shorter events, 6.0 us)
Async XLA Ops:
  0.6 8.7 %copy-start = (s32[2048]{0:T(1024)S(1)}, s32[2048]{0:T(1024)}, u32[]{:S(2)}) copy-start(s32[2048]{0:T(1024)} %param.8) | copy-start | bytes 24580
  4.0 1.3 %collective-permute-start = (f32[16,128]{1,0:T(8,128)S(1)}, f32[16,128]{1,0:T(8,128)S(1)}, u32[]{:S(2)}, u32[]{:S(2)}) collective-permute-start(f32[16,128]{1,0:T(8,128)S(1)} %get-tuple-element.22), channel_id=1, source_target_pairs={{0,1},{1,0},{2,3},{3,2},{4,5},{5,4},{6,7},{7,6},{8,9},{9,8},{10,11... | collective-permute-start | bytes 24584 | tf_op jit(solution)/shard_map/ppermute | solution.py:268
  5.3 4.0 %collective-permute-start.1 = (f32[16,128]{1,0:T(8,128)S(1)}, f32[16,128]{1,0:T(8,128)S(1)}, u32[]{:S(2)}, u32[]{:S(2)}) collective-permute-start(f32[16,128]{1,0:T(8,128)S(1)} %add.18.refs_0_), channel_id=1, source_target_pairs={{0,3},{1,2},{2,1},{3,0},{4,7},{5,6},{6,5},{7,4},{8,11},{9,10},{10,... | collective-permute-start | bytes 24584 | tf_op jit(solution)/shard_map/ppermute | solution.py:268
  9.9 7.6 %collective-permute-start.4 = (f32[136,128]{1,0:T(8,128)S(1)}, f32[136,128]{1,0:T(8,128)S(1)}, u32[]{:S(2)}, u32[]{:S(2)}) collective-permute-start(f32[136,128]{1,0:T(8,128)S(1)} %get-tuple-element.23.refs_0_), channel_id=1, source_target_pairs={{0,24},{4,28},{8,16},{12,20},{16,8},{20,12},{24,0},{28,4},{1,25},{... | collective-permute-start | bytes 208904 | tf_op jit(solution)/shard_map/ppermute | solution.py:268
  14.0 6.3 %collective-permute-start.3 = (f32[136,128]{1,0:T(8,128)S(1)}, f32[136,128]{1,0:T(8,128)S(1)}, u32[]{:S(2)}, u32[]{:S(2)}) collective-permute-start(f32[136,128]{1,0:T(8,128)S(1)} %get-tuple-element.23.refs_0_), channel_id=1, source_target_pairs={{0,16},{4,20},{8,24},{12,28},{16,0},{20,4},{24,8},{28,12},{1,17},{... | collective-permute-start | bytes 208904 | tf_op jit(solution)/shard_map/ppermute | solution.py:268
  14.1 7.8 %collective-permute-start.6 = (f32[136,128]{1,0:T(8,128)S(1)}, f32[136,128]{1,0:T(8,128)S(1)}, u32[]{:S(2)}, u32[]{:S(2)}) collective-permute-start(f32[136,128]{1,0:T(8,128)S(1)} %get-tuple-element.23.refs_0_), channel_id=1, source_target_pairs={{0,12},{4,8},{8,4},{12,0},{16,28},{20,24},{24,20},{28,16},{1,13},{... | collective-permute-start | bytes 208904 | tf_op jit(solution)/shard_map/ppermute | solution.py:268
  15.8 6.1 %collective-permute-start.5 = (f32[136,128]{1,0:T(8,128)S(1)}, f32[136,128]{1,0:T(8,128)S(1)}, u32[]{:S(2)}, u32[]{:S(2)}) collective-permute-start(f32[136,128]{1,0:T(8,128)S(1)} %get-tuple-element.23.refs_0_), channel_id=1, source_target_pairs={{0,4},{4,0},{8,12},{12,8},{16,20},{20,16},{24,28},{28,24},{1,5},{5... | collective-permute-start | bytes 208904 | tf_op jit(solution)/shard_map/ppermute | solution.py:268
  16.2 5.8 %collective-permute-start.2 = (f32[136,128]{1,0:T(8,128)S(1)}, f32[136,128]{1,0:T(8,128)S(1)}, u32[]{:S(2)}, u32[]{:S(2)}) collective-permute-start(f32[136,128]{1,0:T(8,128)S(1)} %get-tuple-element.23.refs_0_), channel_id=1, source_target_pairs={{0,8},{4,12},{8,0},{12,4},{16,24},{20,28},{24,16},{28,20},{1,9},{5... | collective-permute-start | bytes 208904 | tf_op jit(solution)/shard_map/ppermute | solution.py:268
  17.5 4.5 %collective-permute-start.8 = (f32[136,128]{1,0:T(8,128)S(1)}, f32[136,128]{1,0:T(8,128)S(1)}, u32[]{:S(2)}, u32[]{:S(2)}) collective-permute-start(f32[136,128]{1,0:T(8,128)S(1)} %collective-permute-done.4.refs_3_), channel_id=1, source_target_pairs={{0,4},{4,0},{8,12},{12,8},{16,20},{20,16},{24,28},{28,24},{1,5},{5... | collective-permute-start | bytes 208904 | tf_op jit(solution)/shard_map/ppermute | solution.py:268
  20.3 4.3 %collective-permute-start.7 = (f32[136,128]{1,0:T(8,128)S(1)}, f32[136,128]{1,0:T(8,128)S(1)}, u32[]{:S(2)}, u32[]{:S(2)}) collective-permute-start(f32[136,128]{1,0:T(8,128)S(1)} %collective-permute-done.3.refs_2_), channel_id=1, source_target_pairs={{0,4},{4,0},{8,12},{12,8},{16,20},{20,16},{24,28},{28,24},{1,5},{5... | collective-permute-start | bytes 208904 | tf_op jit(solution)/shard_map/ppermute | solution.py:268
  25.9 1.2 %collective-permute-start.9 = (f32[24,128]{1,0:T(8,128)S(1)}, f32[24,128]{1,0:T(8,128)S(1)}, u32[]{:S(2)}, u32[]{:S(2)}) collective-permute-start(f32[24,128]{1,0:T(8,128)S(1)} %get-tuple-element.28), channel_id=1, source_target_pairs={{0,1},{1,0},{2,3},{3,2},{4,5},{5,4},{6,7},{7,6},{8,9},{9,8},{10,11... | collective-permute-start | bytes 36872 | tf_op jit(solution)/shard_map/ppermute | solution.py:268
  27.1 3.1 %collective-permute-start.10 = (f32[24,128]{1,0:T(8,128)S(1)}, f32[24,128]{1,0:T(8,128)S(1)}, u32[]{:S(2)}, u32[]{:S(2)}) collective-permute-start(f32[24,128]{1,0:T(8,128)S(1)} %add.19.refs_0_), channel_id=1, source_target_pairs={{0,3},{1,2},{2,1},{3,0},{4,7},{5,6},{6,5},{7,4},{8,11},{9,10},{10,... | collective-permute-start | bytes 36872 | tf_op jit(solution)/shard_map/ppermute | solution.py:268
  30.9 7.0 %collective-permute-start.13 = (f32[136,128]{1,0:T(8,128)S(1)}, f32[136,128]{1,0:T(8,128)S(1)}, u32[]{:S(2)}, u32[]{:S(2)}) collective-permute-start(f32[136,128]{1,0:T(8,128)S(1)} %get-tuple-element.29.refs_0_), channel_id=1, source_target_pairs={{0,24},{4,28},{8,16},{12,20},{16,8},{20,12},{24,0},{28,4},{1,25},{... | collective-permute-start | bytes 208904 | tf_op jit(solution)/shard_map/ppermute | solution.py:268
  33.3 7.0 %collective-permute-start.12 = (f32[136,128]{1,0:T(8,128)S(1)}, f32[136,128]{1,0:T(8,128)S(1)}, u32[]{:S(2)}, u32[]{:S(2)}) collective-permute-start(f32[136,128]{1,0:T(8,128)S(1)} %get-tuple-element.29.refs_0_), channel_id=1, source_target_pairs={{0,16},{4,20},{8,24},{12,28},{16,0},{20,4},{24,8},{28,12},{1,17},{... | collective-permute-start | bytes 208904 | tf_op jit(solution)/shard_map/ppermute | solution.py:268
  33.5 8.0 %collective-permute-start.15 = (f32[136,128]{1,0:T(8,128)S(1)}, f32[136,128]{1,0:T(8,128)S(1)}, u32[]{:S(2)}, u32[]{:S(2)}) collective-permute-start(f32[136,128]{1,0:T(8,128)S(1)} %get-tuple-element.29.refs_0_), channel_id=1, source_target_pairs={{0,12},{4,8},{8,4},{12,0},{16,28},{20,24},{24,20},{28,16},{1,13},{... | collective-permute-start | bytes 208904 | tf_op jit(solution)/shard_map/ppermute | solution.py:268
  36.3 5.2 %collective-permute-start.14 = (f32[136,128]{1,0:T(8,128)S(1)}, f32[136,128]{1,0:T(8,128)S(1)}, u32[]{:S(2)}, u32[]{:S(2)}) collective-permute-start(f32[136,128]{1,0:T(8,128)S(1)} %get-tuple-element.29.refs_0_), channel_id=1, source_target_pairs={{0,4},{4,0},{8,12},{12,8},{16,20},{20,16},{24,28},{28,24},{1,5},{5... | collective-permute-start | bytes 208904 | tf_op jit(solution)/shard_map/ppermute | solution.py:268
  36.8 5.0 %collective-permute-start.11 = (f32[136,128]{1,0:T(8,128)S(1)}, f32[136,128]{1,0:T(8,128)S(1)}, u32[]{:S(2)}, u32[]{:S(2)}) collective-permute-start(f32[136,128]{1,0:T(8,128)S(1)} %get-tuple-element.29.refs_0_), channel_id=1, source_target_pairs={{0,8},{4,12},{8,0},{12,4},{16,24},{20,28},{24,16},{28,20},{1,9},{5... | collective-permute-start | bytes 208904 | tf_op jit(solution)/shard_map/ppermute | solution.py:268
  37.9 4.3 %collective-permute-start.17 = (f32[136,128]{1,0:T(8,128)S(1)}, f32[136,128]{1,0:T(8,128)S(1)}, u32[]{:S(2)}, u32[]{:S(2)}) collective-permute-start(f32[136,128]{1,0:T(8,128)S(1)} %collective-permute-done.13.refs_3_), channel_id=1, source_target_pairs={{0,4},{4,0},{8,12},{12,8},{16,20},{20,16},{24,28},{28,24},{1,5},{5... | collective-permute-start | bytes 208904 | tf_op jit(solution)/shard_map/ppermute | solution.py:268
  40.3 4.3 %collective-permute-start.16 = (f32[136,128]{1,0:T(8,128)S(1)}, f32[136,128]{1,0:T(8,128)S(1)}, u32[]{:S(2)}, u32[]{:S(2)}) collective-permute-start(f32[136,128]{1,0:T(8,128)S(1)} %collective-permute-done.12.refs_2_), channel_id=1, source_target_pairs={{0,4},{4,0},{8,12},{12,8},{16,20},{20,16},{24,28},{28,24},{1,5},{5... | collective-permute-start | bytes 208904 | tf_op jit(solution)/shard_map/ppermute | solution.py:268
  45.8 1.2 %collective-permute-start.18 = (f32[24,128]{1,0:T(8,128)S(1)}, f32[24,128]{1,0:T(8,128)S(1)}, u32[]{:S(2)}, u32[]{:S(2)}) collective-permute-start(f32[24,128]{1,0:T(8,128)S(1)} %get-tuple-element.33), channel_id=1, source_target_pairs={{0,1},{1,0},{2,3},{3,2},{4,5},{5,4},{6,7},{7,6},{8,9},{9,8},{10,11... | collective-permute-start | bytes 36872 | tf_op jit(solution)/shard_map/ppermute | solution.py:268
  47.0 3.1 %collective-permute-start.19 = (f32[24,128]{1,0:T(8,128)S(1)}, f32[24,128]{1,0:T(8,128)S(1)}, u32[]{:S(2)}, u32[]{:S(2)}) collective-permute-start(f32[24,128]{1,0:T(8,128)S(1)} %add.20.refs_0_), channel_id=1, source_target_pairs={{0,3},{1,2},{2,1},{3,0},{4,7},{5,6},{6,5},{7,4},{8,11},{9,10},{10,... | collective-permute-start | bytes 36872 | tf_op jit(solution)/shard_map/ppermute | solution.py:268
  50.3 4.0 %collective-permute-start.22 = (f32[8,128]{1,0:T(8,128)S(1)}, f32[8,128]{1,0:T(8,128)S(1)}, u32[]{:S(2)}, u32[]{:S(2)}) collective-permute-start(f32[8,128]{1,0:T(8,128)S(1)} %shard_map.73), channel_id=1, source_target_pairs={{0,13},{1,12},{2,15},{3,14},{4,9},{5,8},{6,11},{7,10},{8,5},{9,4},... | collective-permute-start | bytes 12296 | tf_op jit(solution)/shard_map/ppermute | solution.py:278
  50.7 3.6 %collective-permute-start.21 = (f32[8,128]{1,0:T(8,128)S(1)}, f32[8,128]{1,0:T(8,128)S(1)}, u32[]{:S(2)}, u32[]{:S(2)}) collective-permute-start(f32[8,128]{1,0:T(8,128)S(1)} %shard_map.73), channel_id=1, source_target_pairs={{0,9},{1,8},{2,11},{3,10},{4,13},{5,12},{6,15},{7,14},{8,1},{9,0},... | collective-permute-start | bytes 12296 | tf_op jit(solution)/shard_map/ppermute | solution.py:278
  52.7 3.0 %collective-permute-start.20 = (f32[8,128]{1,0:T(8,128)S(1)}, f32[8,128]{1,0:T(8,128)S(1)}, u32[]{:S(2)}, u32[]{:S(2)}) collective-permute-start(f32[8,128]{1,0:T(8,128)S(1)} %shard_map.73), channel_id=1, source_target_pairs={{0,5},{1,4},{2,7},{3,6},{4,1},{5,0},{6,3},{7,2},{8,13},{9,12},{10,... | collective-permute-start | bytes 12296 | tf_op jit(solution)/shard_map/ppermute | solution.py:278
  55.7 3.9 %collective-permute-start.23 = (f32[8,128]{1,0:T(8,128)S(1)}, f32[8,128]{1,0:T(8,128)S(1)}, u32[]{:S(2)}, u32[]{:S(2)}) collective-permute-start(f32[8,128]{1,0:T(8,128)S(1)} %add_add_fusion.refs_0_), channel_id=1, source_target_pairs={{0,17},{1,16},{2,19},{3,18},{4,21},{5,20},{6,23},{7,22},{8,25},{9,... | collective-permute-start | bytes 12296 | tf_op jit(solution)/shard_map/ppermute | solution.py:278

commit v8 on v7

--- a/solution.py
+++ b/solution.py
@@ -148,12 +148,8 @@
     return both[:, :width] + both[:, width:]
 
 
-def start_kernel(count, values, ids, picked, own, *refs):
-    parts = refs[:count]
-    gradient, start_slot, onehot, payload, halves = refs[count:]
-    tiles = values.shape[0]
+def fill_onehot(ids, share, parts, onehot):
     slots, width = ids.shape
-    share = own.shape[0]
     offset = lax.axis_index("inst") * share
     blocks = (row_iota((share, width)) + offset).astype(F32)
     for k, part in enumerate(parts):
@@ -161,9 +157,24 @@
         place = slice(k * slots, (k + 1) * slots)
         onehot[:slots, place] = jnp.where(ids[...] == sent, 1.0, 0.0).astype(BF16)
         onehot[slots:, place] = jnp.where(blocks == sent, 1.0, 0.0).astype(BF16)
+
+
+def start_early_kernel(count, share, ids, *refs):
+    parts, (onehot, sums, halves) = refs[:count], refs[count:]
+    fill_onehot(ids, share, parts, onehot)
+    stack_halves(parts, ids.shape[0], halves)
+    sums[...] = pick_sums(onehot[...], halves)
+
+
+def start_kernel(count, values, ids, picked, own, early, *refs):
+    parts = refs[:count]
+    gradient, start_slot, onehot, payload, halves = refs[count:]
+    tiles = values.shape[0]
+    slots, width = ids.shape
+    fill_onehot(ids, own.shape[0], parts, onehot)
     stack_halves(parts, slots, halves)
-    start_slot[...] = -(picked[...] + pick_sums(onehot[:slots, :], halves))
-    slope = own[...] + pick_sums(onehot[slots:, :], halves)
+    start_slot[...] = -(picked[...] + early[:slots, :] + pick_sums(onehot[:slots, :], halves))
+    slope = own[...] + early[slots:, :] + pick_sums(onehot[slots:, :], halves)
     gradient[...] = slope
     forward_all(values, start_slot, payload)
     payload[tiles:, :] = scalar_rows(width, total(slope * slope))
@@ -185,22 +196,32 @@
     payload[slots:, :] = scalar_rows(width, norm_part, total(rounded * here))
 
 
-def turn_kernel(count, values, onehot, start_slot, gradient, *refs):
+def turn_early_kernel(count, onehot, *refs):
+    parts, (sums, scalars, halves) = refs[:count], refs[count:]
+    slots = parts[0].shape[0] - SUB
+    stack_halves(parts, slots, halves)
+    sums[...] = pick_sums(onehot[...], halves)
+    scalars[...] = sum((part[slots:, :] for part in parts[1:]), parts[0][slots:, :])
+
+
+def turn_kernel(count, values, onehot, start_slot, gradient, early, early_scalars, *refs):
     parts = refs[:count]
     next_share, known, payload, halves, next_slot = refs[count:]
     tiles = values.shape[0]
     slots, width = start_slot.shape
-    scalars = parts[0][slots:, :]
-    for part in parts[1:]:
+    scalars = early_scalars[...]
+    for part in parts:
         scalars = scalars + part[slots:, :]
     norm_now = read_scalar(scalars[0:1, :], 0)
     curve_now = read_scalar(scalars[0:1, :], 1)
     alpha = norm_now / (norm_now + curve_now)
     stack_halves(parts, slots, halves)
     start = start_slot[...]
-    next_slot[...] = start - alpha * (start + pick_sums(onehot[:slots, :], halves))
+    summed = early[:slots, :] + pick_sums(onehot[:slots, :], halves)
+    next_slot[...] = start - alpha * (start + summed)
     start_own = -gradient[...]
-    turned = start_own - alpha * (start_own + pick_sums(onehot[slots:, :], halves))
+    summed = early[slots:, :] + pick_sums(onehot[slots:, :], halves)
+    turned = start_own - alpha * (start_own + summed)
     next_share[...] = turned
     forward_all(values, next_slot, payload)
     payload[tiles:, :] = scalar_rows(width, total(turned * turned), total(turned * start_own))
@@ -303,7 +324,7 @@
 
 def inst_sum_parts(array):
     size = lax.axis_size("inst")
-    stages = [(1, 2, 3), (4,)] if size == 8 else [(1 << b,) for b in range(size.bit_length() - 1)]
+    stages = [(2, 4, 6), (1,)] if size == 8 else [(1 << b,) for b in range(size.bit_length() - 1)]
     parts = [array]
     for stage in stages:
         array = sum(parts[1:], parts[0])
@@ -344,28 +365,48 @@
         (near((slots + SUB, width)), near((tiles, rows))),
         (labels.reshape(tiles, rows), values_here, ids, *feat_parts(part)),
     )
-    halves = pltpu.VMEM((insts * slots, 2 * width), BF16)
+    late = 2
+    early = insts - late
+    wanted = slots + share
+
+    def halves(count):
+        return pltpu.VMEM((count * slots, 2 * width), BF16)
+
+    parts = inst_parts(payload)
+    onehot_early, sums = call(
+        functools.partial(start_early_kernel, early, share),
+        (near((wanted, early * slots), BF16), near((wanted, width))),
+        (ids, *parts[:early]),
+        scratch_shapes=[halves(early)],
+    )
     gradient, start_slot, onehot, payload = call(
-        functools.partial(start_kernel, insts),
+        functools.partial(start_kernel, late),
         (
             near((share, width)),
             near((slots, width)),
-            near((slots + share, insts * slots), BF16),
+            near((wanted, late * slots), BF16),
             near((tiles + SUB, rows)),
         ),
-        (values_here, ids, picked, own, *inst_parts(payload)),
-        scratch_shapes=[halves],
+        (values_here, ids, picked, own, sums, *parts[early:]),
+        scratch_shapes=[halves(late)],
     )
     along, payload = call(
         functools.partial(curve_kernel, pair),
         (near((tiles, rows)), near((slots + SUB, width))),
         (values_here, ids, curvature, *feat_parts(payload)),
     )
+    parts = inst_parts(payload)
+    sums, scalars = call(
+        functools.partial(turn_early_kernel, early),
+        (near((wanted, width)), near((SUB, width))),
+        (onehot_early, *parts[:early]),
+        scratch_shapes=[halves(early)],
+    )
     next_share, known, payload = call(
-        functools.partial(turn_kernel, insts),
+        functools.partial(turn_kernel, late),
         (near((share, width)), near((SUB, width)), near((tiles + SUB, rows))),
-        (values_here, onehot, start_slot, gradient, *inst_parts(payload)),
-        scratch_shapes=[halves, pltpu.VMEM((slots, width), F32)],
+        (values_here, onehot, start_slot, gradient, sums, scalars, *parts[early:]),
+        scratch_shapes=[halves(late), pltpu.VMEM((slots, width), F32)],
     )
     scalars = call(
         functools.partial(inner_kernel, pair),

time: 60.6 us -> 61.6 us (1.017)
  starting transfers between devices: 29.1 us -> 33.1 us
  waiting for transfers between devices: 22.1 us -> 18.8 us
    ppermute x20, waiting for transfers between devices: 17.4 us -> 14 us  [swap(): return lax.ppermute(array, axis, [(i, i ^ distance) for i in range(size)])]
    ppermute x20, starting transfers between devices: 25 us -> 27.7 us  [swap(): return lax.ppermute(array, axis, [(i, i ^ distance) for i in range(size)])]
    ppermute x4, starting transfers between devices: 4.02 us -> 5.39 us  [swap_both(): return lax.ppermute(array, ('inst', 'feat'), pairs)]
    pallas_call x7 -> x9, Pallas kernels: 7.24 us -> 7.58 us  [call(): pl.pallas_call(kernel, out_shape=out_shape, in_specs=in_specs, out_specs=...]
  transfers between devices with their start and end apart: 24 -> 24, of which waited for: 18 -> 16; matrix products, arithmetic and copies ran while one was open for 1% -> 1% of each run, Pallas kernels for 0% -> 1%
where the time goes in v8:
time: 61.6 us; the launch traced here: 61.5 us
  starting transfers between devices  33.1 us (54%)
  waiting for transfers between devices  18.8 us (31%)
  Pallas kernels  7.58 us (12%)
  local copies, waits for them, and re-layouts  1.32 us (2%)
  between operations  0.72 us (1%)
    ppermute x20, starting transfers between devices, swap(): return lax.ppermute(array, axis, [(i, i ^ distance) for i in range(size)])  27.7 us
    ppermute x20, waiting for transfers between devices, swap(): return lax.ppermute(array, axis, [(i, i ^ distance) for i in range(size)])  14 us
    pallas_call x9, Pallas kernels, call(): pl.pallas_call(kernel, out_shape=out_shape, in_specs=in_specs, out_specs=...  7.58 us
    ppermute x4, starting transfers between devices, swap_both(): return lax.ppermute(array, ('inst', 'feat'), pairs)  5.39 us
    ppermute x4, waiting for transfers between devices, swap_both(): return lax.ppermute(array, ('inst', 'feat'), pairs)  4.77 us
    unnamed x4, local copies, waits for them, and re-layouts  1.32 us
  transfers between devices with their start and end apart: 24, of which 16 were waited for; matrix products, arithmetic and copies ran while one was open for 1% of the time, Pallas kernels for 1%

profile of v8, /device:TPU:0, one launch (start us, length us, event | category | flops | bytes accessed | tf_op | source)
XLA Modules:
  0.0 61.5 jit_solution(15647000932640793026)
XLA Ops:
  0.6 3.3 %shard_map.68 = (bf16[16,8,128,128]{3,2,1,0:T(8,128)(2,1)S(1)}, f32[128,128]{1,0:T(8,128)S(1)}, f32[128,128]{1,0:T(8,128)S(1)}, f32[256,128]{1,0:T(8,128)S(1)}, f32[16,128]{1,0:T(8,128)S(1)}) custom-call(s32[8,16]{1,0:T(8,128)} %bitcast.4, s32[1,16]{1,0:T(1,128)} %bitcast.5, f32[2048,128]{1,0:T(8,128)} %weights.1, bf16[16,8,128,128]{3,2,1,0:T(8,128)(2,1)} %values_in.1), custom_call_target="tpu_custom_call" | custom-call | tf_op jit(solution)/shard_map/pallas_call | solution.py:277
  4.5 0.8 %collective-permute-done = f32[16,128]{1,0:T(8,128)S(1)} collective-permute-done((f32[16,128]{1,0:T(8,128)S(1)}, f32[16,128]{1,0:T(8,128)S(1)}, u32[]{:S(2)}, u32[]{:S(2)}) %collective-permute-start) | collective-permute-done | bytes 8224 | tf_op jit(solution)/shard_map/ppermute | solution.py:289
  5.3 2.6 %collective-permute-start.1 = (f32[16,128]{1,0:T(8,128)S(1)}, f32[16,128]{1,0:T(8,128)S(1)}, u32[]{:S(2)}, u32[]{:S(2)}) collective-permute-start(f32[16,128]{1,0:T(8,128)S(1)} %add.18.refs_0_), channel_id=1, source_target_pairs={{0,3},{1,2},{2,1},{3,0},{4,7},{5,6},{6,5},{7,4},{8,11},{9,10},{10,... | collective-permute-start | bytes 24584 | tf_op jit(solution)/shard_map/ppermute | solution.py:289
  7.9 1.4 %collective-permute-done.1.refs_1_ = f32[16,128]{1,0:T(8,128)S(1)} collective-permute-done((f32[16,128]{1,0:T(8,128)S(1)}, f32[16,128]{1,0:T(8,128)S(1)}, u32[]{:S(2)}, u32[]{:S(2)}) %collective-permute-start.1) | collective-permute-done | bytes 8224 | tf_op jit(solution)/shard_map/ppermute | solution.py:289
  9.9 3.1 %collective-permute-start.3 = (f32[136,128]{1,0:T(8,128)S(1)}, f32[136,128]{1,0:T(8,128)S(1)}, u32[]{:S(2)}, u32[]{:S(2)}) collective-permute-start(f32[136,128]{1,0:T(8,128)S(1)} %get-tuple-element.27.refs_0_), channel_id=1, source_target_pairs={{0,16},{4,20},{8,24},{12,28},{16,0},{20,4},{24,8},{28,12},{1,17},{... | collective-permute-start | bytes 208904 | tf_op jit(solution)/shard_map/ppermute | solution.py:289
  13.0 1.3 %collective-permute-start.4 = (f32[136,128]{1,0:T(8,128)S(1)}, f32[136,128]{1,0:T(8,128)S(1)}, u32[]{:S(2)}, u32[]{:S(2)}) collective-permute-start(f32[136,128]{1,0:T(8,128)S(1)} %get-tuple-element.27.refs_0_), channel_id=1, source_target_pairs={{0,24},{4,28},{8,16},{12,20},{16,8},{20,12},{24,0},{28,4},{1,25},{... | collective-permute-start | bytes 208904 | tf_op jit(solution)/shard_map/ppermute | solution.py:289
  14.6 1.5 %collective-permute-start.5 = (f32[136,128]{1,0:T(8,128)S(1)}, f32[136,128]{1,0:T(8,128)S(1)}, u32[]{:S(2)}, u32[]{:S(2)}) collective-permute-start(f32[136,128]{1,0:T(8,128)S(1)} %get-tuple-element.27.refs_0_), channel_id=1, source_target_pairs={{0,4},{4,0},{8,12},{12,8},{16,20},{20,16},{24,28},{28,24},{1,5},{5... | collective-permute-start | bytes 208904 | tf_op jit(solution)/shard_map/ppermute | solution.py:289
  16.1 1.7 %collective-permute-start.6 = (f32[136,128]{1,0:T(8,128)S(1)}, f32[136,128]{1,0:T(8,128)S(1)}, u32[]{:S(2)}, u32[]{:S(2)}) collective-permute-start(f32[136,128]{1,0:T(8,128)S(1)} %get-tuple-element.27.refs_0_), channel_id=1, source_target_pairs={{0,12},{4,8},{8,4},{12,0},{16,28},{20,24},{24,20},{28,16},{1,13},{... | collective-permute-start | bytes 208904 | tf_op jit(solution)/shard_map/ppermute | solution.py:289
  17.9 2.0 %collective-permute-start.7 = (f32[136,128]{1,0:T(8,128)S(1)}, f32[136,128]{1,0:T(8,128)S(1)}, u32[]{:S(2)}, u32[]{:S(2)}) collective-permute-start(f32[136,128]{1,0:T(8,128)S(1)} %collective-permute-done.3.refs_2_), channel_id=1, source_target_pairs={{0,4},{4,0},{8,12},{12,8},{16,20},{20,16},{24,28},{28,24},{1,5},{5... | collective-permute-start | bytes 208904 | tf_op jit(solution)/shard_map/ppermute | solution.py:289
  19.9 1.3 %collective-permute-start.8 = (f32[136,128]{1,0:T(8,128)S(1)}, f32[136,128]{1,0:T(8,128)S(1)}, u32[]{:S(2)}, u32[]{:S(2)}) collective-permute-start(f32[136,128]{1,0:T(8,128)S(1)} %collective-permute-done.4.refs_3_), channel_id=1, source_target_pairs={{0,4},{4,0},{8,12},{12,8},{16,20},{20,16},{24,28},{28,24},{1,5},{5... | collective-permute-start | bytes 208904 | tf_op jit(solution)/shard_map/ppermute | solution.py:289
  21.1 1.5 %collective-permute-done.6.refs_5_ = f32[136,128]{1,0:T(8,128)S(1)} collective-permute-done((f32[136,128]{1,0:T(8,128)S(1)}, f32[136,128]{1,0:T(8,128)S(1)}, u32[]{:S(2)}, u32[]{:S(2)}) %collective-permute-start.6) | collective-permute-done | bytes 69664 | tf_op jit(solution)/shard_map/ppermute | solution.py:289
  23.5 0.7 %collective-permute-done.8.refs_1_ = f32[136,128]{1,0:T(8,128)S(1)} collective-permute-done((f32[136,128]{1,0:T(8,128)S(1)}, f32[136,128]{1,0:T(8,128)S(1)}, u32[]{:S(2)}, u32[]{:S(2)}) %collective-permute-start.8) | collective-permute-done | bytes 69664 | tf_op jit(solution)/shard_map/ppermute | solution.py:289
  24.3 1.0 %shard_map.71 = (f32[256,128]{1,0:T(8,128)S(1)}, f32[128,128]{1,0:T(8,128)S(1)}, bf16[384,256]{1,0:T(8,128)(2,1)S(1)}, f32[24,128]{1,0:T(8,128)S(1)}) custom-call(bf16[16,8,128,128]{3,2,1,0:T(8,128)(2,1)S(1)} %get-tuple-element.22.values, f32[128,128]{1,0:T(8,128)S(1)} %get-tuple-element.23.ids, f32[128,128]{1,0:T(8,128)S(1)} %get-tuple-element.24.picked, ...), custom_call_target="tpu_custom_call" | custom-call | tf_op jit(solution)/shard_map/pallas_call | solution.py:277
  25.3 1.2 %collective-permute-done.9 = f32[24,128]{1,0:T(8,128)S(1)} collective-permute-done((f32[24,128]{1,0:T(8,128)S(1)}, f32[24,128]{1,0:T(8,128)S(1)}, u32[]{:S(2)}, u32[]{:S(2)}) %collective-permute-start.9) | collective-permute-done | bytes 12320 | tf_op jit(solution)/shard_map/ppermute | solution.py:289
  26.5 1.3 %collective-permute-start.10 = (f32[24,128]{1,0:T(8,128)S(1)}, f32[24,128]{1,0:T(8,128)S(1)}, u32[]{:S(2)}, u32[]{:S(2)}) collective-permute-start(f32[24,128]{1,0:T(8,128)S(1)} %add.19.refs_0_), channel_id=1, source_target_pairs={{0,3},{1,2},{2,1},{3,0},{4,7},{5,6},{6,5},{7,4},{8,11},{9,10},{10,... | collective-permute-start | bytes 36872 | tf_op jit(solution)/shard_map/ppermute | solution.py:289
  27.7 1.9 %collective-permute-done.10.refs_1_ = f32[24,128]{1,0:T(8,128)S(1)} collective-permute-done((f32[24,128]{1,0:T(8,128)S(1)}, f32[24,128]{1,0:T(8,128)S(1)}, u32[]{:S(2)}, u32[]{:S(2)}) %collective-permute-start.10) | collective-permute-done | bytes 12320 | tf_op jit(solution)/shard_map/ppermute | solution.py:289
  30.2 2.8 %collective-permute-start.12 = (f32[136,128]{1,0:T(8,128)S(1)}, f32[136,128]{1,0:T(8,128)S(1)}, u32[]{:S(2)}, u32[]{:S(2)}) collective-permute-start(f32[136,128]{1,0:T(8,128)S(1)} %get-tuple-element.35.refs_0_), channel_id=1, source_target_pairs={{0,16},{4,20},{8,24},{12,28},{16,0},{20,4},{24,8},{28,12},{1,17},{... | collective-permute-start | bytes 208904 | tf_op jit(solution)/shard_map/ppermute | solution.py:289
  33.0 1.8 %collective-permute-start.13 = (f32[136,128]{1,0:T(8,128)S(1)}, f32[136,128]{1,0:T(8,128)S(1)}, u32[]{:S(2)}, u32[]{:S(2)}) collective-permute-start(f32[136,128]{1,0:T(8,128)S(1)} %get-tuple-element.35.refs_0_), channel_id=1, source_target_pairs={{0,24},{4,28},{8,16},{12,20},{16,8},{20,12},{24,0},{28,4},{1,25},{... | collective-permute-start | bytes 208904 | tf_op jit(solution)/shard_map/ppermute | solution.py:289
  35.8 2.5 %collective-permute-start.15 = (f32[136,128]{1,0:T(8,128)S(1)}, f32[136,128]{1,0:T(8,128)S(1)}, u32[]{:S(2)}, u32[]{:S(2)}) collective-permute-start(f32[136,128]{1,0:T(8,128)S(1)} %get-tuple-element.35.refs_0_), channel_id=1, source_target_pairs={{0,12},{4,8},{8,4},{12,0},{16,28},{20,24},{24,20},{28,16},{1,13},{... | collective-permute-start | bytes 208904 | tf_op jit(solution)/shard_map/ppermute | solution.py:289
  38.3 1.5 %collective-permute-start.16 = (f32[136,128]{1,0:T(8,128)S(1)}, f32[136,128]{1,0:T(8,128)S(1)}, u32[]{:S(2)}, u32[]{:S(2)}) collective-permute-start(f32[136,128]{1,0:T(8,128)S(1)} %collective-permute-done.12.refs_2_), channel_id=1, source_target_pairs={{0,4},{4,0},{8,12},{12,8},{16,20},{20,16},{24,28},{28,24},{1,5},{5... | collective-permute-start | bytes 208904 | tf_op jit(solution)/shard_map/ppermute | solution.py:289
  39.9 1.2 %collective-permute-start.17 = (f32[136,128]{1,0:T(8,128)S(1)}, f32[136,128]{1,0:T(8,128)S(1)}, u32[]{:S(2)}, u32[]{:S(2)}) collective-permute-start(f32[136,128]{1,0:T(8,128)S(1)} %collective-permute-done.13.refs_3_), channel_id=1, source_target_pairs={{0,4},{4,0},{8,12},{12,8},{16,20},{20,16},{24,28},{28,24},{1,5},{5... | collective-permute-start | bytes 208904 | tf_op jit(solution)/shard_map/ppermute | solution.py:289
  41.1 1.4 %collective-permute-done.15.refs_5_ = f32[136,128]{1,0:T(8,128)S(1)} collective-permute-done((f32[136,128]{1,0:T(8,128)S(1)}, f32[136,128]{1,0:T(8,128)S(1)}, u32[]{:S(2)}, u32[]{:S(2)}) %collective-permute-start.15) | collective-permute-done | bytes 69664 | tf_op jit(solution)/shard_map/ppermute | solution.py:289
  42.9 0.8 %collective-permute-done.16.refs_0_ = f32[136,128]{1,0:T(8,128)S(1)} collective-permute-done((f32[136,128]{1,0:T(8,128)S(1)}, f32[136,128]{1,0:T(8,128)S(1)}, u32[]{:S(2)}, u32[]{:S(2)}) %collective-permute-start.16) | collective-permute-done | bytes 69664 | tf_op jit(solution)/shard_map/ppermute | solution.py:289
  43.7 0.7 %collective-permute-done.17.refs_1_ = f32[136,128]{1,0:T(8,128)S(1)} collective-permute-done((f32[136,128]{1,0:T(8,128)S(1)}, f32[136,128]{1,0:T(8,128)S(1)}, u32[]{:S(2)}, u32[]{:S(2)}) %collective-permute-start.17) | collective-permute-done | bytes 69664 | tf_op jit(solution)/shard_map/ppermute | solution.py:289
  44.4 1.0 %shard_map.74 = (f32[256,128]{1,0:T(8,128)S(1)}, f32[8,128]{1,0:T(8,128)S(1)}, f32[24,128]{1,0:T(8,128)S(1)}) custom-call(bf16[16,8,128,128]{3,2,1,0:T(8,128)(2,1)S(1)} %get-tuple-element.22.values, bf16[384,256]{1,0:T(8,128)(2,1)S(1)} %get-tuple-element.29.onehot, f32[128,128]{1,0:T(8,128)S(1)} %get-tuple-element.30.start_slot, ...), custom_call_target="tpu_custom_call" | custom-call | tf_op jit(solution)/shard_map/pallas_call | solution.py:277
  45.5 1.2 %collective-permute-done.18 = f32[24,128]{1,0:T(8,128)S(1)} collective-permute-done((f32[24,128]{1,0:T(8,128)S(1)}, f32[24,128]{1,0:T(8,128)S(1)}, u32[]{:S(2)}, u32[]{:S(2)}) %collective-permute-start.18) | collective-permute-done | bytes 12320 | tf_op jit(solution)/shard_map/ppermute | solution.py:289
  46.6 1.3 %collective-permute-start.19 = (f32[24,128]{1,0:T(8,128)S(1)}, f32[24,128]{1,0:T(8,128)S(1)}, u32[]{:S(2)}, u32[]{:S(2)}) collective-permute-start(f32[24,128]{1,0:T(8,128)S(1)} %add.20.refs_0_), channel_id=1, source_target_pairs={{0,3},{1,2},{2,1},{3,0},{4,7},{5,6},{6,5},{7,4},{8,11},{9,10},{10,... | collective-permute-start | bytes 36872 | tf_op jit(solution)/shard_map/ppermute | solution.py:289
  47.9 1.9 %collective-permute-done.19.refs_1_ = f32[24,128]{1,0:T(8,128)S(1)} collective-permute-done((f32[24,128]{1,0:T(8,128)S(1)}, f32[24,128]{1,0:T(8,128)S(1)}, u32[]{:S(2)}, u32[]{:S(2)}) %collective-permute-start.19) | collective-permute-done | bytes 12320 | tf_op jit(solution)/shard_map/ppermute | solution.py:289
  49.9 3.8 %collective-permute-start.22 = (f32[8,128]{1,0:T(8,128)S(1)}, f32[8,128]{1,0:T(8,128)S(1)}, u32[]{:S(2)}, u32[]{:S(2)}) collective-permute-start(f32[8,128]{1,0:T(8,128)S(1)} %shard_map.75), channel_id=1, source_target_pairs={{0,25},{1,24},{2,27},{3,26},{4,29},{5,28},{6,31},{7,30},{8,17},{9,... | collective-permute-start | bytes 12296 | tf_op jit(solution)/shard_map/ppermute | solution.py:299
  55.0 2.6 %collective-permute-done.21 = f32[8,128]{1,0:T(8,128)S(1)} collective-permute-done((f32[8,128]{1,0:T(8,128)S(1)}, f32[8,128]{1,0:T(8,128)S(1)}, u32[]{:S(2)}, u32[]{:S(2)}) %collective-permute-start.21) | collective-permute-done | bytes 4128 | tf_op jit(solution)/shard_map/ppermute | solution.py:299
  57.6 1.0 %collective-permute-start.23 = (f32[8,128]{1,0:T(8,128)S(1)}, f32[8,128]{1,0:T(8,128)S(1)}, u32[]{:S(2)}, u32[]{:S(2)}) collective-permute-start(f32[8,128]{1,0:T(8,128)S(1)} %add_add_fusion.refs_0_), channel_id=1, source_target_pairs={{0,5},{1,4},{2,7},{3,6},{4,1},{5,0},{6,3},{7,2},{8,13},{9,12},{10,... | collective-permute-start | bytes 12296 | tf_op jit(solution)/shard_map/ppermute | solution.py:299
  59.3 1.4 %collective-permute-done.23.refs_1_ = f32[8,128]{1,0:T(8,128)S(1)} collective-permute-done((f32[8,128]{1,0:T(8,128)S(1)}, f32[8,128]{1,0:T(8,128)S(1)}, u32[]{:S(2)}, u32[]{:S(2)}) %collective-permute-start.23) | collective-permute-done | bytes 4128 | tf_op jit(solution)/shard_map/ppermute | solution.py:299
  (33 shorter events, 7.5 us)
Async XLA Ops:
  0.6 8.7 %copy-start = (s32[2048]{0:T(1024)S(1)}, s32[2048]{0:T(1024)}, u32[]{:S(2)}) copy-start(s32[2048]{0:T(1024)} %param.8) | copy-start | bytes 24580
  4.0 1.3 %collective-permute-start = (f32[16,128]{1,0:T(8,128)S(1)}, f32[16,128]{1,0:T(8,128)S(1)}, u32[]{:S(2)}, u32[]{:S(2)}) collective-permute-start(f32[16,128]{1,0:T(8,128)S(1)} %get-tuple-element.26), channel_id=1, source_target_pairs={{0,1},{1,0},{2,3},{3,2},{4,5},{5,4},{6,7},{7,6},{8,9},{9,8},{10,11... | collective-permute-start | bytes 24584 | tf_op jit(solution)/shard_map/ppermute | solution.py:289
  5.3 4.0 %collective-permute-start.1 = (f32[16,128]{1,0:T(8,128)S(1)}, f32[16,128]{1,0:T(8,128)S(1)}, u32[]{:S(2)}, u32[]{:S(2)}) collective-permute-start(f32[16,128]{1,0:T(8,128)S(1)} %add.18.refs_0_), channel_id=1, source_target_pairs={{0,3},{1,2},{2,1},{3,0},{4,7},{5,6},{6,5},{7,4},{8,11},{9,10},{10,... | collective-permute-start | bytes 24584 | tf_op jit(solution)/shard_map/ppermute | solution.py:289
  9.9 7.9 %collective-permute-start.3 = (f32[136,128]{1,0:T(8,128)S(1)}, f32[136,128]{1,0:T(8,128)S(1)}, u32[]{:S(2)}, u32[]{:S(2)}) collective-permute-start(f32[136,128]{1,0:T(8,128)S(1)} %get-tuple-element.27.refs_0_), channel_id=1, source_target_pairs={{0,16},{4,20},{8,24},{12,28},{16,0},{20,4},{24,8},{28,12},{1,17},{... | collective-permute-start | bytes 208904 | tf_op jit(solution)/shard_map/ppermute | solution.py:289
  13.0 6.8 %collective-permute-start.4 = (f32[136,128]{1,0:T(8,128)S(1)}, f32[136,128]{1,0:T(8,128)S(1)}, u32[]{:S(2)}, u32[]{:S(2)}) collective-permute-start(f32[136,128]{1,0:T(8,128)S(1)} %get-tuple-element.27.refs_0_), channel_id=1, source_target_pairs={{0,24},{4,28},{8,16},{12,20},{16,8},{20,12},{24,0},{28,4},{1,25},{... | collective-permute-start | bytes 208904 | tf_op jit(solution)/shard_map/ppermute | solution.py:289
  14.4 6.7 %collective-permute-start.2 = (f32[136,128]{1,0:T(8,128)S(1)}, f32[136,128]{1,0:T(8,128)S(1)}, u32[]{:S(2)}, u32[]{:S(2)}) collective-permute-start(f32[136,128]{1,0:T(8,128)S(1)} %get-tuple-element.27.refs_0_), channel_id=1, source_target_pairs={{0,8},{4,12},{8,0},{12,4},{16,24},{20,28},{24,16},{28,20},{1,9},{5... | collective-permute-start | bytes 208904 | tf_op jit(solution)/shard_map/ppermute | solution.py:289
  14.6 6.5 %collective-permute-start.5 = (f32[136,128]{1,0:T(8,128)S(1)}, f32[136,128]{1,0:T(8,128)S(1)}, u32[]{:S(2)}, u32[]{:S(2)}) collective-permute-start(f32[136,128]{1,0:T(8,128)S(1)} %get-tuple-element.27.refs_0_), channel_id=1, source_target_pairs={{0,4},{4,0},{8,12},{12,8},{16,20},{20,16},{24,28},{28,24},{1,5},{5... | collective-permute-start | bytes 208904 | tf_op jit(solution)/shard_map/ppermute | solution.py:289
  16.1 6.4 %collective-permute-start.6 = (f32[136,128]{1,0:T(8,128)S(1)}, f32[136,128]{1,0:T(8,128)S(1)}, u32[]{:S(2)}, u32[]{:S(2)}) collective-permute-start(f32[136,128]{1,0:T(8,128)S(1)} %get-tuple-element.27.refs_0_), channel_id=1, source_target_pairs={{0,12},{4,8},{8,4},{12,0},{16,28},{20,24},{24,20},{28,16},{1,13},{... | collective-permute-start | bytes 208904 | tf_op jit(solution)/shard_map/ppermute | solution.py:289
  17.9 5.6 %collective-permute-start.7 = (f32[136,128]{1,0:T(8,128)S(1)}, f32[136,128]{1,0:T(8,128)S(1)}, u32[]{:S(2)}, u32[]{:S(2)}) collective-permute-start(f32[136,128]{1,0:T(8,128)S(1)} %collective-permute-done.3.refs_2_), channel_id=1, source_target_pairs={{0,4},{4,0},{8,12},{12,8},{16,20},{20,16},{24,28},{28,24},{1,5},{5... | collective-permute-start | bytes 208904 | tf_op jit(solution)/shard_map/ppermute | solution.py:289
  19.9 4.4 %collective-permute-start.8 = (f32[136,128]{1,0:T(8,128)S(1)}, f32[136,128]{1,0:T(8,128)S(1)}, u32[]{:S(2)}, u32[]{:S(2)}) collective-permute-start(f32[136,128]{1,0:T(8,128)S(1)} %collective-permute-done.4.refs_3_), channel_id=1, source_target_pairs={{0,4},{4,0},{8,12},{12,8},{16,20},{20,16},{24,28},{28,24},{1,5},{5... | collective-permute-start | bytes 208904 | tf_op jit(solution)/shard_map/ppermute | solution.py:289
  25.2 1.2 %collective-permute-start.9 = (f32[24,128]{1,0:T(8,128)S(1)}, f32[24,128]{1,0:T(8,128)S(1)}, u32[]{:S(2)}, u32[]{:S(2)}) collective-permute-start(f32[24,128]{1,0:T(8,128)S(1)} %get-tuple-element.34), channel_id=1, source_target_pairs={{0,1},{1,0},{2,3},{3,2},{4,5},{5,4},{6,7},{7,6},{8,9},{9,8},{10,11... | collective-permute-start | bytes 36872 | tf_op jit(solution)/shard_map/ppermute | solution.py:289
  26.5 3.1 %collective-permute-start.10 = (f32[24,128]{1,0:T(8,128)S(1)}, f32[24,128]{1,0:T(8,128)S(1)}, u32[]{:S(2)}, u32[]{:S(2)}) collective-permute-start(f32[24,128]{1,0:T(8,128)S(1)} %add.19.refs_0_), channel_id=1, source_target_pairs={{0,3},{1,2},{2,1},{3,0},{4,7},{5,6},{6,5},{7,4},{8,11},{9,10},{10,... | collective-permute-start | bytes 36872 | tf_op jit(solution)/shard_map/ppermute | solution.py:289
  30.2 8.1 %collective-permute-start.12 = (f32[136,128]{1,0:T(8,128)S(1)}, f32[136,128]{1,0:T(8,128)S(1)}, u32[]{:S(2)}, u32[]{:S(2)}) collective-permute-start(f32[136,128]{1,0:T(8,128)S(1)} %get-tuple-element.35.refs_0_), channel_id=1, source_target_pairs={{0,16},{4,20},{8,24},{12,28},{16,0},{20,4},{24,8},{28,12},{1,17},{... | collective-permute-start | bytes 208904 | tf_op jit(solution)/shard_map/ppermute | solution.py:289
  33.0 6.8 %collective-permute-start.13 = (f32[136,128]{1,0:T(8,128)S(1)}, f32[136,128]{1,0:T(8,128)S(1)}, u32[]{:S(2)}, u32[]{:S(2)}) collective-permute-start(f32[136,128]{1,0:T(8,128)S(1)} %get-tuple-element.35.refs_0_), channel_id=1, source_target_pairs={{0,24},{4,28},{8,16},{12,20},{16,8},{20,12},{24,0},{28,4},{1,25},{... | collective-permute-start | bytes 208904 | tf_op jit(solution)/shard_map/ppermute | solution.py:289
  34.8 6.3 %collective-permute-start.11 = (f32[136,128]{1,0:T(8,128)S(1)}, f32[136,128]{1,0:T(8,128)S(1)}, u32[]{:S(2)}, u32[]{:S(2)}) collective-permute-start(f32[136,128]{1,0:T(8,128)S(1)} %get-tuple-element.35.refs_0_), channel_id=1, source_target_pairs={{0,8},{4,12},{8,0},{12,4},{16,24},{20,28},{24,16},{28,20},{1,9},{5... | collective-permute-start | bytes 208904 | tf_op jit(solution)/shard_map/ppermute | solution.py:289
  35.3 5.8 %collective-permute-start.14 = (f32[136,128]{1,0:T(8,128)S(1)}, f32[136,128]{1,0:T(8,128)S(1)}, u32[]{:S(2)}, u32[]{:S(2)}) collective-permute-start(f32[136,128]{1,0:T(8,128)S(1)} %get-tuple-element.35.refs_0_), channel_id=1, source_target_pairs={{0,4},{4,0},{8,12},{12,8},{16,20},{20,16},{24,28},{28,24},{1,5},{5... | collective-permute-start | bytes 208904 | tf_op jit(solution)/shard_map/ppermute | solution.py:289
  35.8 6.7 %collective-permute-start.15 = (f32[136,128]{1,0:T(8,128)S(1)}, f32[136,128]{1,0:T(8,128)S(1)}, u32[]{:S(2)}, u32[]{:S(2)}) collective-permute-start(f32[136,128]{1,0:T(8,128)S(1)} %get-tuple-element.35.refs_0_), channel_id=1, source_target_pairs={{0,12},{4,8},{8,4},{12,0},{16,28},{20,24},{24,20},{28,16},{1,13},{... | collective-permute-start | bytes 208904 | tf_op jit(solution)/shard_map/ppermute | solution.py:289
  38.3 5.4 %collective-permute-start.16 = (f32[136,128]{1,0:T(8,128)S(1)}, f32[136,128]{1,0:T(8,128)S(1)}, u32[]{:S(2)}, u32[]{:S(2)}) collective-permute-start(f32[136,128]{1,0:T(8,128)S(1)} %collective-permute-done.12.refs_2_), channel_id=1, source_target_pairs={{0,4},{4,0},{8,12},{12,8},{16,20},{20,16},{24,28},{28,24},{1,5},{5... | collective-permute-start | bytes 208904 | tf_op jit(solution)/shard_map/ppermute | solution.py:289
  39.9 4.5 %collective-permute-start.17 = (f32[136,128]{1,0:T(8,128)S(1)}, f32[136,128]{1,0:T(8,128)S(1)}, u32[]{:S(2)}, u32[]{:S(2)}) collective-permute-start(f32[136,128]{1,0:T(8,128)S(1)} %collective-permute-done.13.refs_3_), channel_id=1, source_target_pairs={{0,4},{4,0},{8,12},{12,8},{16,20},{20,16},{24,28},{28,24},{1,5},{5... | collective-permute-start | bytes 208904 | tf_op jit(solution)/shard_map/ppermute | solution.py:289
  45.4 1.2 %collective-permute-start.18 = (f32[24,128]{1,0:T(8,128)S(1)}, f32[24,128]{1,0:T(8,128)S(1)}, u32[]{:S(2)}, u32[]{:S(2)}) collective-permute-start(f32[24,128]{1,0:T(8,128)S(1)} %get-tuple-element.41), channel_id=1, source_target_pairs={{0,1},{1,0},{2,3},{3,2},{4,5},{5,4},{6,7},{7,6},{8,9},{9,8},{10,11... | collective-permute-start | bytes 36872 | tf_op jit(solution)/shard_map/ppermute | solution.py:289
  46.6 3.1 %collective-permute-start.19 = (f32[24,128]{1,0:T(8,128)S(1)}, f32[24,128]{1,0:T(8,128)S(1)}, u32[]{:S(2)}, u32[]{:S(2)}) collective-permute-start(f32[24,128]{1,0:T(8,128)S(1)} %add.20.refs_0_), channel_id=1, source_target_pairs={{0,3},{1,2},{2,1},{3,0},{4,7},{5,6},{6,5},{7,4},{8,11},{9,10},{10,... | collective-permute-start | bytes 36872 | tf_op jit(solution)/shard_map/ppermute | solution.py:289
  49.9 5.1 %collective-permute-start.22 = (f32[8,128]{1,0:T(8,128)S(1)}, f32[8,128]{1,0:T(8,128)S(1)}, u32[]{:S(2)}, u32[]{:S(2)}) collective-permute-start(f32[8,128]{1,0:T(8,128)S(1)} %shard_map.75), channel_id=1, source_target_pairs={{0,25},{1,24},{2,27},{3,26},{4,29},{5,28},{6,31},{7,30},{8,17},{9,... | collective-permute-start | bytes 12296 | tf_op jit(solution)/shard_map/ppermute | solution.py:299
  53.7 3.9 %collective-permute-start.21 = (f32[8,128]{1,0:T(8,128)S(1)}, f32[8,128]{1,0:T(8,128)S(1)}, u32[]{:S(2)}, u32[]{:S(2)}) collective-permute-start(f32[8,128]{1,0:T(8,128)S(1)} %shard_map.75), channel_id=1, source_target_pairs={{0,17},{1,16},{2,19},{3,18},{4,21},{5,20},{6,23},{7,22},{8,25},{9,... | collective-permute-start | bytes 12296 | tf_op jit(solution)/shard_map/ppermute | solution.py:299
  53.7 3.9 %collective-permute-start.20 = (f32[8,128]{1,0:T(8,128)S(1)}, f32[8,128]{1,0:T(8,128)S(1)}, u32[]{:S(2)}, u32[]{:S(2)}) collective-permute-start(f32[8,128]{1,0:T(8,128)S(1)} %shard_map.75), channel_id=1, source_target_pairs={{0,9},{1,8},{2,11},{3,10},{4,13},{5,12},{6,15},{7,14},{8,1},{9,0},... | collective-permute-start | bytes 12296 | tf_op jit(solution)/shard_map/ppermute | solution.py:299
  57.6 3.1 %collective-permute-start.23 = (f32[8,128]{1,0:T(8,128)S(1)}, f32[8,128]{1,0:T(8,128)S(1)}, u32[]{:S(2)}, u32[]{:S(2)}) collective-permute-start(f32[8,128]{1,0:T(8,128)S(1)} %add_add_fusion.refs_0_), channel_id=1, source_target_pairs={{0,5},{1,4},{2,7},{3,6},{4,1},{5,0},{6,3},{7,2},{8,13},{9,12},{10,... | collective-permute-start | bytes 12296 | tf_op jit(solution)/shard_map/ppermute | solution.py:299

commit v9 on v8

--- a/solution.py
+++ b/solution.py
@@ -315,9 +315,9 @@
         gathered = lax.all_gather(array, "inst", axis=0)
         return [gathered[i] for i in range(size)]
     parts = {0: array}
-    for distance in (2, 4, 6, 1, 3):
+    for distance in (6, 4, 3, 1, 2):
         parts[distance] = swap(array, "inst", distance)
-    for distance in (4, 6):
+    for distance in (6, 4):
         parts[distance ^ 1] = swap(parts[distance], "inst", 1)
     return list(parts.values())
 

time: 61.6 us -> 59.7 us (0.969)
  starting transfers between devices: 33.1 us -> 30.5 us
    ppermute x20, starting transfers between devices: 27.7 us -> 25.1 us  [swap(): return lax.ppermute(array, axis, [(i, i ^ distance) for i in range(size)])]
    ppermute x20, waiting for transfers between devices: 14 us -> 16.6 us  [swap(): return lax.ppermute(array, axis, [(i, i ^ distance) for i in range(size)])]
    ppermute x4, waiting for transfers between devices: 4.77 us -> 2.78 us  [swap_both(): return lax.ppermute(array, ('inst', 'feat'), pairs)]
  transfers between devices with their start and end apart: 24 -> 24, of which waited for: 16 -> 17; matrix products, arithmetic and copies ran while one was open for 1% -> 1% of each run, Pallas kernels for 1% -> 1%
where the time goes in v9:
time: 59.7 us; the launch traced here: 59.5 us
  starting transfers between devices  30.5 us (51%)
  waiting for transfers between devices  19.4 us (32%)
  Pallas kernels  7.58 us (13%)
  local copies, waits for them, and re-layouts  1.32 us (2%)
  between operations  0.73 us (1%)
    ppermute x20, starting transfers between devices, swap(): return lax.ppermute(array, axis, [(i, i ^ distance) for i in range(size)])  25.1 us
    ppermute x20, waiting for transfers between devices, swap(): return lax.ppermute(array, axis, [(i, i ^ distance) for i in range(size)])  16.6 us
    pallas_call x9, Pallas kernels, call(): pl.pallas_call(kernel, out_shape=out_shape, in_specs=in_specs, out_specs=...  7.58 us
    ppermute x4, starting transfers between devices, swap_both(): return lax.ppermute(array, ('inst', 'feat'), pairs)  5.46 us
    ppermute x4, waiting for transfers between devices, swap_both(): return lax.ppermute(array, ('inst', 'feat'), pairs)  2.78 us
    unnamed x4, local copies, waits for them, and re-layouts  1.32 us
  transfers between devices with their start and end apart: 24, of which 17 were waited for; matrix products, arithmetic and copies ran while one was open for 1% of the time, Pallas kernels for 1%

profile of v9, /device:TPU:0, one launch (start us, length us, event | category | flops | bytes accessed | tf_op | source)
XLA Modules:
  0.0 59.5 jit_solution(15623420832961855885)
XLA Ops:
  0.6 3.3 %shard_map.68 = (bf16[16,8,128,128]{3,2,1,0:T(8,128)(2,1)S(1)}, f32[128,128]{1,0:T(8,128)S(1)}, f32[128,128]{1,0:T(8,128)S(1)}, f32[256,128]{1,0:T(8,128)S(1)}, f32[16,128]{1,0:T(8,128)S(1)}) custom-call(s32[8,16]{1,0:T(8,128)} %bitcast.4, s32[1,16]{1,0:T(1,128)} %bitcast.5, f32[2048,128]{1,0:T(8,128)} %weights.1, bf16[16,8,128,128]{3,2,1,0:T(8,128)(2,1)} %values_in.1), custom_call_target="tpu_custom_call" | custom-call | tf_op jit(solution)/shard_map/pallas_call | solution.py:277
  4.5 0.8 %collective-permute-done = f32[16,128]{1,0:T(8,128)S(1)} collective-permute-done((f32[16,128]{1,0:T(8,128)S(1)}, f32[16,128]{1,0:T(8,128)S(1)}, u32[]{:S(2)}, u32[]{:S(2)}) %collective-permute-start) | collective-permute-done | bytes 8224 | tf_op jit(solution)/shard_map/ppermute | solution.py:289
  5.3 2.6 %collective-permute-start.1 = (f32[16,128]{1,0:T(8,128)S(1)}, f32[16,128]{1,0:T(8,128)S(1)}, u32[]{:S(2)}, u32[]{:S(2)}) collective-permute-start(f32[16,128]{1,0:T(8,128)S(1)} %add.18.refs_0_), channel_id=1, source_target_pairs={{0,3},{1,2},{2,1},{3,0},{4,7},{5,6},{6,5},{7,4},{8,11},{9,10},{10,... | collective-permute-start | bytes 24584 | tf_op jit(solution)/shard_map/ppermute | solution.py:289
  7.9 1.4 %collective-permute-done.1.refs_1_ = f32[16,128]{1,0:T(8,128)S(1)} collective-permute-done((f32[16,128]{1,0:T(8,128)S(1)}, f32[16,128]{1,0:T(8,128)S(1)}, u32[]{:S(2)}, u32[]{:S(2)}) %collective-permute-start.1) | collective-permute-done | bytes 8224 | tf_op jit(solution)/shard_map/ppermute | solution.py:289
  9.9 4.1 %collective-permute-start.2 = (f32[136,128]{1,0:T(8,128)S(1)}, f32[136,128]{1,0:T(8,128)S(1)}, u32[]{:S(2)}, u32[]{:S(2)}) collective-permute-start(f32[136,128]{1,0:T(8,128)S(1)} %get-tuple-element.27.refs_0_), channel_id=1, source_target_pairs={{0,24},{4,28},{8,16},{12,20},{16,8},{20,12},{24,0},{28,4},{1,25},{... | collective-permute-start | bytes 208904 | tf_op jit(solution)/shard_map/ppermute | solution.py:289
  14.1 1.7 %collective-permute-start.4 = (f32[136,128]{1,0:T(8,128)S(1)}, f32[136,128]{1,0:T(8,128)S(1)}, u32[]{:S(2)}, u32[]{:S(2)}) collective-permute-start(f32[136,128]{1,0:T(8,128)S(1)} %get-tuple-element.27.refs_0_), channel_id=1, source_target_pairs={{0,12},{4,8},{8,4},{12,0},{16,28},{20,24},{24,20},{28,16},{1,13},{... | collective-permute-start | bytes 208904 | tf_op jit(solution)/shard_map/ppermute | solution.py:289
  16.2 1.4 %collective-permute-start.6 = (f32[136,128]{1,0:T(8,128)S(1)}, f32[136,128]{1,0:T(8,128)S(1)}, u32[]{:S(2)}, u32[]{:S(2)}) collective-permute-start(f32[136,128]{1,0:T(8,128)S(1)} %get-tuple-element.27.refs_0_), channel_id=1, source_target_pairs={{0,8},{4,12},{8,0},{12,4},{16,24},{20,28},{24,16},{28,20},{1,9},{5... | collective-permute-start | bytes 208904 | tf_op jit(solution)/shard_map/ppermute | solution.py:289
  17.5 1.5 %collective-permute-start.7 = (f32[136,128]{1,0:T(8,128)S(1)}, f32[136,128]{1,0:T(8,128)S(1)}, u32[]{:S(2)}, u32[]{:S(2)}) collective-permute-start(f32[136,128]{1,0:T(8,128)S(1)} %collective-permute-done.2.refs_1_), channel_id=1, source_target_pairs={{0,4},{4,0},{8,12},{12,8},{16,20},{20,16},{24,28},{28,24},{1,5},{5... | collective-permute-start | bytes 208904 | tf_op jit(solution)/shard_map/ppermute | solution.py:289
  19.1 1.3 %collective-permute-done.3.refs_2_ = f32[136,128]{1,0:T(8,128)S(1)} collective-permute-done((f32[136,128]{1,0:T(8,128)S(1)}, f32[136,128]{1,0:T(8,128)S(1)}, u32[]{:S(2)}, u32[]{:S(2)}) %collective-permute-start.3) | collective-permute-done | bytes 69664 | tf_op jit(solution)/shard_map/ppermute | solution.py:289
  20.3 1.5 %collective-permute-start.8 = (f32[136,128]{1,0:T(8,128)S(1)}, f32[136,128]{1,0:T(8,128)S(1)}, u32[]{:S(2)}, u32[]{:S(2)}) collective-permute-start(f32[136,128]{1,0:T(8,128)S(1)} %collective-permute-done.3.refs_2_), channel_id=1, source_target_pairs={{0,4},{4,0},{8,12},{12,8},{16,20},{20,16},{24,28},{28,24},{1,5},{5... | collective-permute-start | bytes 208904 | tf_op jit(solution)/shard_map/ppermute | solution.py:289
  22.4 2.3 %collective-permute-done.8.refs_1_ = f32[136,128]{1,0:T(8,128)S(1)} collective-permute-done((f32[136,128]{1,0:T(8,128)S(1)}, f32[136,128]{1,0:T(8,128)S(1)}, u32[]{:S(2)}, u32[]{:S(2)}) %collective-permute-start.8) | collective-permute-done | bytes 69664 | tf_op jit(solution)/shard_map/ppermute | solution.py:289
  24.7 1.0 %shard_map.71 = (f32[256,128]{1,0:T(8,128)S(1)}, f32[128,128]{1,0:T(8,128)S(1)}, bf16[384,256]{1,0:T(8,128)(2,1)S(1)}, f32[24,128]{1,0:T(8,128)S(1)}) custom-call(bf16[16,8,128,128]{3,2,1,0:T(8,128)(2,1)S(1)} %get-tuple-element.22.values, f32[128,128]{1,0:T(8,128)S(1)} %get-tuple-element.23.ids, f32[128,128]{1,0:T(8,128)S(1)} %get-tuple-element.24.picked, ...), custom_call_target="tpu_custom_call" | custom-call | tf_op jit(solution)/shard_map/pallas_call | solution.py:277
  25.7 1.2 %collective-permute-done.9 = f32[24,128]{1,0:T(8,128)S(1)} collective-permute-done((f32[24,128]{1,0:T(8,128)S(1)}, f32[24,128]{1,0:T(8,128)S(1)}, u32[]{:S(2)}, u32[]{:S(2)}) %collective-permute-start.9) | collective-permute-done | bytes 12320 | tf_op jit(solution)/shard_map/ppermute | solution.py:289
  26.9 1.3 %collective-permute-start.10 = (f32[24,128]{1,0:T(8,128)S(1)}, f32[24,128]{1,0:T(8,128)S(1)}, u32[]{:S(2)}, u32[]{:S(2)}) collective-permute-start(f32[24,128]{1,0:T(8,128)S(1)} %add.19.refs_0_), channel_id=1, source_target_pairs={{0,3},{1,2},{2,1},{3,0},{4,7},{5,6},{6,5},{7,4},{8,11},{9,10},{10,... | collective-permute-start | bytes 36872 | tf_op jit(solution)/shard_map/ppermute | solution.py:289
  28.1 1.9 %collective-permute-done.10.refs_1_ = f32[24,128]{1,0:T(8,128)S(1)} collective-permute-done((f32[24,128]{1,0:T(8,128)S(1)}, f32[24,128]{1,0:T(8,128)S(1)}, u32[]{:S(2)}, u32[]{:S(2)}) %collective-permute-start.10) | collective-permute-done | bytes 12320 | tf_op jit(solution)/shard_map/ppermute | solution.py:289
  30.6 2.4 %collective-permute-start.11 = (f32[136,128]{1,0:T(8,128)S(1)}, f32[136,128]{1,0:T(8,128)S(1)}, u32[]{:S(2)}, u32[]{:S(2)}) collective-permute-start(f32[136,128]{1,0:T(8,128)S(1)} %get-tuple-element.35.refs_0_), channel_id=1, source_target_pairs={{0,24},{4,28},{8,16},{12,20},{16,8},{20,12},{24,0},{28,4},{1,25},{... | collective-permute-start | bytes 208904 | tf_op jit(solution)/shard_map/ppermute | solution.py:289
  33.2 2.8 %collective-permute-start.13 = (f32[136,128]{1,0:T(8,128)S(1)}, f32[136,128]{1,0:T(8,128)S(1)}, u32[]{:S(2)}, u32[]{:S(2)}) collective-permute-start(f32[136,128]{1,0:T(8,128)S(1)} %get-tuple-element.35.refs_0_), channel_id=1, source_target_pairs={{0,12},{4,8},{8,4},{12,0},{16,28},{20,24},{24,20},{28,16},{1,13},{... | collective-permute-start | bytes 208904 | tf_op jit(solution)/shard_map/ppermute | solution.py:289
  36.7 1.0 %collective-permute-done.11.refs_1_ = f32[136,128]{1,0:T(8,128)S(1)} collective-permute-done((f32[136,128]{1,0:T(8,128)S(1)}, f32[136,128]{1,0:T(8,128)S(1)}, u32[]{:S(2)}, u32[]{:S(2)}) %collective-permute-start.11) | collective-permute-done | bytes 69664 | tf_op jit(solution)/shard_map/ppermute | solution.py:289
  37.7 1.4 %collective-permute-start.16 = (f32[136,128]{1,0:T(8,128)S(1)}, f32[136,128]{1,0:T(8,128)S(1)}, u32[]{:S(2)}, u32[]{:S(2)}) collective-permute-start(f32[136,128]{1,0:T(8,128)S(1)} %collective-permute-done.11.refs_1_), channel_id=1, source_target_pairs={{0,4},{4,0},{8,12},{12,8},{16,20},{20,16},{24,28},{28,24},{1,5},{5... | collective-permute-start | bytes 208904 | tf_op jit(solution)/shard_map/ppermute | solution.py:289
  39.1 1.0 %collective-permute-done.12.refs_2_ = f32[136,128]{1,0:T(8,128)S(1)} collective-permute-done((f32[136,128]{1,0:T(8,128)S(1)}, f32[136,128]{1,0:T(8,128)S(1)}, u32[]{:S(2)}, u32[]{:S(2)}) %collective-permute-start.12) | collective-permute-done | bytes 69664 | tf_op jit(solution)/shard_map/ppermute | solution.py:289
  40.1 1.2 %collective-permute-start.17 = (f32[136,128]{1,0:T(8,128)S(1)}, f32[136,128]{1,0:T(8,128)S(1)}, u32[]{:S(2)}, u32[]{:S(2)}) collective-permute-start(f32[136,128]{1,0:T(8,128)S(1)} %collective-permute-done.12.refs_2_), channel_id=1, source_target_pairs={{0,4},{4,0},{8,12},{12,8},{16,20},{20,16},{24,28},{28,24},{1,5},{5... | collective-permute-start | bytes 208904 | tf_op jit(solution)/shard_map/ppermute | solution.py:289
  42.0 2.4 %collective-permute-done.17.refs_1_ = f32[136,128]{1,0:T(8,128)S(1)} collective-permute-done((f32[136,128]{1,0:T(8,128)S(1)}, f32[136,128]{1,0:T(8,128)S(1)}, u32[]{:S(2)}, u32[]{:S(2)}) %collective-permute-start.17) | collective-permute-done | bytes 69664 | tf_op jit(solution)/shard_map/ppermute | solution.py:289
  44.4 1.0 %shard_map.74 = (f32[256,128]{1,0:T(8,128)S(1)}, f32[8,128]{1,0:T(8,128)S(1)}, f32[24,128]{1,0:T(8,128)S(1)}) custom-call(bf16[16,8,128,128]{3,2,1,0:T(8,128)(2,1)S(1)} %get-tuple-element.22.values, bf16[384,256]{1,0:T(8,128)(2,1)S(1)} %get-tuple-element.29.onehot, f32[128,128]{1,0:T(8,128)S(1)} %get-tuple-element.30.start_slot, ...), custom_call_target="tpu_custom_call" | custom-call | tf_op jit(solution)/shard_map/pallas_call | solution.py:277
  45.4 1.2 %collective-permute-done.18 = f32[24,128]{1,0:T(8,128)S(1)} collective-permute-done((f32[24,128]{1,0:T(8,128)S(1)}, f32[24,128]{1,0:T(8,128)S(1)}, u32[]{:S(2)}, u32[]{:S(2)}) %collective-permute-start.18) | collective-permute-done | bytes 12320 | tf_op jit(solution)/shard_map/ppermute | solution.py:289
  46.6 1.3 %collective-permute-start.19 = (f32[24,128]{1,0:T(8,128)S(1)}, f32[24,128]{1,0:T(8,128)S(1)}, u32[]{:S(2)}, u32[]{:S(2)}) collective-permute-start(f32[24,128]{1,0:T(8,128)S(1)} %add.20.refs_0_), channel_id=1, source_target_pairs={{0,3},{1,2},{2,1},{3,0},{4,7},{5,6},{6,5},{7,4},{8,11},{9,10},{10,... | collective-permute-start | bytes 36872 | tf_op jit(solution)/shard_map/ppermute | solution.py:289
  47.9 1.9 %collective-permute-done.19.refs_1_ = f32[24,128]{1,0:T(8,128)S(1)} collective-permute-done((f32[24,128]{1,0:T(8,128)S(1)}, f32[24,128]{1,0:T(8,128)S(1)}, u32[]{:S(2)}, u32[]{:S(2)}) %collective-permute-start.19) | collective-permute-done | bytes 12320 | tf_op jit(solution)/shard_map/ppermute | solution.py:289
  49.8 1.9 %collective-permute-start.22 = (f32[8,128]{1,0:T(8,128)S(1)}, f32[8,128]{1,0:T(8,128)S(1)}, u32[]{:S(2)}, u32[]{:S(2)}) collective-permute-start(f32[8,128]{1,0:T(8,128)S(1)} %shard_map.75), channel_id=1, source_target_pairs={{0,25},{1,24},{2,27},{3,26},{4,29},{5,28},{6,31},{7,30},{8,17},{9,... | collective-permute-start | bytes 12296 | tf_op jit(solution)/shard_map/ppermute | solution.py:299
  51.7 2.1 %collective-permute-start.20 = (f32[8,128]{1,0:T(8,128)S(1)}, f32[8,128]{1,0:T(8,128)S(1)}, u32[]{:S(2)}, u32[]{:S(2)}) collective-permute-start(f32[8,128]{1,0:T(8,128)S(1)} %shard_map.75), channel_id=1, source_target_pairs={{0,9},{1,8},{2,11},{3,10},{4,13},{5,12},{6,15},{7,14},{8,1},{9,0},... | collective-permute-start | bytes 12296 | tf_op jit(solution)/shard_map/ppermute | solution.py:299
  53.8 1.0 %collective-permute-done.22 = f32[8,128]{1,0:T(8,128)S(1)} collective-permute-done((f32[8,128]{1,0:T(8,128)S(1)}, f32[8,128]{1,0:T(8,128)S(1)}, u32[]{:S(2)}, u32[]{:S(2)}) %collective-permute-start.22) | collective-permute-done | bytes 4128 | tf_op jit(solution)/shard_map/ppermute | solution.py:299
  54.7 0.9 %collective-permute-done.21 = f32[8,128]{1,0:T(8,128)S(1)} collective-permute-done((f32[8,128]{1,0:T(8,128)S(1)}, f32[8,128]{1,0:T(8,128)S(1)}, u32[]{:S(2)}, u32[]{:S(2)}) %collective-permute-start.21) | collective-permute-done | bytes 4128 | tf_op jit(solution)/shard_map/ppermute | solution.py:299
  55.7 1.5 %collective-permute-start.23 = (f32[8,128]{1,0:T(8,128)S(1)}, f32[8,128]{1,0:T(8,128)S(1)}, u32[]{:S(2)}, u32[]{:S(2)}) collective-permute-start(f32[8,128]{1,0:T(8,128)S(1)} %add_add_fusion.refs_0_), channel_id=1, source_target_pairs={{0,5},{1,4},{2,7},{3,6},{4,1},{5,0},{6,3},{7,2},{8,13},{9,12},{10,... | collective-permute-start | bytes 12296 | tf_op jit(solution)/shard_map/ppermute | solution.py:299
  57.8 0.9 %collective-permute-done.23.refs_1_ = f32[8,128]{1,0:T(8,128)S(1)} collective-permute-done((f32[8,128]{1,0:T(8,128)S(1)}, f32[8,128]{1,0:T(8,128)S(1)}, u32[]{:S(2)}, u32[]{:S(2)}) %collective-permute-start.23) | collective-permute-done | bytes 4128 | tf_op jit(solution)/shard_map/ppermute | solution.py:299
  (33 shorter events, 5.9 us)
Async XLA Ops:
  0.6 8.7 %copy-start = (s32[2048]{0:T(1024)S(1)}, s32[2048]{0:T(1024)}, u32[]{:S(2)}) copy-start(s32[2048]{0:T(1024)} %param.8) | copy-start | bytes 24580
  4.0 1.3 %collective-permute-start = (f32[16,128]{1,0:T(8,128)S(1)}, f32[16,128]{1,0:T(8,128)S(1)}, u32[]{:S(2)}, u32[]{:S(2)}) collective-permute-start(f32[16,128]{1,0:T(8,128)S(1)} %get-tuple-element.26), channel_id=1, source_target_pairs={{0,1},{1,0},{2,3},{3,2},{4,5},{5,4},{6,7},{7,6},{8,9},{9,8},{10,11... | collective-permute-start | bytes 24584 | tf_op jit(solution)/shard_map/ppermute | solution.py:289
  5.3 4.0 %collective-permute-start.1 = (f32[16,128]{1,0:T(8,128)S(1)}, f32[16,128]{1,0:T(8,128)S(1)}, u32[]{:S(2)}, u32[]{:S(2)}) collective-permute-start(f32[16,128]{1,0:T(8,128)S(1)} %add.18.refs_0_), channel_id=1, source_target_pairs={{0,3},{1,2},{2,1},{3,0},{4,7},{5,6},{6,5},{7,4},{8,11},{9,10},{10,... | collective-permute-start | bytes 24584 | tf_op jit(solution)/shard_map/ppermute | solution.py:289
  9.9 7.6 %collective-permute-start.2 = (f32[136,128]{1,0:T(8,128)S(1)}, f32[136,128]{1,0:T(8,128)S(1)}, u32[]{:S(2)}, u32[]{:S(2)}) collective-permute-start(f32[136,128]{1,0:T(8,128)S(1)} %get-tuple-element.27.refs_0_), channel_id=1, source_target_pairs={{0,24},{4,28},{8,16},{12,20},{16,8},{20,12},{24,0},{28,4},{1,25},{... | collective-permute-start | bytes 208904 | tf_op jit(solution)/shard_map/ppermute | solution.py:289
  14.1 6.3 %collective-permute-start.3 = (f32[136,128]{1,0:T(8,128)S(1)}, f32[136,128]{1,0:T(8,128)S(1)}, u32[]{:S(2)}, u32[]{:S(2)}) collective-permute-start(f32[136,128]{1,0:T(8,128)S(1)} %get-tuple-element.27.refs_0_), channel_id=1, source_target_pairs={{0,16},{4,20},{8,24},{12,28},{16,0},{20,4},{24,8},{28,12},{1,17},{... | collective-permute-start | bytes 208904 | tf_op jit(solution)/shard_map/ppermute | solution.py:289
  14.1 7.8 %collective-permute-start.4 = (f32[136,128]{1,0:T(8,128)S(1)}, f32[136,128]{1,0:T(8,128)S(1)}, u32[]{:S(2)}, u32[]{:S(2)}) collective-permute-start(f32[136,128]{1,0:T(8,128)S(1)} %get-tuple-element.27.refs_0_), channel_id=1, source_target_pairs={{0,12},{4,8},{8,4},{12,0},{16,28},{20,24},{24,20},{28,16},{1,13},{... | collective-permute-start | bytes 208904 | tf_op jit(solution)/shard_map/ppermute | solution.py:289
  15.8 6.1 %collective-permute-start.5 = (f32[136,128]{1,0:T(8,128)S(1)}, f32[136,128]{1,0:T(8,128)S(1)}, u32[]{:S(2)}, u32[]{:S(2)}) collective-permute-start(f32[136,128]{1,0:T(8,128)S(1)} %get-tuple-element.27.refs_0_), channel_id=1, source_target_pairs={{0,4},{4,0},{8,12},{12,8},{16,20},{20,16},{24,28},{28,24},{1,5},{5... | collective-permute-start | bytes 208904 | tf_op jit(solution)/shard_map/ppermute | solution.py:289
  16.2 5.8 %collective-permute-start.6 = (f32[136,128]{1,0:T(8,128)S(1)}, f32[136,128]{1,0:T(8,128)S(1)}, u32[]{:S(2)}, u32[]{:S(2)}) collective-permute-start(f32[136,128]{1,0:T(8,128)S(1)} %get-tuple-element.27.refs_0_), channel_id=1, source_target_pairs={{0,8},{4,12},{8,0},{12,4},{16,24},{20,28},{24,16},{28,20},{1,9},{5... | collective-permute-start | bytes 208904 | tf_op jit(solution)/shard_map/ppermute | solution.py:289
  17.5 4.8 %collective-permute-start.7 = (f32[136,128]{1,0:T(8,128)S(1)}, f32[136,128]{1,0:T(8,128)S(1)}, u32[]{:S(2)}, u32[]{:S(2)}) collective-permute-start(f32[136,128]{1,0:T(8,128)S(1)} %collective-permute-done.2.refs_1_), channel_id=1, source_target_pairs={{0,4},{4,0},{8,12},{12,8},{16,20},{20,16},{24,28},{28,24},{1,5},{5... | collective-permute-start | bytes 208904 | tf_op jit(solution)/shard_map/ppermute | solution.py:289
  20.3 4.3 %collective-permute-start.8 = (f32[136,128]{1,0:T(8,128)S(1)}, f32[136,128]{1,0:T(8,128)S(1)}, u32[]{:S(2)}, u32[]{:S(2)}) collective-permute-start(f32[136,128]{1,0:T(8,128)S(1)} %collective-permute-done.3.refs_2_), channel_id=1, source_target_pairs={{0,4},{4,0},{8,12},{12,8},{16,20},{20,16},{24,28},{28,24},{1,5},{5... | collective-permute-start | bytes 208904 | tf_op jit(solution)/shard_map/ppermute | solution.py:289
  25.6 1.2 %collective-permute-start.9 = (f32[24,128]{1,0:T(8,128)S(1)}, f32[24,128]{1,0:T(8,128)S(1)}, u32[]{:S(2)}, u32[]{:S(2)}) collective-permute-start(f32[24,128]{1,0:T(8,128)S(1)} %get-tuple-element.34), channel_id=1, source_target_pairs={{0,1},{1,0},{2,3},{3,2},{4,5},{5,4},{6,7},{7,6},{8,9},{9,8},{10,11... | collective-permute-start | bytes 36872 | tf_op jit(solution)/shard_map/ppermute | solution.py:289
  26.9 3.1 %collective-permute-start.10 = (f32[24,128]{1,0:T(8,128)S(1)}, f32[24,128]{1,0:T(8,128)S(1)}, u32[]{:S(2)}, u32[]{:S(2)}) collective-permute-start(f32[24,128]{1,0:T(8,128)S(1)} %add.19.refs_0_), channel_id=1, source_target_pairs={{0,3},{1,2},{2,1},{3,0},{4,7},{5,6},{6,5},{7,4},{8,11},{9,10},{10,... | collective-permute-start | bytes 36872 | tf_op jit(solution)/shard_map/ppermute | solution.py:289
  30.6 7.0 %collective-permute-start.11 = (f32[136,128]{1,0:T(8,128)S(1)}, f32[136,128]{1,0:T(8,128)S(1)}, u32[]{:S(2)}, u32[]{:S(2)}) collective-permute-start(f32[136,128]{1,0:T(8,128)S(1)} %get-tuple-element.35.refs_0_), channel_id=1, source_target_pairs={{0,24},{4,28},{8,16},{12,20},{16,8},{20,12},{24,0},{28,4},{1,25},{... | collective-permute-start | bytes 208904 | tf_op jit(solution)/shard_map/ppermute | solution.py:289
  33.1 7.0 %collective-permute-start.12 = (f32[136,128]{1,0:T(8,128)S(1)}, f32[136,128]{1,0:T(8,128)S(1)}, u32[]{:S(2)}, u32[]{:S(2)}) collective-permute-start(f32[136,128]{1,0:T(8,128)S(1)} %get-tuple-element.35.refs_0_), channel_id=1, source_target_pairs={{0,16},{4,20},{8,24},{12,28},{16,0},{20,4},{24,8},{28,12},{1,17},{... | collective-permute-start | bytes 208904 | tf_op jit(solution)/shard_map/ppermute | solution.py:289
  33.2 8.0 %collective-permute-start.13 = (f32[136,128]{1,0:T(8,128)S(1)}, f32[136,128]{1,0:T(8,128)S(1)}, u32[]{:S(2)}, u32[]{:S(2)}) collective-permute-start(f32[136,128]{1,0:T(8,128)S(1)} %get-tuple-element.35.refs_0_), channel_id=1, source_target_pairs={{0,12},{4,8},{8,4},{12,0},{16,28},{20,24},{24,20},{28,16},{1,13},{... | collective-permute-start | bytes 208904 | tf_op jit(solution)/shard_map/ppermute | solution.py:289
  36.0 5.2 %collective-permute-start.14 = (f32[136,128]{1,0:T(8,128)S(1)}, f32[136,128]{1,0:T(8,128)S(1)}, u32[]{:S(2)}, u32[]{:S(2)}) collective-permute-start(f32[136,128]{1,0:T(8,128)S(1)} %get-tuple-element.35.refs_0_), channel_id=1, source_target_pairs={{0,4},{4,0},{8,12},{12,8},{16,20},{20,16},{24,28},{28,24},{1,5},{5... | collective-permute-start | bytes 208904 | tf_op jit(solution)/shard_map/ppermute | solution.py:289
  36.5 5.0 %collective-permute-start.15 = (f32[136,128]{1,0:T(8,128)S(1)}, f32[136,128]{1,0:T(8,128)S(1)}, u32[]{:S(2)}, u32[]{:S(2)}) collective-permute-start(f32[136,128]{1,0:T(8,128)S(1)} %get-tuple-element.35.refs_0_), channel_id=1, source_target_pairs={{0,8},{4,12},{8,0},{12,4},{16,24},{20,28},{24,16},{28,20},{1,9},{5... | collective-permute-start | bytes 208904 | tf_op jit(solution)/shard_map/ppermute | solution.py:289
  37.7 4.3 %collective-permute-start.16 = (f32[136,128]{1,0:T(8,128)S(1)}, f32[136,128]{1,0:T(8,128)S(1)}, u32[]{:S(2)}, u32[]{:S(2)}) collective-permute-start(f32[136,128]{1,0:T(8,128)S(1)} %collective-permute-done.11.refs_1_), channel_id=1, source_target_pairs={{0,4},{4,0},{8,12},{12,8},{16,20},{20,16},{24,28},{28,24},{1,5},{5... | collective-permute-start | bytes 208904 | tf_op jit(solution)/shard_map/ppermute | solution.py:289
  40.1 4.3 %collective-permute-start.17 = (f32[136,128]{1,0:T(8,128)S(1)}, f32[136,128]{1,0:T(8,128)S(1)}, u32[]{:S(2)}, u32[]{:S(2)}) collective-permute-start(f32[136,128]{1,0:T(8,128)S(1)} %collective-permute-done.12.refs_2_), channel_id=1, source_target_pairs={{0,4},{4,0},{8,12},{12,8},{16,20},{20,16},{24,28},{28,24},{1,5},{5... | collective-permute-start | bytes 208904 | tf_op jit(solution)/shard_map/ppermute | solution.py:289
  45.4 1.2 %collective-permute-start.18 = (f32[24,128]{1,0:T(8,128)S(1)}, f32[24,128]{1,0:T(8,128)S(1)}, u32[]{:S(2)}, u32[]{:S(2)}) collective-permute-start(f32[24,128]{1,0:T(8,128)S(1)} %get-tuple-element.41), channel_id=1, source_target_pairs={{0,1},{1,0},{2,3},{3,2},{4,5},{5,4},{6,7},{7,6},{8,9},{9,8},{10,11... | collective-permute-start | bytes 36872 | tf_op jit(solution)/shard_map/ppermute | solution.py:289
  46.6 3.1 %collective-permute-start.19 = (f32[24,128]{1,0:T(8,128)S(1)}, f32[24,128]{1,0:T(8,128)S(1)}, u32[]{:S(2)}, u32[]{:S(2)}) collective-permute-start(f32[24,128]{1,0:T(8,128)S(1)} %add.20.refs_0_), channel_id=1, source_target_pairs={{0,3},{1,2},{2,1},{3,0},{4,7},{5,6},{6,5},{7,4},{8,11},{9,10},{10,... | collective-permute-start | bytes 36872 | tf_op jit(solution)/shard_map/ppermute | solution.py:289
  49.8 4.9 %collective-permute-start.22 = (f32[8,128]{1,0:T(8,128)S(1)}, f32[8,128]{1,0:T(8,128)S(1)}, u32[]{:S(2)}, u32[]{:S(2)}) collective-permute-start(f32[8,128]{1,0:T(8,128)S(1)} %shard_map.75), channel_id=1, source_target_pairs={{0,25},{1,24},{2,27},{3,26},{4,29},{5,28},{6,31},{7,30},{8,17},{9,... | collective-permute-start | bytes 12296 | tf_op jit(solution)/shard_map/ppermute | solution.py:299
  51.7 4.0 %collective-permute-start.21 = (f32[8,128]{1,0:T(8,128)S(1)}, f32[8,128]{1,0:T(8,128)S(1)}, u32[]{:S(2)}, u32[]{:S(2)}) collective-permute-start(f32[8,128]{1,0:T(8,128)S(1)} %shard_map.75), channel_id=1, source_target_pairs={{0,17},{1,16},{2,19},{3,18},{4,21},{5,20},{6,23},{7,22},{8,25},{9,... | collective-permute-start | bytes 12296 | tf_op jit(solution)/shard_map/ppermute | solution.py:299
  51.7 4.0 %collective-permute-start.20 = (f32[8,128]{1,0:T(8,128)S(1)}, f32[8,128]{1,0:T(8,128)S(1)}, u32[]{:S(2)}, u32[]{:S(2)}) collective-permute-start(f32[8,128]{1,0:T(8,128)S(1)} %shard_map.75), channel_id=1, source_target_pairs={{0,9},{1,8},{2,11},{3,10},{4,13},{5,12},{6,15},{7,14},{8,1},{9,0},... | collective-permute-start | bytes 12296 | tf_op jit(solution)/shard_map/ppermute | solution.py:299
  55.7 3.1 %collective-permute-start.23 = (f32[8,128]{1,0:T(8,128)S(1)}, f32[8,128]{1,0:T(8,128)S(1)}, u32[]{:S(2)}, u32[]{:S(2)}) collective-permute-start(f32[8,128]{1,0:T(8,128)S(1)} %add_add_fusion.refs_0_), channel_id=1, source_target_pairs={{0,5},{1,4},{2,7},{3,6},{4,1},{5,0},{6,3},{7,2},{8,13},{9,12},{10,... | collective-permute-start | bytes 12296 | tf_op jit(solution)/shard_map/ppermute | solution.py:299

commit v10 on v9

--- a/solution.py
+++ b/solution.py
@@ -100,17 +100,20 @@
     load.start()
     for small in smalls:
         small.wait()
-    for t in range(tiles):
+    def gather(t, carry):
         count = live[0, t]
+        base = pl.multiple_of(t * slots, SUB)
         for j in range(slots):
-            slot = t * slots + j
             column = columns[j, t]
             used = j < count
             row = weights_here[pl.ds(column, 1), :]
-            picked[slot : slot + 1, :] = jnp.where(used, row, 0.0)
-            ids[slot : slot + 1, :] = jnp.full(
+            picked[pl.ds(base + j, 1), :] = jnp.where(used, row, 0.0)
+            ids[pl.ds(base + j, 1), :] = jnp.full(
                 (1, width), jnp.where(used, column, -2), jnp.int32
             ).astype(F32)
+        return carry
+
+    lax.fori_loop(0, tiles, gather, 0)
     offset = pl.multiple_of(lax.axis_index("inst") * share, SUB)
     own[...] = weights_here[pl.ds(offset, share), :]
     load.wait()
@@ -415,7 +418,7 @@
     )
     step = call(
         last_kernel,
-        near((share, width)),
+        jax.ShapeDtypeStruct((share, width), F32),
         (known, gradient, next_share, *inst_sum_parts(scalars)),
     )
     return (step, gradient)

time: 59.7 us -> 59.7 us (level)
  Pallas kernels: 7.58 us -> 8.24 us
  local copies, waits for them, and re-layouts: 1.32 us -> 0.66 us
    unnamed x4 -> x3, local copies, waits for them, and re-layouts: 1.32 us -> 0.66 us
    pallas_call x9, Pallas kernels: 7.58 us -> 8.24 us  [call(): pl.pallas_call(kernel, out_shape=out_shape, in_specs=in_specs, out_specs=...]
where the time goes in v10:
time: 59.7 us; the launch traced here: 59.5 us
  starting transfers between devices  30.5 us (51%)
  waiting for transfers between devices  19.4 us (32%)
  Pallas kernels  8.24 us (14%)
  between operations  0.72 us (1%)
  local copies, waits for them, and re-layouts  0.66 us (1%)
    ppermute x20, starting transfers between devices, swap(): return lax.ppermute(array, axis, [(i, i ^ distance) for i in range(size)])  25.1 us
    ppermute x20, waiting for transfers between devices, swap(): return lax.ppermute(array, axis, [(i, i ^ distance) for i in range(size)])  16.6 us
    pallas_call x9, Pallas kernels, call(): pl.pallas_call(kernel, out_shape=out_shape, in_specs=in_specs, out_specs=...  8.24 us
    ppermute x4, starting transfers between devices, swap_both(): return lax.ppermute(array, ('inst', 'feat'), pairs)  5.46 us
    ppermute x4, waiting for transfers between devices, swap_both(): return lax.ppermute(array, ('inst', 'feat'), pairs)  2.78 us
  transfers between devices with their start and end apart: 24, of which 17 were waited for; matrix products, arithmetic and copies ran while one was open for 1% of the time, Pallas kernels for 1%

profile of v10, /device:TPU:0, one launch (start us, length us, event | category | flops | bytes accessed | tf_op | source)
XLA Modules:
  0.0 59.5 jit_solution(646741903457600735)
XLA Ops:
  0.6 3.3 %shard_map.68 = (bf16[16,8,128,128]{3,2,1,0:T(8,128)(2,1)S(1)}, f32[128,128]{1,0:T(8,128)S(1)}, f32[128,128]{1,0:T(8,128)S(1)}, f32[256,128]{1,0:T(8,128)S(1)}, f32[16,128]{1,0:T(8,128)S(1)}) custom-call(s32[8,16]{1,0:T(8,128)} %bitcast.4, s32[1,16]{1,0:T(1,128)} %bitcast.5, f32[2048,128]{1,0:T(8,128)} %weights.1, bf16[16,8,128,128]{3,2,1,0:T(8,128)(2,1)} %values_in.1), custom_call_target="tpu_custom_call" | custom-call | tf_op jit(solution)/shard_map/pallas_call | solution.py:280
  4.5 0.8 %collective-permute-done = f32[16,128]{1,0:T(8,128)S(1)} collective-permute-done((f32[16,128]{1,0:T(8,128)S(1)}, f32[16,128]{1,0:T(8,128)S(1)}, u32[]{:S(2)}, u32[]{:S(2)}) %collective-permute-start) | collective-permute-done | bytes 8224 | tf_op jit(solution)/shard_map/ppermute | solution.py:292
  5.3 2.6 %collective-permute-start.1 = (f32[16,128]{1,0:T(8,128)S(1)}, f32[16,128]{1,0:T(8,128)S(1)}, u32[]{:S(2)}, u32[]{:S(2)}) collective-permute-start(f32[16,128]{1,0:T(8,128)S(1)} %add.18.refs_0_), channel_id=1, source_target_pairs={{0,3},{1,2},{2,1},{3,0},{4,7},{5,6},{6,5},{7,4},{8,11},{9,10},{10,... | collective-permute-start | bytes 24584 | tf_op jit(solution)/shard_map/ppermute | solution.py:292
  7.9 1.4 %collective-permute-done.1.refs_1_ = f32[16,128]{1,0:T(8,128)S(1)} collective-permute-done((f32[16,128]{1,0:T(8,128)S(1)}, f32[16,128]{1,0:T(8,128)S(1)}, u32[]{:S(2)}, u32[]{:S(2)}) %collective-permute-start.1) | collective-permute-done | bytes 8224 | tf_op jit(solution)/shard_map/ppermute | solution.py:292
  9.9 4.1 %collective-permute-start.2 = (f32[136,128]{1,0:T(8,128)S(1)}, f32[136,128]{1,0:T(8,128)S(1)}, u32[]{:S(2)}, u32[]{:S(2)}) collective-permute-start(f32[136,128]{1,0:T(8,128)S(1)} %get-tuple-element.27.refs_0_), channel_id=1, source_target_pairs={{0,24},{4,28},{8,16},{12,20},{16,8},{20,12},{24,0},{28,4},{1,25},{... | collective-permute-start | bytes 208904 | tf_op jit(solution)/shard_map/ppermute | solution.py:292
  14.1 1.7 %collective-permute-start.4 = (f32[136,128]{1,0:T(8,128)S(1)}, f32[136,128]{1,0:T(8,128)S(1)}, u32[]{:S(2)}, u32[]{:S(2)}) collective-permute-start(f32[136,128]{1,0:T(8,128)S(1)} %get-tuple-element.27.refs_0_), channel_id=1, source_target_pairs={{0,12},{4,8},{8,4},{12,0},{16,28},{20,24},{24,20},{28,16},{1,13},{... | collective-permute-start | bytes 208904 | tf_op jit(solution)/shard_map/ppermute | solution.py:292
  16.2 1.4 %collective-permute-start.6 = (f32[136,128]{1,0:T(8,128)S(1)}, f32[136,128]{1,0:T(8,128)S(1)}, u32[]{:S(2)}, u32[]{:S(2)}) collective-permute-start(f32[136,128]{1,0:T(8,128)S(1)} %get-tuple-element.27.refs_0_), channel_id=1, source_target_pairs={{0,8},{4,12},{8,0},{12,4},{16,24},{20,28},{24,16},{28,20},{1,9},{5... | collective-permute-start | bytes 208904 | tf_op jit(solution)/shard_map/ppermute | solution.py:292
  17.5 1.5 %collective-permute-start.7 = (f32[136,128]{1,0:T(8,128)S(1)}, f32[136,128]{1,0:T(8,128)S(1)}, u32[]{:S(2)}, u32[]{:S(2)}) collective-permute-start(f32[136,128]{1,0:T(8,128)S(1)} %collective-permute-done.2.refs_1_), channel_id=1, source_target_pairs={{0,4},{4,0},{8,12},{12,8},{16,20},{20,16},{24,28},{28,24},{1,5},{5... | collective-permute-start | bytes 208904 | tf_op jit(solution)/shard_map/ppermute | solution.py:292
  19.1 1.3 %collective-permute-done.3.refs_2_ = f32[136,128]{1,0:T(8,128)S(1)} collective-permute-done((f32[136,128]{1,0:T(8,128)S(1)}, f32[136,128]{1,0:T(8,128)S(1)}, u32[]{:S(2)}, u32[]{:S(2)}) %collective-permute-start.3) | collective-permute-done | bytes 69664 | tf_op jit(solution)/shard_map/ppermute | solution.py:292
  20.3 1.5 %collective-permute-start.8 = (f32[136,128]{1,0:T(8,128)S(1)}, f32[136,128]{1,0:T(8,128)S(1)}, u32[]{:S(2)}, u32[]{:S(2)}) collective-permute-start(f32[136,128]{1,0:T(8,128)S(1)} %collective-permute-done.3.refs_2_), channel_id=1, source_target_pairs={{0,4},{4,0},{8,12},{12,8},{16,20},{20,16},{24,28},{28,24},{1,5},{5... | collective-permute-start | bytes 208904 | tf_op jit(solution)/shard_map/ppermute | solution.py:292
  22.4 2.3 %collective-permute-done.8.refs_1_ = f32[136,128]{1,0:T(8,128)S(1)} collective-permute-done((f32[136,128]{1,0:T(8,128)S(1)}, f32[136,128]{1,0:T(8,128)S(1)}, u32[]{:S(2)}, u32[]{:S(2)}) %collective-permute-start.8) | collective-permute-done | bytes 69664 | tf_op jit(solution)/shard_map/ppermute | solution.py:292
  24.7 1.0 %shard_map.71 = (f32[256,128]{1,0:T(8,128)S(1)}, f32[128,128]{1,0:T(8,128)S(1)}, bf16[384,256]{1,0:T(8,128)(2,1)S(1)}, f32[24,128]{1,0:T(8,128)S(1)}) custom-call(bf16[16,8,128,128]{3,2,1,0:T(8,128)(2,1)S(1)} %get-tuple-element.22.values, f32[128,128]{1,0:T(8,128)S(1)} %get-tuple-element.23.ids, f32[128,128]{1,0:T(8,128)S(1)} %get-tuple-element.24.picked, ...), custom_call_target="tpu_custom_call" | custom-call | tf_op jit(solution)/shard_map/pallas_call | solution.py:280
  25.7 1.2 %collective-permute-done.9 = f32[24,128]{1,0:T(8,128)S(1)} collective-permute-done((f32[24,128]{1,0:T(8,128)S(1)}, f32[24,128]{1,0:T(8,128)S(1)}, u32[]{:S(2)}, u32[]{:S(2)}) %collective-permute-start.9) | collective-permute-done | bytes 12320 | tf_op jit(solution)/shard_map/ppermute | solution.py:292
  26.9 1.3 %collective-permute-start.10 = (f32[24,128]{1,0:T(8,128)S(1)}, f32[24,128]{1,0:T(8,128)S(1)}, u32[]{:S(2)}, u32[]{:S(2)}) collective-permute-start(f32[24,128]{1,0:T(8,128)S(1)} %add.19.refs_0_), channel_id=1, source_target_pairs={{0,3},{1,2},{2,1},{3,0},{4,7},{5,6},{6,5},{7,4},{8,11},{9,10},{10,... | collective-permute-start | bytes 36872 | tf_op jit(solution)/shard_map/ppermute | solution.py:292
  28.1 1.9 %collective-permute-done.10.refs_1_ = f32[24,128]{1,0:T(8,128)S(1)} collective-permute-done((f32[24,128]{1,0:T(8,128)S(1)}, f32[24,128]{1,0:T(8,128)S(1)}, u32[]{:S(2)}, u32[]{:S(2)}) %collective-permute-start.10) | collective-permute-done | bytes 12320 | tf_op jit(solution)/shard_map/ppermute | solution.py:292
  30.6 2.4 %collective-permute-start.11 = (f32[136,128]{1,0:T(8,128)S(1)}, f32[136,128]{1,0:T(8,128)S(1)}, u32[]{:S(2)}, u32[]{:S(2)}) collective-permute-start(f32[136,128]{1,0:T(8,128)S(1)} %get-tuple-element.35.refs_0_), channel_id=1, source_target_pairs={{0,24},{4,28},{8,16},{12,20},{16,8},{20,12},{24,0},{28,4},{1,25},{... | collective-permute-start | bytes 208904 | tf_op jit(solution)/shard_map/ppermute | solution.py:292
  33.2 2.8 %collective-permute-start.13 = (f32[136,128]{1,0:T(8,128)S(1)}, f32[136,128]{1,0:T(8,128)S(1)}, u32[]{:S(2)}, u32[]{:S(2)}) collective-permute-start(f32[136,128]{1,0:T(8,128)S(1)} %get-tuple-element.35.refs_0_), channel_id=1, source_target_pairs={{0,12},{4,8},{8,4},{12,0},{16,28},{20,24},{24,20},{28,16},{1,13},{... | collective-permute-start | bytes 208904 | tf_op jit(solution)/shard_map/ppermute | solution.py:292
  36.7 1.0 %collective-permute-done.11.refs_1_ = f32[136,128]{1,0:T(8,128)S(1)} collective-permute-done((f32[136,128]{1,0:T(8,128)S(1)}, f32[136,128]{1,0:T(8,128)S(1)}, u32[]{:S(2)}, u32[]{:S(2)}) %collective-permute-start.11) | collective-permute-done | bytes 69664 | tf_op jit(solution)/shard_map/ppermute | solution.py:292
  37.7 1.4 %collective-permute-start.16 = (f32[136,128]{1,0:T(8,128)S(1)}, f32[136,128]{1,0:T(8,128)S(1)}, u32[]{:S(2)}, u32[]{:S(2)}) collective-permute-start(f32[136,128]{1,0:T(8,128)S(1)} %collective-permute-done.11.refs_1_), channel_id=1, source_target_pairs={{0,4},{4,0},{8,12},{12,8},{16,20},{20,16},{24,28},{28,24},{1,5},{5... | collective-permute-start | bytes 208904 | tf_op jit(solution)/shard_map/ppermute | solution.py:292
  39.1 1.0 %collective-permute-done.12.refs_2_ = f32[136,128]{1,0:T(8,128)S(1)} collective-permute-done((f32[136,128]{1,0:T(8,128)S(1)}, f32[136,128]{1,0:T(8,128)S(1)}, u32[]{:S(2)}, u32[]{:S(2)}) %collective-permute-start.12) | collective-permute-done | bytes 69664 | tf_op jit(solution)/shard_map/ppermute | solution.py:292
  40.1 1.2 %collective-permute-start.17 = (f32[136,128]{1,0:T(8,128)S(1)}, f32[136,128]{1,0:T(8,128)S(1)}, u32[]{:S(2)}, u32[]{:S(2)}) collective-permute-start(f32[136,128]{1,0:T(8,128)S(1)} %collective-permute-done.12.refs_2_), channel_id=1, source_target_pairs={{0,4},{4,0},{8,12},{12,8},{16,20},{20,16},{24,28},{28,24},{1,5},{5... | collective-permute-start | bytes 208904 | tf_op jit(solution)/shard_map/ppermute | solution.py:292
  42.0 2.4 %collective-permute-done.17.refs_1_ = f32[136,128]{1,0:T(8,128)S(1)} collective-permute-done((f32[136,128]{1,0:T(8,128)S(1)}, f32[136,128]{1,0:T(8,128)S(1)}, u32[]{:S(2)}, u32[]{:S(2)}) %collective-permute-start.17) | collective-permute-done | bytes 69664 | tf_op jit(solution)/shard_map/ppermute | solution.py:292
  44.4 1.0 %shard_map.74 = (f32[256,128]{1,0:T(8,128)S(1)}, f32[8,128]{1,0:T(8,128)S(1)}, f32[24,128]{1,0:T(8,128)S(1)}) custom-call(bf16[16,8,128,128]{3,2,1,0:T(8,128)(2,1)S(1)} %get-tuple-element.22.values, bf16[384,256]{1,0:T(8,128)(2,1)S(1)} %get-tuple-element.29.onehot, f32[128,128]{1,0:T(8,128)S(1)} %get-tuple-element.30.start_slot, ...), custom_call_target="tpu_custom_call" | custom-call | tf_op jit(solution)/shard_map/pallas_call | solution.py:280
  45.4 1.2 %collective-permute-done.18 = f32[24,128]{1,0:T(8,128)S(1)} collective-permute-done((f32[24,128]{1,0:T(8,128)S(1)}, f32[24,128]{1,0:T(8,128)S(1)}, u32[]{:S(2)}, u32[]{:S(2)}) %collective-permute-start.18) | collective-permute-done | bytes 12320 | tf_op jit(solution)/shard_map/ppermute | solution.py:292
  46.6 1.3 %collective-permute-start.19 = (f32[24,128]{1,0:T(8,128)S(1)}, f32[24,128]{1,0:T(8,128)S(1)}, u32[]{:S(2)}, u32[]{:S(2)}) collective-permute-start(f32[24,128]{1,0:T(8,128)S(1)} %add.20.refs_0_), channel_id=1, source_target_pairs={{0,3},{1,2},{2,1},{3,0},{4,7},{5,6},{6,5},{7,4},{8,11},{9,10},{10,... | collective-permute-start | bytes 36872 | tf_op jit(solution)/shard_map/ppermute | solution.py:292
  47.9 1.9 %collective-permute-done.19.refs_1_ = f32[24,128]{1,0:T(8,128)S(1)} collective-permute-done((f32[24,128]{1,0:T(8,128)S(1)}, f32[24,128]{1,0:T(8,128)S(1)}, u32[]{:S(2)}, u32[]{:S(2)}) %collective-permute-start.19) | collective-permute-done | bytes 12320 | tf_op jit(solution)/shard_map/ppermute | solution.py:292
  49.8 1.9 %collective-permute-start.22 = (f32[8,128]{1,0:T(8,128)S(1)}, f32[8,128]{1,0:T(8,128)S(1)}, u32[]{:S(2)}, u32[]{:S(2)}) collective-permute-start(f32[8,128]{1,0:T(8,128)S(1)} %shard_map.75), channel_id=1, source_target_pairs={{0,25},{1,24},{2,27},{3,26},{4,29},{5,28},{6,31},{7,30},{8,17},{9,... | collective-permute-start | bytes 12296 | tf_op jit(solution)/shard_map/ppermute | solution.py:302
  51.7 2.1 %collective-permute-start.20 = (f32[8,128]{1,0:T(8,128)S(1)}, f32[8,128]{1,0:T(8,128)S(1)}, u32[]{:S(2)}, u32[]{:S(2)}) collective-permute-start(f32[8,128]{1,0:T(8,128)S(1)} %shard_map.75), channel_id=1, source_target_pairs={{0,9},{1,8},{2,11},{3,10},{4,13},{5,12},{6,15},{7,14},{8,1},{9,0},... | collective-permute-start | bytes 12296 | tf_op jit(solution)/shard_map/ppermute | solution.py:302
  53.8 1.0 %collective-permute-done.22 = f32[8,128]{1,0:T(8,128)S(1)} collective-permute-done((f32[8,128]{1,0:T(8,128)S(1)}, f32[8,128]{1,0:T(8,128)S(1)}, u32[]{:S(2)}, u32[]{:S(2)}) %collective-permute-start.22) | collective-permute-done | bytes 4128 | tf_op jit(solution)/shard_map/ppermute | solution.py:302
  54.7 0.9 %collective-permute-done.21 = f32[8,128]{1,0:T(8,128)S(1)} collective-permute-done((f32[8,128]{1,0:T(8,128)S(1)}, f32[8,128]{1,0:T(8,128)S(1)}, u32[]{:S(2)}, u32[]{:S(2)}) %collective-permute-start.21) | collective-permute-done | bytes 4128 | tf_op jit(solution)/shard_map/ppermute | solution.py:302
  55.7 1.5 %collective-permute-start.23 = (f32[8,128]{1,0:T(8,128)S(1)}, f32[8,128]{1,0:T(8,128)S(1)}, u32[]{:S(2)}, u32[]{:S(2)}) collective-permute-start(f32[8,128]{1,0:T(8,128)S(1)} %add_add_fusion.refs_0_), channel_id=1, source_target_pairs={{0,5},{1,4},{2,7},{3,6},{4,1},{5,0},{6,3},{7,2},{8,13},{9,12},{10,... | collective-permute-start | bytes 12296 | tf_op jit(solution)/shard_map/ppermute | solution.py:302
  57.8 0.9 %collective-permute-done.23.refs_1_ = f32[8,128]{1,0:T(8,128)S(1)} collective-permute-done((f32[8,128]{1,0:T(8,128)S(1)}, f32[8,128]{1,0:T(8,128)S(1)}, u32[]{:S(2)}, u32[]{:S(2)}) %collective-permute-start.23) | collective-permute-done | bytes 4128 | tf_op jit(solution)/shard_map/ppermute | solution.py:302
  (32 shorter events, 5.9 us)
Async XLA Ops:
  0.6 8.7 %copy-start = (s32[2048]{0:T(1024)S(1)}, s32[2048]{0:T(1024)}, u32[]{:S(2)}) copy-start(s32[2048]{0:T(1024)} %param.8) | copy-start | bytes 24580
  4.0 1.3 %collective-permute-start = (f32[16,128]{1,0:T(8,128)S(1)}, f32[16,128]{1,0:T(8,128)S(1)}, u32[]{:S(2)}, u32[]{:S(2)}) collective-permute-start(f32[16,128]{1,0:T(8,128)S(1)} %get-tuple-element.26), channel_id=1, source_target_pairs={{0,1},{1,0},{2,3},{3,2},{4,5},{5,4},{6,7},{7,6},{8,9},{9,8},{10,11... | collective-permute-start | bytes 24584 | tf_op jit(solution)/shard_map/ppermute | solution.py:292
  5.3 4.0 %collective-permute-start.1 = (f32[16,128]{1,0:T(8,128)S(1)}, f32[16,128]{1,0:T(8,128)S(1)}, u32[]{:S(2)}, u32[]{:S(2)}) collective-permute-start(f32[16,128]{1,0:T(8,128)S(1)} %add.18.refs_0_), channel_id=1, source_target_pairs={{0,3},{1,2},{2,1},{3,0},{4,7},{5,6},{6,5},{7,4},{8,11},{9,10},{10,... | collective-permute-start | bytes 24584 | tf_op jit(solution)/shard_map/ppermute | solution.py:292
  9.9 7.6 %collective-permute-start.2 = (f32[136,128]{1,0:T(8,128)S(1)}, f32[136,128]{1,0:T(8,128)S(1)}, u32[]{:S(2)}, u32[]{:S(2)}) collective-permute-start(f32[136,128]{1,0:T(8,128)S(1)} %get-tuple-element.27.refs_0_), channel_id=1, source_target_pairs={{0,24},{4,28},{8,16},{12,20},{16,8},{20,12},{24,0},{28,4},{1,25},{... | collective-permute-start | bytes 208904 | tf_op jit(solution)/shard_map/ppermute | solution.py:292
  14.1 6.3 %collective-permute-start.3 = (f32[136,128]{1,0:T(8,128)S(1)}, f32[136,128]{1,0:T(8,128)S(1)}, u32[]{:S(2)}, u32[]{:S(2)}) collective-permute-start(f32[136,128]{1,0:T(8,128)S(1)} %get-tuple-element.27.refs_0_), channel_id=1, source_target_pairs={{0,16},{4,20},{8,24},{12,28},{16,0},{20,4},{24,8},{28,12},{1,17},{... | collective-permute-start | bytes 208904 | tf_op jit(solution)/shard_map/ppermute | solution.py:292
  14.1 7.8 %collective-permute-start.4 = (f32[136,128]{1,0:T(8,128)S(1)}, f32[136,128]{1,0:T(8,128)S(1)}, u32[]{:S(2)}, u32[]{:S(2)}) collective-permute-start(f32[136,128]{1,0:T(8,128)S(1)} %get-tuple-element.27.refs_0_), channel_id=1, source_target_pairs={{0,12},{4,8},{8,4},{12,0},{16,28},{20,24},{24,20},{28,16},{1,13},{... | collective-permute-start | bytes 208904 | tf_op jit(solution)/shard_map/ppermute | solution.py:292
  15.8 6.1 %collective-permute-start.5 = (f32[136,128]{1,0:T(8,128)S(1)}, f32[136,128]{1,0:T(8,128)S(1)}, u32[]{:S(2)}, u32[]{:S(2)}) collective-permute-start(f32[136,128]{1,0:T(8,128)S(1)} %get-tuple-element.27.refs_0_), channel_id=1, source_target_pairs={{0,4},{4,0},{8,12},{12,8},{16,20},{20,16},{24,28},{28,24},{1,5},{5... | collective-permute-start | bytes 208904 | tf_op jit(solution)/shard_map/ppermute | solution.py:292
  16.2 5.8 %collective-permute-start.6 = (f32[136,128]{1,0:T(8,128)S(1)}, f32[136,128]{1,0:T(8,128)S(1)}, u32[]{:S(2)}, u32[]{:S(2)}) collective-permute-start(f32[136,128]{1,0:T(8,128)S(1)} %get-tuple-element.27.refs_0_), channel_id=1, source_target_pairs={{0,8},{4,12},{8,0},{12,4},{16,24},{20,28},{24,16},{28,20},{1,9},{5... | collective-permute-start | bytes 208904 | tf_op jit(solution)/shard_map/ppermute | solution.py:292
  17.5 4.8 %collective-permute-start.7 = (f32[136,128]{1,0:T(8,128)S(1)}, f32[136,128]{1,0:T(8,128)S(1)}, u32[]{:S(2)}, u32[]{:S(2)}) collective-permute-start(f32[136,128]{1,0:T(8,128)S(1)} %collective-permute-done.2.refs_1_), channel_id=1, source_target_pairs={{0,4},{4,0},{8,12},{12,8},{16,20},{20,16},{24,28},{28,24},{1,5},{5... | collective-permute-start | bytes 208904 | tf_op jit(solution)/shard_map/ppermute | solution.py:292
  20.3 4.3 %collective-permute-start.8 = (f32[136,128]{1,0:T(8,128)S(1)}, f32[136,128]{1,0:T(8,128)S(1)}, u32[]{:S(2)}, u32[]{:S(2)}) collective-permute-start(f32[136,128]{1,0:T(8,128)S(1)} %collective-permute-done.3.refs_2_), channel_id=1, source_target_pairs={{0,4},{4,0},{8,12},{12,8},{16,20},{20,16},{24,28},{28,24},{1,5},{5... | collective-permute-start | bytes 208904 | tf_op jit(solution)/shard_map/ppermute | solution.py:292
  25.6 1.2 %collective-permute-start.9 = (f32[24,128]{1,0:T(8,128)S(1)}, f32[24,128]{1,0:T(8,128)S(1)}, u32[]{:S(2)}, u32[]{:S(2)}) collective-permute-start(f32[24,128]{1,0:T(8,128)S(1)} %get-tuple-element.34), channel_id=1, source_target_pairs={{0,1},{1,0},{2,3},{3,2},{4,5},{5,4},{6,7},{7,6},{8,9},{9,8},{10,11... | collective-permute-start | bytes 36872 | tf_op jit(solution)/shard_map/ppermute | solution.py:292
  26.9 3.1 %collective-permute-start.10 = (f32[24,128]{1,0:T(8,128)S(1)}, f32[24,128]{1,0:T(8,128)S(1)}, u32[]{:S(2)}, u32[]{:S(2)}) collective-permute-start(f32[24,128]{1,0:T(8,128)S(1)} %add.19.refs_0_), channel_id=1, source_target_pairs={{0,3},{1,2},{2,1},{3,0},{4,7},{5,6},{6,5},{7,4},{8,11},{9,10},{10,... | collective-permute-start | bytes 36872 | tf_op jit(solution)/shard_map/ppermute | solution.py:292
  30.6 7.0 %collective-permute-start.11 = (f32[136,128]{1,0:T(8,128)S(1)}, f32[136,128]{1,0:T(8,128)S(1)}, u32[]{:S(2)}, u32[]{:S(2)}) collective-permute-start(f32[136,128]{1,0:T(8,128)S(1)} %get-tuple-element.35.refs_0_), channel_id=1, source_target_pairs={{0,24},{4,28},{8,16},{12,20},{16,8},{20,12},{24,0},{28,4},{1,25},{... | collective-permute-start | bytes 208904 | tf_op jit(solution)/shard_map/ppermute | solution.py:292
  33.1 7.0 %collective-permute-start.12 = (f32[136,128]{1,0:T(8,128)S(1)}, f32[136,128]{1,0:T(8,128)S(1)}, u32[]{:S(2)}, u32[]{:S(2)}) collective-permute-start(f32[136,128]{1,0:T(8,128)S(1)} %get-tuple-element.35.refs_0_), channel_id=1, source_target_pairs={{0,16},{4,20},{8,24},{12,28},{16,0},{20,4},{24,8},{28,12},{1,17},{... | collective-permute-start | bytes 208904 | tf_op jit(solution)/shard_map/ppermute | solution.py:292
  33.2 8.0 %collective-permute-start.13 = (f32[136,128]{1,0:T(8,128)S(1)}, f32[136,128]{1,0:T(8,128)S(1)}, u32[]{:S(2)}, u32[]{:S(2)}) collective-permute-start(f32[136,128]{1,0:T(8,128)S(1)} %get-tuple-element.35.refs_0_), channel_id=1, source_target_pairs={{0,12},{4,8},{8,4},{12,0},{16,28},{20,24},{24,20},{28,16},{1,13},{... | collective-permute-start | bytes 208904 | tf_op jit(solution)/shard_map/ppermute | solution.py:292
  36.0 5.2 %collective-permute-start.14 = (f32[136,128]{1,0:T(8,128)S(1)}, f32[136,128]{1,0:T(8,128)S(1)}, u32[]{:S(2)}, u32[]{:S(2)}) collective-permute-start(f32[136,128]{1,0:T(8,128)S(1)} %get-tuple-element.35.refs_0_), channel_id=1, source_target_pairs={{0,4},{4,0},{8,12},{12,8},{16,20},{20,16},{24,28},{28,24},{1,5},{5... | collective-permute-start | bytes 208904 | tf_op jit(solution)/shard_map/ppermute | solution.py:292
  36.5 5.0 %collective-permute-start.15 = (f32[136,128]{1,0:T(8,128)S(1)}, f32[136,128]{1,0:T(8,128)S(1)}, u32[]{:S(2)}, u32[]{:S(2)}) collective-permute-start(f32[136,128]{1,0:T(8,128)S(1)} %get-tuple-element.35.refs_0_), channel_id=1, source_target_pairs={{0,8},{4,12},{8,0},{12,4},{16,24},{20,28},{24,16},{28,20},{1,9},{5... | collective-permute-start | bytes 208904 | tf_op jit(solution)/shard_map/ppermute | solution.py:292
  37.7 4.3 %collective-permute-start.16 = (f32[136,128]{1,0:T(8,128)S(1)}, f32[136,128]{1,0:T(8,128)S(1)}, u32[]{:S(2)}, u32[]{:S(2)}) collective-permute-start(f32[136,128]{1,0:T(8,128)S(1)} %collective-permute-done.11.refs_1_), channel_id=1, source_target_pairs={{0,4},{4,0},{8,12},{12,8},{16,20},{20,16},{24,28},{28,24},{1,5},{5... | collective-permute-start | bytes 208904 | tf_op jit(solution)/shard_map/ppermute | solution.py:292
  40.1 4.3 %collective-permute-start.17 = (f32[136,128]{1,0:T(8,128)S(1)}, f32[136,128]{1,0:T(8,128)S(1)}, u32[]{:S(2)}, u32[]{:S(2)}) collective-permute-start(f32[136,128]{1,0:T(8,128)S(1)} %collective-permute-done.12.refs_2_), channel_id=1, source_target_pairs={{0,4},{4,0},{8,12},{12,8},{16,20},{20,16},{24,28},{28,24},{1,5},{5... | collective-permute-start | bytes 208904 | tf_op jit(solution)/shard_map/ppermute | solution.py:292
  45.4 1.2 %collective-permute-start.18 = (f32[24,128]{1,0:T(8,128)S(1)}, f32[24,128]{1,0:T(8,128)S(1)}, u32[]{:S(2)}, u32[]{:S(2)}) collective-permute-start(f32[24,128]{1,0:T(8,128)S(1)} %get-tuple-element.41), channel_id=1, source_target_pairs={{0,1},{1,0},{2,3},{3,2},{4,5},{5,4},{6,7},{7,6},{8,9},{9,8},{10,11... | collective-permute-start | bytes 36872 | tf_op jit(solution)/shard_map/ppermute | solution.py:292
  46.6 3.1 %collective-permute-start.19 = (f32[24,128]{1,0:T(8,128)S(1)}, f32[24,128]{1,0:T(8,128)S(1)}, u32[]{:S(2)}, u32[]{:S(2)}) collective-permute-start(f32[24,128]{1,0:T(8,128)S(1)} %add.20.refs_0_), channel_id=1, source_target_pairs={{0,3},{1,2},{2,1},{3,0},{4,7},{5,6},{6,5},{7,4},{8,11},{9,10},{10,... | collective-permute-start | bytes 36872 | tf_op jit(solution)/shard_map/ppermute | solution.py:292
  49.8 4.9 %collective-permute-start.22 = (f32[8,128]{1,0:T(8,128)S(1)}, f32[8,128]{1,0:T(8,128)S(1)}, u32[]{:S(2)}, u32[]{:S(2)}) collective-permute-start(f32[8,128]{1,0:T(8,128)S(1)} %shard_map.75), channel_id=1, source_target_pairs={{0,25},{1,24},{2,27},{3,26},{4,29},{5,28},{6,31},{7,30},{8,17},{9,... | collective-permute-start | bytes 12296 | tf_op jit(solution)/shard_map/ppermute | solution.py:302
  51.7 4.0 %collective-permute-start.21 = (f32[8,128]{1,0:T(8,128)S(1)}, f32[8,128]{1,0:T(8,128)S(1)}, u32[]{:S(2)}, u32[]{:S(2)}) collective-permute-start(f32[8,128]{1,0:T(8,128)S(1)} %shard_map.75), channel_id=1, source_target_pairs={{0,17},{1,16},{2,19},{3,18},{4,21},{5,20},{6,23},{7,22},{8,25},{9,... | collective-permute-start | bytes 12296 | tf_op jit(solution)/shard_map/ppermute | solution.py:302
  51.7 4.0 %collective-permute-start.20 = (f32[8,128]{1,0:T(8,128)S(1)}, f32[8,128]{1,0:T(8,128)S(1)}, u32[]{:S(2)}, u32[]{:S(2)}) collective-permute-start(f32[8,128]{1,0:T(8,128)S(1)} %shard_map.75), channel_id=1, source_target_pairs={{0,9},{1,8},{2,11},{3,10},{4,13},{5,12},{6,15},{7,14},{8,1},{9,0},... | collective-permute-start | bytes 12296 | tf_op jit(solution)/shard_map/ppermute | solution.py:302
  55.7 3.1 %collective-permute-start.23 = (f32[8,128]{1,0:T(8,128)S(1)}, f32[8,128]{1,0:T(8,128)S(1)}, u32[]{:S(2)}, u32[]{:S(2)}) collective-permute-start(f32[8,128]{1,0:T(8,128)S(1)} %add_add_fusion.refs_0_), channel_id=1, source_target_pairs={{0,5},{1,4},{2,7},{3,6},{4,1},{5,0},{6,3},{7,2},{8,13},{9,12},{10,... | collective-permute-start | bytes 12296 | tf_op jit(solution)/shard_map/ppermute | solution.py:302
